TPU v7x, 128 devices: a whole 4x4x4 slice. The times are simulated.
128 devices in a mesh: tm: 8 (over y, z_hi), space: 16 (over x, z_lo, core).
Axes of the slice: x: 4, y: 4, z: 4 (z_hi: 2, z_lo: 2; z = z_hi * 2 + z_lo), core: 2. Of those that a mesh axis runs over, the one named last changes fastest.
Arguments:
- state_old: float32 [8, 128, 64, 1024], P('tm', 'space'), may hold values from -6 to 6
- velocity: float32 [3, 128, 64, 1024], P(None, 'space'), may hold values from -0.12 to 0.12
- diffusivity: float32 [128, 64, 1024], P('space'), may hold values from 0.01 to 0.08
Outputs:
- new_state: float32 [8, 128, 64, 1024], P('tm', 'space')
All inputs are finite; a program needn't handle non-finite values.
Results may differ from a plain program's by a relative error of at most 0.00012.
Values sent between devices are 32-bit elements; how exact they have to be, the bound alone decides.
No kernel may reach another device: no remote copies, remote signals or barrier semaphores. Data moves between devices by JAX's collectives and lax.ppermute only.
A program may use at most 128 MiB of HBM per device.

v0:
```python
import jax
import jax.numpy as jnp
from jax import lax
from jax.sharding import PartitionSpec as P


def extended(block, sides, width):
    for axis, dim in sides:
        count = lax.axis_size(axis)
        forward = [(i, i + 1) for i in range(count - 1)]
        backward = [(target, source) for source, target in forward]
        low = lax.ppermute(
            lax.slice_in_dim(block, block.shape[dim] - width, None, axis=dim), axis, forward
        )
        high = lax.ppermute(lax.slice_in_dim(block, 0, width, axis=dim), axis, backward)
        block = jnp.concatenate([low, block, high], axis=dim)
    return block


def passed_along(value, axis, steps):
    count = lax.axis_size(axis)
    first, last = (max(0, -steps), min(count, count - steps))
    return lax.ppermute(value, axis, [(source, source + steps) for source in range(first, last)])


def pair_table(block_width):
    rows_fine = jnp.arange(block_width)[:, None] // 2
    cols_coarse = jnp.arange(block_width // 2)[None, :]
    return (rows_fine == cols_coarse).astype(jnp.float32)


def restrict(field_now):
    width = field_now.shape[-1]
    block_width = 256
    lead = field_now.shape[:-1]
    blocked = field_now.reshape(lead + (width // block_width, block_width))
    halved_x = jnp.dot(blocked, pair_table(block_width), precision=lax.Precision.HIGHEST)
    halved_x = halved_x.reshape(lead + (width // 2,))
    depth = halved_x.shape[-3]
    height = halved_x.shape[-2]
    outer = halved_x.shape[:-3]
    split_y = halved_x.reshape(outer + (depth, height // 2, 2, width // 2))
    halved_y = split_y[..., 0, :] + split_y[..., 1, :]
    split_z = halved_y.reshape(outer + (depth // 2, 2, height // 2, width // 2))
    halved_z = split_z[..., 0, :, :] + split_z[..., 1, :, :]
    return halved_z * 0.125


def prolong(coarse_field):
    depth, height, width = coarse_field.shape[-3:]
    outer = coarse_field.shape[:-3]
    spread_out = jnp.broadcast_to(
        coarse_field[..., :, None, :, None, :], outer + (depth, 2, height, 2, width)
    )
    spread_out = spread_out.reshape(outer + (2 * depth, 2 * height, width))
    block_width = 128
    lead = spread_out.shape[:-1]
    blocked = spread_out.reshape(lead + (width // block_width, block_width))
    copied = jnp.dot(blocked, pair_table(2 * block_width).T, precision=lax.Precision.HIGHEST)
    return copied.reshape(lead + (2 * width,))


def upwind(velocity_part, centre, behind, forward):
    return jnp.maximum(velocity_part, 0.0) * (centre - behind) + jnp.minimum(velocity_part, 0.0) * (
        forward - centre
    )


def advance(padded, velocity, diffusivity, spacing, time_step):
    centre = padded[1:-1]
    layer_above = padded[2:]
    layer_below = padded[:-2]
    east_cell = jnp.roll(centre, -1, 2)
    west_cell = jnp.roll(centre, 1, 2)
    north_cell = jnp.roll(centre, -1, 1)
    south_cell = jnp.roll(centre, 1, 1)
    spread = (
        east_cell + west_cell + north_cell + south_cell + layer_above + layer_below - 6.0 * centre
    ) / (spacing * spacing)
    drift = (
        upwind(velocity[0], centre, west_cell, east_cell)
        + upwind(velocity[1], centre, south_cell, north_cell)
        + upwind(velocity[2], centre, layer_below, layer_above)
    )
    return centre + time_step * (diffusivity * spread - drift / spacing)


def shards(state_old, velocity, diffusivity):
    time_index = lax.axis_index("tm")
    groups = lax.axis_size("tm")
    start_field = state_old[0]
    coarse_velocity = restrict(velocity)
    coarse_diffusivity = restrict(diffusivity)

    def coarse(coarse_field):
        padded = extended(coarse_field, (("space", 0),), 1)
        return advance(padded, coarse_velocity, coarse_diffusivity, 2.0, 2.0)

    fine_field = start_field
    for sweep_index in range(2):
        padded = extended(fine_field, (("space", 0),), 1)
        fine_field = advance(padded, velocity, diffusivity, 1.0, 1.0)
    own_coarse = restrict(start_field)
    defect = fine_field - prolong(coarse(own_coarse))
    coarse_jump = restrict(defect)

    def relay_turn(turn_index, carried):
        moved = coarse(carried) + coarse_jump
        received = passed_along(moved, "tm", 1)
        return jnp.where(time_index == turn_index + 1, received, carried)

    carried = lax.fori_loop(0, groups - 1, relay_turn, own_coarse)
    result = prolong(coarse(carried)) + defect
    return result[None]


def solution(mesh):
    return jax.shard_map(
        shards,
        mesh=mesh,
        in_specs=(
            P("tm", "space", None, None),
            P(None, "space", None, None),
            P("space", None, None),
        ),
        out_specs=P("tm", "space", None, None),
        check_vma=False,
    )
```

profile of v0, /device:TPU:18, one launch (start us, length us, event | category | flops | bytes accessed | tf_op | source)
XLA Modules:
  0.0 268.2 jit_solution(480987480978406644)
XLA Ops:
  1.9 3.2 %collective-permute-start.3 = (f32[1,64,1024]{2,1,0:T(8,128)}, f32[1,64,1024]{2,1,0:T(8,128)}, u32[]{:S(2)}, u32[]{:S(2)}) collective-permute-start(f32[1,64,1024]{2,1,0:T(8,128)} %get-tuple-element.157), channel_id=1, source_target_pairs={{1,0},{2,1},{3,2},{4,3},{5,4},{6,5},{7,6},{8,7},{9,8},{10,9},{11,1... | collective-permute-start | bytes 786440 | tf_op jit(solution)/shard_map/ppermute | solution.py:15
  7.1 2.2 reshape_squeeze.3
  12.2 4.7 %collective-permute-start.7 = (f32[1,32,512]{2,1,0:T(8,128)S(1)}, f32[1,32,512]{2,1,0:T(8,128)S(1)}, u32[]{:S(2)}, u32[]{:S(2)}) collective-permute-start(f32[1,32,512]{2,1,0:T(8,128)S(1)} %get-tuple-element.177), channel_id=1, source_target_pairs={{1,0},{2,1},{3,2},{4,3},{5,4},{6,5},{7,6},{8,7},{9,8},{10,9},{11,1... | collective-permute-start | bytes 196616 | tf_op jit(solution)/shard_map/ppermute | solution.py:15
  22.2 5.6 %fusion.61 = f32[3,8,64,4,128]{4,2,3,1,0:T(8,128)S(1)} fusion(f32[3,8,8,4,8,256]{5,4,3,2,1,0:T(8,128)} %bitcast.227, s32[256]{0:T(256)S(1)} %and_select_fusion), kind=kOutput, calls=%fused_computation.93 | convolution fusion | flops 2415951872 | bytes 9438208 | tf_op jit(solution)/shard_map/dot_general | solution.py:37
  27.8 3.7 %copy.15 = f32[3,8,64,4,128]{4,3,1,2,0:T(4,128)} copy(f32[3,8,64,4,128]{4,2,3,1,0:T(8,128)S(1)} %fusion.61) | data formatting | bytes 6291456 | tf_op jit(solution)/shard_map/dot_general | solution.py:37
  31.5 5.0 %reshape_reshape.20 = f32[3,8,32,2,512]{4,1,3,2,0:T(8,128)} reshape(f32[3,8,64,4,128]{4,3,1,2,0:T(4,128)} %copy.15) | data formatting | bytes 6291456 | tf_op jit(solution)/shard_map/reshape;reshape | solution.py:42
  36.5 2.2 slice_add_fusion
  40.9 2.4 fusion.141
  43.3 2.7 %fusion.139 = (f32[8,64,1023]{2,1,0:T(8,128)}, f32[8,64,1023]{2,1,0:T(8,128)}) fusion(f32[8,64,1024]{2,1,0:T(8,128)S(1)} %bitcast.225), kind=kLoop, calls=%fused_computation.205 | loop fusion | bytes 8380416 | tf_op jit(solution)/shard_map/jit(_roll_static)/slice | solution.py:73
  48.9 2.6 reshape_reshape.19
  51.5 2.1 slice_add_fusion.2
  56.3 2.1 fusion.99
  59.6 3.3 %reshape_reshape.21 = f32[8,64,4,128]{3,2,1,0:T(4,128)} reshape(f32[4,2,32,2,512]{4,3,2,1,0:T(2,128)} %broadcast_in_dim.6) | data formatting | bytes 2097152 | tf_op jit(solution)/shard_map/reshape;reshape | solution.py:58
  62.9 2.4 convolution_bitcast_fusion.1
  67.6 6.3 %fusion.47 = f32[8,64,1024]{2,1,0:T(8,128)S(1)} fusion(f32[8,64,1024]{2,1,0:T(8,128)S(1)} %bitcast.226, f32[1,64,1024]{2,1,0:T(8,128)} %collective-permute-done.4, f32[8,64,1024]{2,1,0:T(8,128)S(1)} %copy-done.2, f32[1,64,1024]{2,1,0:T(8,128)} %collective-permute-done.3, f32[8,63,1024]{2,1,0:T(8,128)S(1)} %copy-done.6, f32[8,1,1024]{2,1,0:T(1,128)S(1)} %copy-done.11, ...), kind=kLoop, calls=%fused_computation.61 | loop fusion | flops 20447232 | bytes 21495808 | tf_op jit(solution)/shard_map/add | solution.py:85
  75.4 4.7 %collective-permute-start.5 = (f32[1,64,1024]{2,1,0:T(8,128)S(1)}, f32[1,64,1024]{2,1,0:T(8,128)S(1)}, u32[]{:S(2)}, u32[]{:S(2)}) collective-permute-start(f32[1,64,1024]{2,1,0:T(8,128)S(1)} %get-tuple-element.147), channel_id=1, source_target_pairs={{1,0},{2,1},{3,2},{4,3},{5,4},{6,5},{7,6},{8,7},{9,8},{10,9},{11,1... | collective-permute-start | bytes 786440 | tf_op jit(solution)/shard_map/ppermute | solution.py:15
  80.1 2.1 collective-permute-start.6
  84.0 4.7 %collective-permute-done.6 = f32[1,64,1024]{2,1,0:T(8,128)S(1)} collective-permute-done((f32[1,64,1024]{2,1,0:T(8,128)S(1)}, f32[1,64,1024]{2,1,0:T(8,128)S(1)}, u32[]{:S(2)}, u32[]{:S(2)}) %collective-permute-start.6) | collective-permute-done | bytes 262176 | tf_op jit(solution)/shard_map/ppermute | solution.py:12
  88.7 3.9 %fusion.35 = f32[8,64,1024]{2,1,0:T(8,128)S(1)} fusion(f32[8,64,1024]{2,1,0:T(8,128)S(1)} %bitcast.234, f32[8,64,1024]{2,1,0:T(8,128)S(1)} %fusion.47, f32[1,64,1024]{2,1,0:T(8,128)S(1)} %collective-permute-done.6, f32[8,64,1024]{2,1,0:T(8,128)S(1)} %copy-done.2, f32[1,64,1024]{2,1,0:T(8,128)S(1)} %collective-permute-done.5, ...), kind=kLoop, calls=%fused_computation.47 | loop fusion | flops 20971520 | bytes 23592960 | tf_op jit(solution)/shard_map/sub | solution.py:104
  95.4 2.6 reshape_reshape.22
  100.4 151.1 %while.13 = (s32[]{:T(128)}, f32[4,32,512]{2,1,0:T(8,128)S(1)}, s32[]{:T(128)}, f32[4,32,512]{2,1,0:T(8,128)S(1)}, f32[3,4,32,512]{3,2,1,0:T(8,128)S(1)}, /*index=5*/f32[4,32,512]{2,1,0:T(8,128)}, s32[]{:T(128)}) while((s32[]{:T(128)}, f32[4,32,512]{2,1,0:T(8,128)S(1)}, s32[]{:T(128)}, f32[4,32,512]{2,1,0:T(8,128)S(1)}, ...), condition=%wide.region_1.2_spmd, body=%wide.region_0.1_spmd.sunk | while | flops 2883587 | bytes 8782059 | solution.py:112
  100.4 2.1 collective-permute-start
  102.4 4.5 %collective-permute-start.1 = (f32[1,32,512]{2,1,0:T(8,128)S(1)}, f32[1,32,512]{2,1,0:T(8,128)S(1)}, u32[]{:S(2)}, u32[]{:S(2)}) collective-permute-start(f32[1,32,512]{2,1,0:T(8,128)S(1)} %get-tuple-element.227), channel_id=1, source_target_pairs={{1,0},{2,1},{3,2},{4,3},{5,4},{6,5},{7,6},{8,7},{9,8},{10,9},{11,1... | collective-permute-start | bytes 196616 | tf_op jit(solution)/shard_map/while/body/eval_jaxpr/ppermute | solution.py:15
  110.0 5.5 %collective-permute-start.2 = (f32[4,32,512]{2,1,0:T(8,128)}, f32[4,32,512]{2,1,0:T(8,128)}, u32[]{:S(2)}, u32[]{:S(2)}) collective-permute-start(f32[4,32,512]{2,1,0:T(8,128)} %fusion.165), channel_id=1, source_target_pairs={{0,16},{16,32},{32,48},{48,64},{64,80},{80,96},{96,112},{1,17},{17... | collective-permute-start | bytes 786440 | tf_op jit(solution)/shard_map/while/body/eval_jaxpr/ppermute | solution.py:23
  115.5 7.3 %collective-permute-done.2 = f32[4,32,512]{2,1,0:T(8,128)} collective-permute-done((f32[4,32,512]{2,1,0:T(8,128)}, f32[4,32,512]{2,1,0:T(8,128)}, u32[]{:S(2)}, u32[]{:S(2)}) %collective-permute-start.2) | collective-permute-done | bytes 262176 | tf_op jit(solution)/shard_map/while/body/eval_jaxpr/ppermute | solution.py:23
  122.9 2.1 collective-permute-start
  125.0 4.5 %collective-permute-start.1 = (f32[1,32,512]{2,1,0:T(8,128)S(1)}, f32[1,32,512]{2,1,0:T(8,128)S(1)}, u32[]{:S(2)}, u32[]{:S(2)}) collective-permute-start(f32[1,32,512]{2,1,0:T(8,128)S(1)} %get-tuple-element.227), channel_id=1, source_target_pairs={{1,0},{2,1},{3,2},{4,3},{5,4},{6,5},{7,6},{8,7},{9,8},{10,9},{11,1... | collective-permute-start | bytes 196616 | tf_op jit(solution)/shard_map/while/body/eval_jaxpr/ppermute | solution.py:15
  132.5 4.6 %collective-permute-start.2 = (f32[4,32,512]{2,1,0:T(8,128)}, f32[4,32,512]{2,1,0:T(8,128)}, u32[]{:S(2)}, u32[]{:S(2)}) collective-permute-start(f32[4,32,512]{2,1,0:T(8,128)} %fusion.165), channel_id=1, source_target_pairs={{0,16},{16,32},{32,48},{48,64},{64,80},{80,96},{96,112},{1,17},{17... | collective-permute-start | bytes 786440 | tf_op jit(solution)/shard_map/while/body/eval_jaxpr/ppermute | solution.py:23
  137.1 6.9 %collective-permute-done.2 = f32[4,32,512]{2,1,0:T(8,128)} collective-permute-done((f32[4,32,512]{2,1,0:T(8,128)}, f32[4,32,512]{2,1,0:T(8,128)}, u32[]{:S(2)}, u32[]{:S(2)}) %collective-permute-start.2) | collective-permute-done | bytes 262176 | tf_op jit(solution)/shard_map/while/body/eval_jaxpr/ppermute | solution.py:23
  144.1 2.1 collective-permute-start
  146.2 4.5 %collective-permute-start.1 = (f32[1,32,512]{2,1,0:T(8,128)S(1)}, f32[1,32,512]{2,1,0:T(8,128)S(1)}, u32[]{:S(2)}, u32[]{:S(2)}) collective-permute-start(f32[1,32,512]{2,1,0:T(8,128)S(1)} %get-tuple-element.227), channel_id=1, source_target_pairs={{1,0},{2,1},{3,2},{4,3},{5,4},{6,5},{7,6},{8,7},{9,8},{10,9},{11,1... | collective-permute-start | bytes 196616 | tf_op jit(solution)/shard_map/while/body/eval_jaxpr/ppermute | solution.py:15
  153.7 3.7 %collective-permute-start.2 = (f32[4,32,512]{2,1,0:T(8,128)}, f32[4,32,512]{2,1,0:T(8,128)}, u32[]{:S(2)}, u32[]{:S(2)}) collective-permute-start(f32[4,32,512]{2,1,0:T(8,128)} %fusion.165), channel_id=1, source_target_pairs={{0,16},{16,32},{32,48},{48,64},{64,80},{80,96},{96,112},{1,17},{17... | collective-permute-start | bytes 786440 | tf_op jit(solution)/shard_map/while/body/eval_jaxpr/ppermute | solution.py:23
  157.4 8.1 %collective-permute-done.2 = f32[4,32,512]{2,1,0:T(8,128)} collective-permute-done((f32[4,32,512]{2,1,0:T(8,128)}, f32[4,32,512]{2,1,0:T(8,128)}, u32[]{:S(2)}, u32[]{:S(2)}) %collective-permute-start.2) | collective-permute-done | bytes 262176 | tf_op jit(solution)/shard_map/while/body/eval_jaxpr/ppermute | solution.py:23
  165.7 2.1 collective-permute-start
  167.7 4.5 %collective-permute-start.1 = (f32[1,32,512]{2,1,0:T(8,128)S(1)}, f32[1,32,512]{2,1,0:T(8,128)S(1)}, u32[]{:S(2)}, u32[]{:S(2)}) collective-permute-start(f32[1,32,512]{2,1,0:T(8,128)S(1)} %get-tuple-element.227), channel_id=1, source_target_pairs={{1,0},{2,1},{3,2},{4,3},{5,4},{6,5},{7,6},{8,7},{9,8},{10,9},{11,1... | collective-permute-start | bytes 196616 | tf_op jit(solution)/shard_map/while/body/eval_jaxpr/ppermute | solution.py:15
  175.3 2.8 %collective-permute-start.2 = (f32[4,32,512]{2,1,0:T(8,128)}, f32[4,32,512]{2,1,0:T(8,128)}, u32[]{:S(2)}, u32[]{:S(2)}) collective-permute-start(f32[4,32,512]{2,1,0:T(8,128)} %fusion.165), channel_id=1, source_target_pairs={{0,16},{16,32},{32,48},{48,64},{64,80},{80,96},{96,112},{1,17},{17... | collective-permute-start | bytes 786440 | tf_op jit(solution)/shard_map/while/body/eval_jaxpr/ppermute | solution.py:23
  178.1 8.7 %collective-permute-done.2 = f32[4,32,512]{2,1,0:T(8,128)} collective-permute-done((f32[4,32,512]{2,1,0:T(8,128)}, f32[4,32,512]{2,1,0:T(8,128)}, u32[]{:S(2)}, u32[]{:S(2)}) %collective-permute-start.2) | collective-permute-done | bytes 262176 | tf_op jit(solution)/shard_map/while/body/eval_jaxpr/ppermute | solution.py:23
  189.9 4.5 %collective-permute-start.1 = (f32[1,32,512]{2,1,0:T(8,128)S(1)}, f32[1,32,512]{2,1,0:T(8,128)S(1)}, u32[]{:S(2)}, u32[]{:S(2)}) collective-permute-start(f32[1,32,512]{2,1,0:T(8,128)S(1)} %get-tuple-element.227), channel_id=1, source_target_pairs={{1,0},{2,1},{3,2},{4,3},{5,4},{6,5},{7,6},{8,7},{9,8},{10,9},{11,1... | collective-permute-start | bytes 196616 | tf_op jit(solution)/shard_map/while/body/eval_jaxpr/ppermute | solution.py:15
  199.4 9.5 %collective-permute-done.2 = f32[4,32,512]{2,1,0:T(8,128)} collective-permute-done((f32[4,32,512]{2,1,0:T(8,128)}, f32[4,32,512]{2,1,0:T(8,128)}, u32[]{:S(2)}, u32[]{:S(2)}) %collective-permute-start.2) | collective-permute-done | bytes 262176 | tf_op jit(solution)/shard_map/while/body/eval_jaxpr/ppermute | solution.py:23
  209.0 2.1 collective-permute-start
  211.1 4.5 %collective-permute-start.1 = (f32[1,32,512]{2,1,0:T(8,128)S(1)}, f32[1,32,512]{2,1,0:T(8,128)S(1)}, u32[]{:S(2)}, u32[]{:S(2)}) collective-permute-start(f32[1,32,512]{2,1,0:T(8,128)S(1)} %get-tuple-element.227), channel_id=1, source_target_pairs={{1,0},{2,1},{3,2},{4,3},{5,4},{6,5},{7,6},{8,7},{9,8},{10,9},{11,1... | collective-permute-start | bytes 196616 | tf_op jit(solution)/shard_map/while/body/eval_jaxpr/ppermute | solution.py:15
  218.6 2.2 collective-permute-start.2
  220.9 9.2 %collective-permute-done.2 = f32[4,32,512]{2,1,0:T(8,128)} collective-permute-done((f32[4,32,512]{2,1,0:T(8,128)}, f32[4,32,512]{2,1,0:T(8,128)}, u32[]{:S(2)}, u32[]{:S(2)}) %collective-permute-start.2) | collective-permute-done | bytes 262176 | tf_op jit(solution)/shard_map/while/body/eval_jaxpr/ppermute | solution.py:23
  232.3 4.5 %collective-permute-start.1 = (f32[1,32,512]{2,1,0:T(8,128)S(1)}, f32[1,32,512]{2,1,0:T(8,128)S(1)}, u32[]{:S(2)}, u32[]{:S(2)}) collective-permute-start(f32[1,32,512]{2,1,0:T(8,128)S(1)} %get-tuple-element.227), channel_id=1, source_target_pairs={{1,0},{2,1},{3,2},{4,3},{5,4},{6,5},{7,6},{8,7},{9,8},{10,9},{11,1... | collective-permute-start | bytes 196616 | tf_op jit(solution)/shard_map/while/body/eval_jaxpr/ppermute | solution.py:15
  241.8 9.5 %collective-permute-done.2 = f32[4,32,512]{2,1,0:T(8,128)} collective-permute-done((f32[4,32,512]{2,1,0:T(8,128)}, f32[4,32,512]{2,1,0:T(8,128)}, u32[]{:S(2)}, u32[]{:S(2)}) %collective-permute-start.2) | collective-permute-done | bytes 262176 | tf_op jit(solution)/shard_map/while/body/eval_jaxpr/ppermute | solution.py:23
  251.7 3.0 %collective-permute-start.9 = (f32[1,32,512]{2,1,0:T(8,128)S(1)}, f32[1,32,512]{2,1,0:T(8,128)S(1)}, u32[]{:S(2)}, u32[]{:S(2)}) collective-permute-start(f32[1,32,512]{2,1,0:T(8,128)S(1)} %get-tuple-element.167), channel_id=1, source_target_pairs={{1,0},{2,1},{3,2},{4,3},{5,4},{6,5},{7,6},{8,7},{9,8},{10,9},{11,1... | collective-permute-start | bytes 196616 | tf_op jit(solution)/shard_map/ppermute | solution.py:15
  256.7 4.5 %collective-permute-done.10 = f32[1,32,512]{2,1,0:T(8,128)S(1)} collective-permute-done((f32[1,32,512]{2,1,0:T(8,128)S(1)}, f32[1,32,512]{2,1,0:T(8,128)S(1)}, u32[]{:S(2)}, u32[]{:S(2)}) %collective-permute-start.10) | collective-permute-done | bytes 65568 | tf_op jit(solution)/shard_map/ppermute | solution.py:12
  263.9 2.3 convolution_bitcast_fusion
  (165 shorter events, 68.6 us)
Async XLA Ops:
  1.9 63.8 %collective-permute-start.3 = (f32[1,64,1024]{2,1,0:T(8,128)}, f32[1,64,1024]{2,1,0:T(8,128)}, u32[]{:S(2)}, u32[]{:S(2)}) collective-permute-start(f32[1,64,1024]{2,1,0:T(8,128)} %get-tuple-element.157), channel_id=1, source_target_pairs={{1,0},{2,1},{3,2},{4,3},{5,4},{6,5},{7,6},{8,7},{9,8},{10,9},{11,1... | collective-permute-start | bytes 786440 | tf_op jit(solution)/shard_map/ppermute | solution.py:15
  5.1 60.6 %collective-permute-start.4 = (f32[1,64,1024]{2,1,0:T(8,128)}, f32[1,64,1024]{2,1,0:T(8,128)}, u32[]{:S(2)}, u32[]{:S(2)}) collective-permute-start(f32[1,64,1024]{2,1,0:T(8,128)} %get-tuple-element.158), channel_id=1, source_target_pairs={{0,1},{1,2},{2,3},{3,4},{4,5},{5,6},{6,7},{7,8},{8,9},{9,10},{10,1... | collective-permute-start | bytes 786440 | tf_op jit(solution)/shard_map/ppermute | solution.py:12
  11.7 7.1 %copy-start = (f32[1,8,64,1024]{3,2,1,0:T(8,128)S(1)}, f32[1,8,64,1024]{3,2,1,0:T(8,128)}, u32[]{:S(2)}) copy-start(f32[1,8,64,1024]{3,2,1,0:T(8,128)} %param.5) | copy-start | bytes 6291460
  12.1 9.2 %copy-start.4 = (f32[8,32,1,512]{3,1,0,2:T(8,128)}, f32[8,32,1,512]{3,1,0,2:T(8,128)S(1)}, u32[]{:S(2)}) copy-start(f32[8,32,1,512]{3,1,0,2:T(8,128)S(1)} %copy.10) | copy-start | bytes 1572868
  12.2 43.4 %collective-permute-start.7 = (f32[1,32,512]{2,1,0:T(8,128)S(1)}, f32[1,32,512]{2,1,0:T(8,128)S(1)}, u32[]{:S(2)}, u32[]{:S(2)}) collective-permute-start(f32[1,32,512]{2,1,0:T(8,128)S(1)} %get-tuple-element.177), channel_id=1, source_target_pairs={{1,0},{2,1},{3,2},{4,3},{5,4},{6,5},{7,6},{8,7},{9,8},{10,9},{11,1... | collective-permute-start | bytes 196616 | tf_op jit(solution)/shard_map/ppermute | solution.py:15
  16.8 38.8 %collective-permute-start.8 = (f32[1,32,512]{2,1,0:T(8,128)S(1)}, f32[1,32,512]{2,1,0:T(8,128)S(1)}, u32[]{:S(2)}, u32[]{:S(2)}) collective-permute-start(f32[1,32,512]{2,1,0:T(8,128)S(1)} %get-tuple-element.178), channel_id=1, source_target_pairs={{0,1},{1,2},{2,3},{3,4},{4,5},{5,6},{6,7},{7,8},{8,9},{9,10},{10,1... | collective-permute-start | bytes 196616 | tf_op jit(solution)/shard_map/ppermute | solution.py:12
  43.3 2.8 %copy-start.1 = (f32[8,64,1024]{2,1,0:T(8,128)S(1)}, f32[8,64,1024]{2,1,0:T(8,128)}, u32[]{:S(2)}) copy-start(f32[8,64,1024]{2,1,0:T(8,128)} %param.7) | copy-start | bytes 6291460
  62.9 2.8 %copy-start.6 = (f32[8,63,1024]{2,1,0:T(8,128)S(1)}, f32[8,63,1024]{2,1,0:T(8,128)}, u32[]{:S(2)}) copy-start(f32[8,63,1024]{2,1,0:T(8,128)} %get-tuple-element.154) | copy-start | bytes 6193156
  62.9 2.8 %copy-start.8 = (f32[8,64,1]{2,1,0:T(8,128)S(1)}, f32[8,64,1]{2,1,0:T(8,128)}, u32[]{:S(2)}) copy-start(f32[8,64,1]{2,1,0:T(8,128)} %get-tuple-element.151) | copy-start | bytes 6148
  62.9 2.8 %copy-start.9 = (f32[8,64,1]{2,1,0:T(8,128)S(1)}, f32[8,64,1]{2,1,0:T(8,128)}, u32[]{:S(2)}) copy-start(f32[8,64,1]{2,1,0:T(8,128)} %get-tuple-element.152) | copy-start | bytes 6148
  62.9 2.8 %copy-start.10 = (f32[8,1,1024]{2,1,0:T(1,128)S(1)}, f32[8,1,1024]{2,1,0:T(1,128)}, u32[]{:S(2)}) copy-start(f32[8,1,1024]{2,1,0:T(1,128)} %get-tuple-element.155) | copy-start | bytes 98308
  62.9 2.9 %copy-start.11 = (f32[8,1,1024]{2,1,0:T(1,128)S(1)}, f32[8,1,1024]{2,1,0:T(1,128)}, u32[]{:S(2)}) copy-start(f32[8,1,1024]{2,1,0:T(1,128)} %get-tuple-element.156) | copy-start | bytes 98308
  65.4 2.2 copy-start.5
  73.9 14.7 %slice-start = ((s8[6291456]{0:T(1024)(128)(4,1)}), s8[4194304]{0:T(1024)(128)(4,1)S(1)}, s32[]{:S(2)}) async-start(s8[6291456]{0:T(1024)(128)(4,1)} %bitcast.228), calls=%async_computation | async-start | bytes 8388608
  74.5 14.1 %slice-start.1 = ((s8[6291456]{0:T(1024)(128)(4,1)}), s8[2097152]{0:T(1024)(128)(4,1)S(1)}, s32[]{:S(2)}) async-start(s8[6291456]{0:T(1024)(128)(4,1)} %bitcast.228), calls=%async_computation.1 | async-start | bytes 4194304
  75.4 8.6 %collective-permute-start.5 = (f32[1,64,1024]{2,1,0:T(8,128)S(1)}, f32[1,64,1024]{2,1,0:T(8,128)S(1)}, u32[]{:S(2)}, u32[]{:S(2)}) collective-permute-start(f32[1,64,1024]{2,1,0:T(8,128)S(1)} %get-tuple-element.147), channel_id=1, source_target_pairs={{1,0},{2,1},{3,2},{4,3},{5,4},{6,5},{7,6},{8,7},{9,8},{10,9},{11,1... | collective-permute-start | bytes 786440 | tf_op jit(solution)/shard_map/ppermute | solution.py:15
  80.1 8.6 %collective-permute-start.6 = (f32[1,64,1024]{2,1,0:T(8,128)S(1)}, f32[1,64,1024]{2,1,0:T(8,128)S(1)}, u32[]{:S(2)}, u32[]{:S(2)}) collective-permute-start(f32[1,64,1024]{2,1,0:T(8,128)S(1)} %get-tuple-element.148), channel_id=1, source_target_pairs={{0,1},{1,2},{2,3},{3,4},{4,5},{5,6},{6,7},{7,8},{8,9},{9,10},{10,1... | collective-permute-start | bytes 786440 | tf_op jit(solution)/shard_map/ppermute | solution.py:12
  100.4 8.5 %copy-start.3 = (f32[4,32,512]{2,1,0:T(8,128)S(1)}, f32[4,32,512]{2,1,0:T(8,128)}, u32[]{:S(2)}) copy-start(f32[4,32,512]{2,1,0:T(8,128)} %get-tuple-element.255) | copy-start | bytes 786436 | tf_op jit(solution)/shard_map/while
  100.4 6.9 %collective-permute-start = (f32[1,32,512]{2,1,0:T(8,128)S(1)}, f32[1,32,512]{2,1,0:T(8,128)S(1)}, u32[]{:S(2)}, u32[]{:S(2)}) collective-permute-start(f32[1,32,512]{2,1,0:T(8,128)S(1)} %get-tuple-element.226), channel_id=1, source_target_pairs={{0,1},{1,2},{2,3},{3,4},{4,5},{5,6},{6,7},{7,8},{8,9},{9,10},{10,1... | collective-permute-start | bytes 196616 | tf_op jit(solution)/shard_map/while/body/eval_jaxpr/ppermute | solution.py:12
  102.4 6.4 %collective-permute-start.1 = (f32[1,32,512]{2,1,0:T(8,128)S(1)}, f32[1,32,512]{2,1,0:T(8,128)S(1)}, u32[]{:S(2)}, u32[]{:S(2)}) collective-permute-start(f32[1,32,512]{2,1,0:T(8,128)S(1)} %get-tuple-element.227), channel_id=1, source_target_pairs={{1,0},{2,1},{3,2},{4,3},{5,4},{6,5},{7,6},{8,7},{9,8},{10,9},{11,1... | collective-permute-start | bytes 196616 | tf_op jit(solution)/shard_map/while/body/eval_jaxpr/ppermute | solution.py:15
  110.0 12.8 %collective-permute-start.2 = (f32[4,32,512]{2,1,0:T(8,128)}, f32[4,32,512]{2,1,0:T(8,128)}, u32[]{:S(2)}, u32[]{:S(2)}) collective-permute-start(f32[4,32,512]{2,1,0:T(8,128)} %fusion.165), channel_id=1, source_target_pairs={{0,16},{16,32},{32,48},{48,64},{64,80},{80,96},{96,112},{1,17},{17... | collective-permute-start | bytes 786440 | tf_op jit(solution)/shard_map/while/body/eval_jaxpr/ppermute | solution.py:23
  122.9 8.5 %copy-start.3 = (f32[4,32,512]{2,1,0:T(8,128)S(1)}, f32[4,32,512]{2,1,0:T(8,128)}, u32[]{:S(2)}) copy-start(f32[4,32,512]{2,1,0:T(8,128)} %get-tuple-element.255) | copy-start | bytes 786436 | tf_op jit(solution)/shard_map/while
  122.9 6.9 %collective-permute-start = (f32[1,32,512]{2,1,0:T(8,128)S(1)}, f32[1,32,512]{2,1,0:T(8,128)S(1)}, u32[]{:S(2)}, u32[]{:S(2)}) collective-permute-start(f32[1,32,512]{2,1,0:T(8,128)S(1)} %get-tuple-element.226), channel_id=1, source_target_pairs={{0,1},{1,2},{2,3},{3,4},{4,5},{5,6},{6,7},{7,8},{8,9},{9,10},{10,1... | collective-permute-start | bytes 196616 | tf_op jit(solution)/shard_map/while/body/eval_jaxpr/ppermute | solution.py:12
  125.0 6.4 %collective-permute-start.1 = (f32[1,32,512]{2,1,0:T(8,128)S(1)}, f32[1,32,512]{2,1,0:T(8,128)S(1)}, u32[]{:S(2)}, u32[]{:S(2)}) collective-permute-start(f32[1,32,512]{2,1,0:T(8,128)S(1)} %get-tuple-element.227), channel_id=1, source_target_pairs={{1,0},{2,1},{3,2},{4,3},{5,4},{6,5},{7,6},{8,7},{9,8},{10,9},{11,1... | collective-permute-start | bytes 196616 | tf_op jit(solution)/shard_map/while/body/eval_jaxpr/ppermute | solution.py:15
  132.5 11.5 %collective-permute-start.2 = (f32[4,32,512]{2,1,0:T(8,128)}, f32[4,32,512]{2,1,0:T(8,128)}, u32[]{:S(2)}, u32[]{:S(2)}) collective-permute-start(f32[4,32,512]{2,1,0:T(8,128)} %fusion.165), channel_id=1, source_target_pairs={{0,16},{16,32},{32,48},{48,64},{64,80},{80,96},{96,112},{1,17},{17... | collective-permute-start | bytes 786440 | tf_op jit(solution)/shard_map/while/body/eval_jaxpr/ppermute | solution.py:23
  144.1 8.5 %copy-start.3 = (f32[4,32,512]{2,1,0:T(8,128)S(1)}, f32[4,32,512]{2,1,0:T(8,128)}, u32[]{:S(2)}) copy-start(f32[4,32,512]{2,1,0:T(8,128)} %get-tuple-element.255) | copy-start | bytes 786436 | tf_op jit(solution)/shard_map/while
  144.1 6.9 %collective-permute-start = (f32[1,32,512]{2,1,0:T(8,128)S(1)}, f32[1,32,512]{2,1,0:T(8,128)S(1)}, u32[]{:S(2)}, u32[]{:S(2)}) collective-permute-start(f32[1,32,512]{2,1,0:T(8,128)S(1)} %get-tuple-element.226), channel_id=1, source_target_pairs={{0,1},{1,2},{2,3},{3,4},{4,5},{5,6},{6,7},{7,8},{8,9},{9,10},{10,1... | collective-permute-start | bytes 196616 | tf_op jit(solution)/shard_map/while/body/eval_jaxpr/ppermute | solution.py:12
  146.2 6.4 %collective-permute-start.1 = (f32[1,32,512]{2,1,0:T(8,128)S(1)}, f32[1,32,512]{2,1,0:T(8,128)S(1)}, u32[]{:S(2)}, u32[]{:S(2)}) collective-permute-start(f32[1,32,512]{2,1,0:T(8,128)S(1)} %get-tuple-element.227), channel_id=1, source_target_pairs={{1,0},{2,1},{3,2},{4,3},{5,4},{6,5},{7,6},{8,7},{9,8},{10,9},{11,1... | collective-permute-start | bytes 196616 | tf_op jit(solution)/shard_map/while/body/eval_jaxpr/ppermute | solution.py:15
  153.7 11.8 %collective-permute-start.2 = (f32[4,32,512]{2,1,0:T(8,128)}, f32[4,32,512]{2,1,0:T(8,128)}, u32[]{:S(2)}, u32[]{:S(2)}) collective-permute-start(f32[4,32,512]{2,1,0:T(8,128)} %fusion.165), channel_id=1, source_target_pairs={{0,16},{16,32},{32,48},{48,64},{64,80},{80,96},{96,112},{1,17},{17... | collective-permute-start | bytes 786440 | tf_op jit(solution)/shard_map/while/body/eval_jaxpr/ppermute | solution.py:23
  165.6 8.5 %copy-start.3 = (f32[4,32,512]{2,1,0:T(8,128)S(1)}, f32[4,32,512]{2,1,0:T(8,128)}, u32[]{:S(2)}) copy-start(f32[4,32,512]{2,1,0:T(8,128)} %get-tuple-element.255) | copy-start | bytes 786436 | tf_op jit(solution)/shard_map/while
  165.7 6.9 %collective-permute-start = (f32[1,32,512]{2,1,0:T(8,128)S(1)}, f32[1,32,512]{2,1,0:T(8,128)S(1)}, u32[]{:S(2)}, u32[]{:S(2)}) collective-permute-start(f32[1,32,512]{2,1,0:T(8,128)S(1)} %get-tuple-element.226), channel_id=1, source_target_pairs={{0,1},{1,2},{2,3},{3,4},{4,5},{5,6},{6,7},{7,8},{8,9},{9,10},{10,1... | collective-permute-start | bytes 196616 | tf_op jit(solution)/shard_map/while/body/eval_jaxpr/ppermute | solution.py:12
  167.7 6.4 %collective-permute-start.1 = (f32[1,32,512]{2,1,0:T(8,128)S(1)}, f32[1,32,512]{2,1,0:T(8,128)S(1)}, u32[]{:S(2)}, u32[]{:S(2)}) collective-permute-start(f32[1,32,512]{2,1,0:T(8,128)S(1)} %get-tuple-element.227), channel_id=1, source_target_pairs={{1,0},{2,1},{3,2},{4,3},{5,4},{6,5},{7,6},{8,7},{9,8},{10,9},{11,1... | collective-permute-start | bytes 196616 | tf_op jit(solution)/shard_map/while/body/eval_jaxpr/ppermute | solution.py:15
  175.3 11.5 %collective-permute-start.2 = (f32[4,32,512]{2,1,0:T(8,128)}, f32[4,32,512]{2,1,0:T(8,128)}, u32[]{:S(2)}, u32[]{:S(2)}) collective-permute-start(f32[4,32,512]{2,1,0:T(8,128)} %fusion.165), channel_id=1, source_target_pairs={{0,16},{16,32},{32,48},{48,64},{64,80},{80,96},{96,112},{1,17},{17... | collective-permute-start | bytes 786440 | tf_op jit(solution)/shard_map/while/body/eval_jaxpr/ppermute | solution.py:23
  187.8 8.5 %copy-start.3 = (f32[4,32,512]{2,1,0:T(8,128)S(1)}, f32[4,32,512]{2,1,0:T(8,128)}, u32[]{:S(2)}) copy-start(f32[4,32,512]{2,1,0:T(8,128)} %get-tuple-element.255) | copy-start | bytes 786436 | tf_op jit(solution)/shard_map/while
  187.8 6.9 %collective-permute-start = (f32[1,32,512]{2,1,0:T(8,128)S(1)}, f32[1,32,512]{2,1,0:T(8,128)S(1)}, u32[]{:S(2)}, u32[]{:S(2)}) collective-permute-start(f32[1,32,512]{2,1,0:T(8,128)S(1)} %get-tuple-element.226), channel_id=1, source_target_pairs={{0,1},{1,2},{2,3},{3,4},{4,5},{5,6},{6,7},{7,8},{8,9},{9,10},{10,1... | collective-permute-start | bytes 196616 | tf_op jit(solution)/shard_map/while/body/eval_jaxpr/ppermute | solution.py:12
  189.9 6.4 %collective-permute-start.1 = (f32[1,32,512]{2,1,0:T(8,128)S(1)}, f32[1,32,512]{2,1,0:T(8,128)S(1)}, u32[]{:S(2)}, u32[]{:S(2)}) collective-permute-start(f32[1,32,512]{2,1,0:T(8,128)S(1)} %get-tuple-element.227), channel_id=1, source_target_pairs={{1,0},{2,1},{3,2},{4,3},{5,4},{6,5},{7,6},{8,7},{9,8},{10,9},{11,1... | collective-permute-start | bytes 196616 | tf_op jit(solution)/shard_map/while/body/eval_jaxpr/ppermute | solution.py:15
  197.4 11.5 %collective-permute-start.2 = (f32[4,32,512]{2,1,0:T(8,128)}, f32[4,32,512]{2,1,0:T(8,128)}, u32[]{:S(2)}, u32[]{:S(2)}) collective-permute-start(f32[4,32,512]{2,1,0:T(8,128)} %fusion.165), channel_id=1, source_target_pairs={{0,16},{16,32},{32,48},{48,64},{64,80},{80,96},{96,112},{1,17},{17... | collective-permute-start | bytes 786440 | tf_op jit(solution)/shard_map/while/body/eval_jaxpr/ppermute | solution.py:23
  209.0 8.5 %copy-start.3 = (f32[4,32,512]{2,1,0:T(8,128)S(1)}, f32[4,32,512]{2,1,0:T(8,128)}, u32[]{:S(2)}) copy-start(f32[4,32,512]{2,1,0:T(8,128)} %get-tuple-element.255) | copy-start | bytes 786436 | tf_op jit(solution)/shard_map/while
  209.0 6.9 %collective-permute-start = (f32[1,32,512]{2,1,0:T(8,128)S(1)}, f32[1,32,512]{2,1,0:T(8,128)S(1)}, u32[]{:S(2)}, u32[]{:S(2)}) collective-permute-start(f32[1,32,512]{2,1,0:T(8,128)S(1)} %get-tuple-element.226), channel_id=1, source_target_pairs={{0,1},{1,2},{2,3},{3,4},{4,5},{5,6},{6,7},{7,8},{8,9},{9,10},{10,1... | collective-permute-start | bytes 196616 | tf_op jit(solution)/shard_map/while/body/eval_jaxpr/ppermute | solution.py:12
  211.1 6.4 %collective-permute-start.1 = (f32[1,32,512]{2,1,0:T(8,128)S(1)}, f32[1,32,512]{2,1,0:T(8,128)S(1)}, u32[]{:S(2)}, u32[]{:S(2)}) collective-permute-start(f32[1,32,512]{2,1,0:T(8,128)S(1)} %get-tuple-element.227), channel_id=1, source_target_pairs={{1,0},{2,1},{3,2},{4,3},{5,4},{6,5},{7,6},{8,7},{9,8},{10,9},{11,1... | collective-permute-start | bytes 196616 | tf_op jit(solution)/shard_map/while/body/eval_jaxpr/ppermute | solution.py:15
  218.6 11.5 %collective-permute-start.2 = (f32[4,32,512]{2,1,0:T(8,128)}, f32[4,32,512]{2,1,0:T(8,128)}, u32[]{:S(2)}, u32[]{:S(2)}) collective-permute-start(f32[4,32,512]{2,1,0:T(8,128)} %fusion.165), channel_id=1, source_target_pairs={{0,16},{16,32},{32,48},{48,64},{64,80},{80,96},{96,112},{1,17},{17... | collective-permute-start | bytes 786440 | tf_op jit(solution)/shard_map/while/body/eval_jaxpr/ppermute | solution.py:23
  230.2 8.5 %copy-start.3 = (f32[4,32,512]{2,1,0:T(8,128)S(1)}, f32[4,32,512]{2,1,0:T(8,128)}, u32[]{:S(2)}) copy-start(f32[4,32,512]{2,1,0:T(8,128)} %get-tuple-element.255) | copy-start | bytes 786436 | tf_op jit(solution)/shard_map/while
  230.2 6.9 %collective-permute-start = (f32[1,32,512]{2,1,0:T(8,128)S(1)}, f32[1,32,512]{2,1,0:T(8,128)S(1)}, u32[]{:S(2)}, u32[]{:S(2)}) collective-permute-start(f32[1,32,512]{2,1,0:T(8,128)S(1)} %get-tuple-element.226), channel_id=1, source_target_pairs={{0,1},{1,2},{2,3},{3,4},{4,5},{5,6},{6,7},{7,8},{8,9},{9,10},{10,1... | collective-permute-start | bytes 196616 | tf_op jit(solution)/shard_map/while/body/eval_jaxpr/ppermute | solution.py:12
  232.3 6.4 %collective-permute-start.1 = (f32[1,32,512]{2,1,0:T(8,128)S(1)}, f32[1,32,512]{2,1,0:T(8,128)S(1)}, u32[]{:S(2)}, u32[]{:S(2)}) collective-permute-start(f32[1,32,512]{2,1,0:T(8,128)S(1)} %get-tuple-element.227), channel_id=1, source_target_pairs={{1,0},{2,1},{3,2},{4,3},{5,4},{6,5},{7,6},{8,7},{9,8},{10,9},{11,1... | collective-permute-start | bytes 196616 | tf_op jit(solution)/shard_map/while/body/eval_jaxpr/ppermute | solution.py:15
  239.8 11.5 %collective-permute-start.2 = (f32[4,32,512]{2,1,0:T(8,128)}, f32[4,32,512]{2,1,0:T(8,128)}, u32[]{:S(2)}, u32[]{:S(2)}) collective-permute-start(f32[4,32,512]{2,1,0:T(8,128)} %fusion.165), channel_id=1, source_target_pairs={{0,16},{16,32},{32,48},{48,64},{64,80},{80,96},{96,112},{1,17},{17... | collective-permute-start | bytes 786440 | tf_op jit(solution)/shard_map/while/body/eval_jaxpr/ppermute | solution.py:23
  251.4 9.8 %copy-start.7 = (f32[3,4,1,32,512]{4,3,1,2,0:T(8,128)S(1)}, f32[3,4,1,32,512]{4,3,1,2,0:T(8,128)}, u32[]{:S(2)}) copy-start(f32[3,4,1,32,512]{4,3,1,2,0:T(8,128)} %fusion.73) | copy-start | bytes 2359300
  251.7 5.0 %collective-permute-start.9 = (f32[1,32,512]{2,1,0:T(8,128)S(1)}, f32[1,32,512]{2,1,0:T(8,128)S(1)}, u32[]{:S(2)}, u32[]{:S(2)}) collective-permute-start(f32[1,32,512]{2,1,0:T(8,128)S(1)} %get-tuple-element.167), channel_id=1, source_target_pairs={{1,0},{2,1},{3,2},{4,3},{5,4},{6,5},{7,6},{8,7},{9,8},{10,9},{11,1... | collective-permute-start | bytes 196616 | tf_op jit(solution)/shard_map/ppermute | solution.py:15
  254.7 6.5 %collective-permute-start.10 = (f32[1,32,512]{2,1,0:T(8,128)S(1)}, f32[1,32,512]{2,1,0:T(8,128)S(1)}, u32[]{:S(2)}, u32[]{:S(2)}) collective-permute-start(f32[1,32,512]{2,1,0:T(8,128)S(1)} %get-tuple-element.168), channel_id=1, source_target_pairs={{0,1},{1,2},{2,3},{3,4},{4,5},{5,6},{6,7},{7,8},{8,9},{9,10},{10,1... | collective-permute-start | bytes 196616 | tf_op jit(solution)/shard_map/ppermute | solution.py:12
  (3 other events, 2.9 us)
where the time goes:
time: 270 us; the launch traced here: 268 us
  starting transfers between devices  92.3 us (34%)
  waiting for transfers between devices  81 us (30%)
  local copies, waits for them, and re-layouts  48.3 us (18%)
  other arithmetic  31.6 us (12%)
  matrix products  13.9 us (5%)
    ppermute x7, waiting for transfers between devices, passed_along(): lax.ppermute(value, axis, [(source, source + steps) for source in range(f...  59.2 us
    ppermute x11, starting transfers between devices, extended(): lax.ppermute(lax.slice_in_dim(block, 0, width, axis=dim), axis, backward)  47.4 us
    ppermute x7, starting transfers between devices, passed_along(): lax.ppermute(value, axis, [(source, source + steps) for source in range(f...  22.6 us
    ppermute x11, starting transfers between devices, extended(): lax.ppermute(lax.slice_in_dim(block, block.shape[dim] - width, None, axis...  22.3 us
    ppermute x11, waiting for transfers between devices, extended(): lax.ppermute(lax.slice_in_dim(block, 0, width, axis=dim), axis, backward)  12.6 us
    another operation x4, local copies, waits for them, and re-layouts, restrict(): split_y = halved_x.reshape(outer + (depth, height // 2, 2, width // 2))  10.7 us
    ppermute x11, waiting for transfers between devices, extended(): lax.ppermute(lax.slice_in_dim(block, block.shape[dim] - width, None, axis...  9.22 us
    dot_general x4, matrix products, restrict(): jnp.dot(blocked, pair_table(block_width), precision=lax.Precision.HIGHEST)  9.2 us
  transfers between devices with their start and end apart: 29, of which 17 were waited for; matrix products, arithmetic and copies ran while one was open for 20% of the time, Pallas kernels for 0%

commit v1 on v0

v1 whole, which is shorter than its diff:
```python
import functools

import jax
import jax.numpy as jnp
from jax import lax
from jax.experimental import pallas as pl
from jax.experimental.pallas import tpu as pltpu
from jax.sharding import Mesh
from jax.sharding import PartitionSpec as P

F32 = jnp.float32
BF16 = jnp.bfloat16
NY, NX = 64, 1024
LZ = 8
CX, CL = 512, 128
GROUPS = 8
QUAD = 4
BLOCKS = GROUPS * QUAD
XB = CX // BLOCKS
WIN = XB + 16
TOP = 8
PADDED = NY + 16
SPACE = ("px", "pz", "core")
GROUP = ("tm", "pz", "core")


def params(mib):
    return pltpu.CompilerParams(vmem_limit_bytes=mib * 1024 * 1024)


def split3(x):
    hi = x.astype(BF16)
    rest = x - hi.astype(F32)
    mid = rest.astype(BF16)
    return hi, mid, (rest - mid.astype(F32)).astype(BF16)


def dot(a, b, ca, cb):
    return lax.dot_general(a, b, (((ca,), (cb,)), ((), ())), preferred_element_type=F32)


def table(shape, test):
    rows = lax.broadcasted_iota(jnp.int32, shape, 0)
    cols = lax.broadcasted_iota(jnp.int32, shape, 1)
    return test(rows, cols).astype(F32).astype(BF16)


def restrict_block(part, pairs):
    halve = table((128, 256), lambda r, c: r == c // 2)
    t1 = sum(dot(halve, p, 1, 1) for p in split3(part))
    return sum(dot(p, pairs, 1, 0) for p in split3(t1)) * 0.125


def advanced(c, w, e, s, n, b, t, ax, ay, az, k):
    lap = ((w + e) + (s + n)) + ((b + t) - 6.0 * c)
    dx = jnp.abs(ax) * (jnp.where(ax > 0, w, e) - c)
    dy = jnp.abs(ay) * (jnp.where(ay > 0, s, n) - c)
    dz = jnp.abs(az) * (jnp.where(az > 0, b, t) - c)
    return (c + k * lap) + ((dx + dy) + dz)


def wrap_rows(ref, z):
    ref[z, TOP - 1 : TOP, :] = ref[z, TOP + NY - 1 : TOP + NY, :]
    ref[z, TOP + NY : TOP + NY + 1, :] = ref[z, TOP : TOP + 1, :]


def plane(ref, z, r):
    c = ref[z, TOP + r : TOP + r + 8, :]
    s = ref[z, TOP + r - 1 : TOP + r + 7, :]
    n = ref[z, TOP + r + 1 : TOP + r + 9, :]
    return c, pltpu.roll(c, 1, 1), pltpu.roll(c, NX - 1, 1), s, n


def coarse_coefs(vx, vy, vz, k):
    half = 0.5 * k
    out = []
    for a in (vx, vy, vz):
        out += [half + jnp.maximum(a, 0.0), half - jnp.minimum(a, 0.0)]
    return out


def y_rolled(u, width, axis):
    y = lax.broadcasted_iota(jnp.int32, u.shape, axis) % 32
    s = jnp.where(y == 0, pltpu.roll(u, width - 31, axis), pltpu.roll(u, 1, axis))
    n = jnp.where(y == 31, pltpu.roll(u, 31, axis), pltpu.roll(u, width - 1, axis))
    return s, n


def edges_kernel(slo, shi, vlo, vhi, dlo, dhi, lo, hi, pad, zsum):
    pad[0, TOP : TOP + NY, :] = slo[0]
    pad[1, TOP : TOP + NY, :] = shi[1]
    for side, (out, st, v, d, inner) in enumerate(((lo, slo, vlo, dlo, 1), (hi, shi, vhi, dhi, 0))):
        wrap_rows(pad, side)
        for r in range(0, NY, 8):
            rows = slice(r, r + 8)
            c, w, e, s, n = plane(pad, side, r)
            inside = st[inner, rows, :]
            ax, ay, az = v[0, 0, rows, :], v[1, 0, rows, :], v[2, 0, rows, :]
            k = d[0, rows, :]
            none = jnp.zeros_like(c)
            if side == 0:
                a = advanced(c, w, e, s, n, none, inside, ax, ay, az, k)
                b = k + jnp.maximum(az, 0.0)
            else:
                a = advanced(c, w, e, s, n, inside, none, ax, ay, az, k)
                b = k - jnp.minimum(az, 0.0)
            out[r : r + 8, :] = c
            out[NY + r : NY + r + 8, :] = a
            out[2 * NY + r : 2 * NY + r + 8, :] = b
            zsum[side * NY + r : side * NY + r + 8, :] = c + inside
    pairs = table((128, 128), lambda r, c: r // 2 == c)
    lane = lax.broadcasted_iota(jnp.int32, (128, 128), 1)
    clo = jnp.zeros((128, 128), F32)
    chi = jnp.zeros((128, 128), F32)
    for b in range(4):
        t = restrict_block(zsum[:, 256 * b : 256 * b + 256], pairs)
        tl = jnp.where(lane < 32, t, 0.0)
        th = jnp.where((lane >= 32) & (lane < 64), t, 0.0)
        clo += pltpu.roll(tl, 32 * b, 1) if b else tl
        chi += pltpu.roll(th, (32 * b - 32) % 128, 1) if b != 1 else th
    for i in range(8):
        lo[3 * NY : 3 * NY + 16, 128 * i : 128 * i + 128] = clo[16 * i : 16 * i + 16, :]
        hi[3 * NY : 3 * NY + 16, 128 * i : 128 * i + 128] = chi[16 * i : 16 * i + 16, :]


MSG = 3 * NY + 16


def layer_specs():
    return [
        pl.BlockSpec((3, 1, NY, NX), lambda i: (0, 0, 0, 0)),
        pl.BlockSpec((3, 1, NY, NX), lambda i: (0, LZ - 1, 0, 0)),
        pl.BlockSpec((1, NY, NX), lambda i: (0, 0, 0)),
        pl.BlockSpec((1, NY, NX), lambda i: (LZ - 1, 0, 0)),
    ]


def whole():
    return pl.BlockSpec(memory_space=pltpu.VMEM)


def anywhere():
    return pl.BlockSpec(memory_space=pl.ANY)


def edges(state, velocity, diffusivity):
    msg = jax.ShapeDtypeStruct((MSG, NX), F32)
    return pl.pallas_call(
        edges_kernel,
        out_shape=[msg, msg],
        grid=(1,),
        in_specs=[
            pl.BlockSpec((2, NY, NX), lambda i: (0, 0, 0)),
            pl.BlockSpec((2, NY, NX), lambda i: (LZ // 2 - 1, 0, 0)),
        ]
        + layer_specs(),
        out_specs=[whole(), whole()],
        scratch_shapes=[pltpu.VMEM((2, PADDED, NX), F32), pltpu.VMEM((2 * NY, NX), F32)],
        compiler_params=params(24),
        name="edges",
    )(state, state, velocity, velocity, diffusivity, diffusivity)


def interior_kernel(st, vel, dif, mid, edge, ct, gcp, cb, rfm, u, u1, v, d, zs, ct0, usem, vsem, dsem):
    ucopy = pltpu.make_async_copy(st, u.at[:, TOP : TOP + NY, :], usem)
    ucopy.start()
    vcopies, dcopies = [], []
    for z in range(LZ):
        vcopies.append(pltpu.make_async_copy(vel.at[:, z], v.at[:, z], vsem.at[z]))
        dcopies.append(pltpu.make_async_copy(dif.at[z], d.at[z], dsem.at[z]))
        vcopies[z].start()
        dcopies[z].start()
    ucopy.wait()
    for z in range(LZ):
        wrap_rows(u, z)
        if z % 2 == 0:
            for r in range(0, NY, 8):
                zs[4, (z // 2) * NY + r : (z // 2) * NY + r + 8, :] = (
                    u[z, TOP + r : TOP + r + 8, :] + u[z + 1, TOP + r : TOP + r + 8, :]
                )

    for z in range(LZ):
        vcopies[z].wait()
        dcopies[z].wait()

    def first(z, _):
        for r in range(0, NY, 8):
            rows = slice(r, r + 8)
            here = slice(TOP + r, TOP + r + 8)
            c, w, e, s, n = plane(u, z, r)
            u1[z, here, :] = advanced(
                c, w, e, s, n, u[z - 1, here, :], u[z + 1, here, :],
                v[0, z, rows, :], v[1, z, rows, :], v[2, z, rows, :], d[z, rows, :],
            )
        wrap_rows(u1, z)
        return 0

    lax.fori_loop(1, LZ - 1, first, 0)
    u1[0, TOP : TOP + NY, :] = jnp.zeros((NY, NX), F32)
    u1[LZ - 1, TOP : TOP + NY, :] = jnp.zeros((NY, NX), F32)
    edge[0] = u1[1, TOP : TOP + NY, :]
    edge[1] = u1[LZ - 2, TOP : TOP + NY, :]

    def second(z, _):
        for r in range(0, NY, 8):
            rows = slice(r, r + 8)
            here = slice(TOP + r, TOP + r + 8)
            c, w, e, s, n = plane(u1, z, r)
            u[z, here, :] = advanced(
                c, w, e, s, n, u1[z - 1, here, :], u1[z + 1, here, :],
                v[0, z, rows, :], v[1, z, rows, :], v[2, z, rows, :], d[z, rows, :],
            )
        return 0

    lax.fori_loop(1, LZ - 1, second, 0)
    edge[2] = u[1, TOP : TOP + NY, :]
    edge[3] = u[LZ - 2, TOP : TOP + NY, :]
    edge[4] = d[1] + jnp.maximum(v[2, 1], 0.0)
    edge[5] = d[LZ - 2] - jnp.minimum(v[2, LZ - 2], 0.0)
    for z in range(2, LZ - 2):
        mid[z - 2] = u[z, TOP : TOP + NY, :]
    for zc in range(4):
        for r in range(0, NY, 8):
            rows = slice(r, r + 8)
            to = slice(zc * NY + r, zc * NY + r + 8)
            for comp in range(3):
                zs[comp, to, :] = v[comp, 2 * zc, rows, :] + v[comp, 2 * zc + 1, rows, :]
            zs[3, to, :] = d[2 * zc, rows, :] + d[2 * zc + 1, rows, :]
            if zc in (1, 2):
                here = slice(TOP + r, TOP + r + 8)
                zs[5, to, :] = u[2 * zc, here, :] + u[2 * zc + 1, here, :]
            else:
                zs[5, to, :] = jnp.zeros((8, NX), F32)

    pairs = table((256, 128), lambda r, c: r // 2 == c)
    for comp in range(6):
        for b in range(4):
            t = restrict_block(zs[comp, :, 256 * b : 256 * b + 256], pairs)
            if comp < 4:
                ct[comp, 8 + 128 * b : 136 + 128 * b, :] = t
            elif comp == 4:
                ct0[8 + 128 * b : 136 + 128 * b, :] = t
            else:
                rfm[128 * b : 128 * b + 128, :] = t
    for comp in range(4):
        ct[comp, 0:8, :] = ct[comp, CX : CX + 8, :]
        ct[comp, CX + 8 : CX + 32, :] = ct[comp, 8:32, :]
    ct0[0:8, :] = ct0[CX : CX + 8, :]
    ct0[CX + 8 : CX + 16, :] = ct0[8:16, :]
    lane = lax.broadcasted_iota(jnp.int32, (64, CL), 1)
    for r in range(0, CX, 64):
        c = ct0[8 + r : 72 + r, :]
        xl, xh, yl, yh, zl, zh = coarse_coefs(*(ct[i, 8 + r : 72 + r, :] for i in range(4)))
        s, n = y_rolled(c, CL, 1)
        b = jnp.where(lane < 32, 0.0, pltpu.roll(c, 32, 1))
        t = jnp.where(lane >= 96, 0.0, pltpu.roll(c, 96, 1))
        w = ct0[7 + r : 71 + r, :]
        e = ct0[9 + r : 73 + r, :]
        gcp[r : r + 64, :] = c + (
            (xl * (w - c) + xh * (e - c)) + (yl * (s - c) + yh * (n - c)) + (zl * (b - c) + zh * (t - c))
        )
        cb[r : r + 64, :] = jnp.where(lane < 32, zl, jnp.where(lane >= 96, zh, 0.0))


CROWS = CX + 32


def interior(state, velocity, diffusivity):
    small = jax.ShapeDtypeStruct((CX, CL), F32)
    return pl.pallas_call(
        interior_kernel,
        out_shape=[
            jax.ShapeDtypeStruct((4, NY, NX), F32),
            jax.ShapeDtypeStruct((6, NY, NX), F32),
            jax.ShapeDtypeStruct((4, CROWS, CL), F32),
            small,
            small,
            small,
        ],
        in_specs=[anywhere()] * 3,
        out_specs=[whole()] * 6,
        scratch_shapes=[
            pltpu.VMEM((LZ, PADDED, NX), F32),
            pltpu.VMEM((LZ, PADDED, NX), F32),
            pltpu.VMEM((3, LZ, NY, NX), F32),
            pltpu.VMEM((LZ, NY, NX), F32),
            pltpu.VMEM((6, 4 * NY, NX), F32),
            pltpu.VMEM((CX + 16, CL), F32),
            pltpu.SemaphoreType.DMA,
            pltpu.SemaphoreType.DMA((LZ,)),
            pltpu.SemaphoreType.DMA((LZ,)),
        ],
        compiler_params=params(40),
        cost_estimate=pl.CostEstimate(flops=60_000_000, bytes_accessed=20_000_000, transcendentals=0),
        name="interior",
    )(state, velocity, diffusivity)


def finish_kernel(rlo, rhi, olo, ohi, edge, vlo, vhi, dlo, dhi, gcp, cb, rfm, ct, ub, msg, gc, pad, zsum, jp):
    slice_index = lax.axis_index("tm")
    for side, (rec, own, v, d) in enumerate(((rlo, olo, vlo, dlo), (rhi, ohi, vhi, dhi))):
        for r in range(0, NY, 8):
            pad[side, TOP + r : TOP + r + 8, :] = (
                own[NY + r : NY + r + 8, :] + own[2 * NY + r : 2 * NY + r + 8, :] * rec[r : r + 8, :]
            )
        wrap_rows(pad, side)
        for r in range(0, NY, 8):
            rows = slice(r, r + 8)
            c, w, e, s, n = plane(pad, side, r)
            outside = rec[NY + r : NY + r + 8, :] + rec[2 * NY + r : 2 * NY + r + 8, :] * own[r : r + 8, :]
            inside = edge[side, rows, :]
            b, t = (outside, inside) if side == 0 else (inside, outside)
            last = advanced(c, w, e, s, n, b, t, v[0, 0, rows, :], v[1, 0, rows, :], v[2, 0, rows, :], d[0, rows, :])
            near = edge[2 + side, rows, :] + edge[4 + side, rows, :] * c
            ub[3 * side, rows, :] = last
            ub[1 + side, rows, :] = near
            zsum[side * NY + r : side * NY + r + 8, :] = last + near
    pairs = table(
        (128, 128), lambda r, c: ((r < 64) & (c == r // 2)) | ((r >= 64) & (c == 96 + (r - 64) // 2))
    )
    lane = lax.broadcasted_iota(jnp.int32, (128, 128), 1)
    halo_lo = jnp.concatenate([rlo[3 * NY : MSG, 128 * i : 128 * i + 128] for i in range(8)], axis=0)
    halo_hi = jnp.concatenate([rhi[3 * NY : MSG, 128 * i : 128 * i + 128] for i in range(8)], axis=0)
    for b in range(4):
        rows = slice(128 * b, 128 * b + 128)
        t = restrict_block(zsum[:, 256 * b : 256 * b + 256], pairs) + rfm[rows, :]
        hl = pltpu.roll(halo_lo, (128 - 32 * b) % 128, 1) if b else halo_lo
        hh = pltpu.roll(halo_hi, (96 - 32 * b) % 128, 1) if b != 3 else halo_hi
        halo = jnp.where(lane < 32, hl, hh)
        g = gcp[rows, :] + cb[rows, :] * halo
        g = jnp.where(slice_index == 0, 0.0, g)
        gc[rows, :] = g
        jp[8 + 128 * b : 136 + 128 * b, :] = t - g
    jp[0:8, :] = jp[CX : CX + 8, :]
    jp[CX + 8 : CX + 24, :] = jp[8:24, :]
    comp = slice_index // 2
    first = pl.multiple_of((slice_index % 2) * 16, 16)
    for i in range(BLOCKS):
        msg[i, 0:WIN, :] = jp[XB * i : XB * i + WIN, :]
        msg[i, WIN : WIN + 16, :] = ct[comp, pl.ds(first + XB * i, 16), :]


def finish(rlo, rhi, olo, ohi, edge, velocity, diffusivity, gcp, cb, rfm, ct):
    return pl.pallas_call(
        finish_kernel,
        out_shape=[
            jax.ShapeDtypeStruct((4, NY, NX), F32),
            jax.ShapeDtypeStruct((BLOCKS, WIN + 16, CL), F32),
            jax.ShapeDtypeStruct((CX, CL), F32),
        ],
        grid=(1,),
        in_specs=[whole()] * 5 + layer_specs() + [whole()] * 4,
        out_specs=[whole()] * 3,
        scratch_shapes=[
            pltpu.VMEM((2, PADDED, NX), F32),
            pltpu.VMEM((2 * NY, NX), F32),
            pltpu.VMEM((CX + 24, CL), F32),
        ],
        compiler_params=params(32),
        name="finish",
    )(rlo, rhi, olo, ohi, edge, velocity, velocity, diffusivity, diffusivity, gcp, cb, rfm, ct)


HALO = 18


def pick_kernel(got, up, down):
    for out, near, far in ((up, 3, 2), (down, 0, 1)):
        for j in range(7):
            out[j] = got[QUAD * j + near, 0:WIN, :]
        for j in range(3):
            out[7 + j] = got[QUAD * j + far, 0:WIN, :]
        for k in range(GROUPS):
            rows = slice(16 * (k % 2), 16 * (k % 2) + 16)
            out[10 + k // 2, rows, :] = got[QUAD * k + near, WIN : WIN + 16, :]
            out[14 + k // 2, rows, :] = got[QUAD * k + far, WIN : WIN + 16, :]


def pick(got):
    halo = jax.ShapeDtypeStruct((HALO, WIN, CL), F32)
    return pl.pallas_call(
        pick_kernel,
        out_shape=[halo, halo],
        in_specs=[whole()],
        out_specs=[whole(), whole()],
        compiler_params=params(16),
        name="pick",
    )(got)


LANES = 8 * CL


def chain_kernel(got, below, above, out, src, cf, e):
    for j in range(7):
        if j < 3:
            src[j, :, 0:CL] = below[7 + j]
            src[j, :, 7 * CL :] = above[7 + j]
        else:
            src[j, :, 0:CL] = jnp.zeros((WIN, CL), F32)
            src[j, :, 7 * CL :] = jnp.zeros((WIN, CL), F32)
        src[j, :, CL : 2 * CL] = below[j]
        src[j, :, 6 * CL : 7 * CL] = above[j]
        for q in range(QUAD):
            src[j, :, (2 + q) * CL : (3 + q) * CL] = got[QUAD * j + q, 0:WIN, :]
    for block in range(8):
        lanes = slice(block * CL, block * CL + CL)
        for half in range(2):
            rows = slice(16 * half, 16 * half + 16)
            if block == 0:
                parts = [below[14 + i, rows, :] for i in range(4)]
            elif block == 1:
                parts = [below[10 + i, rows, :] for i in range(4)]
            elif block == 6:
                parts = [above[10 + i, rows, :] for i in range(4)]
            elif block == 7:
                parts = [above[14 + i, rows, :] for i in range(4)]
            else:
                parts = [got[QUAD * (2 * i + half) + block - 2, WIN : WIN + 16, :] for i in range(4)]
            for i, value in enumerate(coarse_coefs(*parts)):
                cf[i, rows, lanes] = value
    for q in range(QUAD):
        out[q] = jnp.zeros((XB, CL), F32)
    e[...] = src[0]
    for k in range(1, GROUPS):
        c = e[...]
        s, n = y_rolled(c, LANES, 1)
        w, x = pltpu.roll(c, 1, 0), pltpu.roll(c, WIN - 1, 0)
        b, t = pltpu.roll(c, 32, 1), pltpu.roll(c, LANES - 32, 1)
        y = c + (
            (cf[0] * (w - c) + cf[1] * (x - c))
            + (cf[2] * (s - c) + cf[3] * (n - c))
            + (cf[4] * (b - c) + cf[5] * (t - c))
        )
        for q in range(QUAD):
            out[QUAD * k + q] = y[8 : 8 + XB, (2 + q) * CL : (3 + q) * CL]
        if k < GROUPS - 1:
            e[...] = y + src[k]


def chain(got, below, above):
    return pl.pallas_call(
        chain_kernel,
        out_shape=jax.ShapeDtypeStruct((BLOCKS, XB, CL), F32),
        in_specs=[whole()] * 3,
        out_specs=whole(),
        scratch_shapes=[
            pltpu.VMEM((7, WIN, LANES), F32),
            pltpu.VMEM((6, WIN, LANES), F32),
            pltpu.VMEM((WIN, LANES), F32),
        ],
        compiler_params=params(24),
        name="chain",
    )(got, below, above)


def result_kernel(y, gc, mid, ub, out):
    copy_y = table((256, CL), lambda r, c: r // 2 == c)
    copy_x = table((128, 256), lambda r, c: r == c // 2)
    for b in range(4):
        rows = slice(128 * b, 128 * b + 128)
        cols = slice(256 * b, 256 * b + 256)
        parts = split3(y[rows, :] - gc[rows, :])
        fine = sum(dot(dot(copy_y, p, 1, 1).astype(BF16), copy_x, 1, 0) for p in parts)
        for z in range(LZ):
            zc = z // 2
            base = mid[z - 2, :, cols] if 2 <= z < 6 else ub[z if z < 2 else z - 4, :, cols]
            out[z, :, cols] = base + fine[zc * NY : zc * NY + NY, :]


def result(y, gc, mid, ub):
    return pl.pallas_call(
        result_kernel,
        out_shape=jax.ShapeDtypeStruct((LZ, NY, NX), F32),
        in_specs=[whole()] * 4,
        out_specs=whole(),
        compiler_params=params(24),
        name="result",
    )(y, gc, mid, ub)


def shift(value, axes, by):
    count = lax.axis_size(axes)
    return lax.ppermute(value, axes, [(i, i + by) for i in range(count) if 0 <= i + by < count])


def shards(state_old, velocity, diffusivity):
    state = state_old[0]
    olo, ohi = edges(state, velocity, diffusivity)
    rlo = shift(ohi, SPACE, 1)
    rhi = shift(olo, SPACE, -1)
    mid, edge, ct, gcp, cb, rfm = interior(state, velocity, diffusivity)
    ub, msg, gc = finish(rlo, rhi, olo, ohi, edge, velocity, diffusivity, gcp, cb, rfm, ct)
    got = lax.all_to_all(msg, GROUP, 0, 0)
    up, down = pick(got)
    below = shift(up, "px", 1)
    above = shift(down, "px", -1)
    back = lax.all_to_all(chain(got, below, above), GROUP, 0, 0)
    return result(back.reshape(CX, CL), gc, mid, ub)[None]


def solution(mesh):
    fine_mesh = Mesh(mesh.devices.reshape(GROUPS, 4, 2, 2), ("tm",) + SPACE)
    return jax.shard_map(
        shards,
        mesh=fine_mesh,
        in_specs=(
            P("tm", SPACE, None, None),
            P(None, SPACE, None, None),
            P(SPACE, None, None),
        ),
        out_specs=P("tm", SPACE, None, None),
        check_vma=False,
    )
```

time: 270 us -> 88.3 us (0.33)
  the two profiles are of different devices: /device:TPU:18 before, /device:TPU:5 now
where the time goes in v1:
time: 88.3 us; the launch traced here: 86.9 us
  blocking collectives  36.1 us (41%)
  Pallas kernels  25.2 us (29%)
  starting transfers between devices  11.3 us (13%)
  waiting for transfers between devices  8.15 us (9%)
  local copies, waits for them, and re-layouts  5.98 us (7%)
    all_to_all x1, blocking collectives, shards(): got = lax.all_to_all(msg, GROUP, 0, 0)  22.8 us
    pallas_call x1, Pallas kernels, interior(): pl.pallas_call(interior_kernel, out_shape=[jax.ShapeDtypeStruct((4, NY, N...  17.7 us
    all_to_all x1, blocking collectives, shards(): back = lax.all_to_all(chain(got, below, above), GROUP, 0, 0)  13.2 us
    ppermute x4, starting transfers between devices, shift(): lax.ppermute(value, axes, [(i, i + by) for i in range(count) if 0 <= i +...  11.3 us
    ppermute x4, waiting for transfers between devices, shift(): lax.ppermute(value, axes, [(i, i + by) for i in range(count) if 0 <= i +...  8.15 us
    unnamed x12, local copies, waits for them, and re-layouts  5.98 us
    pallas_call x1, Pallas kernels, result(): pl.pallas_call(result_kernel, out_shape=jax.ShapeDtypeStruct((LZ, NY, NX)...  2.43 us
  transfers between devices with their start and end apart: 4, of which 3 were waited for; matrix products, arithmetic and copies ran while one was open for 0% of the time, Pallas kernels for 20%

profile of v1, /device:TPU:5, one launch (start us, length us, event | category | flops | bytes accessed | tf_op | source)
XLA Modules:
  0.0 86.9 jit_solution(15145693620075351278)
XLA Ops:
  0.0 0.0 copy-start
  0.0 2.8 %copy-done = f32[3,8,64,1024]{3,2,1,0:T(8,128)S(1)} copy-done((f32[3,8,64,1024]{3,2,1,0:T(8,128)S(1)}, f32[3,8,64,1024]{3,2,1,0:T(8,128)}, u32[]{:S(2)}) %copy-start) | copy-done | bytes 6291480
  2.8 0.0 copy-start.2
  2.8 1.6 %copy-done.2 = f32[8,64,1024]{2,1,0:T(8,128)S(1)} copy-done((f32[8,64,1024]{2,1,0:T(8,128)S(1)}, f32[8,64,1024]{2,1,0:T(8,128)}, u32[]{:S(2)}) %copy-start.2) | copy-done | bytes 2097176
  4.4 0.0 copy-start.4
  4.4 1.6 %copy-done.4 = f32[1,8,64,1024]{3,2,1,0:T(8,128)S(1)} copy-done((f32[1,8,64,1024]{3,2,1,0:T(8,128)S(1)}, f32[1,8,64,1024]{3,2,1,0:T(8,128)}, u32[]{:S(2)}) %copy-start.4) | copy-done | bytes 2097176
  6.0 0.0 copy-start.3
  6.0 0.0 copy-start.5
  6.0 1.7 %edges.1 = (f32[208,1024]{1,0:T(8,128)S(1)}, f32[208,1024]{1,0:T(8,128)S(1)}) custom-call(f32[8,64,1024]{2,1,0:T(8,128)S(1)} %bitcast.3, f32[8,64,1024]{2,1,0:T(8,128)S(1)} %bitcast.4, f32[3,8,64,1024]{3,2,1,0:T(8,128)S(1)} %copy-done, f32[3,8,64,1024]{3,2,1,0:T(8,128)S(1)} %copy-done, f32[8,64,1024]{2,1,0:T(8,128)S(1)} %copy-done.2, ...), custom_call_target="tpu_custom_call" | custom-call | tf_op jit(solution)/shard_map/edges/pallas_call | solution.py:148
  7.6 4.1 %collective-permute-start = (f32[208,1024]{1,0:T(8,128)S(1)}, f32[208,1024]{1,0:T(8,128)S(1)}, u32[]{:S(2)}, u32[]{:S(2)}) collective-permute-start(f32[208,1024]{1,0:T(8,128)S(1)} %get-tuple-element.18.ohi), channel_id=1, source_target_pairs={{0,1},{1,2},{2,3},{3,4},{4,5},{5,6},{6,7},{7,8},{8,9},{9,10},{10,1... | collective-permute-start | bytes 2555912 | tf_op jit(solution)/shard_map/ppermute | solution.py:484
  11.7 1.9 %collective-permute-start.1 = (f32[208,1024]{1,0:T(8,128)S(1)}, f32[208,1024]{1,0:T(8,128)S(1)}, u32[]{:S(2)}, u32[]{:S(2)}) collective-permute-start(f32[208,1024]{1,0:T(8,128)S(1)} %get-tuple-element.19.olo), channel_id=1, source_target_pairs={{1,0},{2,1},{3,2},{4,3},{5,4},{6,5},{7,6},{8,7},{9,8},{10,9},{11,1... | collective-permute-start | bytes 2555912 | tf_op jit(solution)/shard_map/ppermute | solution.py:484
  13.7 0.0 copy-done.3
  13.7 0.0 copy-done.5
  13.7 0.0 copy-start.1
  13.7 17.7 %interior.1 = (f32[4,64,1024]{2,1,0:T(8,128)S(1)}, f32[6,64,1024]{2,1,0:T(8,128)S(1)}, f32[4,544,128]{2,1,0:T(8,128)S(1)}, f32[512,128]{1,0:T(8,128)S(1)}, f32[5...) custom-call(f32[8,64,1024]{2,1,0:T(8,128)S(1)} %bitcast.5, f32[3,8,64,1024]{3,2,1,0:T(8,128)} %vhi.3, f32[8,64,1024]{2,1,0:T(8,128)S(1)} %copy-done.3), custom_call_target="tpu_custom_call" | custom-call | flops 60000000 | bytes 20000000 | tf_op jit(solution)/shard_map/interior/pallas_call | solution.py:270
  31.4 0.0 collective-permute-done.rlo
  31.4 0.2 collective-permute-done.1.rhi
  31.7 0.0 copy-done.1
  31.7 1.7 %finish.1 = (f32[4,64,1024]{2,1,0:T(8,128)S(1)}, f32[32,48,128]{2,1,0:T(8,128)S(1)}, f32[512,128]{1,0:T(8,128)S(1)}) custom-call(f32[208,1024]{1,0:T(8,128)S(1)} %collective-permute-done.rlo, f32[208,1024]{1,0:T(8,128)S(1)} %collective-permute-done.1.rhi, f32[208,1024]{1,0:T(8,128)S(1)} %get-tuple-element.19.olo, f32[208,1024]{1,0:T(8,128)S(1)} %get-tuple-element.18.ohi, ...), custom_call_target="tpu_custom_call" | custom-call | tf_op jit(solution)/shard_map/finish/pallas_call | solution.py:344
  33.4 22.8 %all_to_all.10.got = f32[32,48,128]{2,1,0:T(8,128)S(1)} all-to-all(f32[32,48,128]{2,1,0:T(8,128)S(1)} %get-tuple-element.25), channel_id=1, replica_groups=mesh['tm'=8,'px'=4,'pz'=2,'core'=2] {'tm','pz','core'}, dimensions={0} | all-to-all | bytes 1572864 | tf_op jit(solution)/shard_map/all_to_all | solution.py:494
  56.3 2.8 %collective-permute-start.2 = (f32[18,32,128]{2,1,0:T(8,128)S(1)}, f32[18,32,128]{2,1,0:T(8,128)S(1)}, u32[]{:S(2)}, u32[]{:S(2)}) collective-permute-start(f32[18,32,128]{2,1,0:T(8,128)S(1)} %get-tuple-element.26), channel_id=1, source_target_pairs={{0,4},{4,8},{8,12},{1,5},{5,9},{9,13},{2,6},{6,10},{10,14},{3,7},{... | collective-permute-start | bytes 884744 | tf_op jit(solution)/shard_map/ppermute | solution.py:484
  59.1 2.5 %collective-permute-start.3 = (f32[18,32,128]{2,1,0:T(8,128)S(1)}, f32[18,32,128]{2,1,0:T(8,128)S(1)}, u32[]{:S(2)}, u32[]{:S(2)}) collective-permute-start(f32[18,32,128]{2,1,0:T(8,128)S(1)} %get-tuple-element.27), channel_id=1, source_target_pairs={{4,0},{8,4},{12,8},{5,1},{9,5},{13,9},{6,2},{10,6},{14,10},{7,3},{... | collective-permute-start | bytes 884744 | tf_op jit(solution)/shard_map/ppermute | solution.py:484
  61.6 5.3 %collective-permute-done.2.below = f32[18,32,128]{2,1,0:T(8,128)S(1)} collective-permute-done((f32[18,32,128]{2,1,0:T(8,128)S(1)}, f32[18,32,128]{2,1,0:T(8,128)S(1)}, u32[]{:S(2)}, u32[]{:S(2)}) %collective-permute-start.2) | collective-permute-done | bytes 294944 | tf_op jit(solution)/shard_map/ppermute | solution.py:484
  66.9 2.6 %collective-permute-done.3.above = f32[18,32,128]{2,1,0:T(8,128)S(1)} collective-permute-done((f32[18,32,128]{2,1,0:T(8,128)S(1)}, f32[18,32,128]{2,1,0:T(8,128)S(1)}, u32[]{:S(2)}, u32[]{:S(2)}) %collective-permute-start.3) | collective-permute-done | bytes 294944 | tf_op jit(solution)/shard_map/ppermute | solution.py:484
  69.5 1.7 %chain.1 = f32[32,16,128]{2,1,0:T(8,128)S(1)} custom-call(f32[32,48,128]{2,1,0:T(8,128)S(1)} %all_to_all.10.got, f32[18,32,128]{2,1,0:T(8,128)S(1)} %collective-permute-done.2.below, f32[18,32,128]{2,1,0:T(8,128)S(1)} %collective-permute-done.3.above), custom_call_target="tpu_custom_call" | custom-call | tf_op jit(solution)/shard_map/chain/pallas_call | solution.py:442
  71.2 13.2 %all_to_all.11 = f32[32,16,128]{2,1,0:T(8,128)S(1)} all-to-all(f32[32,16,128]{2,1,0:T(8,128)S(1)} %chain.1), channel_id=1, replica_groups=mesh['tm'=8,'px'=4,'pz'=2,'core'=2] {'tm','pz','core'}, dimensions={0} | all-to-all | bytes 524288 | tf_op jit(solution)/shard_map/all_to_all | solution.py:498
  84.4 2.4 %result.1 = f32[8,64,1024]{2,1,0:T(8,128)} custom-call(f32[512,128]{1,0:T(8,128)S(1)} %bitcast.6, f32[512,128]{1,0:T(8,128)S(1)} %get-tuple-element.28.gc, f32[4,64,1024]{2,1,0:T(8,128)S(1)} %get-tuple-element.29.mid, f32[4,64,1024]{2,1,0:T(8,128)S(1)} %get-tuple-element.30.ub), custom_call_target="tpu_custom_call" | custom-call | tf_op jit(solution)/shard_map/result/pallas_call | solution.py:472
  (1 shorter events, 0.0 us)
Async XLA Ops:
  0.0 2.8 %copy-start = (f32[3,8,64,1024]{3,2,1,0:T(8,128)S(1)}, f32[3,8,64,1024]{3,2,1,0:T(8,128)}, u32[]{:S(2)}) copy-start(f32[3,8,64,1024]{3,2,1,0:T(8,128)} %vhi.3) | copy-start | bytes 18874372
  2.8 1.6 %copy-start.2 = (f32[8,64,1024]{2,1,0:T(8,128)S(1)}, f32[8,64,1024]{2,1,0:T(8,128)}, u32[]{:S(2)}) copy-start(f32[8,64,1024]{2,1,0:T(8,128)} %dhi.3) | copy-start | bytes 6291460
  4.4 1.6 %copy-start.4 = (f32[1,8,64,1024]{3,2,1,0:T(8,128)S(1)}, f32[1,8,64,1024]{3,2,1,0:T(8,128)}, u32[]{:S(2)}) copy-start(f32[1,8,64,1024]{3,2,1,0:T(8,128)} %param.3) | copy-start | bytes 6291460
  6.0 7.7 %copy-start.3 = (f32[8,64,1024]{2,1,0:T(8,128)S(1)}, f32[8,64,1024]{2,1,0:T(8,128)}, u32[]{:S(2)}) copy-start(f32[8,64,1024]{2,1,0:T(8,128)} %dhi.3) | copy-start | bytes 6291460
  6.0 7.7 %copy-start.5 = (f32[1,8,64,1024]{3,2,1,0:T(8,128)S(1)}, f32[1,8,64,1024]{3,2,1,0:T(8,128)}, u32[]{:S(2)}) copy-start(f32[1,8,64,1024]{3,2,1,0:T(8,128)} %param.3) | copy-start | bytes 6291460
  7.6 23.8 %collective-permute-start = (f32[208,1024]{1,0:T(8,128)S(1)}, f32[208,1024]{1,0:T(8,128)S(1)}, u32[]{:S(2)}, u32[]{:S(2)}) collective-permute-start(f32[208,1024]{1,0:T(8,128)S(1)} %get-tuple-element.18.ohi), channel_id=1, source_target_pairs={{0,1},{1,2},{2,3},{3,4},{4,5},{5,6},{6,7},{7,8},{8,9},{9,10},{10,1... | collective-permute-start | bytes 2555912 | tf_op jit(solution)/shard_map/ppermute | solution.py:484
  11.7 19.9 %collective-permute-start.1 = (f32[208,1024]{1,0:T(8,128)S(1)}, f32[208,1024]{1,0:T(8,128)S(1)}, u32[]{:S(2)}, u32[]{:S(2)}) collective-permute-start(f32[208,1024]{1,0:T(8,128)S(1)} %get-tuple-element.19.olo), channel_id=1, source_target_pairs={{1,0},{2,1},{3,2},{4,3},{5,4},{6,5},{7,6},{8,7},{9,8},{10,9},{11,1... | collective-permute-start | bytes 2555912 | tf_op jit(solution)/shard_map/ppermute | solution.py:484
  13.7 18.0 %copy-start.1 = (f32[3,8,64,1024]{3,2,1,0:T(8,128)S(1)}, f32[3,8,64,1024]{3,2,1,0:T(8,128)}, u32[]{:S(2)}) copy-start(f32[3,8,64,1024]{3,2,1,0:T(8,128)} %vhi.3) | copy-start | bytes 18874372
  56.3 10.6 %collective-permute-start.2 = (f32[18,32,128]{2,1,0:T(8,128)S(1)}, f32[18,32,128]{2,1,0:T(8,128)S(1)}, u32[]{:S(2)}, u32[]{:S(2)}) collective-permute-start(f32[18,32,128]{2,1,0:T(8,128)S(1)} %get-tuple-element.26), channel_id=1, source_target_pairs={{0,4},{4,8},{8,12},{1,5},{5,9},{9,13},{2,6},{6,10},{10,14},{3,7},{... | collective-permute-start | bytes 884744 | tf_op jit(solution)/shard_map/ppermute | solution.py:484
  59.1 10.4 %collective-permute-start.3 = (f32[18,32,128]{2,1,0:T(8,128)S(1)}, f32[18,32,128]{2,1,0:T(8,128)S(1)}, u32[]{:S(2)}, u32[]{:S(2)}) collective-permute-start(f32[18,32,128]{2,1,0:T(8,128)S(1)} %get-tuple-element.27), channel_id=1, source_target_pairs={{4,0},{8,4},{12,8},{5,1},{9,5},{13,9},{6,2},{10,6},{14,10},{7,3},{... | collective-permute-start | bytes 884744 | tf_op jit(solution)/shard_map/ppermute | solution.py:484

commit v2 on v1

v2 whole, which is shorter than its diff:
```python
import jax
import jax.numpy as jnp
from jax import lax
from jax.experimental import pallas as pl
from jax.experimental.pallas import tpu as pltpu
from jax.sharding import Mesh
from jax.sharding import PartitionSpec as P

F32 = jnp.float32
BF16 = jnp.bfloat16
NY, NX = 64, 1024
LZ = 8
CX, CL = 512, 128
GROUPS = 8
QUAD = 4
BLOCKS = GROUPS * QUAD
XB = CX // BLOCKS
WIN = XB + 16
TOP = 8
PADDED = NY + 16
SPACE = ("px", "pz", "core")
GROUP = ("tm", "pz", "core")


def params(mib):
    return pltpu.CompilerParams(vmem_limit_bytes=mib * 1024 * 1024)


def split3(x):
    hi = x.astype(BF16)
    rest = x - hi.astype(F32)
    mid = rest.astype(BF16)
    return hi, mid, (rest - mid.astype(F32)).astype(BF16)


def dot(a, b, ca, cb):
    return lax.dot_general(a, b, (((ca,), (cb,)), ((), ())), preferred_element_type=F32)


def table(shape, test):
    rows = lax.broadcasted_iota(jnp.int32, shape, 0)
    cols = lax.broadcasted_iota(jnp.int32, shape, 1)
    return test(rows, cols).astype(F32).astype(BF16)


def halved_x(part):
    halve = table((128, 256), lambda r, c: r == c // 2)
    return sum(dot(halve, p, 1, 1) for p in split3(part)) * 0.125


def put_columns(ref, at, value):
    for i in range(NX // 128):
        ref[i, at, :] = value[:, 128 * i : 128 * i + 128]


def paired(ref, column, first, rows):
    return ref[column, pl.ds(first, rows, 2), :] + ref[column, pl.ds(first + 1, rows, 2), :]


def advanced(c, w, e, s, n, b, t, ax, ay, az, k):
    lap = ((w + e) + (s + n)) + ((b + t) - 6.0 * c)
    dx = jnp.abs(ax) * (jnp.where(ax > 0, w, e) - c)
    dy = jnp.abs(ay) * (jnp.where(ay > 0, s, n) - c)
    dz = jnp.abs(az) * (jnp.where(az > 0, b, t) - c)
    return (c + k * lap) + ((dx + dy) + dz)


def wrap_rows(ref, z):
    ref[z, TOP - 1 : TOP, :] = ref[z, TOP + NY - 1 : TOP + NY, :]
    ref[z, TOP + NY : TOP + NY + 1, :] = ref[z, TOP : TOP + 1, :]


def plane(ref, z, r):
    c = ref[z, TOP + r : TOP + r + 8, :]
    s = ref[z, TOP + r - 1 : TOP + r + 7, :]
    n = ref[z, TOP + r + 1 : TOP + r + 9, :]
    return c, pltpu.roll(c, 1, 1), pltpu.roll(c, NX - 1, 1), s, n


def coarse_coefs(vx, vy, vz, k):
    half = 0.5 * k
    out = []
    for a in (vx, vy, vz):
        out += [half + jnp.maximum(a, 0.0), half - jnp.minimum(a, 0.0)]
    return out


def y_rolled(u, width, axis):
    y = lax.broadcasted_iota(jnp.int32, u.shape, axis) % 32
    s = jnp.where(y == 0, pltpu.roll(u, width - 31, axis), pltpu.roll(u, 1, axis))
    n = jnp.where(y == 31, pltpu.roll(u, 31, axis), pltpu.roll(u, width - 1, axis))
    return s, n


MSG = 3 * NY + 16
CROWS = CX + 32


def edges_kernel(st, vel, dif, lo, hi, pad, inner, v, d, zs, sems):
    copies = []
    for side, (z, near) in enumerate(((0, 1), (LZ - 1, LZ - 2))):
        pairs = (
            (st.at[z], pad.at[side, TOP : TOP + NY, :]),
            (vel.at[:, z], v.at[side]),
            (dif.at[z], d.at[side]),
            (st.at[near], inner.at[side]),
        )
        copies.append([pltpu.make_async_copy(a, b, sems.at[side, i]) for i, (a, b) in enumerate(pairs)])
    for group in copies:
        for copy in group:
            copy.start()
    for side, out in enumerate((lo, hi)):
        for copy in copies[side]:
            copy.wait()
        wrap_rows(pad, side)
        for r in range(0, NY, 8):
            rows = slice(r, r + 8)
            c, w, e, s, n = plane(pad, side, r)
            inside = inner[side, rows, :]
            ax, ay, az = v[side, 0, rows, :], v[side, 1, rows, :], v[side, 2, rows, :]
            k = d[side, rows, :]
            none = jnp.zeros_like(c)
            if side == 0:
                a = advanced(c, w, e, s, n, none, inside, ax, ay, az, k)
                b = k + jnp.maximum(az, 0.0)
            else:
                a = advanced(c, w, e, s, n, inside, none, ax, ay, az, k)
                b = k - jnp.minimum(az, 0.0)
            out[r : r + 8, :] = c
            out[NY + r : NY + r + 8, :] = a
            out[2 * NY + r : 2 * NY + r + 8, :] = b
            put_columns(zs, slice(side * NY + r, side * NY + r + 8), c + inside)
    lane = lax.broadcasted_iota(jnp.int32, (128, 128), 1)
    clo = jnp.zeros((128, 128), F32)
    chi = jnp.zeros((128, 128), F32)
    for b in range(4):
        part = jnp.concatenate([paired(zs, 2 * b + i, 0, 64) for i in range(2)], axis=1)
        t = halved_x(jnp.concatenate([part, jnp.zeros_like(part)], axis=0))
        tl = jnp.where(lane < 32, t, 0.0)
        th = jnp.where((lane >= 32) & (lane < 64), t, 0.0)
        clo += pltpu.roll(tl, 32 * b, 1) if b else tl
        chi += pltpu.roll(th, (32 * b - 32) % 128, 1) if b != 1 else th
    for i in range(8):
        lo[3 * NY : 3 * NY + 16, 128 * i : 128 * i + 128] = clo[16 * i : 16 * i + 16, :]
        hi[3 * NY : 3 * NY + 16, 128 * i : 128 * i + 128] = chi[16 * i : 16 * i + 16, :]


def whole():
    return pl.BlockSpec(memory_space=pltpu.VMEM)


def remains():
    return pl.BlockSpec(memory_space=pltpu.HBM)


def edges(state, velocity, diffusivity):
    msg = jax.ShapeDtypeStruct((MSG, NX), F32)
    return pl.pallas_call(
        edges_kernel,
        out_shape=[msg, msg],
        in_specs=[remains()] * 3,
        out_specs=[whole(), whole()],
        scratch_shapes=[
            pltpu.VMEM((2, PADDED, NX), F32),
            pltpu.VMEM((2, NY, NX), F32),
            pltpu.VMEM((2, 3, NY, NX), F32),
            pltpu.VMEM((2, NY, NX), F32),
            pltpu.VMEM((8, 2 * NY, 128), F32),
            pltpu.SemaphoreType.DMA((2, 4)),
        ],
        compiler_params=params(16),
        name="edges",
    )(state, velocity, diffusivity)


def interior_kernel(st, v, d, fin, edge, ct, gcp, cb, ymid, u, u1, zs, ct0, usem):
    copy = pltpu.make_async_copy(st, u.at[:, TOP : TOP + NY, :], usem)
    copy.start()
    for zc in range(4):
        for r in range(0, NY, 8):
            to, rows = slice(zc * NY + r, zc * NY + r + 8), slice(r, r + 8)
            for comp in range(3):
                put_columns(zs.at[comp], to, v[comp, 2 * zc, rows, :] + v[comp, 2 * zc + 1, rows, :])
            put_columns(zs.at[3], to, d[2 * zc, rows, :] + d[2 * zc + 1, rows, :])
    copy.wait()
    for z in range(LZ):
        wrap_rows(u, z)
    for zc in range(4):
        for r in range(0, NY, 8):
            here = slice(TOP + r, TOP + r + 8)
            put_columns(zs.at[4], slice(zc * NY + r, zc * NY + r + 8), u[2 * zc, here, :] + u[2 * zc + 1, here, :])

    def first(z, _):
        for r in range(0, NY, 8):
            rows = slice(r, r + 8)
            here = slice(TOP + r, TOP + r + 8)
            c, w, e, s, n = plane(u, z, r)
            u1[z, here, :] = advanced(
                c, w, e, s, n, u[z - 1, here, :], u[z + 1, here, :],
                v[0, z, rows, :], v[1, z, rows, :], v[2, z, rows, :], d[z, rows, :],
            )
        wrap_rows(u1, z)
        return 0

    lax.fori_loop(1, LZ - 1, first, 0)
    u1[0, TOP : TOP + NY, :] = jnp.zeros((NY, NX), F32)
    u1[LZ - 1, TOP : TOP + NY, :] = jnp.zeros((NY, NX), F32)
    edge[0] = u1[1, TOP : TOP + NY, :]
    edge[1] = u1[LZ - 2, TOP : TOP + NY, :]

    def second(z, _):
        for r in range(0, NY, 8):
            rows = slice(r, r + 8)
            here = slice(TOP + r, TOP + r + 8)
            c, w, e, s, n = plane(u1, z, r)
            fin[z - 1, rows, :] = advanced(
                c, w, e, s, n, u1[z - 1, here, :], u1[z + 1, here, :],
                v[0, z, rows, :], v[1, z, rows, :], v[2, z, rows, :], d[z, rows, :],
            )
        return 0

    lax.fori_loop(1, LZ - 1, second, 0)
    edge[2] = d[1] + jnp.maximum(v[2, 1], 0.0)
    edge[3] = d[LZ - 2] - jnp.minimum(v[2, LZ - 2], 0.0)
    for zc in (1, 2):
        for r in range(0, NY, 8):
            rows = slice(r, r + 8)
            put_columns(zs.at[5], slice((zc - 1) * NY + r, (zc - 1) * NY + r + 8), fin[2 * zc - 1, rows, :] + fin[2 * zc, rows, :])
    for i in range(8):
        ymid[i] = paired(zs.at[5], i, 0, 64)

    for comp in range(5):
        for b in range(4):
            t = halved_x(jnp.concatenate([paired(zs.at[comp], 2 * b + i, 0, 128) for i in range(2)], axis=1))
            if comp < 4:
                ct[comp, 8 + 128 * b : 136 + 128 * b, :] = t
            else:
                ct0[8 + 128 * b : 136 + 128 * b, :] = t
    for comp in range(4):
        ct[comp, 0:8, :] = ct[comp, CX : CX + 8, :]
        ct[comp, CX + 8 : CX + 32, :] = ct[comp, 8:32, :]
    ct0[0:8, :] = ct0[CX : CX + 8, :]
    ct0[CX + 8 : CX + 16, :] = ct0[8:16, :]
    lane = lax.broadcasted_iota(jnp.int32, (64, CL), 1)
    for r in range(0, CX, 64):
        c = ct0[8 + r : 72 + r, :]
        xl, xh, yl, yh, zl, zh = coarse_coefs(*(ct[i, 8 + r : 72 + r, :] for i in range(4)))
        s, n = y_rolled(c, CL, 1)
        b = jnp.where(lane < 32, 0.0, pltpu.roll(c, 32, 1))
        t = jnp.where(lane >= 96, 0.0, pltpu.roll(c, 96, 1))
        w = ct0[7 + r : 71 + r, :]
        e = ct0[9 + r : 73 + r, :]
        gcp[r : r + 64, :] = c + (
            (xl * (w - c) + xh * (e - c)) + (yl * (s - c) + yh * (n - c)) + (zl * (b - c) + zh * (t - c))
        )
        cb[r : r + 64, :] = jnp.where(lane < 32, zl, jnp.where(lane >= 96, zh, 0.0))


def interior(state, velocity, diffusivity):
    small = jax.ShapeDtypeStruct((CX, CL), F32)
    return pl.pallas_call(
        interior_kernel,
        out_shape=[
            jax.ShapeDtypeStruct((LZ - 2, NY, NX), F32),
            jax.ShapeDtypeStruct((4, NY, NX), F32),
            jax.ShapeDtypeStruct((4, CROWS, CL), F32),
            small,
            small,
            jax.ShapeDtypeStruct((8, 64, 128), F32),
        ],
        in_specs=[remains(), whole(), whole()],
        out_specs=[whole()] * 6,
        scratch_shapes=[
            pltpu.VMEM((LZ, PADDED, NX), F32),
            pltpu.VMEM((LZ, PADDED, NX), F32),
            pltpu.VMEM((6, 8, 4 * NY, 128), F32),
            pltpu.VMEM((CX + 16, CL), F32),
            pltpu.SemaphoreType.DMA,
        ],
        compiler_params=params(32),
        cost_estimate=pl.CostEstimate(flops=60_000_000, bytes_accessed=20_000_000, transcendentals=0),
        name="interior",
    )(state, velocity, diffusivity)


def finish_kernel(rlo, rhi, olo, ohi, fin, edge, vel, dif, gcp, cb, ymid, ct, ub, msg, gc, pad, v, d, zs, jp, sems):
    copies = []
    for side, z in enumerate((0, LZ - 1)):
        copies.append(pltpu.make_async_copy(vel.at[:, z], v.at[side], sems.at[side, 0]))
        copies.append(pltpu.make_async_copy(dif.at[z], d.at[side], sems.at[side, 1]))
    for copy in copies:
        copy.start()
    slice_index = lax.axis_index("tm")
    for side, (rec, own) in enumerate(((rlo, olo), (rhi, ohi))):
        for r in range(0, NY, 8):
            pad[side, TOP + r : TOP + r + 8, :] = (
                own[NY + r : NY + r + 8, :] + own[2 * NY + r : 2 * NY + r + 8, :] * rec[r : r + 8, :]
            )
        wrap_rows(pad, side)
        copies[2 * side].wait()
        copies[2 * side + 1].wait()
        for r in range(0, NY, 8):
            rows = slice(r, r + 8)
            c, w, e, s, n = plane(pad, side, r)
            outside = rec[NY + r : NY + r + 8, :] + rec[2 * NY + r : 2 * NY + r + 8, :] * own[r : r + 8, :]
            inside = edge[side, rows, :]
            b, t = (outside, inside) if side == 0 else (inside, outside)
            last = advanced(
                c, w, e, s, n, b, t,
                v[side, 0, rows, :], v[side, 1, rows, :], v[side, 2, rows, :], d[side, rows, :],
            )
            near = fin[5 * side, rows, :] + edge[2 + side, rows, :] * c
            ub[3 * side, rows, :] = last
            ub[1 + side, rows, :] = near
            put_columns(zs, slice(side * NY + r, side * NY + r + 8), last + near)
    lane = lax.broadcasted_iota(jnp.int32, (128, 128), 1)
    halo_lo = jnp.concatenate([rlo[3 * NY : MSG, 128 * i : 128 * i + 128] for i in range(8)], axis=0)
    halo_hi = jnp.concatenate([rhi[3 * NY : MSG, 128 * i : 128 * i + 128] for i in range(8)], axis=0)
    for b in range(4):
        rows = slice(128 * b, 128 * b + 128)
        t = halved_x(
            jnp.concatenate(
                [
                    jnp.concatenate([paired(zs, i, 0, 32), ymid[i], paired(zs, i, NY, 32)], axis=0)
                    for i in (2 * b, 2 * b + 1)
                ],
                axis=1,
            )
        )
        hl = pltpu.roll(halo_lo, (128 - 32 * b) % 128, 1) if b else halo_lo
        hh = pltpu.roll(halo_hi, (96 - 32 * b) % 128, 1) if b != 3 else halo_hi
        halo = jnp.where(lane < 32, hl, hh)
        g = gcp[rows, :] + cb[rows, :] * halo
        g = jnp.where(slice_index == 0, 0.0, g)
        gc[rows, :] = g
        jp[8 + 128 * b : 136 + 128 * b, :] = t - g
    jp[0:8, :] = jp[CX : CX + 8, :]
    jp[CX + 8 : CX + 24, :] = jp[8:24, :]
    comp = slice_index // 2
    first = pl.multiple_of((slice_index % 2) * 16, 16)
    for i in range(BLOCKS):
        msg[i, 0:WIN, :] = jp[XB * i : XB * i + WIN, :]
        msg[i, WIN : WIN + 16, :] = ct[comp, pl.ds(first + XB * i, 16), :]


def finish(rlo, rhi, olo, ohi, fin, edge, velocity, diffusivity, gcp, cb, ymid, ct):
    return pl.pallas_call(
        finish_kernel,
        out_shape=[
            jax.ShapeDtypeStruct((4, NY, NX), F32),
            jax.ShapeDtypeStruct((BLOCKS, WIN + 16, CL), F32),
            jax.ShapeDtypeStruct((CX, CL), F32),
        ],
        in_specs=[whole()] * 6 + [remains()] * 2 + [whole()] * 4,
        out_specs=[whole()] * 3,
        scratch_shapes=[
            pltpu.VMEM((2, PADDED, NX), F32),
            pltpu.VMEM((2, 3, NY, NX), F32),
            pltpu.VMEM((2, NY, NX), F32),
            pltpu.VMEM((8, 2 * NY, 128), F32),
            pltpu.VMEM((CX + 24, CL), F32),
            pltpu.SemaphoreType.DMA((2, 2)),
        ],
        compiler_params=params(24),
        name="finish",
    )(rlo, rhi, olo, ohi, fin, edge, velocity, diffusivity, gcp, cb, ymid, ct)


HALO = 13
SHARED = ((0, 6, 96), (1, 5, 64), (2, 4, 32))


def pick_kernel(got, up, down):
    lane = lax.broadcasted_iota(jnp.int32, (WIN, CL), 1)

    def coef(i, slab):
        return jnp.concatenate([got[QUAD * (2 * i + h) + slab, WIN : WIN + 16, :] for h in range(2)], axis=0)

    for out, near, far in ((up, 3, 2), (down, 0, 1)):
        for j in range(4):
            out[j] = got[QUAD * j + near, 0:WIN, :]
            out[7 + j] = coef(j, near)
        for j, other, width in SHARED:
            mine = lane >= CL - width if near == 3 else lane < width
            turn = CL - width if near == 3 else width
            out[4 + j] = jnp.where(
                mine, got[QUAD * j + far, 0:WIN, :], pltpu.roll(got[QUAD * other + near, 0:WIN, :], turn, 1)
            )
        for j in range(2):
            mine = lane >= 64 if near == 3 else lane < 64
            out[11 + j] = jnp.where(mine, coef(2 * j, far), pltpu.roll(coef(2 * j + 1, far), 64, 1))


def pick(got):
    halo = jax.ShapeDtypeStruct((HALO, WIN, CL), F32)
    return pl.pallas_call(
        pick_kernel,
        out_shape=[halo, halo],
        in_specs=[whole()],
        out_specs=[whole(), whole()],
        compiler_params=params(16),
        name="pick",
    )(got)


LANES = 8 * CL


def chain_kernel(got, below, above, out, src, cf, e):
    for j in range(7):
        for q in range(QUAD):
            src[j, :, (2 + q) * CL : (3 + q) * CL] = got[QUAD * j + q, 0:WIN, :]
        for halo, near, far in ((below, 1, 0), (above, 6, 7)):
            if j < 4:
                src[j, :, near * CL : near * CL + CL] = halo[j]
            if j >= 3:
                src[j, :, far * CL : far * CL + CL] = jnp.zeros((WIN, CL), F32)
    for halo, near, far in ((below, 1, 0), (above, 6, 7)):
        for j, other, width in SHARED:
            turn = width if near == 1 else CL - width
            src[j, :, far * CL : far * CL + CL] = halo[4 + j]
            src[other, :, near * CL : near * CL + CL] = pltpu.roll(halo[4 + j], turn, 1)
    for block in range(8):
        lanes = slice(block * CL, block * CL + CL)
        halo = below if block < 2 else above
        for half in range(2):
            rows = slice(16 * half, 16 * half + 16)
            if block in (1, 6):
                parts = [halo[7 + i, rows, :] for i in range(4)]
            elif block in (0, 7):
                parts = [
                    pltpu.roll(halo[11 + i // 2, rows, :], 64, 1) if i % 2 else halo[11 + i // 2, rows, :]
                    for i in range(4)
                ]
            else:
                parts = [got[QUAD * (2 * i + half) + block - 2, WIN : WIN + 16, :] for i in range(4)]
            for i, value in enumerate(coarse_coefs(*parts)):
                cf[i, rows, lanes] = value
    for q in range(QUAD):
        out[q] = jnp.zeros((XB, CL), F32)
    e[...] = src[0]
    for k in range(1, GROUPS):
        c = e[...]
        s, n = y_rolled(c, LANES, 1)
        w, x = pltpu.roll(c, 1, 0), pltpu.roll(c, WIN - 1, 0)
        b, t = pltpu.roll(c, 32, 1), pltpu.roll(c, LANES - 32, 1)
        y = c + (
            (cf[0] * (w - c) + cf[1] * (x - c))
            + (cf[2] * (s - c) + cf[3] * (n - c))
            + (cf[4] * (b - c) + cf[5] * (t - c))
        )
        for q in range(QUAD):
            out[QUAD * k + q] = y[8 : 8 + XB, (2 + q) * CL : (3 + q) * CL]
        if k < GROUPS - 1:
            e[...] = y + src[k]


def chain(got, below, above):
    return pl.pallas_call(
        chain_kernel,
        out_shape=jax.ShapeDtypeStruct((BLOCKS, XB, CL), F32),
        in_specs=[whole()] * 3,
        out_specs=whole(),
        scratch_shapes=[
            pltpu.VMEM((7, WIN, LANES), F32),
            pltpu.VMEM((6, WIN, LANES), F32),
            pltpu.VMEM((WIN, LANES), F32),
        ],
        compiler_params=params(24),
        name="chain",
    )(got, below, above)


def result_kernel(y, gc, fin, ub, out, buf, sems):
    copy_y = table((256, CL), lambda r, c: r // 2 == c)
    copy_x = table((128, 256), lambda r, c: r == c // 2)
    copies = []
    for b in range(4):
        rows = slice(128 * b, 128 * b + 128)
        cols = slice(256 * b, 256 * b + 256)
        parts = split3(y[rows, :] - gc[rows, :])
        fine = sum(dot(dot(copy_y, p, 1, 1).astype(BF16), copy_x, 1, 0) for p in parts)
        for z in range(LZ):
            base = fin[z - 1, :, cols] if 2 <= z < 6 else ub[z if z < 2 else z - 4, :, cols]
            buf[z, :, cols] = base + fine[z // 2 * NY : z // 2 * NY + NY, :]
        copies.append(pltpu.make_async_copy(buf.at[:, :, cols], out.at[:, :, cols], sems.at[b]))
        copies[b].start()
    for copy in copies:
        copy.wait()


def result(y, gc, fin, ub):
    return pl.pallas_call(
        result_kernel,
        out_shape=jax.ShapeDtypeStruct((LZ, NY, NX), F32),
        in_specs=[whole()] * 4,
        out_specs=remains(),
        scratch_shapes=[pltpu.VMEM((LZ, NY, NX), F32), pltpu.SemaphoreType.DMA((4,))],
        compiler_params=params(16),
        name="result",
    )(y, gc, fin, ub)


def shift(value, axes, by):
    count = lax.axis_size(axes)
    return lax.ppermute(value, axes, [(i, i + by) for i in range(count) if 0 <= i + by < count])


def shards(state_old, velocity, diffusivity):
    state = state_old[0]
    olo, ohi = edges(state, velocity, diffusivity)
    rlo = shift(ohi, SPACE, 1)
    rhi = shift(olo, SPACE, -1)
    fin, edge, ct, gcp, cb, ymid = interior(state, velocity, diffusivity)
    ub, msg, gc = finish(rlo, rhi, olo, ohi, fin, edge, velocity, diffusivity, gcp, cb, ymid, ct)
    got = lax.all_to_all(msg, GROUP, 0, 0)
    up, down = pick(got)
    below = shift(up, "px", 1)
    above = shift(down, "px", -1)
    back = lax.all_to_all(chain(got, below, above), GROUP, 0, 0)
    return result(back.reshape(CX, CL), gc, fin, ub)[None]


def solution(mesh):
    fine_mesh = Mesh(mesh.devices.reshape(GROUPS, 4, 2, 2), ("tm",) + SPACE)
    return jax.shard_map(
        shards,
        mesh=fine_mesh,
        in_specs=(
            P("tm", SPACE, None, None),
            P(None, SPACE, None, None),
            P(SPACE, None, None),
        ),
        out_specs=P("tm", SPACE, None, None),
        check_vma=False,
    )
```

time: 88.3 us -> 85.5 us (0.968)
  Pallas kernels: 25.2 us -> 14.2 us
  waiting for transfers between devices: 8.15 us -> 16.9 us
    pallas_call x2, Pallas kernels: 19.3 us -> 8.76 us  [the longest x1 7.22 us: interior(): pl.pallas_call(interior_kernel, out_shape=[jax.ShapeDtypeStruct((LZ - 2,...]
    ppermute x4, waiting for transfers between devices: 8.15 us -> 16.9 us  [shift(): lax.ppermute(value, axes, [(i, i + by) for i in range(count) if 0 <= i +...]
  transfers between devices with their start and end apart: 4 -> 4, of which waited for: 3 -> 4; matrix products, arithmetic and copies ran while one was open for 0% -> 0% of each run, Pallas kernels for 20% -> 9%
where the time goes in v2:
time: 85.5 us; the launch traced here: 84 us
  blocking collectives  35.3 us (41%)
  waiting for transfers between devices  16.9 us (20%)
  Pallas kernels  14.2 us (17%)
  starting transfers between devices  11.6 us (14%)
  local copies, waits for them, and re-layouts  5.98 us (7%)
    all_to_all x1, blocking collectives, shards(): got = lax.all_to_all(msg, GROUP, 0, 0)  22.1 us
    ppermute x4, waiting for transfers between devices, shift(): lax.ppermute(value, axes, [(i, i + by) for i in range(count) if 0 <= i +...  16.9 us
    all_to_all x1, blocking collectives, shards(): back = lax.all_to_all(chain(got, below, above), GROUP, 0, 0)  13.2 us
    ppermute x4, starting transfers between devices, shift(): lax.ppermute(value, axes, [(i, i + by) for i in range(count) if 0 <= i +...  11.6 us
    pallas_call x1, Pallas kernels, interior(): pl.pallas_call(interior_kernel, out_shape=[jax.ShapeDtypeStruct((LZ - 2,...  7.22 us
    unnamed x12, local copies, waits for them, and re-layouts  5.98 us
    pallas_call x1, Pallas kernels, result(): pl.pallas_call(result_kernel, out_shape=jax.ShapeDtypeStruct((LZ, NY, NX)...  1.93 us
    pallas_call x1, Pallas kernels, chain(): pl.pallas_call(chain_kernel, out_shape=jax.ShapeDtypeStruct((BLOCKS, XB,...  1.79 us
  transfers between devices with their start and end apart: 4, of which 4 were waited for; matrix products, arithmetic and copies ran while one was open for 0% of the time, Pallas kernels for 9%

profile of v2, /device:TPU:5, one launch (start us, length us, event | category | flops | bytes accessed | tf_op | source)
XLA Modules:
  0.0 84.0 jit_solution(7506907199014965863)
XLA Ops:
  0.0 0.0 copy-start
  0.0 2.8 %copy-done = f32[3,8,64,1024]{3,2,1,0:T(8,128)S(1)} copy-done((f32[3,8,64,1024]{3,2,1,0:T(8,128)S(1)}, f32[3,8,64,1024]{3,2,1,0:T(8,128)}, u32[]{:S(2)}) %copy-start) | copy-done | bytes 6291480
  2.8 0.0 copy-start.2
  2.8 1.6 %copy-done.2 = f32[8,64,1024]{2,1,0:T(8,128)S(1)} copy-done((f32[8,64,1024]{2,1,0:T(8,128)S(1)}, f32[8,64,1024]{2,1,0:T(8,128)}, u32[]{:S(2)}) %copy-start.2) | copy-done | bytes 2097176
  4.4 0.0 copy-start.4
  4.4 1.6 %copy-done.4 = f32[1,8,64,1024]{3,2,1,0:T(8,128)S(1)} copy-done((f32[1,8,64,1024]{3,2,1,0:T(8,128)S(1)}, f32[1,8,64,1024]{3,2,1,0:T(8,128)}, u32[]{:S(2)}) %copy-start.4) | copy-done | bytes 2097176
  6.0 0.0 copy-start.1
  6.0 0.0 copy-start.3
  6.0 0.0 copy-start.5
  6.0 1.5 %edges.1 = (f32[208,1024]{1,0:T(8,128)S(1)}, f32[208,1024]{1,0:T(8,128)S(1)}) custom-call(f32[8,64,1024]{2,1,0:T(8,128)S(1)} %bitcast.3, f32[3,8,64,1024]{3,2,1,0:T(8,128)S(1)} %copy-done, f32[8,64,1024]{2,1,0:T(8,128)S(1)} %copy-done.2), custom_call_target="tpu_custom_call" | custom-call | tf_op jit(solution)/shard_map/edges/pallas_call | solution.py:158
  7.5 4.4 %collective-permute-start = (f32[208,1024]{1,0:T(8,128)S(1)}, f32[208,1024]{1,0:T(8,128)S(1)}, u32[]{:S(2)}, u32[]{:S(2)}) collective-permute-start(f32[208,1024]{1,0:T(8,128)S(1)} %get-tuple-element.18.ohi), channel_id=1, source_target_pairs={{0,1},{1,2},{2,3},{3,4},{4,5},{5,6},{6,7},{7,8},{8,9},{9,10},{10,1... | collective-permute-start | bytes 2555912 | tf_op jit(solution)/shard_map/ppermute | solution.py:506
  11.9 1.9 %collective-permute-start.1 = (f32[208,1024]{1,0:T(8,128)S(1)}, f32[208,1024]{1,0:T(8,128)S(1)}, u32[]{:S(2)}, u32[]{:S(2)}) collective-permute-start(f32[208,1024]{1,0:T(8,128)S(1)} %get-tuple-element.19.olo), channel_id=1, source_target_pairs={{1,0},{2,1},{3,2},{4,3},{5,4},{6,5},{7,6},{8,7},{9,8},{10,9},{11,1... | collective-permute-start | bytes 2555912 | tf_op jit(solution)/shard_map/ppermute | solution.py:506
  13.8 0.0 copy-done.1
  13.8 0.0 copy-done.3
  13.8 0.0 copy-done.5
  13.9 7.2 %interior.1 = (f32[6,64,1024]{2,1,0:T(8,128)S(1)}, f32[4,64,1024]{2,1,0:T(8,128)S(1)}, f32[4,544,128]{2,1,0:T(8,128)S(1)}, f32[512,128]{1,0:T(8,128)S(1)}, f32[5...) custom-call(f32[8,64,1024]{2,1,0:T(8,128)S(1)} %bitcast.4, f32[3,8,64,1024]{3,2,1,0:T(8,128)S(1)} %copy-done.1, ...), custom_call_target="tpu_custom_call" | custom-call | flops 60000000 | bytes 20000000 | tf_op jit(solution)/shard_map/interior/pallas_call | solution.py:261
  21.1 9.6 %collective-permute-done.rlo = f32[208,1024]{1,0:T(8,128)S(1)} collective-permute-done((f32[208,1024]{1,0:T(8,128)S(1)}, f32[208,1024]{1,0:T(8,128)S(1)}, u32[]{:S(2)}, u32[]{:S(2)}) %collective-permute-start) | collective-permute-done | bytes 852000 | tf_op jit(solution)/shard_map/ppermute | solution.py:506
  30.6 1.2 %collective-permute-done.1.rhi = f32[208,1024]{1,0:T(8,128)S(1)} collective-permute-done((f32[208,1024]{1,0:T(8,128)S(1)}, f32[208,1024]{1,0:T(8,128)S(1)}, u32[]{:S(2)}, u32[]{:S(2)}) %collective-permute-start.1) | collective-permute-done | bytes 852000 | tf_op jit(solution)/shard_map/ppermute | solution.py:506
  31.8 1.6 %finish.1 = (f32[4,64,1024]{2,1,0:T(8,128)S(1)}, f32[32,48,128]{2,1,0:T(8,128)S(1)}, f32[512,128]{1,0:T(8,128)S(1)}) custom-call(f32[208,1024]{1,0:T(8,128)S(1)} %collective-permute-done.rlo, f32[208,1024]{1,0:T(8,128)S(1)} %collective-permute-done.1.rhi, f32[208,1024]{1,0:T(8,128)S(1)} %get-tuple-element.19.olo, f32[208,1024]{1,0:T(8,128)S(1)} %get-tuple-element.18.ohi, ...), custom_call_target="tpu_custom_call" | custom-call | tf_op jit(solution)/shard_map/finish/pallas_call | solution.py:347
  33.4 22.1 %all_to_all.10.got = f32[32,48,128]{2,1,0:T(8,128)S(1)} all-to-all(f32[32,48,128]{2,1,0:T(8,128)S(1)} %get-tuple-element.26), channel_id=1, replica_groups=mesh['tm'=8,'px'=4,'pz'=2,'core'=2] {'tm','pz','core'}, dimensions={0} | all-to-all | bytes 1572864 | tf_op jit(solution)/shard_map/all_to_all | solution.py:516
  55.5 0.1 pick.1
  55.6 2.8 %collective-permute-start.2 = (f32[13,32,128]{2,1,0:T(8,128)S(1)}, f32[13,32,128]{2,1,0:T(8,128)S(1)}, u32[]{:S(2)}, u32[]{:S(2)}) collective-permute-start(f32[13,32,128]{2,1,0:T(8,128)S(1)} %get-tuple-element.27), channel_id=1, source_target_pairs={{0,4},{4,8},{8,12},{1,5},{5,9},{9,13},{2,6},{6,10},{10,14},{3,7},{... | collective-permute-start | bytes 638984 | tf_op jit(solution)/shard_map/ppermute | solution.py:506
  58.5 2.5 %collective-permute-start.3 = (f32[13,32,128]{2,1,0:T(8,128)S(1)}, f32[13,32,128]{2,1,0:T(8,128)S(1)}, u32[]{:S(2)}, u32[]{:S(2)}) collective-permute-start(f32[13,32,128]{2,1,0:T(8,128)S(1)} %get-tuple-element.28), channel_id=1, source_target_pairs={{4,0},{8,4},{12,8},{5,1},{9,5},{13,9},{6,2},{10,6},{14,10},{7,3},{... | collective-permute-start | bytes 638984 | tf_op jit(solution)/shard_map/ppermute | solution.py:506
  60.9 3.5 %collective-permute-done.2.below = f32[13,32,128]{2,1,0:T(8,128)S(1)} collective-permute-done((f32[13,32,128]{2,1,0:T(8,128)S(1)}, f32[13,32,128]{2,1,0:T(8,128)S(1)}, u32[]{:S(2)}, u32[]{:S(2)}) %collective-permute-start.2) | collective-permute-done | bytes 213024 | tf_op jit(solution)/shard_map/ppermute | solution.py:506
  64.5 2.6 %collective-permute-done.3.above = f32[13,32,128]{2,1,0:T(8,128)S(1)} collective-permute-done((f32[13,32,128]{2,1,0:T(8,128)S(1)}, f32[13,32,128]{2,1,0:T(8,128)S(1)}, u32[]{:S(2)}, u32[]{:S(2)}) %collective-permute-start.3) | collective-permute-done | bytes 213024 | tf_op jit(solution)/shard_map/ppermute | solution.py:506
  67.1 1.8 %chain.1 = f32[32,16,128]{2,1,0:T(8,128)S(1)} custom-call(f32[32,48,128]{2,1,0:T(8,128)S(1)} %all_to_all.10.got, f32[13,32,128]{2,1,0:T(8,128)S(1)} %collective-permute-done.2.below, f32[13,32,128]{2,1,0:T(8,128)S(1)} %collective-permute-done.3.above), custom_call_target="tpu_custom_call" | custom-call | tf_op jit(solution)/shard_map/chain/pallas_call | solution.py:459
  68.9 13.2 %all_to_all.11 = f32[32,16,128]{2,1,0:T(8,128)S(1)} all-to-all(f32[32,16,128]{2,1,0:T(8,128)S(1)} %chain.1), channel_id=1, replica_groups=mesh['tm'=8,'px'=4,'pz'=2,'core'=2] {'tm','pz','core'}, dimensions={0} | all-to-all | bytes 524288 | tf_op jit(solution)/shard_map/all_to_all | solution.py:520
  82.1 1.9 %result.1 = f32[8,64,1024]{2,1,0:T(8,128)} custom-call(f32[512,128]{1,0:T(8,128)S(1)} %bitcast.5, f32[512,128]{1,0:T(8,128)S(1)} %get-tuple-element.29.gc, f32[6,64,1024]{2,1,0:T(8,128)S(1)} %get-tuple-element.20.fin, f32[4,64,1024]{2,1,0:T(8,128)S(1)} %get-tuple-element.30.ub), custom_call_target="tpu_custom_call" | custom-call | tf_op jit(solution)/shard_map/result/pallas_call | solution.py:493
Async XLA Ops:
  0.0 2.8 %copy-start = (f32[3,8,64,1024]{3,2,1,0:T(8,128)S(1)}, f32[3,8,64,1024]{3,2,1,0:T(8,128)}, u32[]{:S(2)}) copy-start(f32[3,8,64,1024]{3,2,1,0:T(8,128)} %vel.3) | copy-start | bytes 18874372
  2.8 1.6 %copy-start.2 = (f32[8,64,1024]{2,1,0:T(8,128)S(1)}, f32[8,64,1024]{2,1,0:T(8,128)}, u32[]{:S(2)}) copy-start(f32[8,64,1024]{2,1,0:T(8,128)} %dif.3) | copy-start | bytes 6291460
  4.4 1.6 %copy-start.4 = (f32[1,8,64,1024]{3,2,1,0:T(8,128)S(1)}, f32[1,8,64,1024]{3,2,1,0:T(8,128)}, u32[]{:S(2)}) copy-start(f32[1,8,64,1024]{3,2,1,0:T(8,128)} %param.3) | copy-start | bytes 6291460
  6.0 7.9 %copy-start.1 = (f32[3,8,64,1024]{3,2,1,0:T(8,128)S(1)}, f32[3,8,64,1024]{3,2,1,0:T(8,128)}, u32[]{:S(2)}) copy-start(f32[3,8,64,1024]{3,2,1,0:T(8,128)} %vel.3) | copy-start | bytes 18874372
  6.0 7.9 %copy-start.3 = (f32[8,64,1024]{2,1,0:T(8,128)S(1)}, f32[8,64,1024]{2,1,0:T(8,128)}, u32[]{:S(2)}) copy-start(f32[8,64,1024]{2,1,0:T(8,128)} %dif.3) | copy-start | bytes 6291460
  6.0 7.9 %copy-start.5 = (f32[1,8,64,1024]{3,2,1,0:T(8,128)S(1)}, f32[1,8,64,1024]{3,2,1,0:T(8,128)}, u32[]{:S(2)}) copy-start(f32[1,8,64,1024]{3,2,1,0:T(8,128)} %param.3) | copy-start | bytes 6291460
  7.5 23.1 %collective-permute-start = (f32[208,1024]{1,0:T(8,128)S(1)}, f32[208,1024]{1,0:T(8,128)S(1)}, u32[]{:S(2)}, u32[]{:S(2)}) collective-permute-start(f32[208,1024]{1,0:T(8,128)S(1)} %get-tuple-element.18.ohi), channel_id=1, source_target_pairs={{0,1},{1,2},{2,3},{3,4},{4,5},{5,6},{6,7},{7,8},{8,9},{9,10},{10,1... | collective-permute-start | bytes 2555912 | tf_op jit(solution)/shard_map/ppermute | solution.py:506
  11.9 19.9 %collective-permute-start.1 = (f32[208,1024]{1,0:T(8,128)S(1)}, f32[208,1024]{1,0:T(8,128)S(1)}, u32[]{:S(2)}, u32[]{:S(2)}) collective-permute-start(f32[208,1024]{1,0:T(8,128)S(1)} %get-tuple-element.19.olo), channel_id=1, source_target_pairs={{1,0},{2,1},{3,2},{4,3},{5,4},{6,5},{7,6},{8,7},{9,8},{10,9},{11,1... | collective-permute-start | bytes 2555912 | tf_op jit(solution)/shard_map/ppermute | solution.py:506
  55.6 8.8 %collective-permute-start.2 = (f32[13,32,128]{2,1,0:T(8,128)S(1)}, f32[13,32,128]{2,1,0:T(8,128)S(1)}, u32[]{:S(2)}, u32[]{:S(2)}) collective-permute-start(f32[13,32,128]{2,1,0:T(8,128)S(1)} %get-tuple-element.27), channel_id=1, source_target_pairs={{0,4},{4,8},{8,12},{1,5},{5,9},{9,13},{2,6},{6,10},{10,14},{3,7},{... | collective-permute-start | bytes 638984 | tf_op jit(solution)/shard_map/ppermute | solution.py:506
  58.5 8.6 %collective-permute-start.3 = (f32[13,32,128]{2,1,0:T(8,128)S(1)}, f32[13,32,128]{2,1,0:T(8,128)S(1)}, u32[]{:S(2)}, u32[]{:S(2)}) collective-permute-start(f32[13,32,128]{2,1,0:T(8,128)S(1)} %get-tuple-element.28), channel_id=1, source_target_pairs={{4,0},{8,4},{12,8},{5,1},{9,5},{13,9},{6,2},{10,6},{14,10},{7,3},{... | collective-permute-start | bytes 638984 | tf_op jit(solution)/shard_map/ppermute | solution.py:506

commit v3 on v2

--- a/solution.py
+++ b/solution.py
@@ -92,11 +92,11 @@
     return s, n
 
 
-MSG = 3 * NY + 16
+MSG = 2 * NY + 16
 CROWS = CX + 32
 
 
-def edges_kernel(st, vel, dif, lo, hi, pad, inner, v, d, zs, sems):
+def edges_kernel(st, vel, dif, lo, hi, blo, bhi, pad, inner, v, d, zs, sems):
     copies = []
     for side, (z, near) in enumerate(((0, 1), (LZ - 1, LZ - 2))):
         pairs = (
@@ -109,7 +109,7 @@
     for group in copies:
         for copy in group:
             copy.start()
-    for side, out in enumerate((lo, hi)):
+    for side, (out, factor) in enumerate(((lo, blo), (hi, bhi))):
         for copy in copies[side]:
             copy.wait()
         wrap_rows(pad, side)
@@ -128,7 +128,7 @@
                 b = k - jnp.minimum(az, 0.0)
             out[r : r + 8, :] = c
             out[NY + r : NY + r + 8, :] = a
-            out[2 * NY + r : 2 * NY + r + 8, :] = b
+            factor[rows, :] = b
             put_columns(zs, slice(side * NY + r, side * NY + r + 8), c + inside)
     lane = lax.broadcasted_iota(jnp.int32, (128, 128), 1)
     clo = jnp.zeros((128, 128), F32)
@@ -141,8 +141,8 @@
         clo += pltpu.roll(tl, 32 * b, 1) if b else tl
         chi += pltpu.roll(th, (32 * b - 32) % 128, 1) if b != 1 else th
     for i in range(8):
-        lo[3 * NY : 3 * NY + 16, 128 * i : 128 * i + 128] = clo[16 * i : 16 * i + 16, :]
-        hi[3 * NY : 3 * NY + 16, 128 * i : 128 * i + 128] = chi[16 * i : 16 * i + 16, :]
+        lo[2 * NY : MSG, 128 * i : 128 * i + 128] = clo[16 * i : 16 * i + 16, :]
+        hi[2 * NY : MSG, 128 * i : 128 * i + 128] = chi[16 * i : 16 * i + 16, :]
 
 
 def whole():
@@ -155,11 +155,12 @@
 
 def edges(state, velocity, diffusivity):
     msg = jax.ShapeDtypeStruct((MSG, NX), F32)
+    factor = jax.ShapeDtypeStruct((NY, NX), F32)
     return pl.pallas_call(
         edges_kernel,
-        out_shape=[msg, msg],
+        out_shape=[msg, msg, factor, factor],
         in_specs=[remains()] * 3,
-        out_specs=[whole(), whole()],
+        out_specs=[whole()] * 4,
         scratch_shapes=[
             pltpu.VMEM((2, PADDED, NX), F32),
             pltpu.VMEM((2, NY, NX), F32),
@@ -168,20 +169,23 @@
             pltpu.VMEM((8, 2 * NY, 128), F32),
             pltpu.SemaphoreType.DMA((2, 4)),
         ],
-        compiler_params=params(16),
+        compiler_params=params(58),
         name="edges",
     )(state, velocity, diffusivity)
 
 
-def interior_kernel(st, v, d, fin, edge, ct, gcp, cb, ymid, u, u1, zs, ct0, usem):
+def interior_kernel(st, vel, dif, fin, edge, ct, gcp, cb, ymid, u, u1, v, d, zs, ct0, usem, sems):
+    def layer(z):
+        return (
+            pltpu.make_async_copy(vel.at[:, z], v.at[:, z], sems.at[z, 0]),
+            pltpu.make_async_copy(dif.at[z], d.at[z], sems.at[z, 1]),
+        )
+
     copy = pltpu.make_async_copy(st, u.at[:, TOP : TOP + NY, :], usem)
     copy.start()
-    for zc in range(4):
-        for r in range(0, NY, 8):
-            to, rows = slice(zc * NY + r, zc * NY + r + 8), slice(r, r + 8)
-            for comp in range(3):
-                put_columns(zs.at[comp], to, v[comp, 2 * zc, rows, :] + v[comp, 2 * zc + 1, rows, :])
-            put_columns(zs.at[3], to, d[2 * zc, rows, :] + d[2 * zc + 1, rows, :])
+    for z in (1, 2, 3, 4, 5, 6, 0, 7):
+        for part in layer(z):
+            part.start()
     copy.wait()
     for z in range(LZ):
         wrap_rows(u, z)
@@ -191,6 +195,8 @@
             put_columns(zs.at[4], slice(zc * NY + r, zc * NY + r + 8), u[2 * zc, here, :] + u[2 * zc + 1, here, :])
 
     def first(z, _):
+        for part in layer(z):
+            part.wait()
         for r in range(0, NY, 8):
             rows = slice(r, r + 8)
             here = slice(TOP + r, TOP + r + 8)
@@ -229,6 +235,15 @@
     for i in range(8):
         ymid[i] = paired(zs.at[5], i, 0, 64)
 
+    for z in (0, LZ - 1):
+        for part in layer(z):
+            part.wait()
+    for zc in range(4):
+        for r in range(0, NY, 8):
+            to, rows = slice(zc * NY + r, zc * NY + r + 8), slice(r, r + 8)
+            for comp in range(3):
+                put_columns(zs.at[comp], to, v[comp, 2 * zc, rows, :] + v[comp, 2 * zc + 1, rows, :])
+            put_columns(zs.at[3], to, d[2 * zc, rows, :] + d[2 * zc + 1, rows, :])
     for comp in range(5):
         for b in range(4):
             t = halved_x(jnp.concatenate([paired(zs.at[comp], 2 * b + i, 0, 128) for i in range(2)], axis=1))
@@ -268,22 +283,25 @@
             small,
             jax.ShapeDtypeStruct((8, 64, 128), F32),
         ],
-        in_specs=[remains(), whole(), whole()],
+        in_specs=[remains()] * 3,
         out_specs=[whole()] * 6,
         scratch_shapes=[
             pltpu.VMEM((LZ, PADDED, NX), F32),
             pltpu.VMEM((LZ, PADDED, NX), F32),
+            pltpu.VMEM((3, LZ, NY, NX), F32),
+            pltpu.VMEM((LZ, NY, NX), F32),
             pltpu.VMEM((6, 8, 4 * NY, 128), F32),
             pltpu.VMEM((CX + 16, CL), F32),
             pltpu.SemaphoreType.DMA,
+            pltpu.SemaphoreType.DMA((LZ, 2)),
         ],
-        compiler_params=params(32),
+        compiler_params=params(48),
         cost_estimate=pl.CostEstimate(flops=60_000_000, bytes_accessed=20_000_000, transcendentals=0),
         name="interior",
     )(state, velocity, diffusivity)
 
 
-def finish_kernel(rlo, rhi, olo, ohi, fin, edge, vel, dif, gcp, cb, ymid, ct, ub, msg, gc, pad, v, d, zs, jp, sems):
+def finish_kernel(rlo, rhi, rblo, rbhi, olo, ohi, oblo, obhi, fin, edge, vel, dif, gcp, cb, ymid, ct, ub, msg, gc, pad, v, d, zs, jp, sems):
     copies = []
     for side, z in enumerate((0, LZ - 1)):
         copies.append(pltpu.make_async_copy(vel.at[:, z], v.at[side], sems.at[side, 0]))
@@ -291,10 +309,10 @@
     for copy in copies:
         copy.start()
     slice_index = lax.axis_index("tm")
-    for side, (rec, own) in enumerate(((rlo, olo), (rhi, ohi))):
+    for side, (rec, recb, own, ownb) in enumerate(((rlo, rblo, olo, oblo), (rhi, rbhi, ohi, obhi))):
         for r in range(0, NY, 8):
             pad[side, TOP + r : TOP + r + 8, :] = (
-                own[NY + r : NY + r + 8, :] + own[2 * NY + r : 2 * NY + r + 8, :] * rec[r : r + 8, :]
+                own[NY + r : NY + r + 8, :] + ownb[r : r + 8, :] * rec[r : r + 8, :]
             )
         wrap_rows(pad, side)
         copies[2 * side].wait()
@@ -302,7 +320,7 @@
         for r in range(0, NY, 8):
             rows = slice(r, r + 8)
             c, w, e, s, n = plane(pad, side, r)
-            outside = rec[NY + r : NY + r + 8, :] + rec[2 * NY + r : 2 * NY + r + 8, :] * own[r : r + 8, :]
+            outside = rec[NY + r : NY + r + 8, :] + recb[r : r + 8, :] * own[r : r + 8, :]
             inside = edge[side, rows, :]
             b, t = (outside, inside) if side == 0 else (inside, outside)
             last = advanced(
@@ -314,8 +332,8 @@
             ub[1 + side, rows, :] = near
             put_columns(zs, slice(side * NY + r, side * NY + r + 8), last + near)
     lane = lax.broadcasted_iota(jnp.int32, (128, 128), 1)
-    halo_lo = jnp.concatenate([rlo[3 * NY : MSG, 128 * i : 128 * i + 128] for i in range(8)], axis=0)
-    halo_hi = jnp.concatenate([rhi[3 * NY : MSG, 128 * i : 128 * i + 128] for i in range(8)], axis=0)
+    halo_lo = jnp.concatenate([rlo[2 * NY : MSG, 128 * i : 128 * i + 128] for i in range(8)], axis=0)
+    halo_hi = jnp.concatenate([rhi[2 * NY : MSG, 128 * i : 128 * i + 128] for i in range(8)], axis=0)
     for b in range(4):
         rows = slice(128 * b, 128 * b + 128)
         t = halved_x(
@@ -343,7 +361,7 @@
         msg[i, WIN : WIN + 16, :] = ct[comp, pl.ds(first + XB * i, 16), :]
 
 
-def finish(rlo, rhi, olo, ohi, fin, edge, velocity, diffusivity, gcp, cb, ymid, ct):
+def finish(messages, fin, edge, velocity, diffusivity, gcp, cb, ymid, ct):
     return pl.pallas_call(
         finish_kernel,
         out_shape=[
@@ -351,7 +369,7 @@
             jax.ShapeDtypeStruct((BLOCKS, WIN + 16, CL), F32),
             jax.ShapeDtypeStruct((CX, CL), F32),
         ],
-        in_specs=[whole()] * 6 + [remains()] * 2 + [whole()] * 4,
+        in_specs=[whole()] * 10 + [remains()] * 2 + [whole()] * 4,
         out_specs=[whole()] * 3,
         scratch_shapes=[
             pltpu.VMEM((2, PADDED, NX), F32),
@@ -363,7 +381,7 @@
         ],
         compiler_params=params(24),
         name="finish",
-    )(rlo, rhi, olo, ohi, fin, edge, velocity, diffusivity, gcp, cb, ymid, ct)
+    )(*messages, fin, edge, velocity, diffusivity, gcp, cb, ymid, ct)
 
 
 HALO = 13
@@ -506,13 +524,27 @@
     return lax.ppermute(value, axes, [(i, i + by) for i in range(count) if 0 <= i + by < count])
 
 
+def shift_copy(value, by):
+    slabs = 16
+    pairs = []
+    for t in range(GROUPS):
+        for i in range(slabs):
+            if 0 <= i + by < slabs:
+                t_from = t if i // 2 == (i + by) // 2 else t ^ 1
+                pairs.append((t_from * slabs + i, t * slabs + i + by))
+    return lax.ppermute(value, ("tm",) + SPACE, pairs)
+
+
 def shards(state_old, velocity, diffusivity):
     state = state_old[0]
-    olo, ohi = edges(state, velocity, diffusivity)
+    olo, ohi, oblo, obhi = edges(state, velocity, diffusivity)
     rlo = shift(ohi, SPACE, 1)
     rhi = shift(olo, SPACE, -1)
+    rblo = shift_copy(obhi, 1)
+    rbhi = shift_copy(oblo, -1)
     fin, edge, ct, gcp, cb, ymid = interior(state, velocity, diffusivity)
-    ub, msg, gc = finish(rlo, rhi, olo, ohi, fin, edge, velocity, diffusivity, gcp, cb, ymid, ct)
+    messages = (rlo, rhi, rblo, rbhi, olo, ohi, oblo, obhi)
+    ub, msg, gc = finish(messages, fin, edge, velocity, diffusivity, gcp, cb, ymid, ct)
     got = lax.all_to_all(msg, GROUP, 0, 0)
     up, down = pick(got)
     below = shift(up, "px", 1)

time: 85.5 us -> 82.3 us (0.963)
  waiting for transfers between devices: 16.9 us -> 6.15 us
  starting transfers between devices: 11.6 us -> 19.4 us
  local copies, waits for them, and re-layouts: 5.98 us -> 0.04 us
  Pallas kernels: 14.2 us -> 20.1 us
    ppermute x4, waiting for transfers between devices: 16.9 us -> 6.15 us  [shift(): lax.ppermute(value, axes, [(i, i + by) for i in range(count) if 0 <= i +...]
    ppermute x0 -> x2, starting transfers between devices: none -> 8.08 us  [shift_copy(): return lax.ppermute(value, ('tm',) + SPACE, pairs)]
    unnamed x12 -> x14, local copies, waits for them, and re-layouts: 5.98 us -> 0.04 us
    pallas_call x1, Pallas kernels: 7.22 us -> 10.8 us  [interior(): pl.pallas_call(interior_kernel, out_shape=[jax.ShapeDtypeStruct((LZ - 2,...]
    pallas_call x1, Pallas kernels: 1.54 us -> 3.83 us  [edges(): pl.pallas_call(edges_kernel, out_shape=[msg, msg, factor, factor], in_spe...]
  transfers between devices with their start and end apart: 4 -> 6, of which waited for: 4 -> 2; matrix products, arithmetic and copies ran while one was open for 0% -> 0% of each run, Pallas kernels for 9% -> 13%
where the time goes in v3:
time: 82.3 us; the launch traced here: 80.9 us
  blocking collectives  34.9 us (42%)
  Pallas kernels  20.1 us (24%)
  starting transfers between devices  19.4 us (24%)
  waiting for transfers between devices  6.15 us (7%)
    all_to_all x1, blocking collectives, shards(): got = lax.all_to_all(msg, GROUP, 0, 0)  21.7 us
    all_to_all x1, blocking collectives, shards(): back = lax.all_to_all(chain(got, below, above), GROUP, 0, 0)  13.2 us
    ppermute x4, starting transfers between devices, shift(): lax.ppermute(value, axes, [(i, i + by) for i in range(count) if 0 <= i +...  11.3 us
    pallas_call x1, Pallas kernels, interior(): pl.pallas_call(interior_kernel, out_shape=[jax.ShapeDtypeStruct((LZ - 2,...  10.8 us
    ppermute x2, starting transfers between devices, shift_copy(): return lax.ppermute(value, ('tm',) + SPACE, pairs)  8.08 us
    ppermute x4, waiting for transfers between devices, shift(): lax.ppermute(value, axes, [(i, i + by) for i in range(count) if 0 <= i +...  6.15 us
    pallas_call x1, Pallas kernels, edges(): pl.pallas_call(edges_kernel, out_shape=[msg, msg, factor, factor], in_spe...  3.83 us
    pallas_call x1, Pallas kernels, result(): pl.pallas_call(result_kernel, out_shape=jax.ShapeDtypeStruct((LZ, NY, NX)...  1.93 us
  transfers between devices with their start and end apart: 6, of which 2 were waited for; matrix products, arithmetic and copies ran while one was open for 0% of the time, Pallas kernels for 13%

profile of v3, /device:TPU:5, one launch (start us, length us, event | category | flops | bytes accessed | tf_op | source)
XLA Modules:
  0.0 80.9 jit_solution(3476587601696318516)
XLA Ops:
  0.0 0.0 slice-start
  0.0 3.8 %edges.1 = (f32[144,1024]{1,0:T(8,128)}, f32[144,1024]{1,0:T(8,128)}, f32[64,1024]{1,0:T(8,128)}, f32[64,1024]{1,0:T(8,128)}) custom-call(f32[8,64,1024]{2,1,0:T(8,128)} %bitcast.6, f32[3,8,64,1024]{3,2,1,0:T(8,128)} %vel.5, f32[8,64,1024]{2,1,0:T(8,128)} %dif.5), custom_call_target="tpu_custom_call" | custom-call | tf_op jit(solution)/shard_map/edges/pallas_call | solution.py:159
  3.8 4.1 %collective-permute-start = (f32[144,1024]{1,0:T(8,128)}, f32[144,1024]{1,0:T(8,128)S(1)}, u32[]{:S(2)}, u32[]{:S(2)}) collective-permute-start(f32[144,1024]{1,0:T(8,128)} %get-tuple-element.20.ohi), channel_id=1, source_target_pairs={{0,1},{1,2},{2,3},{3,4},{4,5},{5,6},{6,7},{7,8},{8,9},{9,10},{10,1... | collective-permute-start | bytes 1769480 | tf_op jit(solution)/shard_map/ppermute | solution.py:524
  8.0 1.9 %collective-permute-start.1 = (f32[144,1024]{1,0:T(8,128)}, f32[144,1024]{1,0:T(8,128)S(1)}, u32[]{:S(2)}, u32[]{:S(2)}) collective-permute-start(f32[144,1024]{1,0:T(8,128)} %get-tuple-element.21.olo), channel_id=1, source_target_pairs={{1,0},{2,1},{3,2},{4,3},{5,4},{6,5},{7,6},{8,7},{9,8},{10,9},{11,1... | collective-permute-start | bytes 1769480 | tf_op jit(solution)/shard_map/ppermute | solution.py:524
  9.9 5.8 %collective-permute-start.2 = (f32[64,1024]{1,0:T(8,128)}, f32[64,1024]{1,0:T(8,128)S(1)}, u32[]{:S(2)}, u32[]{:S(2)}) collective-permute-start(f32[64,1024]{1,0:T(8,128)} %get-tuple-element.22.obhi), channel_id=1, source_target_pairs={{0,1},{17,2},{2,3},{19,4},{4,5},{21,6},{6,7},{23,8},{8,9},{25,10},... | collective-permute-start | bytes 786440 | tf_op jit(solution)/shard_map/ppermute | solution.py:535
  15.6 0.0 slice-start.1
  15.7 0.0 copy-start
  15.7 0.0 copy-start.1
  15.7 0.0 copy-start.2
  15.7 0.0 copy-start.3
  15.7 0.0 copy-start.4
  15.7 2.3 %collective-permute-start.3 = (f32[64,1024]{1,0:T(8,128)}, f32[64,1024]{1,0:T(8,128)S(1)}, u32[]{:S(2)}, u32[]{:S(2)}) collective-permute-start(f32[64,1024]{1,0:T(8,128)} %get-tuple-element.23.oblo), channel_id=1, source_target_pairs={{1,0},{18,1},{3,2},{20,3},{5,4},{22,5},{7,6},{24,7},{9,8},{26,9},{... | collective-permute-start | bytes 786440 | tf_op jit(solution)/shard_map/ppermute | solution.py:535
  18.0 10.8 %interior.1 = (f32[6,64,1024]{2,1,0:T(8,128)S(1)}, f32[4,64,1024]{2,1,0:T(8,128)S(1)}, f32[4,544,128]{2,1,0:T(8,128)S(1)}, f32[512,128]{1,0:T(8,128)S(1)}, f32[5...) custom-call(f32[8,64,1024]{2,1,0:T(8,128)} %bitcast.7, f32[3,8,64,1024]{3,2,1,0:T(8,128)} %vel.5, f32[8,64,1024]{2,1,0:T(8,128)} %dif.5), custom_call_target="tpu_custom_call" | custom-call | flops 60000000 | bytes 20000000 | tf_op jit(solution)/shard_map/interior/pallas_call | solution.py:276
  28.9 0.0 collective-permute-done.2.rblo
  28.9 0.0 collective-permute-done.3.rbhi
  28.9 0.0 collective-permute-done.rlo
  28.9 0.0 collective-permute-done.1.rhi
  28.9 0.0 slice-done
  28.9 0.0 slice-done.1
  28.9 0.0 copy-done
  28.9 0.0 copy-done.1
  29.0 0.0 copy-done.2
  29.0 0.0 copy-done.3
  29.0 0.0 copy-done.4
  29.0 1.6 %finish.1 = (f32[4,64,1024]{2,1,0:T(8,128)S(1)}, f32[32,48,128]{2,1,0:T(8,128)S(1)}, f32[512,128]{1,0:T(8,128)S(1)}) custom-call(f32[144,1024]{1,0:T(8,128)S(1)} %collective-permute-done.rlo, f32[144,1024]{1,0:T(8,128)S(1)} %collective-permute-done.1.rhi, f32[64,1024]{1,0:T(8,128)S(1)} %collective-permute-done.2.rblo, ...), custom_call_target="tpu_custom_call" | custom-call | tf_op jit(solution)/shard_map/finish/pallas_call | solution.py:365
  30.6 21.7 %all_to_all.10.got = f32[32,48,128]{2,1,0:T(8,128)S(1)} all-to-all(f32[32,48,128]{2,1,0:T(8,128)S(1)} %get-tuple-element.30), channel_id=1, replica_groups=mesh['tm'=8,'px'=4,'pz'=2,'core'=2] {'tm','pz','core'}, dimensions={0} | all-to-all | bytes 1572864 | tf_op jit(solution)/shard_map/all_to_all | solution.py:548
  52.4 0.1 pick.1
  52.5 2.8 %collective-permute-start.4 = (f32[13,32,128]{2,1,0:T(8,128)S(1)}, f32[13,32,128]{2,1,0:T(8,128)S(1)}, u32[]{:S(2)}, u32[]{:S(2)}) collective-permute-start(f32[13,32,128]{2,1,0:T(8,128)S(1)} %get-tuple-element.31), channel_id=1, source_target_pairs={{0,4},{4,8},{8,12},{1,5},{5,9},{9,13},{2,6},{6,10},{10,14},{3,7},{... | collective-permute-start | bytes 638984 | tf_op jit(solution)/shard_map/ppermute | solution.py:524
  55.3 2.5 %collective-permute-start.5 = (f32[13,32,128]{2,1,0:T(8,128)S(1)}, f32[13,32,128]{2,1,0:T(8,128)S(1)}, u32[]{:S(2)}, u32[]{:S(2)}) collective-permute-start(f32[13,32,128]{2,1,0:T(8,128)S(1)} %get-tuple-element.32), channel_id=1, source_target_pairs={{4,0},{8,4},{12,8},{5,1},{9,5},{13,9},{6,2},{10,6},{14,10},{7,3},{... | collective-permute-start | bytes 638984 | tf_op jit(solution)/shard_map/ppermute | solution.py:524
  57.8 3.5 %collective-permute-done.4.below = f32[13,32,128]{2,1,0:T(8,128)S(1)} collective-permute-done((f32[13,32,128]{2,1,0:T(8,128)S(1)}, f32[13,32,128]{2,1,0:T(8,128)S(1)}, u32[]{:S(2)}, u32[]{:S(2)}) %collective-permute-start.4) | collective-permute-done | bytes 213024 | tf_op jit(solution)/shard_map/ppermute | solution.py:524
  61.3 2.6 %collective-permute-done.5.above = f32[13,32,128]{2,1,0:T(8,128)S(1)} collective-permute-done((f32[13,32,128]{2,1,0:T(8,128)S(1)}, f32[13,32,128]{2,1,0:T(8,128)S(1)}, u32[]{:S(2)}, u32[]{:S(2)}) %collective-permute-start.5) | collective-permute-done | bytes 213024 | tf_op jit(solution)/shard_map/ppermute | solution.py:524
  63.9 1.8 %chain.1 = f32[32,16,128]{2,1,0:T(8,128)S(1)} custom-call(f32[32,48,128]{2,1,0:T(8,128)S(1)} %all_to_all.10.got, f32[13,32,128]{2,1,0:T(8,128)S(1)} %collective-permute-done.4.below, f32[13,32,128]{2,1,0:T(8,128)S(1)} %collective-permute-done.5.above), custom_call_target="tpu_custom_call" | custom-call | tf_op jit(solution)/shard_map/chain/pallas_call | solution.py:477
  65.7 13.2 %all_to_all.11 = f32[32,16,128]{2,1,0:T(8,128)S(1)} all-to-all(f32[32,16,128]{2,1,0:T(8,128)S(1)} %chain.1), channel_id=1, replica_groups=mesh['tm'=8,'px'=4,'pz'=2,'core'=2] {'tm','pz','core'}, dimensions={0} | all-to-all | bytes 524288 | tf_op jit(solution)/shard_map/all_to_all | solution.py:552
  78.9 1.9 %result.1 = f32[8,64,1024]{2,1,0:T(8,128)} custom-call(f32[512,128]{1,0:T(8,128)S(1)} %bitcast.5, f32[512,128]{1,0:T(8,128)S(1)} %get-tuple-element.33.gc, f32[6,64,1024]{2,1,0:T(8,128)S(1)} %get-tuple-element.24.fin, f32[4,64,1024]{2,1,0:T(8,128)S(1)} %get-tuple-element.34.ub), custom_call_target="tpu_custom_call" | custom-call | tf_op jit(solution)/shard_map/result/pallas_call | solution.py:511
  (1 shorter events, 0.0 us)
Async XLA Ops:
  0.0 28.9 %slice-start = ((s8[6291456]{0:T(1024)(128)(4,1)}), s8[2097152]{0:T(1024)(128)(4,1)S(1)}, s32[]{:S(2)}) async-start(s8[6291456]{0:T(1024)(128)(4,1)} %bitcast.3), calls=%async_computation.2 | async-start | bytes 4194304
  3.8 25.1 %collective-permute-start = (f32[144,1024]{1,0:T(8,128)}, f32[144,1024]{1,0:T(8,128)S(1)}, u32[]{:S(2)}, u32[]{:S(2)}) collective-permute-start(f32[144,1024]{1,0:T(8,128)} %get-tuple-element.20.ohi), channel_id=1, source_target_pairs={{0,1},{1,2},{2,3},{3,4},{4,5},{5,6},{6,7},{7,8},{8,9},{9,10},{10,1... | collective-permute-start | bytes 1769480 | tf_op jit(solution)/shard_map/ppermute | solution.py:524
  8.0 21.0 %collective-permute-start.1 = (f32[144,1024]{1,0:T(8,128)}, f32[144,1024]{1,0:T(8,128)S(1)}, u32[]{:S(2)}, u32[]{:S(2)}) collective-permute-start(f32[144,1024]{1,0:T(8,128)} %get-tuple-element.21.olo), channel_id=1, source_target_pairs={{1,0},{2,1},{3,2},{4,3},{5,4},{6,5},{7,6},{8,7},{9,8},{10,9},{11,1... | collective-permute-start | bytes 1769480 | tf_op jit(solution)/shard_map/ppermute | solution.py:524
  9.9 19.0 %collective-permute-start.2 = (f32[64,1024]{1,0:T(8,128)}, f32[64,1024]{1,0:T(8,128)S(1)}, u32[]{:S(2)}, u32[]{:S(2)}) collective-permute-start(f32[64,1024]{1,0:T(8,128)} %get-tuple-element.22.obhi), channel_id=1, source_target_pairs={{0,1},{17,2},{2,3},{19,4},{4,5},{21,6},{6,7},{23,8},{8,9},{25,10},... | collective-permute-start | bytes 786440 | tf_op jit(solution)/shard_map/ppermute | solution.py:535
  15.6 13.3 %slice-start.1 = ((s8[6291456]{0:T(1024)(128)(4,1)}), s8[4194304]{0:T(1024)(128)(4,1)S(1)}, s32[]{:S(2)}) async-start(s8[6291456]{0:T(1024)(128)(4,1)} %bitcast.3), calls=%async_computation.3 | async-start | bytes 8388608
  15.7 13.3 %copy-start = (f32[8,64,1024]{2,1,0:T(8,128)S(1)}, f32[8,64,1024]{2,1,0:T(8,128)}, u32[]{:S(2)}) copy-start(f32[8,64,1024]{2,1,0:T(8,128)} %dif.5) | copy-start | bytes 6291460
  15.7 13.3 %copy-start.1 = (f32[144,1024]{1,0:T(8,128)S(1)}, f32[144,1024]{1,0:T(8,128)}, u32[]{:S(2)}) copy-start(f32[144,1024]{1,0:T(8,128)} %get-tuple-element.21.olo) | copy-start | bytes 1769476
  15.7 13.3 %copy-start.2 = (f32[144,1024]{1,0:T(8,128)S(1)}, f32[144,1024]{1,0:T(8,128)}, u32[]{:S(2)}) copy-start(f32[144,1024]{1,0:T(8,128)} %get-tuple-element.20.ohi) | copy-start | bytes 1769476
  15.7 13.3 %copy-start.3 = (f32[64,1024]{1,0:T(8,128)S(1)}, f32[64,1024]{1,0:T(8,128)}, u32[]{:S(2)}) copy-start(f32[64,1024]{1,0:T(8,128)} %get-tuple-element.23.oblo) | copy-start | bytes 786436
  15.7 13.3 %copy-start.4 = (f32[64,1024]{1,0:T(8,128)S(1)}, f32[64,1024]{1,0:T(8,128)}, u32[]{:S(2)}) copy-start(f32[64,1024]{1,0:T(8,128)} %get-tuple-element.22.obhi) | copy-start | bytes 786436
  15.7 13.2 %collective-permute-start.3 = (f32[64,1024]{1,0:T(8,128)}, f32[64,1024]{1,0:T(8,128)S(1)}, u32[]{:S(2)}, u32[]{:S(2)}) collective-permute-start(f32[64,1024]{1,0:T(8,128)} %get-tuple-element.23.oblo), channel_id=1, source_target_pairs={{1,0},{18,1},{3,2},{20,3},{5,4},{22,5},{7,6},{24,7},{9,8},{26,9},{... | collective-permute-start | bytes 786440 | tf_op jit(solution)/shard_map/ppermute | solution.py:535
  52.5 8.8 %collective-permute-start.4 = (f32[13,32,128]{2,1,0:T(8,128)S(1)}, f32[13,32,128]{2,1,0:T(8,128)S(1)}, u32[]{:S(2)}, u32[]{:S(2)}) collective-permute-start(f32[13,32,128]{2,1,0:T(8,128)S(1)} %get-tuple-element.31), channel_id=1, source_target_pairs={{0,4},{4,8},{8,12},{1,5},{5,9},{9,13},{2,6},{6,10},{10,14},{3,7},{... | collective-permute-start | bytes 638984 | tf_op jit(solution)/shard_map/ppermute | solution.py:524
  55.3 8.6 %collective-permute-start.5 = (f32[13,32,128]{2,1,0:T(8,128)S(1)}, f32[13,32,128]{2,1,0:T(8,128)S(1)}, u32[]{:S(2)}, u32[]{:S(2)}) collective-permute-start(f32[13,32,128]{2,1,0:T(8,128)S(1)} %get-tuple-element.32), channel_id=1, source_target_pairs={{4,0},{8,4},{12,8},{5,1},{9,5},{13,9},{6,2},{10,6},{14,10},{7,3},{... | collective-permute-start | bytes 638984 | tf_op jit(solution)/shard_map/ppermute | solution.py:524

commit v4 on v3

--- a/solution.py
+++ b/solution.py
@@ -92,57 +92,62 @@
     return s, n
 
 
-MSG = 2 * NY + 16
+FAR = 2 * NY + 16
+NEAR = FAR + NY
 CROWS = CX + 32
 
 
-def edges_kernel(st, vel, dif, lo, hi, blo, bhi, pad, inner, v, d, zs, sems):
+def edge_is_top(kind):
+    return lax.axis_index("core") == kind
+
+
+def edges_kernel(st, vel, dif, near, far, factor, pad, inner, v, d, zs, sems):
     copies = []
-    for side, (z, near) in enumerate(((0, 1), (LZ - 1, LZ - 2))):
+    tops = [edge_is_top(kind) for kind in range(2)]
+    for kind, top in enumerate(tops):
+        z, beside = jnp.where(top, LZ - 1, 0), jnp.where(top, LZ - 2, 1)
         pairs = (
-            (st.at[z], pad.at[side, TOP : TOP + NY, :]),
-            (vel.at[:, z], v.at[side]),
-            (dif.at[z], d.at[side]),
-            (st.at[near], inner.at[side]),
+            (st.at[z], pad.at[kind, TOP : TOP + NY, :]),
+            (vel.at[:, z], v.at[kind]),
+            (dif.at[z], d.at[kind]),
+            (st.at[beside], inner.at[kind]),
         )
-        copies.append([pltpu.make_async_copy(a, b, sems.at[side, i]) for i, (a, b) in enumerate(pairs)])
+        copies.append([pltpu.make_async_copy(a, b, sems.at[kind, i]) for i, (a, b) in enumerate(pairs)])
     for group in copies:
         for copy in group:
             copy.start()
-    for side, (out, factor) in enumerate(((lo, blo), (hi, bhi))):
-        for copy in copies[side]:
+    for kind, top in enumerate(tops):
+        out = (near, far)[kind]
+        for copy in copies[kind]:
             copy.wait()
-        wrap_rows(pad, side)
+        wrap_rows(pad, kind)
         for r in range(0, NY, 8):
             rows = slice(r, r + 8)
-            c, w, e, s, n = plane(pad, side, r)
-            inside = inner[side, rows, :]
-            ax, ay, az = v[side, 0, rows, :], v[side, 1, rows, :], v[side, 2, rows, :]
-            k = d[side, rows, :]
-            none = jnp.zeros_like(c)
-            if side == 0:
-                a = advanced(c, w, e, s, n, none, inside, ax, ay, az, k)
-                b = k + jnp.maximum(az, 0.0)
+            c, w, e, s, n = plane(pad, kind, r)
+            inside = inner[kind, rows, :]
+            ax, ay, k = v[kind, 0, rows, :], v[kind, 1, rows, :], d[kind, rows, :]
+            up = jnp.where(top, v[kind, 2, rows, :], -v[kind, 2, rows, :])
+            out[r : r + 8, :] = c
+            out[NY + r : NY + r + 8, :] = advanced(c, w, e, s, n, inside, jnp.zeros_like(c), ax, ay, up, k)
+            b = k - jnp.minimum(up, 0.0)
+            if kind == 0:
+                near[FAR + r : FAR + r + 8, :] = b
             else:
-                a = advanced(c, w, e, s, n, inside, none, ax, ay, az, k)
-                b = k - jnp.minimum(az, 0.0)
-            out[r : r + 8, :] = c
-            out[NY + r : NY + r + 8, :] = a
-            factor[rows, :] = b
-            put_columns(zs, slice(side * NY + r, side * NY + r + 8), c + inside)
+                factor[rows, :] = b
+            put_columns(zs, slice(kind * NY + r, kind * NY + r + 8), c + inside)
     lane = lax.broadcasted_iota(jnp.int32, (128, 128), 1)
-    clo = jnp.zeros((128, 128), F32)
-    chi = jnp.zeros((128, 128), F32)
+    cnear = jnp.zeros((128, 128), F32)
+    cfar = jnp.zeros((128, 128), F32)
     for b in range(4):
         part = jnp.concatenate([paired(zs, 2 * b + i, 0, 64) for i in range(2)], axis=1)
         t = halved_x(jnp.concatenate([part, jnp.zeros_like(part)], axis=0))
-        tl = jnp.where(lane < 32, t, 0.0)
-        th = jnp.where((lane >= 32) & (lane < 64), t, 0.0)
-        clo += pltpu.roll(tl, 32 * b, 1) if b else tl
-        chi += pltpu.roll(th, (32 * b - 32) % 128, 1) if b != 1 else th
+        tn = jnp.where(lane < 32, t, 0.0)
+        tf = jnp.where((lane >= 32) & (lane < 64), t, 0.0)
+        cnear += pltpu.roll(tn, 32 * b, 1) if b else tn
+        cfar += pltpu.roll(tf, (32 * b - 32) % 128, 1) if b != 1 else tf
     for i in range(8):
-        lo[2 * NY : MSG, 128 * i : 128 * i + 128] = clo[16 * i : 16 * i + 16, :]
-        hi[2 * NY : MSG, 128 * i : 128 * i + 128] = chi[16 * i : 16 * i + 16, :]
+        near[2 * NY : FAR, 128 * i : 128 * i + 128] = cnear[16 * i : 16 * i + 16, :]
+        far[2 * NY : FAR, 128 * i : 128 * i + 128] = cfar[16 * i : 16 * i + 16, :]
 
 
 def whole():
@@ -154,13 +159,15 @@
 
 
 def edges(state, velocity, diffusivity):
-    msg = jax.ShapeDtypeStruct((MSG, NX), F32)
-    factor = jax.ShapeDtypeStruct((NY, NX), F32)
     return pl.pallas_call(
         edges_kernel,
-        out_shape=[msg, msg, factor, factor],
+        out_shape=[
+            jax.ShapeDtypeStruct((NEAR, NX), F32),
+            jax.ShapeDtypeStruct((FAR, NX), F32),
+            jax.ShapeDtypeStruct((NY, NX), F32),
+        ],
         in_specs=[remains()] * 3,
-        out_specs=[whole()] * 4,
+        out_specs=[whole()] * 3,
         scratch_shapes=[
             pltpu.VMEM((2, PADDED, NX), F32),
             pltpu.VMEM((2, NY, NX), F32),
@@ -174,7 +181,11 @@
     )(state, velocity, diffusivity)
 
 
-def interior_kernel(st, vel, dif, fin, edge, ct, gcp, cb, ymid, u, u1, v, d, zs, ct0, usem, sems):
+def quad_rank():
+    return lax.axis_index("pz") * 2 + lax.axis_index("core")
+
+
+def interior_kernel(st, vel, dif, fin, edge, bound, w0, w1, w2, w3, gcp, cb, ymid, u, u1, ct, v, d, zs, ct0, usem, sems):
     def layer(z):
         return (
             pltpu.make_async_copy(vel.at[:, z], v.at[:, z], sems.at[z, 0]),
@@ -235,9 +246,12 @@
     for i in range(8):
         ymid[i] = paired(zs.at[5], i, 0, 64)
 
-    for z in (0, LZ - 1):
+    for side, z in enumerate((0, LZ - 1)):
         for part in layer(z):
             part.wait()
+        for comp in range(3):
+            bound[side, comp] = v[comp, z]
+        bound[side, 3] = d[z]
     for zc in range(4):
         for r in range(0, NY, 8):
             to, rows = slice(zc * NY + r, zc * NY + r + 8), slice(r, r + 8)
@@ -254,6 +268,11 @@
     for comp in range(4):
         ct[comp, 0:8, :] = ct[comp, CX : CX + 8, :]
         ct[comp, CX + 8 : CX + 32, :] = ct[comp, 8:32, :]
+    mine = quad_rank()
+    for i, out in enumerate((w0, w1, w2, w3)):
+        block = lax.axis_index("tm") * QUAD + (mine ^ i)
+        for comp in range(4):
+            out[comp] = ct[comp, pl.ds(pl.multiple_of(block * XB, XB), WIN), :]
     ct0[0:8, :] = ct0[CX : CX + 8, :]
     ct0[CX + 8 : CX + 16, :] = ct0[8:16, :]
     lane = lax.broadcasted_iota(jnp.int32, (64, CL), 1)
@@ -273,21 +292,27 @@
 
 def interior(state, velocity, diffusivity):
     small = jax.ShapeDtypeStruct((CX, CL), F32)
+    window = jax.ShapeDtypeStruct((4, WIN, CL), F32)
     return pl.pallas_call(
         interior_kernel,
         out_shape=[
             jax.ShapeDtypeStruct((LZ - 2, NY, NX), F32),
             jax.ShapeDtypeStruct((4, NY, NX), F32),
-            jax.ShapeDtypeStruct((4, CROWS, CL), F32),
+            jax.ShapeDtypeStruct((2, 4, NY, NX), F32),
+            window,
+            window,
+            window,
+            window,
             small,
             small,
             jax.ShapeDtypeStruct((8, 64, 128), F32),
         ],
         in_specs=[remains()] * 3,
-        out_specs=[whole()] * 6,
+        out_specs=[whole()] * 10,
         scratch_shapes=[
             pltpu.VMEM((LZ, PADDED, NX), F32),
             pltpu.VMEM((LZ, PADDED, NX), F32),
+            pltpu.VMEM((4, CROWS, CL), F32),
             pltpu.VMEM((3, LZ, NY, NX), F32),
             pltpu.VMEM((LZ, NY, NX), F32),
             pltpu.VMEM((6, 8, 4 * NY, 128), F32),
@@ -301,45 +326,39 @@
     )(state, velocity, diffusivity)
 
 
-def finish_kernel(rlo, rhi, rblo, rbhi, olo, ohi, oblo, obhi, fin, edge, vel, dif, gcp, cb, ymid, ct, ub, msg, gc, pad, v, d, zs, jp, sems):
-    copies = []
-    for side, z in enumerate((0, LZ - 1)):
-        copies.append(pltpu.make_async_copy(vel.at[:, z], v.at[side], sems.at[side, 0]))
-        copies.append(pltpu.make_async_copy(dif.at[z], d.at[side], sems.at[side, 1]))
-    for copy in copies:
-        copy.start()
-    slice_index = lax.axis_index("tm")
-    for side, (rec, recb, own, ownb) in enumerate(((rlo, rblo, olo, oblo), (rhi, rbhi, ohi, obhi))):
-        for r in range(0, NY, 8):
-            pad[side, TOP + r : TOP + r + 8, :] = (
-                own[NY + r : NY + r + 8, :] + ownb[r : r + 8, :] * rec[r : r + 8, :]
+def finish_kernel(rnear, rfar, rfac, onear, ofar, ofac, fin, edge, bound, gcp, cb, ymid, ub, msg, gc, pad, zs, jp):
+    for kind, (rec, own, recb, ownb, at) in enumerate(
+        ((rnear, onear, rnear, onear, FAR), (rfar, ofar, rfac, ofac, 0))
+    ):
+        top = edge_is_top(kind)
+        side = jnp.where(top, 1, 0)
+        for r in range(0, NY, 8):
+            pad[kind, TOP + r : TOP + r + 8, :] = (
+                own[NY + r : NY + r + 8, :] + ownb[at + r : at + r + 8, :] * rec[r : r + 8, :]
             )
-        wrap_rows(pad, side)
-        copies[2 * side].wait()
-        copies[2 * side + 1].wait()
+        wrap_rows(pad, kind)
         for r in range(0, NY, 8):
             rows = slice(r, r + 8)
-            c, w, e, s, n = plane(pad, side, r)
-            outside = rec[NY + r : NY + r + 8, :] + recb[r : r + 8, :] * own[r : r + 8, :]
+            c, w, e, s, n = plane(pad, kind, r)
+            outside = rec[NY + r : NY + r + 8, :] + recb[at + r : at + r + 8, :] * own[r : r + 8, :]
             inside = edge[side, rows, :]
-            b, t = (outside, inside) if side == 0 else (inside, outside)
-            last = advanced(
-                c, w, e, s, n, b, t,
-                v[side, 0, rows, :], v[side, 1, rows, :], v[side, 2, rows, :], d[side, rows, :],
-            )
+            ax, ay, az, k = (bound[side, i, rows, :] for i in range(4))
+            last = advanced(c, w, e, s, n, inside, outside, ax, ay, jnp.where(top, az, -az), k)
             near = fin[5 * side, rows, :] + edge[2 + side, rows, :] * c
             ub[3 * side, rows, :] = last
             ub[1 + side, rows, :] = near
-            put_columns(zs, slice(side * NY + r, side * NY + r + 8), last + near)
+            put_columns(zs.at[side], rows, last + near)
     lane = lax.broadcasted_iota(jnp.int32, (128, 128), 1)
-    halo_lo = jnp.concatenate([rlo[2 * NY : MSG, 128 * i : 128 * i + 128] for i in range(8)], axis=0)
-    halo_hi = jnp.concatenate([rhi[2 * NY : MSG, 128 * i : 128 * i + 128] for i in range(8)], axis=0)
+    hnear = jnp.concatenate([rnear[2 * NY : FAR, 128 * i : 128 * i + 128] for i in range(8)], axis=0)
+    hfar = jnp.concatenate([rfar[2 * NY : FAR, 128 * i : 128 * i + 128] for i in range(8)], axis=0)
+    first_core = lax.axis_index("core") == 0
+    halo_lo, halo_hi = jnp.where(first_core, hfar, hnear), jnp.where(first_core, hnear, hfar)
     for b in range(4):
         rows = slice(128 * b, 128 * b + 128)
         t = halved_x(
             jnp.concatenate(
                 [
-                    jnp.concatenate([paired(zs, i, 0, 32), ymid[i], paired(zs, i, NY, 32)], axis=0)
+                    jnp.concatenate([paired(zs.at[0], i, 0, 32), ymid[i], paired(zs.at[1], i, 0, 32)], axis=0)
                     for i in (2 * b, 2 * b + 1)
                 ],
                 axis=1,
@@ -349,111 +368,117 @@
         hh = pltpu.roll(halo_hi, (96 - 32 * b) % 128, 1) if b != 3 else halo_hi
         halo = jnp.where(lane < 32, hl, hh)
         g = gcp[rows, :] + cb[rows, :] * halo
-        g = jnp.where(slice_index == 0, 0.0, g)
+        g = jnp.where(lax.axis_index("tm") == 0, 0.0, g)
         gc[rows, :] = g
         jp[8 + 128 * b : 136 + 128 * b, :] = t - g
     jp[0:8, :] = jp[CX : CX + 8, :]
     jp[CX + 8 : CX + 24, :] = jp[8:24, :]
-    comp = slice_index // 2
-    first = pl.multiple_of((slice_index % 2) * 16, 16)
     for i in range(BLOCKS):
-        msg[i, 0:WIN, :] = jp[XB * i : XB * i + WIN, :]
-        msg[i, WIN : WIN + 16, :] = ct[comp, pl.ds(first + XB * i, 16), :]
-
-
-def finish(messages, fin, edge, velocity, diffusivity, gcp, cb, ymid, ct):
+        msg[i] = jp[XB * i : XB * i + WIN, :]
+
+
+def finish(messages, fin, edge, bound, gcp, cb, ymid):
     return pl.pallas_call(
         finish_kernel,
         out_shape=[
             jax.ShapeDtypeStruct((4, NY, NX), F32),
-            jax.ShapeDtypeStruct((BLOCKS, WIN + 16, CL), F32),
+            jax.ShapeDtypeStruct((BLOCKS, WIN, CL), F32),
             jax.ShapeDtypeStruct((CX, CL), F32),
         ],
-        in_specs=[whole()] * 10 + [remains()] * 2 + [whole()] * 4,
+        in_specs=[whole()] * 12,
         out_specs=[whole()] * 3,
         scratch_shapes=[
             pltpu.VMEM((2, PADDED, NX), F32),
-            pltpu.VMEM((2, 3, NY, NX), F32),
-            pltpu.VMEM((2, NY, NX), F32),
-            pltpu.VMEM((8, 2 * NY, 128), F32),
+            pltpu.VMEM((2, 8, NY, 128), F32),
             pltpu.VMEM((CX + 24, CL), F32),
-            pltpu.SemaphoreType.DMA((2, 2)),
         ],
         compiler_params=params(24),
         name="finish",
-    )(*messages, fin, edge, velocity, diffusivity, gcp, cb, ymid, ct)
+    )(*messages, fin, edge, bound, gcp, cb, ymid)
 
 
 HALO = 13
 SHARED = ((0, 6, 96), (1, 5, 64), (2, 4, 32))
 
 
-def pick_kernel(got, up, down):
+def pick_kernel(got, w0, w1, w2, w3, even, odd, coefs):
     lane = lax.broadcasted_iota(jnp.int32, (WIN, CL), 1)
-
-    def coef(i, slab):
-        return jnp.concatenate([got[QUAD * (2 * i + h) + slab, WIN : WIN + 16, :] for h in range(2)], axis=0)
-
-    for out, near, far in ((up, 3, 2), (down, 0, 1)):
+    mine = quad_rank()
+    for i, window in enumerate((w0, w1, w2, w3)):
+        coefs[mine ^ i] = window[...]
+    for parity, out in enumerate((even, odd)):
+        up = lax.rem(lax.axis_index("px"), 2) == parity
+        near, far = jnp.where(up, 3, 0), jnp.where(up, 2, 1)
+
+        def shared(main, other, width):
+            return jnp.where(
+                up,
+                jnp.where(lane >= CL - width, main, pltpu.roll(other, CL - width, 1)),
+                jnp.where(lane < width, main, pltpu.roll(other, width, 1)),
+            )
+
         for j in range(4):
-            out[j] = got[QUAD * j + near, 0:WIN, :]
-            out[7 + j] = coef(j, near)
+            out[j] = got[QUAD * j + near]
+            out[7 + j] = coefs[near, j]
         for j, other, width in SHARED:
-            mine = lane >= CL - width if near == 3 else lane < width
-            turn = CL - width if near == 3 else width
-            out[4 + j] = jnp.where(
-                mine, got[QUAD * j + far, 0:WIN, :], pltpu.roll(got[QUAD * other + near, 0:WIN, :], turn, 1)
-            )
+            out[4 + j] = shared(got[QUAD * j + far], got[QUAD * other + near], width)
         for j in range(2):
-            mine = lane >= 64 if near == 3 else lane < 64
-            out[11 + j] = jnp.where(mine, coef(2 * j, far), pltpu.roll(coef(2 * j + 1, far), 64, 1))
-
-
-def pick(got):
+            out[11 + j] = shared(coefs[far, 2 * j], coefs[far, 2 * j + 1], 64)
+
+
+def pick(got, windows):
     halo = jax.ShapeDtypeStruct((HALO, WIN, CL), F32)
     return pl.pallas_call(
         pick_kernel,
         out_shape=[halo, halo],
-        in_specs=[whole()],
+        in_specs=[whole()] * 5,
         out_specs=[whole(), whole()],
+        scratch_shapes=[pltpu.VMEM((QUAD, 4, WIN, CL), F32)],
         compiler_params=params(16),
         name="pick",
-    )(got)
+    )(got, *windows)
 
 
 LANES = 8 * CL
 
 
-def chain_kernel(got, below, above, out, src, cf, e):
+def chain_kernel(got, w0, w1, w2, w3, even, odd, out, src, cf, e):
+    first = lax.rem(lax.axis_index("px"), 2) == 0
+
+    def below(i):
+        return jnp.where(first, odd[i], even[i])
+
+    def above(i):
+        return jnp.where(first, even[i], odd[i])
+
+    def put_coefs(values, lanes):
+        for i, value in enumerate(coarse_coefs(*values)):
+            cf[i, :, lanes] = value
+
     for j in range(7):
         for q in range(QUAD):
-            src[j, :, (2 + q) * CL : (3 + q) * CL] = got[QUAD * j + q, 0:WIN, :]
+            src[j, :, (2 + q) * CL : (3 + q) * CL] = got[QUAD * j + q]
         for halo, near, far in ((below, 1, 0), (above, 6, 7)):
             if j < 4:
-                src[j, :, near * CL : near * CL + CL] = halo[j]
+                src[j, :, near * CL : near * CL + CL] = halo(j)
             if j >= 3:
                 src[j, :, far * CL : far * CL + CL] = jnp.zeros((WIN, CL), F32)
     for halo, near, far in ((below, 1, 0), (above, 6, 7)):
         for j, other, width in SHARED:
             turn = width if near == 1 else CL - width
-            src[j, :, far * CL : far * CL + CL] = halo[4 + j]
-            src[other, :, near * CL : near * CL + CL] = pltpu.roll(halo[4 + j], turn, 1)
-    for block in range(8):
-        lanes = slice(block * CL, block * CL + CL)
-        halo = below if block < 2 else above
-        for half in range(2):
-            rows = slice(16 * half, 16 * half + 16)
-            if block in (1, 6):
-                parts = [halo[7 + i, rows, :] for i in range(4)]
-            elif block in (0, 7):
-                parts = [
-                    pltpu.roll(halo[11 + i // 2, rows, :], 64, 1) if i % 2 else halo[11 + i // 2, rows, :]
-                    for i in range(4)
-                ]
-            else:
-                parts = [got[QUAD * (2 * i + half) + block - 2, WIN : WIN + 16, :] for i in range(4)]
-            for i, value in enumerate(coarse_coefs(*parts)):
-                cf[i, rows, lanes] = value
+            block = halo(4 + j)
+            src[j, :, far * CL : far * CL + CL] = block
+            src[other, :, near * CL : near * CL + CL] = pltpu.roll(block, turn, 1)
+        put_coefs([halo(7 + i) for i in range(4)], slice(near * CL, near * CL + CL))
+        pairs = [halo(11), halo(12)]
+        put_coefs(
+            [pairs[0], pltpu.roll(pairs[0], 64, 1), pairs[1], pltpu.roll(pairs[1], 64, 1)],
+            slice(far * CL, far * CL + CL),
+        )
+    mine = quad_rank()
+    for i, window in enumerate((w0, w1, w2, w3)):
+        lanes = pl.ds(pl.multiple_of((2 + (mine ^ i)) * CL, CL), CL)
+        put_coefs([window[comp] for comp in range(4)], lanes)
     for q in range(QUAD):
         out[q] = jnp.zeros((XB, CL), F32)
     e[...] = src[0]
@@ -473,11 +498,11 @@
             e[...] = y + src[k]
 
 
-def chain(got, below, above):
+def chain(got, windows, even, odd):
     return pl.pallas_call(
         chain_kernel,
         out_shape=jax.ShapeDtypeStruct((BLOCKS, XB, CL), F32),
-        in_specs=[whole()] * 3,
+        in_specs=[whole()] * 7,
         out_specs=whole(),
         scratch_shapes=[
             pltpu.VMEM((7, WIN, LANES), F32),
@@ -486,7 +511,7 @@
         ],
         compiler_params=params(24),
         name="chain",
-    )(got, below, above)
+    )(got, *windows, even, odd)
 
 
 def result_kernel(y, gc, fin, ub, out, buf, sems):
@@ -519,37 +544,46 @@
     )(y, gc, fin, ub)
 
 
-def shift(value, axes, by):
-    count = lax.axis_size(axes)
-    return lax.ppermute(value, axes, [(i, i + by) for i in range(count) if 0 <= i + by < count])
-
-
-def shift_copy(value, by):
-    slabs = 16
-    pairs = []
-    for t in range(GROUPS):
-        for i in range(slabs):
-            if 0 <= i + by < slabs:
-                t_from = t if i // 2 == (i + by) // 2 else t ^ 1
-                pairs.append((t_from * slabs + i, t * slabs + i + by))
-    return lax.ppermute(value, ("tm",) + SPACE, pairs)
+def swap(value, axes, partner):
+    pairs = [(i, partner(i)) for i in range(lax.axis_size(axes))]
+    return lax.ppermute(value, axes, [(i, j) for i, j in pairs if j is not None])
+
+
+def off_chip(i):
+    j = i + 1 if i % 2 else i - 1
+    return j if 0 <= j < 16 else None
+
+
+def off_chip_copy(i):
+    j = off_chip(i % 16)
+    return None if j is None else (i // 16 ^ 1) * 16 + j
+
+
+def quad_beside(i):
+    j = i + 1 if i % 2 else i - 1
+    return j if 0 <= j < 4 else None
 
 
 def shards(state_old, velocity, diffusivity):
     state = state_old[0]
-    olo, ohi, oblo, obhi = edges(state, velocity, diffusivity)
-    rlo = shift(ohi, SPACE, 1)
-    rhi = shift(olo, SPACE, -1)
-    rblo = shift_copy(obhi, 1)
-    rbhi = shift_copy(oblo, -1)
-    fin, edge, ct, gcp, cb, ymid = interior(state, velocity, diffusivity)
-    messages = (rlo, rhi, rblo, rbhi, olo, ohi, oblo, obhi)
-    ub, msg, gc = finish(messages, fin, edge, velocity, diffusivity, gcp, cb, ymid, ct)
+    onear, ofar, ofac = edges(state, velocity, diffusivity)
+    rnear = swap(onear, SPACE, lambda i: i ^ 1)
+    rfar = swap(ofar, SPACE, off_chip)
+    rfac = swap(ofac, ("tm",) + SPACE, off_chip_copy)
+    fin, edge, bound, w0, w1, w2, w3, gcp, cb, ymid = interior(state, velocity, diffusivity)
+    windows = (
+        w0,
+        swap(w1, SPACE, lambda i: i ^ 1),
+        swap(w2, SPACE, lambda i: i ^ 2),
+        swap(w3, SPACE, lambda i: i ^ 3),
+    )
+    messages = (rnear, rfar, rfac, onear, ofar, ofac)
+    ub, msg, gc = finish(messages, fin, edge, bound, gcp, cb, ymid)
     got = lax.all_to_all(msg, GROUP, 0, 0)
-    up, down = pick(got)
-    below = shift(up, "px", 1)
-    above = shift(down, "px", -1)
-    back = lax.all_to_all(chain(got, below, above), GROUP, 0, 0)
+    even, odd = pick(got, windows)
+    even = swap(even, "px", lambda i: i ^ 1)
+    odd = swap(odd, "px", quad_beside)
+    back = lax.all_to_all(chain(got, windows, even, odd), GROUP, 0, 0)
     return result(back.reshape(CX, CL), gc, fin, ub)[None]
 
 

time: 82.3 us -> 78.7 us (0.956); the launches traced: 80.9 us -> 78.2 us
  blocking collectives: 34.9 us -> 16.4 us
  waiting for transfers between devices: 6.15 us -> 14.7 us
  local copies, waits for them, and re-layouts: 0.04 us -> 7.27 us
    all_to_all x2 -> x1, blocking collectives: 34.9 us -> 16.4 us  [shards(): back = lax.all_to_all(chain(got, windows, even, odd), GROUP, 0, 0)]
    ppermute x6 -> x8, waiting for transfers between devices: 6.15 us -> 14.7 us  [swap(): lax.ppermute(value, axes, [(i, j) for i, j in pairs if j is not None])]
    unnamed x14 -> x26, local copies, waits for them, and re-layouts: 0.04 us -> 7.27 us
    all_to_all x0 -> x1, starting transfers between devices: none -> 6.1 us  [shards(): got = lax.all_to_all(msg, GROUP, 0, 0)]
    ppermute x6 -> x8, starting transfers between devices: 19.4 us -> 13.7 us  [swap(): lax.ppermute(value, axes, [(i, j) for i, j in pairs if j is not None])]
  transfers between devices with their start and end apart: 6 -> 9, of which waited for: 2 -> 4; matrix products, arithmetic and copies ran while one was open for 0% -> 0% of each run, Pallas kernels for 13% -> 14%
where the time goes in v4:
time: 78.7 us; the launch traced here: 78.2 us
  Pallas kernels  20 us (25%)
  starting transfers between devices  19.8 us (25%)
  blocking collectives  16.4 us (21%)
  waiting for transfers between devices  14.7 us (19%)
  local copies, waits for them, and re-layouts  7.27 us (9%)
    all_to_all x1, blocking collectives, shards(): back = lax.all_to_all(chain(got, windows, even, odd), GROUP, 0, 0)  16.4 us
    ppermute x8, waiting for transfers between devices, swap(): lax.ppermute(value, axes, [(i, j) for i, j in pairs if j is not None])  14.7 us
    ppermute x8, starting transfers between devices, swap(): lax.ppermute(value, axes, [(i, j) for i, j in pairs if j is not None])  13.7 us
    pallas_call x1, Pallas kernels, interior(): pl.pallas_call(interior_kernel, out_shape=[jax.ShapeDtypeStruct((LZ - 2,...  10.9 us
    unnamed x26, local copies, waits for them, and re-layouts  7.27 us
    all_to_all x1, starting transfers between devices, shards(): got = lax.all_to_all(msg, GROUP, 0, 0)  6.1 us
    pallas_call x1, Pallas kernels, edges(): pl.pallas_call(edges_kernel, out_shape=[jax.ShapeDtypeStruct((NEAR, NX),...  3.79 us
    pallas_call x1, Pallas kernels, result(): pl.pallas_call(result_kernel, out_shape=jax.ShapeDtypeStruct((LZ, NY, NX)...  1.93 us
  transfers between devices with their start and end apart: 9, of which 4 were waited for; matrix products, arithmetic and copies ran while one was open for 0% of the time, Pallas kernels for 14%

profile of v4, /device:TPU:5, one launch (start us, length us, event | category | flops | bytes accessed | tf_op | source)
XLA Modules:
  0.0 78.2 jit_solution(1472496404519648496)
XLA Ops:
  0.0 3.8 %edges.1 = (f32[208,1024]{1,0:T(8,128)}, f32[144,1024]{1,0:T(8,128)}, f32[64,1024]{1,0:T(8,128)}) custom-call(f32[8,64,1024]{2,1,0:T(8,128)} %bitcast.4, f32[3,8,64,1024]{3,2,1,0:T(8,128)} %vel.3, f32[8,64,1024]{2,1,0:T(8,128)} %dif.3), custom_call_target="tpu_custom_call" | custom-call | tf_op jit(solution)/shard_map/edges/pallas_call | solution.py:162
  3.8 0.8 collective-permute-start
  4.6 3.4 %collective-permute-start.1 = (f32[144,1024]{1,0:T(8,128)}, f32[144,1024]{1,0:T(8,128)S(1)}, u32[]{:S(2)}, u32[]{:S(2)}) collective-permute-start(f32[144,1024]{1,0:T(8,128)} %get-tuple-element.24.ofar), channel_id=1, source_target_pairs={{1,2},{2,1},{3,4},{4,3},{5,6},{6,5},{7,8},{8,7},{9,10},{10,9},{11,... | collective-permute-start | bytes 1769480 | tf_op jit(solution)/shard_map/ppermute | solution.py:549
  8.0 0.0 copy-start
  8.0 0.0 copy-start.1
  8.0 0.0 copy-start.3
  8.0 4.7 %collective-permute-start.2 = (f32[64,1024]{1,0:T(8,128)}, f32[64,1024]{1,0:T(8,128)S(1)}, u32[]{:S(2)}, u32[]{:S(2)}) collective-permute-start(f32[64,1024]{1,0:T(8,128)} %get-tuple-element.25.ofac), channel_id=1, source_target_pairs={{1,18},{2,17},{3,20},{4,19},{5,22},{6,21},{7,24},{8,23},{9,26},{10... | collective-permute-start | bytes 786440 | tf_op jit(solution)/shard_map/ppermute | solution.py:549
  12.7 10.9 %interior.1 = (f32[6,64,1024]{2,1,0:T(8,128)S(1)}, f32[4,64,1024]{2,1,0:T(8,128)S(1)}, f32[2,4,64,1024]{3,2,1,0:T(8,128)S(1)}, f32[4,32,128]{2,1,0:T(8,128)S(1)}...) custom-call(f32[8,64,1024]{2,1,0:T(8,128)} %bitcast.5, ...), custom_call_target="tpu_custom_call" | custom-call | flops 60000000 | bytes 20000000 | tf_op jit(solution)/shard_map/interior/pallas_call | solution.py:296
  23.7 0.0 copy-start.10
  23.7 0.6 copy-done.10
  24.3 0.0 copy-start.11
  24.3 0.6 copy-done.11
  24.9 0.0 copy-start.12
  24.9 0.6 copy-done.12
  25.5 0.0 collective-permute-done.2.rfac
  25.5 0.0 collective-permute-done.1.rfar
  25.5 0.0 collective-permute-done.rnear
  25.5 0.0 copy-done
  25.5 0.0 copy-done.1
  25.6 0.0 copy-done.3
  25.6 1.3 %finish.1 = (f32[4,64,1024]{2,1,0:T(8,128)S(1)}, f32[32,32,128]{2,1,0:T(8,128)S(1)}, f32[512,128]{1,0:T(8,128)S(1)}) custom-call(f32[208,1024]{1,0:T(8,128)S(1)} %collective-permute-done.rnear, f32[144,1024]{1,0:T(8,128)S(1)} %collective-permute-done.1.rfar, f32[64,1024]{1,0:T(8,128)S(1)} %collective-permute-done.2.rfac, f32[208,1024]{1,0:T(8,128)S(1)} %copy-done, ...), custom_call_target="tpu_custom_call" | custom-call | tf_op jit(solution)/shard_map/finish/pallas_call | solution.py:381
  26.9 0.0 copy-start.2
  26.9 0.8 %copy-done.2 = f32[32,32,128]{2,1,0:T(8,128)} copy-done((f32[32,32,128]{2,1,0:T(8,128)}, f32[32,32,128]{2,1,0:T(8,128)S(1)}, u32[]{:S(2)}) %copy-start.2) | copy-done | bytes 524312
  27.7 6.1 %all-to-all-start = ((f32[32,32,128]{2,1,0:T(8,128)}), f32[32,32,128]{2,1,0:T(8,128)S(1)}, u32[]{:S(2)}, u32[]{:S(2)}) async-start(f32[32,32,128]{2,1,0:T(8,128)} %copy-done.2), calls=%async_computation | async-start | bytes 1048576 | tf_op jit(solution)/shard_map/all_to_all | solution.py:582
  33.8 0.3 collective-permute-start.3
  34.1 1.5 %collective-permute-start.4 = (f32[4,32,128]{2,1,0:T(8,128)}, f32[4,32,128]{2,1,0:T(8,128)S(1)}, u32[]{:S(2)}, u32[]{:S(2)}) collective-permute-start(f32[4,32,128]{2,1,0:T(8,128)} %copy-done.11), channel_id=1, source_target_pairs={{0,2},{1,3},{2,0},{3,1},{4,6},{5,7},{6,4},{7,5},{8,10},{9,11},{10,... | collective-permute-start | bytes 196616 | tf_op jit(solution)/shard_map/ppermute | solution.py:549
  35.6 0.4 collective-permute-start.5
  36.0 0.0 collective-permute-done.3.w1
  36.0 4.9 %collective-permute-done.4.w2 = f32[4,32,128]{2,1,0:T(8,128)S(1)} collective-permute-done((f32[4,32,128]{2,1,0:T(8,128)}, f32[4,32,128]{2,1,0:T(8,128)S(1)}, u32[]{:S(2)}, u32[]{:S(2)}) %collective-permute-start.4) | collective-permute-done | bytes 65568 | tf_op jit(solution)/shard_map/ppermute | solution.py:549
  40.9 0.0 copy-start.4
  40.9 0.6 copy-done.4
  41.5 3.2 %collective-permute-done.5.w3 = f32[4,32,128]{2,1,0:T(8,128)S(1)} collective-permute-done((f32[4,32,128]{2,1,0:T(8,128)}, f32[4,32,128]{2,1,0:T(8,128)S(1)}, u32[]{:S(2)}, u32[]{:S(2)}) %collective-permute-start.5) | collective-permute-done | bytes 65568 | tf_op jit(solution)/shard_map/ppermute | solution.py:549
  44.8 0.0 copy-start.7
  44.8 0.6 copy-done.7
  45.4 0.0 all-to-all-done.got
  45.4 0.0 copy-start.5
  45.4 0.8 %copy-done.5 = f32[4,32,128]{2,1,0:T(8,128)S(1)} copy-done((f32[4,32,128]{2,1,0:T(8,128)S(1)}, f32[4,32,128]{2,1,0:T(8,128)}, u32[]{:S(2)}) %copy-start.5) | copy-done | bytes 65560
  46.3 0.8 %copy-done.8 = f32[4,32,128]{2,1,0:T(8,128)S(1)} copy-done((f32[4,32,128]{2,1,0:T(8,128)S(1)}, f32[4,32,128]{2,1,0:T(8,128)}, u32[]{:S(2)}) %copy-start.8) | copy-done | bytes 65560
  47.1 0.2 pick.1
  47.3 0.7 collective-permute-start.6
  47.9 1.9 %collective-permute-start.7 = (f32[13,32,128]{2,1,0:T(8,128)S(1)}, f32[13,32,128]{2,1,0:T(8,128)S(1)}, u32[]{:S(2)}, u32[]{:S(2)}) collective-permute-start(f32[13,32,128]{2,1,0:T(8,128)S(1)} %get-tuple-element.38), channel_id=1, source_target_pairs={{4,8},{8,4},{5,9},{9,5},{6,10},{10,6},{7,11},{11,7},{20,24},{24,20... | collective-permute-start | bytes 638984 | tf_op jit(solution)/shard_map/ppermute | solution.py:549
  49.9 4.3 %collective-permute-done.6.even = f32[13,32,128]{2,1,0:T(8,128)S(1)} collective-permute-done((f32[13,32,128]{2,1,0:T(8,128)S(1)}, f32[13,32,128]{2,1,0:T(8,128)S(1)}, u32[]{:S(2)}, u32[]{:S(2)}) %collective-permute-start.6) | collective-permute-done | bytes 213024 | tf_op jit(solution)/shard_map/ppermute | solution.py:549
  54.2 2.2 %collective-permute-done.7.odd = f32[13,32,128]{2,1,0:T(8,128)S(1)} collective-permute-done((f32[13,32,128]{2,1,0:T(8,128)S(1)}, f32[13,32,128]{2,1,0:T(8,128)S(1)}, u32[]{:S(2)}, u32[]{:S(2)}) %collective-permute-start.7) | collective-permute-done | bytes 213024 | tf_op jit(solution)/shard_map/ppermute | solution.py:549
  56.3 0.8 %copy-done.6 = f32[4,32,128]{2,1,0:T(8,128)S(1)} copy-done((f32[4,32,128]{2,1,0:T(8,128)S(1)}, f32[4,32,128]{2,1,0:T(8,128)}, u32[]{:S(2)}) %copy-start.6) | copy-done | bytes 65560
  57.2 0.8 %copy-done.9 = f32[4,32,128]{2,1,0:T(8,128)S(1)} copy-done((f32[4,32,128]{2,1,0:T(8,128)S(1)}, f32[4,32,128]{2,1,0:T(8,128)}, u32[]{:S(2)}) %copy-start.9) | copy-done | bytes 65560
  58.0 1.9 %chain.1 = f32[32,16,128]{2,1,0:T(8,128)S(1)} custom-call(f32[32,32,128]{2,1,0:T(8,128)S(1)} %all-to-all-done.got, f32[4,32,128]{2,1,0:T(8,128)S(1)} %get-tuple-element.33.w0, f32[4,32,128]{2,1,0:T(8,128)S(1)} %collective-permute-done.3.w1, f32[4,32,128]{2,1,0:T(8,128)S(1)} %copy-done.6, f32[4,32,128]{2,1,0:T(8,128)S(1)} %copy-done.9, ...), custom_call_target="tpu_custom_call" | custom-call | tf_op jit(solution)/shard_map/chain/pallas_call | solution.py:502
  59.9 16.4 %all_to_all.10 = f32[32,16,128]{2,1,0:T(8,128)S(1)} all-to-all(f32[32,16,128]{2,1,0:T(8,128)S(1)} %chain.1), channel_id=1, replica_groups=mesh['tm'=8,'px'=4,'pz'=2,'core'=2] {'tm','pz','core'}, dimensions={0} | all-to-all | bytes 524288 | tf_op jit(solution)/shard_map/all_to_all | solution.py:586
  76.3 1.9 %result.1 = f32[8,64,1024]{2,1,0:T(8,128)} custom-call(f32[512,128]{1,0:T(8,128)S(1)} %bitcast.3, f32[512,128]{1,0:T(8,128)S(1)} %get-tuple-element.39.gc, f32[6,64,1024]{2,1,0:T(8,128)S(1)} %get-tuple-element.26.fin, f32[4,64,1024]{2,1,0:T(8,128)S(1)} %get-tuple-element.40.ub), custom_call_target="tpu_custom_call" | custom-call | tf_op jit(solution)/shard_map/result/pallas_call | solution.py:536
  (3 shorter events, 0.0 us)
Async XLA Ops:
  3.8 21.7 %collective-permute-start = (f32[208,1024]{1,0:T(8,128)}, f32[208,1024]{1,0:T(8,128)S(1)}, u32[]{:S(2)}, u32[]{:S(2)}) collective-permute-start(f32[208,1024]{1,0:T(8,128)} %get-tuple-element.23.onear), channel_id=1, source_target_pairs={{0,1},{1,0},{2,3},{3,2},{4,5},{5,4},{6,7},{7,6},{8,9},{9,8},{10,11... | collective-permute-start | bytes 2555912 | tf_op jit(solution)/shard_map/ppermute | solution.py:549
  4.6 21.0 %collective-permute-start.1 = (f32[144,1024]{1,0:T(8,128)}, f32[144,1024]{1,0:T(8,128)S(1)}, u32[]{:S(2)}, u32[]{:S(2)}) collective-permute-start(f32[144,1024]{1,0:T(8,128)} %get-tuple-element.24.ofar), channel_id=1, source_target_pairs={{1,2},{2,1},{3,4},{4,3},{5,6},{6,5},{7,8},{8,7},{9,10},{10,9},{11,... | collective-permute-start | bytes 1769480 | tf_op jit(solution)/shard_map/ppermute | solution.py:549
  8.0 17.5 %copy-start = (f32[208,1024]{1,0:T(8,128)S(1)}, f32[208,1024]{1,0:T(8,128)}, u32[]{:S(2)}) copy-start(f32[208,1024]{1,0:T(8,128)} %get-tuple-element.23.onear) | copy-start | bytes 2555908
  8.0 17.5 %copy-start.1 = (f32[144,1024]{1,0:T(8,128)S(1)}, f32[144,1024]{1,0:T(8,128)}, u32[]{:S(2)}) copy-start(f32[144,1024]{1,0:T(8,128)} %get-tuple-element.24.ofar) | copy-start | bytes 1769476
  8.0 17.5 %copy-start.3 = (f32[64,1024]{1,0:T(8,128)S(1)}, f32[64,1024]{1,0:T(8,128)}, u32[]{:S(2)}) copy-start(f32[64,1024]{1,0:T(8,128)} %get-tuple-element.25.ofac) | copy-start | bytes 786436
  8.0 17.5 %collective-permute-start.2 = (f32[64,1024]{1,0:T(8,128)}, f32[64,1024]{1,0:T(8,128)S(1)}, u32[]{:S(2)}, u32[]{:S(2)}) collective-permute-start(f32[64,1024]{1,0:T(8,128)} %get-tuple-element.25.ofac), channel_id=1, source_target_pairs={{1,18},{2,17},{3,20},{4,19},{5,22},{6,21},{7,24},{8,23},{9,26},{10... | collective-permute-start | bytes 786440 | tf_op jit(solution)/shard_map/ppermute | solution.py:549
  23.7 0.6 copy-start.10
  24.3 0.6 copy-start.11
  24.9 0.6 copy-start.12
  26.9 0.8 %copy-start.2 = (f32[32,32,128]{2,1,0:T(8,128)}, f32[32,32,128]{2,1,0:T(8,128)S(1)}, u32[]{:S(2)}) copy-start(f32[32,32,128]{2,1,0:T(8,128)S(1)} %get-tuple-element.32) | copy-start | bytes 1572868
  27.7 17.8 %all-to-all-start = ((f32[32,32,128]{2,1,0:T(8,128)}), f32[32,32,128]{2,1,0:T(8,128)S(1)}, u32[]{:S(2)}, u32[]{:S(2)}) async-start(f32[32,32,128]{2,1,0:T(8,128)} %copy-done.2), calls=%async_computation | async-start | bytes 1048576 | tf_op jit(solution)/shard_map/all_to_all | solution.py:582
  33.8 2.2 %collective-permute-start.3 = (f32[4,32,128]{2,1,0:T(8,128)}, f32[4,32,128]{2,1,0:T(8,128)S(1)}, u32[]{:S(2)}, u32[]{:S(2)}) collective-permute-start(f32[4,32,128]{2,1,0:T(8,128)} %copy-done.12), channel_id=1, source_target_pairs={{0,1},{1,0},{2,3},{3,2},{4,5},{5,4},{6,7},{7,6},{8,9},{9,8},{10,11... | collective-permute-start | bytes 196616 | tf_op jit(solution)/shard_map/ppermute | solution.py:549
  34.1 6.8 %collective-permute-start.4 = (f32[4,32,128]{2,1,0:T(8,128)}, f32[4,32,128]{2,1,0:T(8,128)S(1)}, u32[]{:S(2)}, u32[]{:S(2)}) collective-permute-start(f32[4,32,128]{2,1,0:T(8,128)} %copy-done.11), channel_id=1, source_target_pairs={{0,2},{1,3},{2,0},{3,1},{4,6},{5,7},{6,4},{7,5},{8,10},{9,11},{10,... | collective-permute-start | bytes 196616 | tf_op jit(solution)/shard_map/ppermute | solution.py:549
  35.6 9.2 %collective-permute-start.5 = (f32[4,32,128]{2,1,0:T(8,128)}, f32[4,32,128]{2,1,0:T(8,128)S(1)}, u32[]{:S(2)}, u32[]{:S(2)}) collective-permute-start(f32[4,32,128]{2,1,0:T(8,128)} %copy-done.10), channel_id=1, source_target_pairs={{0,3},{1,2},{2,1},{3,0},{4,7},{5,6},{6,5},{7,4},{8,11},{9,10},{10,... | collective-permute-start | bytes 196616 | tf_op jit(solution)/shard_map/ppermute | solution.py:549
  40.9 0.6 copy-start.4
  44.8 0.6 copy-start.7
  45.4 0.8 %copy-start.5 = (f32[4,32,128]{2,1,0:T(8,128)S(1)}, f32[4,32,128]{2,1,0:T(8,128)}, u32[]{:S(2)}) copy-start(f32[4,32,128]{2,1,0:T(8,128)} %copy-done.4) | copy-start | bytes 196612
  46.3 0.8 %copy-start.8 = (f32[4,32,128]{2,1,0:T(8,128)S(1)}, f32[4,32,128]{2,1,0:T(8,128)}, u32[]{:S(2)}) copy-start(f32[4,32,128]{2,1,0:T(8,128)} %copy-done.7) | copy-start | bytes 196612
  47.3 6.9 %collective-permute-start.6 = (f32[13,32,128]{2,1,0:T(8,128)S(1)}, f32[13,32,128]{2,1,0:T(8,128)S(1)}, u32[]{:S(2)}, u32[]{:S(2)}) collective-permute-start(f32[13,32,128]{2,1,0:T(8,128)S(1)} %get-tuple-element.37), channel_id=1, source_target_pairs={{0,4},{4,0},{8,12},{12,8},{1,5},{5,1},{9,13},{13,9},{2,6},{6,2},{1... | collective-permute-start | bytes 638984 | tf_op jit(solution)/shard_map/ppermute | solution.py:549
  47.9 8.4 %collective-permute-start.7 = (f32[13,32,128]{2,1,0:T(8,128)S(1)}, f32[13,32,128]{2,1,0:T(8,128)S(1)}, u32[]{:S(2)}, u32[]{:S(2)}) collective-permute-start(f32[13,32,128]{2,1,0:T(8,128)S(1)} %get-tuple-element.38), channel_id=1, source_target_pairs={{4,8},{8,4},{5,9},{9,5},{6,10},{10,6},{7,11},{11,7},{20,24},{24,20... | collective-permute-start | bytes 638984 | tf_op jit(solution)/shard_map/ppermute | solution.py:549
  56.3 0.8 %copy-start.6 = (f32[4,32,128]{2,1,0:T(8,128)S(1)}, f32[4,32,128]{2,1,0:T(8,128)}, u32[]{:S(2)}) copy-start(f32[4,32,128]{2,1,0:T(8,128)} %copy-done.4) | copy-start | bytes 196612
  57.2 0.8 %copy-start.9 = (f32[4,32,128]{2,1,0:T(8,128)S(1)}, f32[4,32,128]{2,1,0:T(8,128)}, u32[]{:S(2)}) copy-start(f32[4,32,128]{2,1,0:T(8,128)} %copy-done.7) | copy-start | bytes 196612

commit v5 on v4

--- a/solution.py
+++ b/solution.py
@@ -176,7 +176,7 @@
             pltpu.VMEM((8, 2 * NY, 128), F32),
             pltpu.SemaphoreType.DMA((2, 4)),
         ],
-        compiler_params=params(58),
+        compiler_params=params(52),
         name="edges",
     )(state, velocity, diffusivity)
 
@@ -185,27 +185,84 @@
     return lax.axis_index("pz") * 2 + lax.axis_index("core")
 
 
-def interior_kernel(st, vel, dif, fin, edge, bound, w0, w1, w2, w3, gcp, cb, ymid, u, u1, ct, v, d, zs, ct0, usem, sems):
+def coefs_kernel(vel, dif, ct, w0, w1, w2, w3, v, zs, sems):
+    def part(comp, zc):
+        layers = slice(2 * zc, 2 * zc + 2)
+        source = dif.at[layers] if comp == 3 else vel.at[comp, layers]
+        return pltpu.make_async_copy(source, v.at[comp, layers], sems.at[comp, zc])
+
+    for comp in range(4):
+        for zc in range(4):
+            part(comp, zc).start()
+    for comp in range(4):
+        for zc in range(4):
+            part(comp, zc).wait()
+            for r in range(0, NY, 8):
+                rows = slice(r, r + 8)
+                put_columns(
+                    zs.at[comp], slice(zc * NY + r, zc * NY + r + 8), v[comp, 2 * zc, rows, :] + v[comp, 2 * zc + 1, rows, :]
+                )
+        for b in range(4):
+            ct[comp, 8 + 128 * b : 136 + 128 * b, :] = halved_x(
+                jnp.concatenate([paired(zs.at[comp], 2 * b + i, 0, 128) for i in range(2)], axis=1)
+            )
+        ct[comp, 0:8, :] = ct[comp, CX : CX + 8, :]
+        ct[comp, CX + 8 : CX + 32, :] = ct[comp, 8:32, :]
+    mine = quad_rank()
+    for i, out in enumerate((w0, w1, w2, w3)):
+        block = lax.axis_index("tm") * QUAD + (mine ^ i)
+        for comp in range(4):
+            out[comp] = ct[comp, pl.ds(pl.multiple_of(block * XB, XB), WIN), :]
+
+
+def coefs(velocity, diffusivity):
+    window = jax.ShapeDtypeStruct((4, WIN, CL), F32)
+    return pl.pallas_call(
+        coefs_kernel,
+        out_shape=[jax.ShapeDtypeStruct((4, CROWS, CL), F32), window, window, window, window],
+        in_specs=[remains()] * 2,
+        out_specs=[whole()] * 5,
+        scratch_shapes=[
+            pltpu.VMEM((4, LZ, NY, NX), F32),
+            pltpu.VMEM((4, 8, 4 * NY, 128), F32),
+            pltpu.SemaphoreType.DMA((4, 4)),
+        ],
+        compiler_params=params(50),
+        cost_estimate=pl.CostEstimate(flops=20_000_000, bytes_accessed=9_000_000, transcendentals=0),
+        name="coefs",
+    )(velocity, diffusivity)
+
+
+def interior_kernel(st, vel, dif, ct, fin, edge, bound, gcp, cb, ymid, u, u1, v, d, zs, zf, ct0, usem, sems):
     def layer(z):
         return (
             pltpu.make_async_copy(vel.at[:, z], v.at[:, z], sems.at[z, 0]),
             pltpu.make_async_copy(dif.at[z], d.at[z], sems.at[z, 1]),
         )
 
-    copy = pltpu.make_async_copy(st, u.at[:, TOP : TOP + NY, :], usem)
-    copy.start()
-    for z in (1, 2, 3, 4, 5, 6, 0, 7):
-        for part in layer(z):
+    def state(z):
+        return pltpu.make_async_copy(st.at[z], u.at[z, TOP : TOP + NY, :], usem.at[z])
+
+    for z in range(3):
+        state(z).start()
+    for part in layer(1):
+        part.start()
+    for z in range(3, LZ):
+        state(z).start()
+        for part in layer(z - 1):
             part.start()
-    copy.wait()
-    for z in range(LZ):
+    bounds = []
+    for side, z in enumerate((0, LZ - 1)):
+        bounds.append(pltpu.make_async_copy(vel.at[:, z], bound.at[side, 0:3], sems.at[z, 0]))
+        bounds.append(pltpu.make_async_copy(dif.at[z], bound.at[side, 3], sems.at[z, 1]))
+    for copy in bounds:
+        copy.start()
+    for z in range(2):
+        state(z).wait()
         wrap_rows(u, z)
-    for zc in range(4):
-        for r in range(0, NY, 8):
-            here = slice(TOP + r, TOP + r + 8)
-            put_columns(zs.at[4], slice(zc * NY + r, zc * NY + r + 8), u[2 * zc, here, :] + u[2 * zc + 1, here, :])
-
     def first(z, _):
+        state(z + 1).wait()
+        wrap_rows(u, z + 1)
         for part in layer(z):
             part.wait()
         for r in range(0, NY, 8):
@@ -237,42 +294,25 @@
         return 0
 
     lax.fori_loop(1, LZ - 1, second, 0)
+    for copy in bounds:
+        copy.wait()
     edge[2] = d[1] + jnp.maximum(v[2, 1], 0.0)
     edge[3] = d[LZ - 2] - jnp.minimum(v[2, LZ - 2], 0.0)
     for zc in (1, 2):
         for r in range(0, NY, 8):
             rows = slice(r, r + 8)
-            put_columns(zs.at[5], slice((zc - 1) * NY + r, (zc - 1) * NY + r + 8), fin[2 * zc - 1, rows, :] + fin[2 * zc, rows, :])
+            put_columns(zf, slice((zc - 1) * NY + r, (zc - 1) * NY + r + 8), fin[2 * zc - 1, rows, :] + fin[2 * zc, rows, :])
     for i in range(8):
-        ymid[i] = paired(zs.at[5], i, 0, 64)
-
-    for side, z in enumerate((0, LZ - 1)):
-        for part in layer(z):
-            part.wait()
-        for comp in range(3):
-            bound[side, comp] = v[comp, z]
-        bound[side, 3] = d[z]
+        ymid[i] = paired(zf, i, 0, 64)
+
     for zc in range(4):
         for r in range(0, NY, 8):
-            to, rows = slice(zc * NY + r, zc * NY + r + 8), slice(r, r + 8)
-            for comp in range(3):
-                put_columns(zs.at[comp], to, v[comp, 2 * zc, rows, :] + v[comp, 2 * zc + 1, rows, :])
-            put_columns(zs.at[3], to, d[2 * zc, rows, :] + d[2 * zc + 1, rows, :])
-    for comp in range(5):
-        for b in range(4):
-            t = halved_x(jnp.concatenate([paired(zs.at[comp], 2 * b + i, 0, 128) for i in range(2)], axis=1))
-            if comp < 4:
-                ct[comp, 8 + 128 * b : 136 + 128 * b, :] = t
-            else:
-                ct0[8 + 128 * b : 136 + 128 * b, :] = t
-    for comp in range(4):
-        ct[comp, 0:8, :] = ct[comp, CX : CX + 8, :]
-        ct[comp, CX + 8 : CX + 32, :] = ct[comp, 8:32, :]
-    mine = quad_rank()
-    for i, out in enumerate((w0, w1, w2, w3)):
-        block = lax.axis_index("tm") * QUAD + (mine ^ i)
-        for comp in range(4):
-            out[comp] = ct[comp, pl.ds(pl.multiple_of(block * XB, XB), WIN), :]
+            here = slice(TOP + r, TOP + r + 8)
+            put_columns(zs, slice(zc * NY + r, zc * NY + r + 8), u[2 * zc, here, :] + u[2 * zc + 1, here, :])
+    for b in range(4):
+        ct0[8 + 128 * b : 136 + 128 * b, :] = halved_x(
+            jnp.concatenate([paired(zs, 2 * b + i, 0, 128) for i in range(2)], axis=1)
+        )
     ct0[0:8, :] = ct0[CX : CX + 8, :]
     ct0[CX + 8 : CX + 16, :] = ct0[8:16, :]
     lane = lax.broadcasted_iota(jnp.int32, (64, CL), 1)
@@ -290,43 +330,43 @@
         cb[r : r + 64, :] = jnp.where(lane < 32, zl, jnp.where(lane >= 96, zh, 0.0))
 
 
-def interior(state, velocity, diffusivity):
+def interior(state, velocity, diffusivity, ct):
     small = jax.ShapeDtypeStruct((CX, CL), F32)
-    window = jax.ShapeDtypeStruct((4, WIN, CL), F32)
     return pl.pallas_call(
         interior_kernel,
         out_shape=[
             jax.ShapeDtypeStruct((LZ - 2, NY, NX), F32),
             jax.ShapeDtypeStruct((4, NY, NX), F32),
             jax.ShapeDtypeStruct((2, 4, NY, NX), F32),
-            window,
-            window,
-            window,
-            window,
             small,
             small,
             jax.ShapeDtypeStruct((8, 64, 128), F32),
         ],
-        in_specs=[remains()] * 3,
-        out_specs=[whole()] * 10,
+        in_specs=[remains()] * 3 + [whole()],
+        out_specs=[whole()] * 6,
         scratch_shapes=[
             pltpu.VMEM((LZ, PADDED, NX), F32),
             pltpu.VMEM((LZ, PADDED, NX), F32),
-            pltpu.VMEM((4, CROWS, CL), F32),
             pltpu.VMEM((3, LZ, NY, NX), F32),
             pltpu.VMEM((LZ, NY, NX), F32),
-            pltpu.VMEM((6, 8, 4 * NY, 128), F32),
+            pltpu.VMEM((8, 4 * NY, 128), F32),
+            pltpu.VMEM((8, 2 * NY, 128), F32),
             pltpu.VMEM((CX + 16, CL), F32),
-            pltpu.SemaphoreType.DMA,
+            pltpu.SemaphoreType.DMA((LZ,)),
             pltpu.SemaphoreType.DMA((LZ, 2)),
         ],
-        compiler_params=params(48),
+        compiler_params=params(44),
         cost_estimate=pl.CostEstimate(flops=60_000_000, bytes_accessed=20_000_000, transcendentals=0),
         name="interior",
-    )(state, velocity, diffusivity)
-
-
-def finish_kernel(rnear, rfar, rfac, onear, ofar, ofac, fin, edge, bound, gcp, cb, ymid, ub, msg, gc, pad, zs, jp):
+    )(state, velocity, diffusivity, ct)
+
+
+def finish_kernel(
+    rnear, rfar, rfac, onear, ofar, ofac, w0, w1, w2, w3, fin, edge, bound, gcp, cb, ymid, ub, msg, gc, quad, pad, zs, jp
+):
+    mine = quad_rank()
+    for i, window in enumerate((w0, w1, w2, w3)):
+        quad[mine ^ i] = window[...]
     for kind, (rec, own, recb, ownb, at) in enumerate(
         ((rnear, onear, rnear, onear, FAR), (rfar, ofar, rfac, ofac, 0))
     ):
@@ -377,16 +417,17 @@
         msg[i] = jp[XB * i : XB * i + WIN, :]
 
 
-def finish(messages, fin, edge, bound, gcp, cb, ymid):
+def finish(messages, windows, fin, edge, bound, gcp, cb, ymid):
     return pl.pallas_call(
         finish_kernel,
         out_shape=[
             jax.ShapeDtypeStruct((4, NY, NX), F32),
             jax.ShapeDtypeStruct((BLOCKS, WIN, CL), F32),
             jax.ShapeDtypeStruct((CX, CL), F32),
-        ],
-        in_specs=[whole()] * 12,
-        out_specs=[whole()] * 3,
+            jax.ShapeDtypeStruct((QUAD, 4, WIN, CL), F32),
+        ],
+        in_specs=[whole()] * 16,
+        out_specs=[whole()] * 4,
         scratch_shapes=[
             pltpu.VMEM((2, PADDED, NX), F32),
             pltpu.VMEM((2, 8, NY, 128), F32),
@@ -394,18 +435,15 @@
         ],
         compiler_params=params(24),
         name="finish",
-    )(*messages, fin, edge, bound, gcp, cb, ymid)
+    )(*messages, *windows, fin, edge, bound, gcp, cb, ymid)
 
 
 HALO = 13
 SHARED = ((0, 6, 96), (1, 5, 64), (2, 4, 32))
 
 
-def pick_kernel(got, w0, w1, w2, w3, even, odd, coefs):
+def pick_kernel(got, quad, even, odd):
     lane = lax.broadcasted_iota(jnp.int32, (WIN, CL), 1)
-    mine = quad_rank()
-    for i, window in enumerate((w0, w1, w2, w3)):
-        coefs[mine ^ i] = window[...]
     for parity, out in enumerate((even, odd)):
         up = lax.rem(lax.axis_index("px"), 2) == parity
         near, far = jnp.where(up, 3, 0), jnp.where(up, 2, 1)
@@ -419,30 +457,29 @@
 
         for j in range(4):
             out[j] = got[QUAD * j + near]
-            out[7 + j] = coefs[near, j]
+            out[7 + j] = quad[near, j]
         for j, other, width in SHARED:
             out[4 + j] = shared(got[QUAD * j + far], got[QUAD * other + near], width)
         for j in range(2):
-            out[11 + j] = shared(coefs[far, 2 * j], coefs[far, 2 * j + 1], 64)
-
-
-def pick(got, windows):
+            out[11 + j] = shared(quad[far, 2 * j], quad[far, 2 * j + 1], 64)
+
+
+def pick(got, quad):
     halo = jax.ShapeDtypeStruct((HALO, WIN, CL), F32)
     return pl.pallas_call(
         pick_kernel,
         out_shape=[halo, halo],
-        in_specs=[whole()] * 5,
+        in_specs=[whole()] * 2,
         out_specs=[whole(), whole()],
-        scratch_shapes=[pltpu.VMEM((QUAD, 4, WIN, CL), F32)],
         compiler_params=params(16),
         name="pick",
-    )(got, *windows)
+    )(got, quad)
 
 
 LANES = 8 * CL
 
 
-def chain_kernel(got, w0, w1, w2, w3, even, odd, out, src, cf, e):
+def chain_kernel(got, quad, even, odd, out, src, cf, e):
     first = lax.rem(lax.axis_index("px"), 2) == 0
 
     def below(i):
@@ -475,10 +512,8 @@
             [pairs[0], pltpu.roll(pairs[0], 64, 1), pairs[1], pltpu.roll(pairs[1], 64, 1)],
             slice(far * CL, far * CL + CL),
         )
-    mine = quad_rank()
-    for i, window in enumerate((w0, w1, w2, w3)):
-        lanes = pl.ds(pl.multiple_of((2 + (mine ^ i)) * CL, CL), CL)
-        put_coefs([window[comp] for comp in range(4)], lanes)
+    for q in range(QUAD):
+        put_coefs([quad[q, comp] for comp in range(4)], slice((2 + q) * CL, (3 + q) * CL))
     for q in range(QUAD):
         out[q] = jnp.zeros((XB, CL), F32)
     e[...] = src[0]
@@ -498,11 +533,11 @@
             e[...] = y + src[k]
 
 
-def chain(got, windows, even, odd):
+def chain(got, quad, even, odd):
     return pl.pallas_call(
         chain_kernel,
         out_shape=jax.ShapeDtypeStruct((BLOCKS, XB, CL), F32),
-        in_specs=[whole()] * 7,
+        in_specs=[whole()] * 4,
         out_specs=whole(),
         scratch_shapes=[
             pltpu.VMEM((7, WIN, LANES), F32),
@@ -511,7 +546,7 @@
         ],
         compiler_params=params(24),
         name="chain",
-    )(got, *windows, even, odd)
+    )(got, quad, even, odd)
 
 
 def result_kernel(y, gc, fin, ub, out, buf, sems):
@@ -570,20 +605,21 @@
     rnear = swap(onear, SPACE, lambda i: i ^ 1)
     rfar = swap(ofar, SPACE, off_chip)
     rfac = swap(ofac, ("tm",) + SPACE, off_chip_copy)
-    fin, edge, bound, w0, w1, w2, w3, gcp, cb, ymid = interior(state, velocity, diffusivity)
+    ct, w0, w1, w2, w3 = coefs(velocity, diffusivity)
     windows = (
         w0,
         swap(w1, SPACE, lambda i: i ^ 1),
         swap(w2, SPACE, lambda i: i ^ 2),
         swap(w3, SPACE, lambda i: i ^ 3),
     )
+    fin, edge, bound, gcp, cb, ymid = interior(state, velocity, diffusivity, ct)
     messages = (rnear, rfar, rfac, onear, ofar, ofac)
-    ub, msg, gc = finish(messages, fin, edge, bound, gcp, cb, ymid)
+    ub, msg, gc, quad = finish(messages, windows, fin, edge, bound, gcp, cb, ymid)
     got = lax.all_to_all(msg, GROUP, 0, 0)
-    even, odd = pick(got, windows)
+    even, odd = pick(got, quad)
     even = swap(even, "px", lambda i: i ^ 1)
     odd = swap(odd, "px", quad_beside)
-    back = lax.all_to_all(chain(got, windows, even, odd), GROUP, 0, 0)
+    back = lax.all_to_all(chain(got, quad, even, odd), GROUP, 0, 0)
     return result(back.reshape(CX, CL), gc, fin, ub)[None]
 
 

time: 78.7 us -> 71.5 us (0.909)
  blocking collectives: 16.4 us -> 30.7 us
  waiting for transfers between devices: 14.7 us -> 6.91 us
  local copies, waits for them, and re-layouts: 7.27 us -> 0.01 us
  starting transfers between devices: 19.8 us -> 14.6 us
  Pallas kernels: 20 us -> 18.8 us
    all_to_all x1 -> x2, blocking collectives: 16.4 us -> 30.7 us  [the longest x1 17.8 us: shards(): got = lax.all_to_all(msg, GROUP, 0, 0)]
    ppermute x8, waiting for transfers between devices: 14.7 us -> 6.91 us  [swap(): lax.ppermute(value, axes, [(i, j) for i, j in pairs if j is not None])]
    unnamed x26 -> x4, local copies, waits for them, and re-layouts: 7.27 us -> 0.01 us
    all_to_all x1 -> x0, starting transfers between devices: 6.1 us -> none  [shards(): got = lax.all_to_all(msg, GROUP, 0, 0)]
    pallas_call x1, Pallas kernels: 10.9 us -> 7.04 us  [interior(): pl.pallas_call(interior_kernel, out_shape=[jax.ShapeDtypeStruct((LZ - 2,...]
    pallas_call x0 -> x1, Pallas kernels: none -> 3.85 us  [coefs(): pl.pallas_call(coefs_kernel, out_shape=[jax.ShapeDtypeStruct((4, CROWS, C...]
    pallas_call x1, Pallas kernels: 3.79 us -> 2.76 us  [edges(): pl.pallas_call(edges_kernel, out_shape=[jax.ShapeDtypeStruct((NEAR, NX),...]
    ppermute x8, starting transfers between devices: 13.7 us -> 14.6 us  [swap(): lax.ppermute(value, axes, [(i, j) for i, j in pairs if j is not None])]
  transfers between devices with their start and end apart: 9 -> 8, of which waited for: 4 -> 3; matrix products, arithmetic and copies ran while one was open for 0% -> 0% of each run, Pallas kernels for 14% -> 15%
where the time goes in v5:
time: 71.5 us; the launch traced here: 71.2 us
  blocking collectives  30.7 us (43%)
  Pallas kernels  18.8 us (26%)
  starting transfers between devices  14.6 us (20%)
  waiting for transfers between devices  6.91 us (10%)
    all_to_all x1, blocking collectives, shards(): got = lax.all_to_all(msg, GROUP, 0, 0)  17.8 us
    ppermute x8, starting transfers between devices, swap(): lax.ppermute(value, axes, [(i, j) for i, j in pairs if j is not None])  14.6 us
    all_to_all x1, blocking collectives, shards(): back = lax.all_to_all(chain(got, quad, even, odd), GROUP, 0, 0)  13 us
    pallas_call x1, Pallas kernels, interior(): pl.pallas_call(interior_kernel, out_shape=[jax.ShapeDtypeStruct((LZ - 2,...  7.04 us
    ppermute x8, waiting for transfers between devices, swap(): lax.ppermute(value, axes, [(i, j) for i, j in pairs if j is not None])  6.91 us
    pallas_call x1, Pallas kernels, coefs(): pl.pallas_call(coefs_kernel, out_shape=[jax.ShapeDtypeStruct((4, CROWS, C...  3.85 us
    pallas_call x1, Pallas kernels, edges(): pl.pallas_call(edges_kernel, out_shape=[jax.ShapeDtypeStruct((NEAR, NX),...  2.76 us
    pallas_call x1, Pallas kernels, result(): pl.pallas_call(result_kernel, out_shape=jax.ShapeDtypeStruct((LZ, NY, NX)...  1.93 us
  transfers between devices with their start and end apart: 8, of which 3 were waited for; matrix products, arithmetic and copies ran while one was open for 0% of the time, Pallas kernels for 15%

profile of v5, /device:TPU:5, one launch (start us, length us, event | category | flops | bytes accessed | tf_op | source)
XLA Modules:
  0.0 71.2 jit_solution(182232082426617061)
XLA Ops:
  0.0 0.0 copy-start
  0.0 2.8 %edges.1 = (f32[208,1024]{1,0:T(8,128)S(1)}, f32[144,1024]{1,0:T(8,128)S(1)}, f32[64,1024]{1,0:T(8,128)S(1)}) custom-call(f32[8,64,1024]{2,1,0:T(8,128)} %bitcast.3, f32[3,8,64,1024]{3,2,1,0:T(8,128)} %vel.5, f32[8,64,1024]{2,1,0:T(8,128)} %dif.5), custom_call_target="tpu_custom_call" | custom-call | tf_op jit(solution)/shard_map/edges/pallas_call | solution.py:162
  2.8 0.8 %collective-permute-start = (f32[208,1024]{1,0:T(8,128)S(1)}, f32[208,1024]{1,0:T(8,128)S(1)}, u32[]{:S(2)}, u32[]{:S(2)}) collective-permute-start(f32[208,1024]{1,0:T(8,128)S(1)} %get-tuple-element.25.onear), channel_id=1, source_target_pairs={{0,1},{1,0},{2,3},{3,2},{4,5},{5,4},{6,7},{7,6},{8,9},{9,8},{10,11... | collective-permute-start | bytes 2555912 | tf_op jit(solution)/shard_map/ppermute | solution.py:584
  3.5 3.4 %collective-permute-start.1 = (f32[144,1024]{1,0:T(8,128)S(1)}, f32[144,1024]{1,0:T(8,128)S(1)}, u32[]{:S(2)}, u32[]{:S(2)}) collective-permute-start(f32[144,1024]{1,0:T(8,128)S(1)} %get-tuple-element.26.ofar), channel_id=1, source_target_pairs={{1,2},{2,1},{3,4},{4,3},{5,6},{6,5},{7,8},{8,7},{9,10},{10,9},{11,... | collective-permute-start | bytes 1769480 | tf_op jit(solution)/shard_map/ppermute | solution.py:584
  7.0 0.0 copy-start.1
  7.0 4.7 %collective-permute-start.2 = (f32[64,1024]{1,0:T(8,128)S(1)}, f32[64,1024]{1,0:T(8,128)S(1)}, u32[]{:S(2)}, u32[]{:S(2)}) collective-permute-start(f32[64,1024]{1,0:T(8,128)S(1)} %get-tuple-element.27.ofac), channel_id=1, source_target_pairs={{1,18},{2,17},{3,20},{4,19},{5,22},{6,21},{7,24},{8,23},{9,26},{10... | collective-permute-start | bytes 786440 | tf_op jit(solution)/shard_map/ppermute | solution.py:584
  11.7 0.0 copy-done
  11.7 3.9 %coefs.1 = (f32[4,544,128]{2,1,0:T(8,128)S(1)}, f32[4,32,128]{2,1,0:T(8,128)S(1)}, f32[4,32,128]{2,1,0:T(8,128)S(1)}, f32[4,32,128]{2,1,0:T(8,128)S(1)}, f32[4,32,128]{2,1,0:T(8,128)S(1)}) custom-call(f32[3,8,64,1024]{3,2,1,0:T(8,128)} %vel.5, f32[8,64,1024]{2,1,0:T(8,128)S(1)} %copy-done), custom_call_target="tpu_custom_call" | custom-call | flops 20000000 | bytes 9000000 | tf_op jit(solution)/shard_map/coefs/pallas_call | solution.py:220
  15.5 1.0 %collective-permute-start.3 = (f32[4,32,128]{2,1,0:T(8,128)S(1)}, f32[4,32,128]{2,1,0:T(8,128)S(1)}, u32[]{:S(2)}, u32[]{:S(2)}) collective-permute-start(f32[4,32,128]{2,1,0:T(8,128)S(1)} %get-tuple-element.29), channel_id=1, source_target_pairs={{0,1},{1,0},{2,3},{3,2},{4,5},{5,4},{6,7},{7,6},{8,9},{9,8},{10,11... | collective-permute-start | bytes 196616 | tf_op jit(solution)/shard_map/ppermute | solution.py:584
  16.5 0.8 %collective-permute-start.4 = (f32[4,32,128]{2,1,0:T(8,128)S(1)}, f32[4,32,128]{2,1,0:T(8,128)S(1)}, u32[]{:S(2)}, u32[]{:S(2)}) collective-permute-start(f32[4,32,128]{2,1,0:T(8,128)S(1)} %get-tuple-element.30), channel_id=1, source_target_pairs={{0,2},{1,3},{2,0},{3,1},{4,6},{5,7},{6,4},{7,5},{8,10},{9,11},{10,... | collective-permute-start | bytes 196616 | tf_op jit(solution)/shard_map/ppermute | solution.py:584
  17.3 0.1 collective-permute-done.3.w1
  17.4 1.1 %collective-permute-start.5 = (f32[4,32,128]{2,1,0:T(8,128)S(1)}, f32[4,32,128]{2,1,0:T(8,128)S(1)}, u32[]{:S(2)}, u32[]{:S(2)}) collective-permute-start(f32[4,32,128]{2,1,0:T(8,128)S(1)} %get-tuple-element.31), channel_id=1, source_target_pairs={{0,3},{1,2},{2,1},{3,0},{4,7},{5,6},{6,5},{7,4},{8,11},{9,10},{10,... | collective-permute-start | bytes 196616 | tf_op jit(solution)/shard_map/ppermute | solution.py:584
  18.5 0.0 copy-done.1
  18.5 7.0 %interior.1 = (f32[6,64,1024]{2,1,0:T(8,128)S(1)}, f32[4,64,1024]{2,1,0:T(8,128)S(1)}, f32[2,4,64,1024]{3,2,1,0:T(8,128)S(1)}, f32[512,128]{1,0:T(8,128)S(1)}, f...) custom-call(f32[8,64,1024]{2,1,0:T(8,128)S(1)} %bitcast.4, f32[3,8,64,1024]{3,2,1,0:T(8,128)} %vel.5, ...), custom_call_target="tpu_custom_call" | custom-call | flops 60000000 | bytes 20000000 | tf_op jit(solution)/shard_map/interior/pallas_call | solution.py:335
  25.6 0.0 collective-permute-done.4.w2
  25.6 0.0 collective-permute-done.5.w3
  25.6 0.0 collective-permute-done.2.rfac
  25.6 0.0 collective-permute-done.1.rfar
  25.6 0.0 collective-permute-done.rnear
  25.6 1.3 %finish.1 = (f32[4,64,1024]{2,1,0:T(8,128)S(1)}, f32[32,32,128]{2,1,0:T(8,128)S(1)}, f32[512,128]{1,0:T(8,128)S(1)}, f32[4,4,32,128]{3,2,1,0:T(8,128)S(1)}) custom-call(f32[208,1024]{1,0:T(8,128)S(1)} %collective-permute-done.rnear, f32[144,1024]{1,0:T(8,128)S(1)} %collective-permute-done.1.rfar, f32[64,1024]{1,0:T(8,128)S(1)} %collective-permute-done.2.rfac, ...), custom_call_target="tpu_custom_call" | custom-call | tf_op jit(solution)/shard_map/finish/pallas_call | solution.py:421
  26.9 17.8 %all_to_all.10.got = f32[32,32,128]{2,1,0:T(8,128)S(1)} all-to-all(f32[32,32,128]{2,1,0:T(8,128)S(1)} %get-tuple-element.39), channel_id=1, replica_groups=mesh['tm'=8,'px'=4,'pz'=2,'core'=2] {'tm','pz','core'}, dimensions={0} | all-to-all | bytes 1048576 | tf_op jit(solution)/shard_map/all_to_all | solution.py:618
  44.7 0.1 pick.1
  44.8 0.9 %collective-permute-start.6 = (f32[13,32,128]{2,1,0:T(8,128)S(1)}, f32[13,32,128]{2,1,0:T(8,128)S(1)}, u32[]{:S(2)}, u32[]{:S(2)}) collective-permute-start(f32[13,32,128]{2,1,0:T(8,128)S(1)} %get-tuple-element.41), channel_id=1, source_target_pairs={{0,4},{4,0},{8,12},{12,8},{1,5},{5,1},{9,13},{13,9},{2,6},{6,2},{1... | collective-permute-start | bytes 638984 | tf_op jit(solution)/shard_map/ppermute | solution.py:584
  45.8 1.9 %collective-permute-start.7 = (f32[13,32,128]{2,1,0:T(8,128)S(1)}, f32[13,32,128]{2,1,0:T(8,128)S(1)}, u32[]{:S(2)}, u32[]{:S(2)}) collective-permute-start(f32[13,32,128]{2,1,0:T(8,128)S(1)} %get-tuple-element.42), channel_id=1, source_target_pairs={{4,8},{8,4},{5,9},{9,5},{6,10},{10,6},{7,11},{11,7},{20,24},{24,20... | collective-permute-start | bytes 638984 | tf_op jit(solution)/shard_map/ppermute | solution.py:584
  47.7 4.2 %collective-permute-done.6.even = f32[13,32,128]{2,1,0:T(8,128)S(1)} collective-permute-done((f32[13,32,128]{2,1,0:T(8,128)S(1)}, f32[13,32,128]{2,1,0:T(8,128)S(1)}, u32[]{:S(2)}, u32[]{:S(2)}) %collective-permute-start.6) | collective-permute-done | bytes 213024 | tf_op jit(solution)/shard_map/ppermute | solution.py:584
  51.9 2.6 %collective-permute-done.7.odd = f32[13,32,128]{2,1,0:T(8,128)S(1)} collective-permute-done((f32[13,32,128]{2,1,0:T(8,128)S(1)}, f32[13,32,128]{2,1,0:T(8,128)S(1)}, u32[]{:S(2)}, u32[]{:S(2)}) %collective-permute-start.7) | collective-permute-done | bytes 213024 | tf_op jit(solution)/shard_map/ppermute | solution.py:584
  54.5 1.8 %chain.1 = f32[32,16,128]{2,1,0:T(8,128)S(1)} custom-call(f32[32,32,128]{2,1,0:T(8,128)S(1)} %all_to_all.10.got, f32[4,4,32,128]{3,2,1,0:T(8,128)S(1)} %get-tuple-element.40.quad, f32[13,32,128]{2,1,0:T(8,128)S(1)} %collective-permute-done.6.even, f32[13,32,128]{2,1,0:T(8,128)S(1)} %collective-permute-done.7.odd), custom_call_target="tpu_custom_call" | custom-call | tf_op jit(solution)/shard_map/chain/pallas_call | solution.py:537
  56.3 13.0 %all_to_all.11 = f32[32,16,128]{2,1,0:T(8,128)S(1)} all-to-all(f32[32,16,128]{2,1,0:T(8,128)S(1)} %chain.1), channel_id=1, replica_groups=mesh['tm'=8,'px'=4,'pz'=2,'core'=2] {'tm','pz','core'}, dimensions={0} | all-to-all | bytes 524288 | tf_op jit(solution)/shard_map/all_to_all | solution.py:622
  69.3 1.9 %result.1 = f32[8,64,1024]{2,1,0:T(8,128)} custom-call(f32[512,128]{1,0:T(8,128)S(1)} %bitcast.5, f32[512,128]{1,0:T(8,128)S(1)} %get-tuple-element.43.gc, f32[6,64,1024]{2,1,0:T(8,128)S(1)} %get-tuple-element.33.fin, f32[4,64,1024]{2,1,0:T(8,128)S(1)} %get-tuple-element.44.ub), custom_call_target="tpu_custom_call" | custom-call | tf_op jit(solution)/shard_map/result/pallas_call | solution.py:571
Async XLA Ops:
  0.0 11.7 %copy-start = (f32[8,64,1024]{2,1,0:T(8,128)S(1)}, f32[8,64,1024]{2,1,0:T(8,128)}, u32[]{:S(2)}) copy-start(f32[8,64,1024]{2,1,0:T(8,128)} %dif.5) | copy-start | bytes 6291460
  2.8 22.9 %collective-permute-start = (f32[208,1024]{1,0:T(8,128)S(1)}, f32[208,1024]{1,0:T(8,128)S(1)}, u32[]{:S(2)}, u32[]{:S(2)}) collective-permute-start(f32[208,1024]{1,0:T(8,128)S(1)} %get-tuple-element.25.onear), channel_id=1, source_target_pairs={{0,1},{1,0},{2,3},{3,2},{4,5},{5,4},{6,7},{7,6},{8,9},{9,8},{10,11... | collective-permute-start | bytes 2555912 | tf_op jit(solution)/shard_map/ppermute | solution.py:584
  3.5 22.1 %collective-permute-start.1 = (f32[144,1024]{1,0:T(8,128)S(1)}, f32[144,1024]{1,0:T(8,128)S(1)}, u32[]{:S(2)}, u32[]{:S(2)}) collective-permute-start(f32[144,1024]{1,0:T(8,128)S(1)} %get-tuple-element.26.ofar), channel_id=1, source_target_pairs={{1,2},{2,1},{3,4},{4,3},{5,6},{6,5},{7,8},{8,7},{9,10},{10,9},{11,... | collective-permute-start | bytes 1769480 | tf_op jit(solution)/shard_map/ppermute | solution.py:584
  7.0 11.6 %copy-start.1 = (f32[1,8,64,1024]{3,2,1,0:T(8,128)S(1)}, f32[1,8,64,1024]{3,2,1,0:T(8,128)}, u32[]{:S(2)}) copy-start(f32[1,8,64,1024]{3,2,1,0:T(8,128)} %param.3) | copy-start | bytes 6291460
  7.0 18.6 %collective-permute-start.2 = (f32[64,1024]{1,0:T(8,128)S(1)}, f32[64,1024]{1,0:T(8,128)S(1)}, u32[]{:S(2)}, u32[]{:S(2)}) collective-permute-start(f32[64,1024]{1,0:T(8,128)S(1)} %get-tuple-element.27.ofac), channel_id=1, source_target_pairs={{1,18},{2,17},{3,20},{4,19},{5,22},{6,21},{7,24},{8,23},{9,26},{10... | collective-permute-start | bytes 786440 | tf_op jit(solution)/shard_map/ppermute | solution.py:584
  15.5 1.9 %collective-permute-start.3 = (f32[4,32,128]{2,1,0:T(8,128)S(1)}, f32[4,32,128]{2,1,0:T(8,128)S(1)}, u32[]{:S(2)}, u32[]{:S(2)}) collective-permute-start(f32[4,32,128]{2,1,0:T(8,128)S(1)} %get-tuple-element.29), channel_id=1, source_target_pairs={{0,1},{1,0},{2,3},{3,2},{4,5},{5,4},{6,7},{7,6},{8,9},{9,8},{10,11... | collective-permute-start | bytes 196616 | tf_op jit(solution)/shard_map/ppermute | solution.py:584
  16.5 9.1 %collective-permute-start.4 = (f32[4,32,128]{2,1,0:T(8,128)S(1)}, f32[4,32,128]{2,1,0:T(8,128)S(1)}, u32[]{:S(2)}, u32[]{:S(2)}) collective-permute-start(f32[4,32,128]{2,1,0:T(8,128)S(1)} %get-tuple-element.30), channel_id=1, source_target_pairs={{0,2},{1,3},{2,0},{3,1},{4,6},{5,7},{6,4},{7,5},{8,10},{9,11},{10,... | collective-permute-start | bytes 196616 | tf_op jit(solution)/shard_map/ppermute | solution.py:584
  17.4 8.2 %collective-permute-start.5 = (f32[4,32,128]{2,1,0:T(8,128)S(1)}, f32[4,32,128]{2,1,0:T(8,128)S(1)}, u32[]{:S(2)}, u32[]{:S(2)}) collective-permute-start(f32[4,32,128]{2,1,0:T(8,128)S(1)} %get-tuple-element.31), channel_id=1, source_target_pairs={{0,3},{1,2},{2,1},{3,0},{4,7},{5,6},{6,5},{7,4},{8,11},{9,10},{10,... | collective-permute-start | bytes 196616 | tf_op jit(solution)/shard_map/ppermute | solution.py:584
  44.8 7.1 %collective-permute-start.6 = (f32[13,32,128]{2,1,0:T(8,128)S(1)}, f32[13,32,128]{2,1,0:T(8,128)S(1)}, u32[]{:S(2)}, u32[]{:S(2)}) collective-permute-start(f32[13,32,128]{2,1,0:T(8,128)S(1)} %get-tuple-element.41), channel_id=1, source_target_pairs={{0,4},{4,0},{8,12},{12,8},{1,5},{5,1},{9,13},{13,9},{2,6},{6,2},{1... | collective-permute-start | bytes 638984 | tf_op jit(solution)/shard_map/ppermute | solution.py:584
  45.8 8.7 %collective-permute-start.7 = (f32[13,32,128]{2,1,0:T(8,128)S(1)}, f32[13,32,128]{2,1,0:T(8,128)S(1)}, u32[]{:S(2)}, u32[]{:S(2)}) collective-permute-start(f32[13,32,128]{2,1,0:T(8,128)S(1)} %get-tuple-element.42), channel_id=1, source_target_pairs={{4,8},{8,4},{5,9},{9,5},{6,10},{10,6},{7,11},{11,7},{20,24},{24,20... | collective-permute-start | bytes 638984 | tf_op jit(solution)/shard_map/ppermute | solution.py:584

commit v6 on v5

--- a/solution.py
+++ b/solution.py
@@ -16,8 +16,6 @@
 BLOCKS = GROUPS * QUAD
 XB = CX // BLOCKS
 WIN = XB + 16
-TOP = 8
-PADDED = NY + 16
 SPACE = ("px", "pz", "core")
 GROUP = ("tm", "pz", "core")
 
@@ -65,16 +63,17 @@
     return (c + k * lap) + ((dx + dy) + dz)
 
 
-def wrap_rows(ref, z):
-    ref[z, TOP - 1 : TOP, :] = ref[z, TOP + NY - 1 : TOP + NY, :]
-    ref[z, TOP + NY : TOP + NY + 1, :] = ref[z, TOP : TOP + 1, :]
-
-
-def plane(ref, z, r):
-    c = ref[z, TOP + r : TOP + r + 8, :]
-    s = ref[z, TOP + r - 1 : TOP + r + 7, :]
-    n = ref[z, TOP + r + 1 : TOP + r + 9, :]
-    return c, pltpu.roll(c, 1, 1), pltpu.roll(c, NX - 1, 1), s, n
+def planes(ref, z):
+    row = lax.broadcasted_iota(jnp.int32, (8, NX), 0)
+    c = ref[z, 0:8, :]
+    before = pltpu.roll(ref[z, NY - 8 : NY, :], 1, 0)
+    for r in range(0, NY, 8):
+        after = ref[z, (r + 8) % NY : (r + 8) % NY + 8, :]
+        down = pltpu.roll(c, 1, 0)
+        s = jnp.where(row == 0, before, down)
+        n = jnp.where(row == 7, pltpu.roll(after, 7, 0), pltpu.roll(c, 7, 0))
+        yield r, slice(r, r + 8), (c, pltpu.roll(c, 1, 1), pltpu.roll(c, NX - 1, 1), s, n)
+        c, before = after, down
 
 
 def coarse_coefs(vx, vy, vz, k):
@@ -101,32 +100,42 @@
     return lax.axis_index("core") == kind
 
 
-def edges_kernel(st, vel, dif, near, far, factor, pad, inner, v, d, zs, sems):
-    copies = []
+def edges_kernel(st, vel, dif, near, far, factor, u, vx, vy, vz, d, zs, sems):
     tops = [edge_is_top(kind) for kind in range(2)]
-    for kind, top in enumerate(tops):
-        z, beside = jnp.where(top, LZ - 1, 0), jnp.where(top, LZ - 2, 1)
+
+    def layer(z, which=(0, 1, 2, 3, 4)):
         pairs = (
-            (st.at[z], pad.at[kind, TOP : TOP + NY, :]),
-            (vel.at[:, z], v.at[kind]),
-            (dif.at[z], d.at[kind]),
-            (st.at[beside], inner.at[kind]),
+            (st.at[z], u.at[z]),
+            (vel.at[0, z], vx.at[z]),
+            (vel.at[1, z], vy.at[z]),
+            (vel.at[2, z], vz.at[z]),
+            (dif.at[z], d.at[z]),
         )
-        copies.append([pltpu.make_async_copy(a, b, sems.at[kind, i]) for i, (a, b) in enumerate(pairs)])
-    for group in copies:
-        for copy in group:
+        return [pltpu.make_async_copy(*pairs[i], sems.at[z, i]) for i in which]
+
+    order = []
+    for top in tops:
+        order += [jnp.where(top, LZ - 1, 0), jnp.where(top, LZ - 2, 1)]
+    middle = list(range(2, LZ - 2))
+    early, late = (0,), (1, 2, 3, 4)
+    for kind in range(2):
+        for copy in layer(order[2 * kind]) + layer(order[2 * kind + 1], early):
+            copy.start()
+    for z in (1, LZ - 2):
+        for copy in layer(z, late):
+            copy.start()
+    for z in middle:
+        for copy in layer(z):
             copy.start()
     for kind, top in enumerate(tops):
         out = (near, far)[kind]
-        for copy in copies[kind]:
+        z, beside = order[2 * kind], order[2 * kind + 1]
+        for copy in layer(z) + layer(beside, early):
             copy.wait()
-        wrap_rows(pad, kind)
-        for r in range(0, NY, 8):
-            rows = slice(r, r + 8)
-            c, w, e, s, n = plane(pad, kind, r)
-            inside = inner[kind, rows, :]
-            ax, ay, k = v[kind, 0, rows, :], v[kind, 1, rows, :], d[kind, rows, :]
-            up = jnp.where(top, v[kind, 2, rows, :], -v[kind, 2, rows, :])
+        for r, rows, (c, w, e, s, n) in planes(u, z):
+            inside = u[beside, rows, :]
+            ax, ay, k = vx[z, rows, :], vy[z, rows, :], d[z, rows, :]
+            up = jnp.where(top, vz[z, rows, :], -vz[z, rows, :])
             out[r : r + 8, :] = c
             out[NY + r : NY + r + 8, :] = advanced(c, w, e, s, n, inside, jnp.zeros_like(c), ax, ay, up, k)
             b = k - jnp.minimum(up, 0.0)
@@ -148,6 +157,12 @@
     for i in range(8):
         near[2 * NY : FAR, 128 * i : 128 * i + 128] = cnear[16 * i : 16 * i + 16, :]
         far[2 * NY : FAR, 128 * i : 128 * i + 128] = cfar[16 * i : 16 * i + 16, :]
+    for z in (1, LZ - 2):
+        for copy in layer(z, late):
+            copy.wait()
+    for z in middle:
+        for copy in layer(z):
+            copy.wait()
 
 
 def whole():
@@ -159,24 +174,22 @@
 
 
 def edges(state, velocity, diffusivity):
+    slab = jax.ShapeDtypeStruct((LZ, NY, NX), F32)
     return pl.pallas_call(
         edges_kernel,
         out_shape=[
             jax.ShapeDtypeStruct((NEAR, NX), F32),
             jax.ShapeDtypeStruct((FAR, NX), F32),
             jax.ShapeDtypeStruct((NY, NX), F32),
+        ]
+        + [slab] * 5,
+        in_specs=[remains()] * 3,
+        out_specs=[whole()] * 8,
+        scratch_shapes=[
+            pltpu.VMEM((8, 2 * NY, 128), F32),
+            pltpu.SemaphoreType.DMA((LZ, 5)),
         ],
-        in_specs=[remains()] * 3,
-        out_specs=[whole()] * 3,
-        scratch_shapes=[
-            pltpu.VMEM((2, PADDED, NX), F32),
-            pltpu.VMEM((2, NY, NX), F32),
-            pltpu.VMEM((2, 3, NY, NX), F32),
-            pltpu.VMEM((2, NY, NX), F32),
-            pltpu.VMEM((8, 2 * NY, 128), F32),
-            pltpu.SemaphoreType.DMA((2, 4)),
-        ],
-        compiler_params=params(52),
+        compiler_params=params(42),
         name="edges",
     )(state, velocity, diffusivity)
 
@@ -185,22 +198,13 @@
     return lax.axis_index("pz") * 2 + lax.axis_index("core")
 
 
-def coefs_kernel(vel, dif, ct, w0, w1, w2, w3, v, zs, sems):
-    def part(comp, zc):
-        layers = slice(2 * zc, 2 * zc + 2)
-        source = dif.at[layers] if comp == 3 else vel.at[comp, layers]
-        return pltpu.make_async_copy(source, v.at[comp, layers], sems.at[comp, zc])
-
-    for comp in range(4):
+def coefs_kernel(vx, vy, vz, d, ct, w0, w1, w2, w3, zs):
+    for comp, ref in enumerate((vx, vy, vz, d)):
         for zc in range(4):
-            part(comp, zc).start()
-    for comp in range(4):
-        for zc in range(4):
-            part(comp, zc).wait()
             for r in range(0, NY, 8):
                 rows = slice(r, r + 8)
                 put_columns(
-                    zs.at[comp], slice(zc * NY + r, zc * NY + r + 8), v[comp, 2 * zc, rows, :] + v[comp, 2 * zc + 1, rows, :]
+                    zs.at[comp], slice(zc * NY + r, zc * NY + r + 8), ref[2 * zc, rows, :] + ref[2 * zc + 1, rows, :]
                 )
         for b in range(4):
             ct[comp, 8 + 128 * b : 136 + 128 * b, :] = halved_x(
@@ -215,89 +219,46 @@
             out[comp] = ct[comp, pl.ds(pl.multiple_of(block * XB, XB), WIN), :]
 
 
-def coefs(velocity, diffusivity):
+def coefs(fields):
     window = jax.ShapeDtypeStruct((4, WIN, CL), F32)
     return pl.pallas_call(
         coefs_kernel,
         out_shape=[jax.ShapeDtypeStruct((4, CROWS, CL), F32), window, window, window, window],
-        in_specs=[remains()] * 2,
+        in_specs=[whole()] * 4,
         out_specs=[whole()] * 5,
-        scratch_shapes=[
-            pltpu.VMEM((4, LZ, NY, NX), F32),
-            pltpu.VMEM((4, 8, 4 * NY, 128), F32),
-            pltpu.SemaphoreType.DMA((4, 4)),
-        ],
-        compiler_params=params(50),
+        scratch_shapes=[pltpu.VMEM((4, 8, 4 * NY, 128), F32)],
+        compiler_params=params(12),
         cost_estimate=pl.CostEstimate(flops=20_000_000, bytes_accessed=9_000_000, transcendentals=0),
         name="coefs",
-    )(velocity, diffusivity)
-
-
-def interior_kernel(st, vel, dif, ct, fin, edge, bound, gcp, cb, ymid, u, u1, v, d, zs, zf, ct0, usem, sems):
-    def layer(z):
-        return (
-            pltpu.make_async_copy(vel.at[:, z], v.at[:, z], sems.at[z, 0]),
-            pltpu.make_async_copy(dif.at[z], d.at[z], sems.at[z, 1]),
-        )
-
-    def state(z):
-        return pltpu.make_async_copy(st.at[z], u.at[z, TOP : TOP + NY, :], usem.at[z])
-
-    for z in range(3):
-        state(z).start()
-    for part in layer(1):
-        part.start()
-    for z in range(3, LZ):
-        state(z).start()
-        for part in layer(z - 1):
-            part.start()
-    bounds = []
-    for side, z in enumerate((0, LZ - 1)):
-        bounds.append(pltpu.make_async_copy(vel.at[:, z], bound.at[side, 0:3], sems.at[z, 0]))
-        bounds.append(pltpu.make_async_copy(dif.at[z], bound.at[side, 3], sems.at[z, 1]))
-    for copy in bounds:
-        copy.start()
-    for z in range(2):
-        state(z).wait()
-        wrap_rows(u, z)
+    )(*fields)
+
+
+def interior_kernel(u, vx, vy, vz, d, ct, fin, edge, gcp, cb, ymid, u1, zs, zf, ct0):
     def first(z, _):
-        state(z + 1).wait()
-        wrap_rows(u, z + 1)
-        for part in layer(z):
-            part.wait()
-        for r in range(0, NY, 8):
-            rows = slice(r, r + 8)
-            here = slice(TOP + r, TOP + r + 8)
-            c, w, e, s, n = plane(u, z, r)
-            u1[z, here, :] = advanced(
-                c, w, e, s, n, u[z - 1, here, :], u[z + 1, here, :],
-                v[0, z, rows, :], v[1, z, rows, :], v[2, z, rows, :], d[z, rows, :],
-            )
-        wrap_rows(u1, z)
-        return 0
-
-    lax.fori_loop(1, LZ - 1, first, 0)
-    u1[0, TOP : TOP + NY, :] = jnp.zeros((NY, NX), F32)
-    u1[LZ - 1, TOP : TOP + NY, :] = jnp.zeros((NY, NX), F32)
-    edge[0] = u1[1, TOP : TOP + NY, :]
-    edge[1] = u1[LZ - 2, TOP : TOP + NY, :]
-
-    def second(z, _):
-        for r in range(0, NY, 8):
-            rows = slice(r, r + 8)
-            here = slice(TOP + r, TOP + r + 8)
-            c, w, e, s, n = plane(u1, z, r)
-            fin[z - 1, rows, :] = advanced(
-                c, w, e, s, n, u1[z - 1, here, :], u1[z + 1, here, :],
-                v[0, z, rows, :], v[1, z, rows, :], v[2, z, rows, :], d[z, rows, :],
+        for _, rows, (c, w, e, s, n) in planes(u, z):
+            u1[z, rows, :] = advanced(
+                c, w, e, s, n, u[z - 1, rows, :], u[z + 1, rows, :],
+                vx[z, rows, :], vy[z, rows, :], vz[z, rows, :], d[z, rows, :],
             )
         return 0
 
+    lax.fori_loop(1, LZ - 1, first, 0)
+    u1[0] = jnp.zeros((NY, NX), F32)
+    u1[LZ - 1] = jnp.zeros((NY, NX), F32)
+    edge[0] = u1[1]
+    edge[1] = u1[LZ - 2]
+
+    def second(z, _):
+        for _, rows, (c, w, e, s, n) in planes(u1, z):
+            fin[z - 1, rows, :] = advanced(
+                c, w, e, s, n, u1[z - 1, rows, :], u1[z + 1, rows, :],
+                vx[z, rows, :], vy[z, rows, :], vz[z, rows, :], d[z, rows, :],
+            )
+        return 0
+
     lax.fori_loop(1, LZ - 1, second, 0)
-    for copy in bounds:
-        copy.wait()
-    edge[2] = d[1] + jnp.maximum(v[2, 1], 0.0)
-    edge[3] = d[LZ - 2] - jnp.minimum(v[2, LZ - 2], 0.0)
+    edge[2] = d[1] + jnp.maximum(vz[1], 0.0)
+    edge[3] = d[LZ - 2] - jnp.minimum(vz[LZ - 2], 0.0)
     for zc in (1, 2):
         for r in range(0, NY, 8):
             rows = slice(r, r + 8)
@@ -307,8 +268,8 @@
 
     for zc in range(4):
         for r in range(0, NY, 8):
-            here = slice(TOP + r, TOP + r + 8)
-            put_columns(zs, slice(zc * NY + r, zc * NY + r + 8), u[2 * zc, here, :] + u[2 * zc + 1, here, :])
+            rows = slice(r, r + 8)
+            put_columns(zs, slice(zc * NY + r, zc * NY + r + 8), u[2 * zc, rows, :] + u[2 * zc + 1, rows, :])
     for b in range(4):
         ct0[8 + 128 * b : 136 + 128 * b, :] = halved_x(
             jnp.concatenate([paired(zs, 2 * b + i, 0, 128) for i in range(2)], axis=1)
@@ -330,39 +291,33 @@
         cb[r : r + 64, :] = jnp.where(lane < 32, zl, jnp.where(lane >= 96, zh, 0.0))
 
 
-def interior(state, velocity, diffusivity, ct):
+def interior(state, fields, ct):
     small = jax.ShapeDtypeStruct((CX, CL), F32)
     return pl.pallas_call(
         interior_kernel,
         out_shape=[
             jax.ShapeDtypeStruct((LZ - 2, NY, NX), F32),
             jax.ShapeDtypeStruct((4, NY, NX), F32),
-            jax.ShapeDtypeStruct((2, 4, NY, NX), F32),
             small,
             small,
             jax.ShapeDtypeStruct((8, 64, 128), F32),
         ],
-        in_specs=[remains()] * 3 + [whole()],
-        out_specs=[whole()] * 6,
+        in_specs=[whole()] * 6,
+        out_specs=[whole()] * 5,
         scratch_shapes=[
-            pltpu.VMEM((LZ, PADDED, NX), F32),
-            pltpu.VMEM((LZ, PADDED, NX), F32),
-            pltpu.VMEM((3, LZ, NY, NX), F32),
             pltpu.VMEM((LZ, NY, NX), F32),
             pltpu.VMEM((8, 4 * NY, 128), F32),
             pltpu.VMEM((8, 2 * NY, 128), F32),
             pltpu.VMEM((CX + 16, CL), F32),
-            pltpu.SemaphoreType.DMA((LZ,)),
-            pltpu.SemaphoreType.DMA((LZ, 2)),
         ],
-        compiler_params=params(44),
+        compiler_params=params(16),
         cost_estimate=pl.CostEstimate(flops=60_000_000, bytes_accessed=20_000_000, transcendentals=0),
         name="interior",
-    )(state, velocity, diffusivity, ct)
+    )(state, *fields, ct)
 
 
 def finish_kernel(
-    rnear, rfar, rfac, onear, ofar, ofac, w0, w1, w2, w3, fin, edge, bound, gcp, cb, ymid, ub, msg, gc, quad, pad, zs, jp
+    rnear, rfar, rfac, onear, ofar, ofac, w0, w1, w2, w3, fin, edge, vx, vy, vz, d, gcp, cb, ymid, ub, msg, gc, quad, u1, zs, jp
 ):
     mine = quad_rank()
     for i, window in enumerate((w0, w1, w2, w3)):
@@ -373,16 +328,14 @@
         top = edge_is_top(kind)
         side = jnp.where(top, 1, 0)
         for r in range(0, NY, 8):
-            pad[kind, TOP + r : TOP + r + 8, :] = (
+            u1[kind, r : r + 8, :] = (
                 own[NY + r : NY + r + 8, :] + ownb[at + r : at + r + 8, :] * rec[r : r + 8, :]
             )
-        wrap_rows(pad, kind)
-        for r in range(0, NY, 8):
-            rows = slice(r, r + 8)
-            c, w, e, s, n = plane(pad, kind, r)
+        z = side * (LZ - 1)
+        for r, rows, (c, w, e, s, n) in planes(u1, kind):
             outside = rec[NY + r : NY + r + 8, :] + recb[at + r : at + r + 8, :] * own[r : r + 8, :]
             inside = edge[side, rows, :]
-            ax, ay, az, k = (bound[side, i, rows, :] for i in range(4))
+            ax, ay, az, k = vx[z, rows, :], vy[z, rows, :], vz[z, rows, :], d[z, rows, :]
             last = advanced(c, w, e, s, n, inside, outside, ax, ay, jnp.where(top, az, -az), k)
             near = fin[5 * side, rows, :] + edge[2 + side, rows, :] * c
             ub[3 * side, rows, :] = last
@@ -417,7 +370,7 @@
         msg[i] = jp[XB * i : XB * i + WIN, :]
 
 
-def finish(messages, windows, fin, edge, bound, gcp, cb, ymid):
+def finish(messages, windows, fin, edge, fields, gcp, cb, ymid):
     return pl.pallas_call(
         finish_kernel,
         out_shape=[
@@ -426,16 +379,16 @@
             jax.ShapeDtypeStruct((CX, CL), F32),
             jax.ShapeDtypeStruct((QUAD, 4, WIN, CL), F32),
         ],
-        in_specs=[whole()] * 16,
+        in_specs=[whole()] * 19,
         out_specs=[whole()] * 4,
         scratch_shapes=[
-            pltpu.VMEM((2, PADDED, NX), F32),
+            pltpu.VMEM((2, NY, NX), F32),
             pltpu.VMEM((2, 8, NY, 128), F32),
             pltpu.VMEM((CX + 24, CL), F32),
         ],
-        compiler_params=params(24),
+        compiler_params=params(16),
         name="finish",
-    )(*messages, *windows, fin, edge, bound, gcp, cb, ymid)
+    )(*messages, *windows, fin, edge, *fields, gcp, cb, ymid)
 
 
 HALO = 13
@@ -601,20 +554,20 @@
 
 def shards(state_old, velocity, diffusivity):
     state = state_old[0]
-    onear, ofar, ofac = edges(state, velocity, diffusivity)
+    onear, ofar, ofac, u, *fields = edges(state, velocity, diffusivity)
     rnear = swap(onear, SPACE, lambda i: i ^ 1)
     rfar = swap(ofar, SPACE, off_chip)
     rfac = swap(ofac, ("tm",) + SPACE, off_chip_copy)
-    ct, w0, w1, w2, w3 = coefs(velocity, diffusivity)
+    ct, w0, w1, w2, w3 = coefs(fields)
     windows = (
         w0,
         swap(w1, SPACE, lambda i: i ^ 1),
         swap(w2, SPACE, lambda i: i ^ 2),
         swap(w3, SPACE, lambda i: i ^ 3),
     )
-    fin, edge, bound, gcp, cb, ymid = interior(state, velocity, diffusivity, ct)
+    fin, edge, gcp, cb, ymid = interior(u, fields, ct)
     messages = (rnear, rfar, rfac, onear, ofar, ofac)
-    ub, msg, gc, quad = finish(messages, windows, fin, edge, bound, gcp, cb, ymid)
+    ub, msg, gc, quad = finish(messages, windows, fin, edge, fields, gcp, cb, ymid)
     got = lax.all_to_all(msg, GROUP, 0, 0)
     even, odd = pick(got, quad)
     even = swap(even, "px", lambda i: i ^ 1)

time: 71.5 us -> 72.9 us (1.020)
  Pallas kernels: 18.8 us -> 15.3 us
  waiting for transfers between devices: 6.91 us -> 10.3 us
  blocking collectives: 30.7 us -> 32.5 us
    ppermute x8, waiting for transfers between devices: 6.91 us -> 10.3 us  [swap(): lax.ppermute(value, axes, [(i, j) for i, j in pairs if j is not None])]
    pallas_call x1, Pallas kernels: 3.85 us -> 1.19 us  [coefs(): pl.pallas_call(coefs_kernel, out_shape=[jax.ShapeDtypeStruct((4, CROWS, C...]
    pallas_call x1, Pallas kernels: 7.04 us -> 4.76 us  [interior(): pl.pallas_call(interior_kernel, out_shape=[jax.ShapeDtypeStruct((LZ - 2,...]
    all_to_all x1, blocking collectives: 17.8 us -> 19.5 us  [shards(): got = lax.all_to_all(msg, GROUP, 0, 0)]
    pallas_call x1, Pallas kernels: 2.76 us -> 4.3 us  [edges(): pl.pallas_call(edges_kernel, out_shape=[jax.ShapeDtypeStruct((NEAR, NX),...]
  transfers between devices with their start and end apart: 8 -> 8, of which waited for: 3 -> 5; matrix products, arithmetic and copies ran while one was open for 0% -> 0% of each run, Pallas kernels for 15% -> 8%
where the time goes in v6:
time: 72.9 us; the launch traced here: 72.7 us
  blocking collectives  32.5 us (45%)
  Pallas kernels  15.3 us (21%)
  starting transfers between devices  14.5 us (20%)
  waiting for transfers between devices  10.3 us (14%)
    all_to_all x1, blocking collectives, shards(): got = lax.all_to_all(msg, GROUP, 0, 0)  19.5 us
    ppermute x8, starting transfers between devices, swap(): lax.ppermute(value, axes, [(i, j) for i, j in pairs if j is not None])  14.5 us
    all_to_all x1, blocking collectives, shards(): back = lax.all_to_all(chain(got, quad, even, odd), GROUP, 0, 0)  13 us
    ppermute x8, waiting for transfers between devices, swap(): lax.ppermute(value, axes, [(i, j) for i, j in pairs if j is not None])  10.3 us
    pallas_call x1, Pallas kernels, interior(): pl.pallas_call(interior_kernel, out_shape=[jax.ShapeDtypeStruct((LZ - 2,...  4.76 us
    pallas_call x1, Pallas kernels, edges(): pl.pallas_call(edges_kernel, out_shape=[jax.ShapeDtypeStruct((NEAR, NX),...  4.3 us
    pallas_call x1, Pallas kernels, result(): pl.pallas_call(result_kernel, out_shape=jax.ShapeDtypeStruct((LZ, NY, NX)...  1.93 us
    pallas_call x1, Pallas kernels, chain(): pl.pallas_call(chain_kernel, out_shape=jax.ShapeDtypeStruct((BLOCKS, XB,...  1.83 us
  transfers between devices with their start and end apart: 8, of which 5 were waited for; matrix products, arithmetic and copies ran while one was open for 0% of the time, Pallas kernels for 8%

profile of v6, /device:TPU:5, one launch (start us, length us, event | category | flops | bytes accessed | tf_op | source)
XLA Modules:
  0.0 72.7 jit_solution(5115312190619551008)
XLA Ops:
  0.0 4.3 %edges.1 = (f32[208,1024]{1,0:T(8,128)S(1)}, f32[144,1024]{1,0:T(8,128)S(1)}, f32[64,1024]{1,0:T(8,128)S(1)}, f32[8,64,1024]{2,1,0:T(8,128)S(1)}, f32[8,64,1024]...) custom-call(f32[8,64,1024]{2,1,0:T(8,128)} %bitcast.4, ...), custom_call_target="tpu_custom_call" | custom-call | tf_op jit(solution)/shard_map/edges/pallas_call | solution.py:178
  4.3 0.8 %collective-permute-start = (f32[208,1024]{1,0:T(8,128)S(1)}, f32[208,1024]{1,0:T(8,128)S(1)}, u32[]{:S(2)}, u32[]{:S(2)}) collective-permute-start(f32[208,1024]{1,0:T(8,128)S(1)} %get-tuple-element.29.onear), channel_id=1, source_target_pairs={{0,1},{1,0},{2,3},{3,2},{4,5},{5,4},{6,7},{7,6},{8,9},{9,8},{10,11... | collective-permute-start | bytes 2555912 | tf_op jit(solution)/shard_map/ppermute | solution.py:537
  5.1 3.4 %collective-permute-start.1 = (f32[144,1024]{1,0:T(8,128)S(1)}, f32[144,1024]{1,0:T(8,128)S(1)}, u32[]{:S(2)}, u32[]{:S(2)}) collective-permute-start(f32[144,1024]{1,0:T(8,128)S(1)} %get-tuple-element.30.ofar), channel_id=1, source_target_pairs={{1,2},{2,1},{3,4},{4,3},{5,6},{6,5},{7,8},{8,7},{9,10},{10,9},{11,... | collective-permute-start | bytes 1769480 | tf_op jit(solution)/shard_map/ppermute | solution.py:537
  8.5 4.5 %collective-permute-start.2 = (f32[64,1024]{1,0:T(8,128)S(1)}, f32[64,1024]{1,0:T(8,128)S(1)}, u32[]{:S(2)}, u32[]{:S(2)}) collective-permute-start(f32[64,1024]{1,0:T(8,128)S(1)} %get-tuple-element.31.ofac), channel_id=1, source_target_pairs={{1,18},{2,17},{3,20},{4,19},{5,22},{6,21},{7,24},{8,23},{9,26},{10... | collective-permute-start | bytes 786440 | tf_op jit(solution)/shard_map/ppermute | solution.py:537
  13.0 1.2 %coefs.1 = (f32[4,544,128]{2,1,0:T(8,128)S(1)}, f32[4,32,128]{2,1,0:T(8,128)S(1)}, f32[4,32,128]{2,1,0:T(8,128)S(1)}, f32[4,32,128]{2,1,0:T(8,128)S(1)}, f32[4,32,128]{2,1,0:T(8,128)S(1)}) custom-call(f32[8,64,1024]{2,1,0:T(8,128)S(1)} %get-tuple-element.32.vx, f32[8,64,1024]{2,1,0:T(8,128)S(1)} %get-tuple-element.33.vy, ...), custom_call_target="tpu_custom_call" | custom-call | flops 20000000 | bytes 9000000 | tf_op jit(solution)/shard_map/coefs/pallas_call | solution.py:224
  14.2 1.0 %collective-permute-start.3 = (f32[4,32,128]{2,1,0:T(8,128)S(1)}, f32[4,32,128]{2,1,0:T(8,128)S(1)}, u32[]{:S(2)}, u32[]{:S(2)}) collective-permute-start(f32[4,32,128]{2,1,0:T(8,128)S(1)} %get-tuple-element.37), channel_id=1, source_target_pairs={{0,1},{1,0},{2,3},{3,2},{4,5},{5,4},{6,7},{7,6},{8,9},{9,8},{10,11... | collective-permute-start | bytes 196616 | tf_op jit(solution)/shard_map/ppermute | solution.py:537
  15.3 0.8 %collective-permute-start.4 = (f32[4,32,128]{2,1,0:T(8,128)S(1)}, f32[4,32,128]{2,1,0:T(8,128)S(1)}, u32[]{:S(2)}, u32[]{:S(2)}) collective-permute-start(f32[4,32,128]{2,1,0:T(8,128)S(1)} %get-tuple-element.38), channel_id=1, source_target_pairs={{0,2},{1,3},{2,0},{3,1},{4,6},{5,7},{6,4},{7,5},{8,10},{9,11},{10,... | collective-permute-start | bytes 196616 | tf_op jit(solution)/shard_map/ppermute | solution.py:537
  16.1 0.1 collective-permute-done.3.w1
  16.2 1.1 %collective-permute-start.5 = (f32[4,32,128]{2,1,0:T(8,128)S(1)}, f32[4,32,128]{2,1,0:T(8,128)S(1)}, u32[]{:S(2)}, u32[]{:S(2)}) collective-permute-start(f32[4,32,128]{2,1,0:T(8,128)S(1)} %get-tuple-element.39), channel_id=1, source_target_pairs={{0,3},{1,2},{2,1},{3,0},{4,7},{5,6},{6,5},{7,4},{8,11},{9,10},{10,... | collective-permute-start | bytes 196616 | tf_op jit(solution)/shard_map/ppermute | solution.py:537
  17.3 4.8 %interior.1 = (f32[6,64,1024]{2,1,0:T(8,128)S(1)}, f32[4,64,1024]{2,1,0:T(8,128)S(1)}, f32[512,128]{1,0:T(8,128)S(1)}, f32[512,128]{1,0:T(8,128)S(1)}, f32[8,64,128]{2,1,0:T(8,128)S(1)}) custom-call(f32[8,64,1024]{2,1,0:T(8,128)S(1)} %get-tuple-element.40.u, f32[8,64,1024]{2,1,0:T(8,128)S(1)} %get-tuple-element.32.vx, ...), custom_call_target="tpu_custom_call" | custom-call | flops 60000000 | bytes 20000000 | tf_op jit(solution)/shard_map/interior/pallas_call | solution.py:296
  22.0 1.7 %collective-permute-done.4.w2 = f32[4,32,128]{2,1,0:T(8,128)S(1)} collective-permute-done((f32[4,32,128]{2,1,0:T(8,128)S(1)}, f32[4,32,128]{2,1,0:T(8,128)S(1)}, u32[]{:S(2)}, u32[]{:S(2)}) %collective-permute-start.4) | collective-permute-done | bytes 65568 | tf_op jit(solution)/shard_map/ppermute | solution.py:537
  23.8 1.6 %collective-permute-done.5.w3 = f32[4,32,128]{2,1,0:T(8,128)S(1)} collective-permute-done((f32[4,32,128]{2,1,0:T(8,128)S(1)}, f32[4,32,128]{2,1,0:T(8,128)S(1)}, u32[]{:S(2)}, u32[]{:S(2)}) %collective-permute-start.5) | collective-permute-done | bytes 65568 | tf_op jit(solution)/shard_map/ppermute | solution.py:537
  25.4 0.0 collective-permute-done.2.rfac
  25.4 0.0 collective-permute-done.1.rfar
  25.4 0.0 collective-permute-done.rnear
  25.4 1.2 %finish.1 = (f32[4,64,1024]{2,1,0:T(8,128)S(1)}, f32[32,32,128]{2,1,0:T(8,128)S(1)}, f32[512,128]{1,0:T(8,128)S(1)}, f32[4,4,32,128]{3,2,1,0:T(8,128)S(1)}) custom-call(f32[208,1024]{1,0:T(8,128)S(1)} %collective-permute-done.rnear, f32[144,1024]{1,0:T(8,128)S(1)} %collective-permute-done.1.rfar, f32[64,1024]{1,0:T(8,128)S(1)} %collective-permute-done.2.rfac, ...), custom_call_target="tpu_custom_call" | custom-call | tf_op jit(solution)/shard_map/finish/pallas_call | solution.py:374
  26.6 19.5 %all_to_all.10.got = f32[32,32,128]{2,1,0:T(8,128)S(1)} all-to-all(f32[32,32,128]{2,1,0:T(8,128)S(1)} %get-tuple-element.47), channel_id=1, replica_groups=mesh['tm'=8,'px'=4,'pz'=2,'core'=2] {'tm','pz','core'}, dimensions={0} | all-to-all | bytes 1048576 | tf_op jit(solution)/shard_map/all_to_all | solution.py:571
  46.1 0.1 pick.1
  46.3 0.9 %collective-permute-start.6 = (f32[13,32,128]{2,1,0:T(8,128)S(1)}, f32[13,32,128]{2,1,0:T(8,128)S(1)}, u32[]{:S(2)}, u32[]{:S(2)}) collective-permute-start(f32[13,32,128]{2,1,0:T(8,128)S(1)} %get-tuple-element.49), channel_id=1, source_target_pairs={{0,4},{4,0},{8,12},{12,8},{1,5},{5,1},{9,13},{13,9},{2,6},{6,2},{1... | collective-permute-start | bytes 638984 | tf_op jit(solution)/shard_map/ppermute | solution.py:537
  47.2 1.9 %collective-permute-start.7 = (f32[13,32,128]{2,1,0:T(8,128)S(1)}, f32[13,32,128]{2,1,0:T(8,128)S(1)}, u32[]{:S(2)}, u32[]{:S(2)}) collective-permute-start(f32[13,32,128]{2,1,0:T(8,128)S(1)} %get-tuple-element.50), channel_id=1, source_target_pairs={{4,8},{8,4},{5,9},{9,5},{6,10},{10,6},{7,11},{11,7},{20,24},{24,20... | collective-permute-start | bytes 638984 | tf_op jit(solution)/shard_map/ppermute | solution.py:537
  49.1 4.2 %collective-permute-done.6.even = f32[13,32,128]{2,1,0:T(8,128)S(1)} collective-permute-done((f32[13,32,128]{2,1,0:T(8,128)S(1)}, f32[13,32,128]{2,1,0:T(8,128)S(1)}, u32[]{:S(2)}, u32[]{:S(2)}) %collective-permute-start.6) | collective-permute-done | bytes 213024 | tf_op jit(solution)/shard_map/ppermute | solution.py:537
  53.3 2.6 %collective-permute-done.7.odd = f32[13,32,128]{2,1,0:T(8,128)S(1)} collective-permute-done((f32[13,32,128]{2,1,0:T(8,128)S(1)}, f32[13,32,128]{2,1,0:T(8,128)S(1)}, u32[]{:S(2)}, u32[]{:S(2)}) %collective-permute-start.7) | collective-permute-done | bytes 213024 | tf_op jit(solution)/shard_map/ppermute | solution.py:537
  55.9 1.8 %chain.1 = f32[32,16,128]{2,1,0:T(8,128)S(1)} custom-call(f32[32,32,128]{2,1,0:T(8,128)S(1)} %all_to_all.10.got, f32[4,4,32,128]{3,2,1,0:T(8,128)S(1)} %get-tuple-element.48.quad, f32[13,32,128]{2,1,0:T(8,128)S(1)} %collective-permute-done.6.even, f32[13,32,128]{2,1,0:T(8,128)S(1)} %collective-permute-done.7.odd), custom_call_target="tpu_custom_call" | custom-call | tf_op jit(solution)/shard_map/chain/pallas_call | solution.py:490
  57.7 13.0 %all_to_all.11 = f32[32,16,128]{2,1,0:T(8,128)S(1)} all-to-all(f32[32,16,128]{2,1,0:T(8,128)S(1)} %chain.1), channel_id=1, replica_groups=mesh['tm'=8,'px'=4,'pz'=2,'core'=2] {'tm','pz','core'}, dimensions={0} | all-to-all | bytes 524288 | tf_op jit(solution)/shard_map/all_to_all | solution.py:575
  70.7 1.9 %result.1 = f32[8,64,1024]{2,1,0:T(8,128)} custom-call(f32[512,128]{1,0:T(8,128)S(1)} %bitcast.3, f32[512,128]{1,0:T(8,128)S(1)} %get-tuple-element.51.gc, f32[6,64,1024]{2,1,0:T(8,128)S(1)} %get-tuple-element.42.fin, f32[4,64,1024]{2,1,0:T(8,128)S(1)} %get-tuple-element.52.ub), custom_call_target="tpu_custom_call" | custom-call | tf_op jit(solution)/shard_map/result/pallas_call | solution.py:524
Async XLA Ops:
  4.3 21.1 %collective-permute-start = (f32[208,1024]{1,0:T(8,128)S(1)}, f32[208,1024]{1,0:T(8,128)S(1)}, u32[]{:S(2)}, u32[]{:S(2)}) collective-permute-start(f32[208,1024]{1,0:T(8,128)S(1)} %get-tuple-element.29.onear), channel_id=1, source_target_pairs={{0,1},{1,0},{2,3},{3,2},{4,5},{5,4},{6,7},{7,6},{8,9},{9,8},{10,11... | collective-permute-start | bytes 2555912 | tf_op jit(solution)/shard_map/ppermute | solution.py:537
  5.1 20.3 %collective-permute-start.1 = (f32[144,1024]{1,0:T(8,128)S(1)}, f32[144,1024]{1,0:T(8,128)S(1)}, u32[]{:S(2)}, u32[]{:S(2)}) collective-permute-start(f32[144,1024]{1,0:T(8,128)S(1)} %get-tuple-element.30.ofar), channel_id=1, source_target_pairs={{1,2},{2,1},{3,4},{4,3},{5,6},{6,5},{7,8},{8,7},{9,10},{10,9},{11,... | collective-permute-start | bytes 1769480 | tf_op jit(solution)/shard_map/ppermute | solution.py:537
  8.5 16.9 %collective-permute-start.2 = (f32[64,1024]{1,0:T(8,128)S(1)}, f32[64,1024]{1,0:T(8,128)S(1)}, u32[]{:S(2)}, u32[]{:S(2)}) collective-permute-start(f32[64,1024]{1,0:T(8,128)S(1)} %get-tuple-element.31.ofac), channel_id=1, source_target_pairs={{1,18},{2,17},{3,20},{4,19},{5,22},{6,21},{7,24},{8,23},{9,26},{10... | collective-permute-start | bytes 786440 | tf_op jit(solution)/shard_map/ppermute | solution.py:537
  14.2 1.9 %collective-permute-start.3 = (f32[4,32,128]{2,1,0:T(8,128)S(1)}, f32[4,32,128]{2,1,0:T(8,128)S(1)}, u32[]{:S(2)}, u32[]{:S(2)}) collective-permute-start(f32[4,32,128]{2,1,0:T(8,128)S(1)} %get-tuple-element.37), channel_id=1, source_target_pairs={{0,1},{1,0},{2,3},{3,2},{4,5},{5,4},{6,7},{7,6},{8,9},{9,8},{10,11... | collective-permute-start | bytes 196616 | tf_op jit(solution)/shard_map/ppermute | solution.py:537
  15.3 8.5 %collective-permute-start.4 = (f32[4,32,128]{2,1,0:T(8,128)S(1)}, f32[4,32,128]{2,1,0:T(8,128)S(1)}, u32[]{:S(2)}, u32[]{:S(2)}) collective-permute-start(f32[4,32,128]{2,1,0:T(8,128)S(1)} %get-tuple-element.38), channel_id=1, source_target_pairs={{0,2},{1,3},{2,0},{3,1},{4,6},{5,7},{6,4},{7,5},{8,10},{9,11},{10,... | collective-permute-start | bytes 196616 | tf_op jit(solution)/shard_map/ppermute | solution.py:537
  16.2 9.2 %collective-permute-start.5 = (f32[4,32,128]{2,1,0:T(8,128)S(1)}, f32[4,32,128]{2,1,0:T(8,128)S(1)}, u32[]{:S(2)}, u32[]{:S(2)}) collective-permute-start(f32[4,32,128]{2,1,0:T(8,128)S(1)} %get-tuple-element.39), channel_id=1, source_target_pairs={{0,3},{1,2},{2,1},{3,0},{4,7},{5,6},{6,5},{7,4},{8,11},{9,10},{10,... | collective-permute-start | bytes 196616 | tf_op jit(solution)/shard_map/ppermute | solution.py:537
  46.3 7.1 %collective-permute-start.6 = (f32[13,32,128]{2,1,0:T(8,128)S(1)}, f32[13,32,128]{2,1,0:T(8,128)S(1)}, u32[]{:S(2)}, u32[]{:S(2)}) collective-permute-start(f32[13,32,128]{2,1,0:T(8,128)S(1)} %get-tuple-element.49), channel_id=1, source_target_pairs={{0,4},{4,0},{8,12},{12,8},{1,5},{5,1},{9,13},{13,9},{2,6},{6,2},{1... | collective-permute-start | bytes 638984 | tf_op jit(solution)/shard_map/ppermute | solution.py:537
  47.2 8.7 %collective-permute-start.7 = (f32[13,32,128]{2,1,0:T(8,128)S(1)}, f32[13,32,128]{2,1,0:T(8,128)S(1)}, u32[]{:S(2)}, u32[]{:S(2)}) collective-permute-start(f32[13,32,128]{2,1,0:T(8,128)S(1)} %get-tuple-element.50), channel_id=1, source_target_pairs={{4,8},{8,4},{5,9},{9,5},{6,10},{10,6},{7,11},{11,7},{20,24},{24,20... | collective-permute-start | bytes 638984 | tf_op jit(solution)/shard_map/ppermute | solution.py:537

commit v7 on v6

--- a/solution.py
+++ b/solution.py
@@ -100,42 +100,29 @@
     return lax.axis_index("core") == kind
 
 
-def edges_kernel(st, vel, dif, near, far, factor, u, vx, vy, vz, d, zs, sems):
+def edges_kernel(st, vel, dif, near, far, factor, u, v, d, zs, sems):
     tops = [edge_is_top(kind) for kind in range(2)]
-
-    def layer(z, which=(0, 1, 2, 3, 4)):
+    copies = []
+    for kind, top in enumerate(tops):
+        z, beside = jnp.where(top, LZ - 1, 0), jnp.where(top, LZ - 2, 1)
         pairs = (
-            (st.at[z], u.at[z]),
-            (vel.at[0, z], vx.at[z]),
-            (vel.at[1, z], vy.at[z]),
-            (vel.at[2, z], vz.at[z]),
-            (dif.at[z], d.at[z]),
+            (st.at[z], u.at[kind]),
+            (vel.at[:, z], v.at[kind]),
+            (dif.at[z], d.at[kind]),
+            (st.at[beside], u.at[2 + kind]),
         )
-        return [pltpu.make_async_copy(*pairs[i], sems.at[z, i]) for i in which]
-
-    order = []
-    for top in tops:
-        order += [jnp.where(top, LZ - 1, 0), jnp.where(top, LZ - 2, 1)]
-    middle = list(range(2, LZ - 2))
-    early, late = (0,), (1, 2, 3, 4)
-    for kind in range(2):
-        for copy in layer(order[2 * kind]) + layer(order[2 * kind + 1], early):
+        copies.append([pltpu.make_async_copy(a, b, sems.at[kind, i]) for i, (a, b) in enumerate(pairs)])
+    for kind in (1, 0):
+        for copy in copies[kind]:
             copy.start()
-    for z in (1, LZ - 2):
-        for copy in layer(z, late):
-            copy.start()
-    for z in middle:
-        for copy in layer(z):
-            copy.start()
-    for kind, top in enumerate(tops):
-        out = (near, far)[kind]
-        z, beside = order[2 * kind], order[2 * kind + 1]
-        for copy in layer(z) + layer(beside, early):
+    for kind in (1, 0):
+        top, out = tops[kind], (near, far)[kind]
+        for copy in copies[kind]:
             copy.wait()
-        for r, rows, (c, w, e, s, n) in planes(u, z):
-            inside = u[beside, rows, :]
-            ax, ay, k = vx[z, rows, :], vy[z, rows, :], d[z, rows, :]
-            up = jnp.where(top, vz[z, rows, :], -vz[z, rows, :])
+        for r, rows, (c, w, e, s, n) in planes(u, kind):
+            inside = u[2 + kind, rows, :]
+            ax, ay, k = v[kind, 0, rows, :], v[kind, 1, rows, :], d[kind, rows, :]
+            up = jnp.where(top, v[kind, 2, rows, :], -v[kind, 2, rows, :])
             out[r : r + 8, :] = c
             out[NY + r : NY + r + 8, :] = advanced(c, w, e, s, n, inside, jnp.zeros_like(c), ax, ay, up, k)
             b = k - jnp.minimum(up, 0.0)
@@ -157,12 +144,6 @@
     for i in range(8):
         near[2 * NY : FAR, 128 * i : 128 * i + 128] = cnear[16 * i : 16 * i + 16, :]
         far[2 * NY : FAR, 128 * i : 128 * i + 128] = cfar[16 * i : 16 * i + 16, :]
-    for z in (1, LZ - 2):
-        for copy in layer(z, late):
-            copy.wait()
-    for z in middle:
-        for copy in layer(z):
-            copy.wait()
 
 
 def whole():
@@ -174,22 +155,23 @@
 
 
 def edges(state, velocity, diffusivity):
-    slab = jax.ShapeDtypeStruct((LZ, NY, NX), F32)
     return pl.pallas_call(
         edges_kernel,
         out_shape=[
             jax.ShapeDtypeStruct((NEAR, NX), F32),
             jax.ShapeDtypeStruct((FAR, NX), F32),
             jax.ShapeDtypeStruct((NY, NX), F32),
-        ]
-        + [slab] * 5,
+        ],
         in_specs=[remains()] * 3,
-        out_specs=[whole()] * 8,
+        out_specs=[whole()] * 3,
         scratch_shapes=[
+            pltpu.VMEM((4, NY, NX), F32),
+            pltpu.VMEM((2, 3, NY, NX), F32),
+            pltpu.VMEM((2, NY, NX), F32),
             pltpu.VMEM((8, 2 * NY, 128), F32),
-            pltpu.SemaphoreType.DMA((LZ, 5)),
-        ],
-        compiler_params=params(42),
+            pltpu.SemaphoreType.DMA((2, 4)),
+        ],
+        compiler_params=params(52),
         name="edges",
     )(state, velocity, diffusivity)
 
@@ -198,9 +180,22 @@
     return lax.axis_index("pz") * 2 + lax.axis_index("core")
 
 
-def coefs_kernel(vx, vy, vz, d, ct, w0, w1, w2, w3, zs):
-    for comp, ref in enumerate((vx, vy, vz, d)):
+def coefs_kernel(st, vel, dif, ct, w0, w1, w2, w3, u, vx, vy, vz, d, zs, usem, sems):
+    fields = (vx, vy, vz, d)
+
+    def part(comp, zc):
+        layers = slice(2 * zc, 2 * zc + 2)
+        source = dif.at[layers] if comp == 3 else vel.at[comp, layers]
+        return pltpu.make_async_copy(source, fields[comp].at[layers], sems.at[comp, zc])
+
+    for comp in range(4):
         for zc in range(4):
+            part(comp, zc).start()
+    state = pltpu.make_async_copy(st, u, usem)
+    state.start()
+    for comp, ref in enumerate(fields):
+        for zc in range(4):
+            part(comp, zc).wait()
             for r in range(0, NY, 8):
                 rows = slice(r, r + 8)
                 put_columns(
@@ -214,23 +209,30 @@
         ct[comp, CX + 8 : CX + 32, :] = ct[comp, 8:32, :]
     mine = quad_rank()
     for i, out in enumerate((w0, w1, w2, w3)):
-        block = lax.axis_index("tm") * QUAD + (mine ^ i)
+        slice_index = lax.axis_index("tm")
+        block = (slice_index if i < 2 else slice_index ^ 1) * QUAD + (mine ^ i)
         for comp in range(4):
             out[comp] = ct[comp, pl.ds(pl.multiple_of(block * XB, XB), WIN), :]
-
-
-def coefs(fields):
+    state.wait()
+
+
+def coefs(state, velocity, diffusivity):
     window = jax.ShapeDtypeStruct((4, WIN, CL), F32)
+    slab = jax.ShapeDtypeStruct((LZ, NY, NX), F32)
     return pl.pallas_call(
         coefs_kernel,
-        out_shape=[jax.ShapeDtypeStruct((4, CROWS, CL), F32), window, window, window, window],
-        in_specs=[whole()] * 4,
-        out_specs=[whole()] * 5,
-        scratch_shapes=[pltpu.VMEM((4, 8, 4 * NY, 128), F32)],
-        compiler_params=params(12),
+        out_shape=[jax.ShapeDtypeStruct((4, CROWS, CL), F32)] + [window] * 4 + [slab] * 5,
+        in_specs=[remains()] * 3,
+        out_specs=[whole()] * 10,
+        scratch_shapes=[
+            pltpu.VMEM((4, 8, 4 * NY, 128), F32),
+            pltpu.SemaphoreType.DMA,
+            pltpu.SemaphoreType.DMA((4, 4)),
+        ],
+        compiler_params=params(42),
         cost_estimate=pl.CostEstimate(flops=20_000_000, bytes_accessed=9_000_000, transcendentals=0),
         name="coefs",
-    )(*fields)
+    )(state, velocity, diffusivity)
 
 
 def interior_kernel(u, vx, vy, vz, d, ct, fin, edge, gcp, cb, ymid, u1, zs, zf, ct0):
@@ -554,16 +556,16 @@
 
 def shards(state_old, velocity, diffusivity):
     state = state_old[0]
-    onear, ofar, ofac, u, *fields = edges(state, velocity, diffusivity)
+    onear, ofar, ofac = edges(state, velocity, diffusivity)
     rnear = swap(onear, SPACE, lambda i: i ^ 1)
     rfar = swap(ofar, SPACE, off_chip)
     rfac = swap(ofac, ("tm",) + SPACE, off_chip_copy)
-    ct, w0, w1, w2, w3 = coefs(fields)
+    ct, w0, w1, w2, w3, u, *fields = coefs(state, velocity, diffusivity)
     windows = (
         w0,
         swap(w1, SPACE, lambda i: i ^ 1),
-        swap(w2, SPACE, lambda i: i ^ 2),
-        swap(w3, SPACE, lambda i: i ^ 3),
+        swap(w2, ("tm",) + SPACE, lambda i: i ^ 18),
+        swap(w3, ("tm",) + SPACE, lambda i: i ^ 19),
     )
     fin, edge, gcp, cb, ymid = interior(u, fields, ct)
     messages = (rnear, rfar, rfac, onear, ofar, ofac)

time: 72.9 us -> 69.1 us (0.948)
  waiting for transfers between devices: 10.3 us -> 7.21 us
  blocking collectives: 32.5 us -> 30 us
  Pallas kernels: 15.3 us -> 16.6 us
    pallas_call x1, Pallas kernels: 1.19 us -> 4.25 us  [coefs(): pl.pallas_call(coefs_kernel, out_shape=[jax.ShapeDtypeStruct((4, CROWS, C...]
    ppermute x8, waiting for transfers between devices: 10.3 us -> 7.21 us  [swap(): lax.ppermute(value, axes, [(i, j) for i, j in pairs if j is not None])]
    all_to_all x1, blocking collectives: 19.5 us -> 17 us  [shards(): got = lax.all_to_all(msg, GROUP, 0, 0)]
    pallas_call x1, Pallas kernels: 4.3 us -> 2.53 us  [edges(): pl.pallas_call(edges_kernel, out_shape=[jax.ShapeDtypeStruct((NEAR, NX),...]
  transfers between devices with their start and end apart: 8 -> 8, of which waited for: 5 -> 3; matrix products, arithmetic and copies ran while one was open for 0% -> 0% of each run, Pallas kernels for 8% -> 13%
where the time goes in v7:
time: 69.1 us; the launch traced here: 68.9 us
  blocking collectives  30 us (43%)
  Pallas kernels  16.6 us (24%)
  starting transfers between devices  15 us (22%)
  waiting for transfers between devices  7.21 us (10%)
    all_to_all x1, blocking collectives, shards(): got = lax.all_to_all(msg, GROUP, 0, 0)  17 us
    ppermute x8, starting transfers between devices, swap(): lax.ppermute(value, axes, [(i, j) for i, j in pairs if j is not None])  15 us
    all_to_all x1, blocking collectives, shards(): back = lax.all_to_all(chain(got, quad, even, odd), GROUP, 0, 0)  13 us
    ppermute x8, waiting for transfers between devices, swap(): lax.ppermute(value, axes, [(i, j) for i, j in pairs if j is not None])  7.21 us
    pallas_call x1, Pallas kernels, interior(): pl.pallas_call(interior_kernel, out_shape=[jax.ShapeDtypeStruct((LZ - 2,...  4.76 us
    pallas_call x1, Pallas kernels, coefs(): pl.pallas_call(coefs_kernel, out_shape=[jax.ShapeDtypeStruct((4, CROWS, C...  4.25 us
    pallas_call x1, Pallas kernels, edges(): pl.pallas_call(edges_kernel, out_shape=[jax.ShapeDtypeStruct((NEAR, NX),...  2.53 us
    pallas_call x1, Pallas kernels, result(): pl.pallas_call(result_kernel, out_shape=jax.ShapeDtypeStruct((LZ, NY, NX)...  1.93 us
  transfers between devices with their start and end apart: 8, of which 3 were waited for; matrix products, arithmetic and copies ran while one was open for 0% of the time, Pallas kernels for 13%

profile of v7, /device:TPU:5, one launch (start us, length us, event | category | flops | bytes accessed | tf_op | source)
XLA Modules:
  0.0 68.9 jit_solution(4698450463585156794)
XLA Ops:
  0.0 2.5 %edges.1 = (f32[208,1024]{1,0:T(8,128)S(1)}, f32[144,1024]{1,0:T(8,128)S(1)}, f32[64,1024]{1,0:T(8,128)S(1)}) custom-call(f32[8,64,1024]{2,1,0:T(8,128)} %bitcast.4, f32[3,8,64,1024]{3,2,1,0:T(8,128)} %vel.3, f32[8,64,1024]{2,1,0:T(8,128)} %dif.3), custom_call_target="tpu_custom_call" | custom-call | tf_op jit(solution)/shard_map/edges/pallas_call | solution.py:158
  2.5 0.8 %collective-permute-start = (f32[208,1024]{1,0:T(8,128)S(1)}, f32[208,1024]{1,0:T(8,128)S(1)}, u32[]{:S(2)}, u32[]{:S(2)}) collective-permute-start(f32[208,1024]{1,0:T(8,128)S(1)} %get-tuple-element.29.onear), channel_id=1, source_target_pairs={{0,1},{1,0},{2,3},{3,2},{4,5},{5,4},{6,7},{7,6},{8,9},{9,8},{10,11... | collective-permute-start | bytes 2555912 | tf_op jit(solution)/shard_map/ppermute | solution.py:539
  3.3 3.4 %collective-permute-start.1 = (f32[144,1024]{1,0:T(8,128)S(1)}, f32[144,1024]{1,0:T(8,128)S(1)}, u32[]{:S(2)}, u32[]{:S(2)}) collective-permute-start(f32[144,1024]{1,0:T(8,128)S(1)} %get-tuple-element.30.ofar), channel_id=1, source_target_pairs={{1,2},{2,1},{3,4},{4,3},{5,6},{6,5},{7,8},{8,7},{9,10},{10,9},{11,... | collective-permute-start | bytes 1769480 | tf_op jit(solution)/shard_map/ppermute | solution.py:539
  6.7 4.5 %collective-permute-start.2 = (f32[64,1024]{1,0:T(8,128)S(1)}, f32[64,1024]{1,0:T(8,128)S(1)}, u32[]{:S(2)}, u32[]{:S(2)}) collective-permute-start(f32[64,1024]{1,0:T(8,128)S(1)} %get-tuple-element.31.ofac), channel_id=1, source_target_pairs={{1,18},{2,17},{3,20},{4,19},{5,22},{6,21},{7,24},{8,23},{9,26},{10... | collective-permute-start | bytes 786440 | tf_op jit(solution)/shard_map/ppermute | solution.py:539
  11.3 4.3 %coefs.1 = (f32[4,544,128]{2,1,0:T(8,128)S(1)}, f32[4,32,128]{2,1,0:T(8,128)S(1)}, f32[4,32,128]{2,1,0:T(8,128)S(1)}, f32[4,32,128]{2,1,0:T(8,128)S(1)}, f32[4,3...) custom-call(f32[8,64,1024]{2,1,0:T(8,128)} %bitcast.5, ...), custom_call_target="tpu_custom_call" | custom-call | flops 20000000 | bytes 9000000 | tf_op jit(solution)/shard_map/coefs/pallas_call | solution.py:222
  15.5 1.0 %collective-permute-start.3 = (f32[4,32,128]{2,1,0:T(8,128)S(1)}, f32[4,32,128]{2,1,0:T(8,128)S(1)}, u32[]{:S(2)}, u32[]{:S(2)}) collective-permute-start(f32[4,32,128]{2,1,0:T(8,128)S(1)} %get-tuple-element.33), channel_id=1, source_target_pairs={{0,1},{1,0},{2,3},{3,2},{4,5},{5,4},{6,7},{7,6},{8,9},{9,8},{10,11... | collective-permute-start | bytes 196616 | tf_op jit(solution)/shard_map/ppermute | solution.py:539
  16.5 0.5 collective-permute-start.4
  17.0 0.4 collective-permute-done.3.w1
  17.4 2.0 %collective-permute-start.5 = (f32[4,32,128]{2,1,0:T(8,128)S(1)}, f32[4,32,128]{2,1,0:T(8,128)S(1)}, u32[]{:S(2)}, u32[]{:S(2)}) collective-permute-start(f32[4,32,128]{2,1,0:T(8,128)S(1)} %get-tuple-element.35), channel_id=1, source_target_pairs={{0,19},{1,18},{2,17},{3,16},{4,23},{5,22},{6,21},{7,20},{8,27},{9,... | collective-permute-start | bytes 196616 | tf_op jit(solution)/shard_map/ppermute | solution.py:539
  19.5 4.8 %interior.1 = (f32[6,64,1024]{2,1,0:T(8,128)S(1)}, f32[4,64,1024]{2,1,0:T(8,128)S(1)}, f32[512,128]{1,0:T(8,128)S(1)}, f32[512,128]{1,0:T(8,128)S(1)}, f32[8,64,128]{2,1,0:T(8,128)S(1)}) custom-call(f32[8,64,1024]{2,1,0:T(8,128)S(1)} %get-tuple-element.36.u, f32[8,64,1024]{2,1,0:T(8,128)S(1)} %get-tuple-element.37.vx, ...), custom_call_target="tpu_custom_call" | custom-call | flops 60000000 | bytes 20000000 | tf_op jit(solution)/shard_map/interior/pallas_call | solution.py:298
  24.2 0.0 collective-permute-done.4.w2
  24.3 0.0 collective-permute-done.5.w3
  24.3 0.0 collective-permute-done.2.rfac
  24.3 0.0 collective-permute-done.1.rfar
  24.3 0.0 collective-permute-done.rnear
  24.3 1.2 %finish.1 = (f32[4,64,1024]{2,1,0:T(8,128)S(1)}, f32[32,32,128]{2,1,0:T(8,128)S(1)}, f32[512,128]{1,0:T(8,128)S(1)}, f32[4,4,32,128]{3,2,1,0:T(8,128)S(1)}) custom-call(f32[208,1024]{1,0:T(8,128)S(1)} %collective-permute-done.rnear, f32[144,1024]{1,0:T(8,128)S(1)} %collective-permute-done.1.rfar, f32[64,1024]{1,0:T(8,128)S(1)} %collective-permute-done.2.rfac, ...), custom_call_target="tpu_custom_call" | custom-call | tf_op jit(solution)/shard_map/finish/pallas_call | solution.py:376
  25.5 17.0 %all_to_all.10.got = f32[32,32,128]{2,1,0:T(8,128)S(1)} all-to-all(f32[32,32,128]{2,1,0:T(8,128)S(1)} %get-tuple-element.47), channel_id=1, replica_groups=mesh['tm'=8,'px'=4,'pz'=2,'core'=2] {'tm','pz','core'}, dimensions={0} | all-to-all | bytes 1048576 | tf_op jit(solution)/shard_map/all_to_all | solution.py:573
  42.4 0.1 pick.1
  42.6 0.8 %collective-permute-start.6 = (f32[13,32,128]{2,1,0:T(8,128)S(1)}, f32[13,32,128]{2,1,0:T(8,128)S(1)}, u32[]{:S(2)}, u32[]{:S(2)}) collective-permute-start(f32[13,32,128]{2,1,0:T(8,128)S(1)} %get-tuple-element.49), channel_id=1, source_target_pairs={{0,4},{4,0},{8,12},{12,8},{1,5},{5,1},{9,13},{13,9},{2,6},{6,2},{1... | collective-permute-start | bytes 638984 | tf_op jit(solution)/shard_map/ppermute | solution.py:539
  43.4 1.9 %collective-permute-start.7 = (f32[13,32,128]{2,1,0:T(8,128)S(1)}, f32[13,32,128]{2,1,0:T(8,128)S(1)}, u32[]{:S(2)}, u32[]{:S(2)}) collective-permute-start(f32[13,32,128]{2,1,0:T(8,128)S(1)} %get-tuple-element.50), channel_id=1, source_target_pairs={{4,8},{8,4},{5,9},{9,5},{6,10},{10,6},{7,11},{11,7},{20,24},{24,20... | collective-permute-start | bytes 638984 | tf_op jit(solution)/shard_map/ppermute | solution.py:539
  45.3 4.4 %collective-permute-done.6.even = f32[13,32,128]{2,1,0:T(8,128)S(1)} collective-permute-done((f32[13,32,128]{2,1,0:T(8,128)S(1)}, f32[13,32,128]{2,1,0:T(8,128)S(1)}, u32[]{:S(2)}, u32[]{:S(2)}) %collective-permute-start.6) | collective-permute-done | bytes 213024 | tf_op jit(solution)/shard_map/ppermute | solution.py:539
  49.7 2.4 %collective-permute-done.7.odd = f32[13,32,128]{2,1,0:T(8,128)S(1)} collective-permute-done((f32[13,32,128]{2,1,0:T(8,128)S(1)}, f32[13,32,128]{2,1,0:T(8,128)S(1)}, u32[]{:S(2)}, u32[]{:S(2)}) %collective-permute-start.7) | collective-permute-done | bytes 213024 | tf_op jit(solution)/shard_map/ppermute | solution.py:539
  52.1 1.8 %chain.1 = f32[32,16,128]{2,1,0:T(8,128)S(1)} custom-call(f32[32,32,128]{2,1,0:T(8,128)S(1)} %all_to_all.10.got, f32[4,4,32,128]{3,2,1,0:T(8,128)S(1)} %get-tuple-element.48.quad, f32[13,32,128]{2,1,0:T(8,128)S(1)} %collective-permute-done.6.even, f32[13,32,128]{2,1,0:T(8,128)S(1)} %collective-permute-done.7.odd), custom_call_target="tpu_custom_call" | custom-call | tf_op jit(solution)/shard_map/chain/pallas_call | solution.py:492
  54.0 13.0 %all_to_all.11 = f32[32,16,128]{2,1,0:T(8,128)S(1)} all-to-all(f32[32,16,128]{2,1,0:T(8,128)S(1)} %chain.1), channel_id=1, replica_groups=mesh['tm'=8,'px'=4,'pz'=2,'core'=2] {'tm','pz','core'}, dimensions={0} | all-to-all | bytes 524288 | tf_op jit(solution)/shard_map/all_to_all | solution.py:577
  66.9 1.9 %result.1 = f32[8,64,1024]{2,1,0:T(8,128)} custom-call(f32[512,128]{1,0:T(8,128)S(1)} %bitcast.3, f32[512,128]{1,0:T(8,128)S(1)} %get-tuple-element.51.gc, f32[6,64,1024]{2,1,0:T(8,128)S(1)} %get-tuple-element.42.fin, f32[4,64,1024]{2,1,0:T(8,128)S(1)} %get-tuple-element.52.ub), custom_call_target="tpu_custom_call" | custom-call | tf_op jit(solution)/shard_map/result/pallas_call | solution.py:526
Async XLA Ops:
  2.5 21.8 %collective-permute-start = (f32[208,1024]{1,0:T(8,128)S(1)}, f32[208,1024]{1,0:T(8,128)S(1)}, u32[]{:S(2)}, u32[]{:S(2)}) collective-permute-start(f32[208,1024]{1,0:T(8,128)S(1)} %get-tuple-element.29.onear), channel_id=1, source_target_pairs={{0,1},{1,0},{2,3},{3,2},{4,5},{5,4},{6,7},{7,6},{8,9},{9,8},{10,11... | collective-permute-start | bytes 2555912 | tf_op jit(solution)/shard_map/ppermute | solution.py:539
  3.3 21.0 %collective-permute-start.1 = (f32[144,1024]{1,0:T(8,128)S(1)}, f32[144,1024]{1,0:T(8,128)S(1)}, u32[]{:S(2)}, u32[]{:S(2)}) collective-permute-start(f32[144,1024]{1,0:T(8,128)S(1)} %get-tuple-element.30.ofar), channel_id=1, source_target_pairs={{1,2},{2,1},{3,4},{4,3},{5,6},{6,5},{7,8},{8,7},{9,10},{10,9},{11,... | collective-permute-start | bytes 1769480 | tf_op jit(solution)/shard_map/ppermute | solution.py:539
  6.7 17.5 %collective-permute-start.2 = (f32[64,1024]{1,0:T(8,128)S(1)}, f32[64,1024]{1,0:T(8,128)S(1)}, u32[]{:S(2)}, u32[]{:S(2)}) collective-permute-start(f32[64,1024]{1,0:T(8,128)S(1)} %get-tuple-element.31.ofac), channel_id=1, source_target_pairs={{1,18},{2,17},{3,20},{4,19},{5,22},{6,21},{7,24},{8,23},{9,26},{10... | collective-permute-start | bytes 786440 | tf_op jit(solution)/shard_map/ppermute | solution.py:539
  15.5 1.9 %collective-permute-start.3 = (f32[4,32,128]{2,1,0:T(8,128)S(1)}, f32[4,32,128]{2,1,0:T(8,128)S(1)}, u32[]{:S(2)}, u32[]{:S(2)}) collective-permute-start(f32[4,32,128]{2,1,0:T(8,128)S(1)} %get-tuple-element.33), channel_id=1, source_target_pairs={{0,1},{1,0},{2,3},{3,2},{4,5},{5,4},{6,7},{7,6},{8,9},{9,8},{10,11... | collective-permute-start | bytes 196616 | tf_op jit(solution)/shard_map/ppermute | solution.py:539
  16.5 7.7 %collective-permute-start.4 = (f32[4,32,128]{2,1,0:T(8,128)S(1)}, f32[4,32,128]{2,1,0:T(8,128)S(1)}, u32[]{:S(2)}, u32[]{:S(2)}) collective-permute-start(f32[4,32,128]{2,1,0:T(8,128)S(1)} %get-tuple-element.34), channel_id=1, source_target_pairs={{0,18},{1,19},{2,16},{3,17},{4,22},{5,23},{6,20},{7,21},{8,26},{9,... | collective-permute-start | bytes 196616 | tf_op jit(solution)/shard_map/ppermute | solution.py:539
  17.4 6.8 %collective-permute-start.5 = (f32[4,32,128]{2,1,0:T(8,128)S(1)}, f32[4,32,128]{2,1,0:T(8,128)S(1)}, u32[]{:S(2)}, u32[]{:S(2)}) collective-permute-start(f32[4,32,128]{2,1,0:T(8,128)S(1)} %get-tuple-element.35), channel_id=1, source_target_pairs={{0,19},{1,18},{2,17},{3,16},{4,23},{5,22},{6,21},{7,20},{8,27},{9,... | collective-permute-start | bytes 196616 | tf_op jit(solution)/shard_map/ppermute | solution.py:539
  42.6 7.1 %collective-permute-start.6 = (f32[13,32,128]{2,1,0:T(8,128)S(1)}, f32[13,32,128]{2,1,0:T(8,128)S(1)}, u32[]{:S(2)}, u32[]{:S(2)}) collective-permute-start(f32[13,32,128]{2,1,0:T(8,128)S(1)} %get-tuple-element.49), channel_id=1, source_target_pairs={{0,4},{4,0},{8,12},{12,8},{1,5},{5,1},{9,13},{13,9},{2,6},{6,2},{1... | collective-permute-start | bytes 638984 | tf_op jit(solution)/shard_map/ppermute | solution.py:539
  43.4 8.7 %collective-permute-start.7 = (f32[13,32,128]{2,1,0:T(8,128)S(1)}, f32[13,32,128]{2,1,0:T(8,128)S(1)}, u32[]{:S(2)}, u32[]{:S(2)}) collective-permute-start(f32[13,32,128]{2,1,0:T(8,128)S(1)} %get-tuple-element.50), channel_id=1, source_target_pairs={{4,8},{8,4},{5,9},{9,5},{6,10},{10,6},{7,11},{11,7},{20,24},{24,20... | collective-permute-start | bytes 638984 | tf_op jit(solution)/shard_map/ppermute | solution.py:539

commit v8 on v7

--- a/solution.py
+++ b/solution.py
@@ -84,11 +84,12 @@
     return out
 
 
-def y_rolled(u, width, axis):
-    y = lax.broadcasted_iota(jnp.int32, u.shape, axis) % 32
-    s = jnp.where(y == 0, pltpu.roll(u, width - 31, axis), pltpu.roll(u, 1, axis))
-    n = jnp.where(y == 31, pltpu.roll(u, 31, axis), pltpu.roll(u, width - 1, axis))
-    return s, n
+def lane_neighbours(c):
+    y = lax.rem(lax.broadcasted_iota(jnp.int32, c.shape, 1), 32)
+    below, above = pltpu.roll(c, 32, 1), pltpu.roll(c, CL - 32, 1)
+    s = pltpu.roll(jnp.where(y == 31, above, c), 1, 1)
+    n = pltpu.roll(jnp.where(y == 0, below, c), CL - 1, 1)
+    return below, above, s, n
 
 
 FAR = 2 * NY + 16
@@ -180,7 +181,7 @@
     return lax.axis_index("pz") * 2 + lax.axis_index("core")
 
 
-def coefs_kernel(st, vel, dif, ct, w0, w1, w2, w3, u, vx, vy, vz, d, zs, usem, sems):
+def coefs_kernel(vel, dif, ct, w0, w1, w2, w3, vx, vy, vz, d, zs, sems):
     fields = (vx, vy, vz, d)
 
     def part(comp, zc):
@@ -191,8 +192,6 @@
     for comp in range(4):
         for zc in range(4):
             part(comp, zc).start()
-    state = pltpu.make_async_copy(st, u, usem)
-    state.start()
     for comp, ref in enumerate(fields):
         for zc in range(4):
             part(comp, zc).wait()
@@ -213,26 +212,24 @@
         block = (slice_index if i < 2 else slice_index ^ 1) * QUAD + (mine ^ i)
         for comp in range(4):
             out[comp] = ct[comp, pl.ds(pl.multiple_of(block * XB, XB), WIN), :]
-    state.wait()
-
-
-def coefs(state, velocity, diffusivity):
+
+
+def coefs(velocity, diffusivity):
     window = jax.ShapeDtypeStruct((4, WIN, CL), F32)
     slab = jax.ShapeDtypeStruct((LZ, NY, NX), F32)
     return pl.pallas_call(
         coefs_kernel,
-        out_shape=[jax.ShapeDtypeStruct((4, CROWS, CL), F32)] + [window] * 4 + [slab] * 5,
-        in_specs=[remains()] * 3,
-        out_specs=[whole()] * 10,
+        out_shape=[jax.ShapeDtypeStruct((4, CROWS, CL), F32)] + [window] * 4 + [slab] * 4,
+        in_specs=[remains()] * 2,
+        out_specs=[whole()] * 9,
         scratch_shapes=[
             pltpu.VMEM((4, 8, 4 * NY, 128), F32),
-            pltpu.SemaphoreType.DMA,
             pltpu.SemaphoreType.DMA((4, 4)),
         ],
-        compiler_params=params(42),
+        compiler_params=params(44),
         cost_estimate=pl.CostEstimate(flops=20_000_000, bytes_accessed=9_000_000, transcendentals=0),
         name="coefs",
-    )(state, velocity, diffusivity)
+    )(velocity, diffusivity)
 
 
 def interior_kernel(u, vx, vy, vz, d, ct, fin, edge, gcp, cb, ymid, u1, zs, zf, ct0):
@@ -282,9 +279,9 @@
     for r in range(0, CX, 64):
         c = ct0[8 + r : 72 + r, :]
         xl, xh, yl, yh, zl, zh = coarse_coefs(*(ct[i, 8 + r : 72 + r, :] for i in range(4)))
-        s, n = y_rolled(c, CL, 1)
-        b = jnp.where(lane < 32, 0.0, pltpu.roll(c, 32, 1))
-        t = jnp.where(lane >= 96, 0.0, pltpu.roll(c, 96, 1))
+        b, t, s, n = lane_neighbours(c)
+        b = jnp.where(lane < 32, 0.0, b)
+        t = jnp.where(lane >= 96, 0.0, t)
         w = ct0[7 + r : 71 + r, :]
         e = ct0[9 + r : 73 + r, :]
         gcp[r : r + 64, :] = c + (
@@ -431,10 +428,7 @@
     )(got, quad)
 
 
-LANES = 8 * CL
-
-
-def chain_kernel(got, quad, even, odd, out, src, cf, e):
+def chain_kernel(got, quad, even, odd, out, cf, e):
     first = lax.rem(lax.axis_index("px"), 2) == 0
 
     def below(i):
@@ -443,49 +437,56 @@
     def above(i):
         return jnp.where(first, even[i], odd[i])
 
-    def put_coefs(values, lanes):
+    def source(j, block):
+        if 2 <= block < 6:
+            return got[QUAD * j + block - 2]
+        halo = below if block < 2 else above
+        if block in (0, 7):
+            return halo(4 + j) if j < 3 else None
+        if j < 4:
+            return halo(j)
+        _, other, width = SHARED[6 - j]
+        return pltpu.roll(halo(10 - j), width if block == 1 else CL - width, 1)
+
+    for block in range(8):
+        halo = below if block < 2 else above
+        if 2 <= block < 6:
+            values = [quad[block - 2, i] for i in range(4)]
+        elif block in (1, 6):
+            values = [halo(7 + i) for i in range(4)]
+        else:
+            values = []
+            for i in (11, 12):
+                values += [halo(i), pltpu.roll(halo(i), 64, 1)]
         for i, value in enumerate(coarse_coefs(*values)):
-            cf[i, :, lanes] = value
-
-    for j in range(7):
-        for q in range(QUAD):
-            src[j, :, (2 + q) * CL : (3 + q) * CL] = got[QUAD * j + q]
-        for halo, near, far in ((below, 1, 0), (above, 6, 7)):
-            if j < 4:
-                src[j, :, near * CL : near * CL + CL] = halo(j)
-            if j >= 3:
-                src[j, :, far * CL : far * CL + CL] = jnp.zeros((WIN, CL), F32)
-    for halo, near, far in ((below, 1, 0), (above, 6, 7)):
-        for j, other, width in SHARED:
-            turn = width if near == 1 else CL - width
-            block = halo(4 + j)
-            src[j, :, far * CL : far * CL + CL] = block
-            src[other, :, near * CL : near * CL + CL] = pltpu.roll(block, turn, 1)
-        put_coefs([halo(7 + i) for i in range(4)], slice(near * CL, near * CL + CL))
-        pairs = [halo(11), halo(12)]
-        put_coefs(
-            [pairs[0], pltpu.roll(pairs[0], 64, 1), pairs[1], pltpu.roll(pairs[1], 64, 1)],
-            slice(far * CL, far * CL + CL),
-        )
-    for q in range(QUAD):
-        put_coefs([quad[q, comp] for comp in range(4)], slice((2 + q) * CL, (3 + q) * CL))
+            cf[i, block] = value
+        e[0, block] = source(0, block)
     for q in range(QUAD):
         out[q] = jnp.zeros((XB, CL), F32)
-    e[...] = src[0]
+    lane = lax.broadcasted_iota(jnp.int32, (WIN, CL), 1)
     for k in range(1, GROUPS):
-        c = e[...]
-        s, n = y_rolled(c, LANES, 1)
-        w, x = pltpu.roll(c, 1, 0), pltpu.roll(c, WIN - 1, 0)
-        b, t = pltpu.roll(c, 32, 1), pltpu.roll(c, LANES - 32, 1)
-        y = c + (
-            (cf[0] * (w - c) + cf[1] * (x - c))
-            + (cf[2] * (s - c) + cf[3] * (n - c))
-            + (cf[4] * (b - c) + cf[5] * (t - c))
-        )
-        for q in range(QUAD):
-            out[QUAD * k + q] = y[8 : 8 + XB, (2 + q) * CL : (3 + q) * CL]
-        if k < GROUPS - 1:
-            e[...] = y + src[k]
+        now, later = (k - 1) % 2, k % 2
+        low = 0 if k < 3 else 1 if k < 7 else 2
+        reach = range(max(0, low - 1), min(8, 9 - low))
+        near = {b: lane_neighbours(e[now, b]) for b in reach}
+        for block in range(low, 8 - low):
+            c = e[now, block]
+            b, t, s, n = near[block]
+            if block > 0:
+                b = jnp.where(lane < 32, near[block - 1][0], b)
+            if block < 7:
+                t = jnp.where(lane >= 96, near[block + 1][1], t)
+            w, x = pltpu.roll(c, 1, 0), pltpu.roll(c, WIN - 1, 0)
+            y = c + (
+                (cf[0, block] * (w - c) + cf[1, block] * (x - c))
+                + (cf[2, block] * (s - c) + cf[3, block] * (n - c))
+                + (cf[4, block] * (b - c) + cf[5, block] * (t - c))
+            )
+            if 2 <= block < 6:
+                out[QUAD * k + block - 2] = y[8 : 8 + XB, :]
+            if k < GROUPS - 1:
+                more = source(k, block)
+                e[later, block] = y if more is None else y + more
 
 
 def chain(got, quad, even, odd):
@@ -495,29 +496,33 @@
         in_specs=[whole()] * 4,
         out_specs=whole(),
         scratch_shapes=[
-            pltpu.VMEM((7, WIN, LANES), F32),
-            pltpu.VMEM((6, WIN, LANES), F32),
-            pltpu.VMEM((WIN, LANES), F32),
+            pltpu.VMEM((6, 8, WIN, CL), F32),
+            pltpu.VMEM((2, 8, WIN, CL), F32),
         ],
         compiler_params=params(24),
         name="chain",
     )(got, quad, even, odd)
 
 
-def result_kernel(y, gc, fin, ub, out, buf, sems):
+def result_kernel(y, gc, fin, ub, out, copied, buf, sems):
     copy_y = table((256, CL), lambda r, c: r // 2 == c)
     copy_x = table((128, 256), lambda r, c: r == c // 2)
-    copies = []
     for b in range(4):
         rows = slice(128 * b, 128 * b + 128)
-        cols = slice(256 * b, 256 * b + 256)
-        parts = split3(y[rows, :] - gc[rows, :])
-        fine = sum(dot(dot(copy_y, p, 1, 1).astype(BF16), copy_x, 1, 0) for p in parts)
-        for z in range(LZ):
-            base = fin[z - 1, :, cols] if 2 <= z < 6 else ub[z if z < 2 else z - 4, :, cols]
-            buf[z, :, cols] = base + fine[z // 2 * NY : z // 2 * NY + NY, :]
-        copies.append(pltpu.make_async_copy(buf.at[:, :, cols], out.at[:, :, cols], sems.at[b]))
-        copies[b].start()
+        for i, part in enumerate(split3(y[rows, :] - gc[rows, :])):
+            copied[i, :, rows] = dot(copy_y, part, 1, 1).astype(BF16)
+    copies = []
+    for zc in range(4):
+        rows = slice(zc * NY, zc * NY + NY)
+        for b in range(4):
+            cols = slice(256 * b, 256 * b + 256)
+            fine = sum(dot(copied[i, rows, 128 * b : 128 * b + 128], copy_x, 1, 0) for i in range(3))
+            for z in (2 * zc, 2 * zc + 1):
+                base = fin[z - 1, :, cols] if 2 <= z < 6 else ub[z if z < 2 else z - 4, :, cols]
+                buf[z, :, cols] = base + fine
+        layers = slice(2 * zc, 2 * zc + 2)
+        copies.append(pltpu.make_async_copy(buf.at[layers], out.at[layers], sems.at[zc]))
+        copies[zc].start()
     for copy in copies:
         copy.wait()
 
@@ -528,7 +533,11 @@
         out_shape=jax.ShapeDtypeStruct((LZ, NY, NX), F32),
         in_specs=[whole()] * 4,
         out_specs=remains(),
-        scratch_shapes=[pltpu.VMEM((LZ, NY, NX), F32), pltpu.SemaphoreType.DMA((4,))],
+        scratch_shapes=[
+            pltpu.VMEM((3, 4 * NY, CX), BF16),
+            pltpu.VMEM((LZ, NY, NX), F32),
+            pltpu.SemaphoreType.DMA((4,)),
+        ],
         compiler_params=params(16),
         name="result",
     )(y, gc, fin, ub)
@@ -560,14 +569,14 @@
     rnear = swap(onear, SPACE, lambda i: i ^ 1)
     rfar = swap(ofar, SPACE, off_chip)
     rfac = swap(ofac, ("tm",) + SPACE, off_chip_copy)
-    ct, w0, w1, w2, w3, u, *fields = coefs(state, velocity, diffusivity)
+    ct, w0, w1, w2, w3, *fields = coefs(velocity, diffusivity)
     windows = (
         w0,
         swap(w1, SPACE, lambda i: i ^ 1),
         swap(w2, ("tm",) + SPACE, lambda i: i ^ 18),
         swap(w3, ("tm",) + SPACE, lambda i: i ^ 19),
     )
-    fin, edge, gcp, cb, ymid = interior(u, fields, ct)
+    fin, edge, gcp, cb, ymid = interior(state, fields, ct)
     messages = (rnear, rfar, rfac, onear, ofar, ofac)
     ub, msg, gc, quad = finish(messages, windows, fin, edge, fields, gcp, cb, ymid)
     got = lax.all_to_all(msg, GROUP, 0, 0)

time: 69.1 us -> 68.8 us (level)
  no operation moved by 1% of the time
where the time goes in v8:
time: 68.8 us; the launch traced here: 68.5 us
  blocking collectives  30 us (44%)
  Pallas kernels  16.1 us (23%)
  starting transfers between devices  15.1 us (22%)
  waiting for transfers between devices  7.21 us (10%)
    all_to_all x1, blocking collectives, shards(): got = lax.all_to_all(msg, GROUP, 0, 0)  17 us
    ppermute x8, starting transfers between devices, swap(): lax.ppermute(value, axes, [(i, j) for i, j in pairs if j is not None])  15.1 us
    all_to_all x1, blocking collectives, shards(): back = lax.all_to_all(chain(got, quad, even, odd), GROUP, 0, 0)  13 us
    ppermute x8, waiting for transfers between devices, swap(): lax.ppermute(value, axes, [(i, j) for i, j in pairs if j is not None])  7.21 us
    pallas_call x1, Pallas kernels, interior(): pl.pallas_call(interior_kernel, out_shape=[jax.ShapeDtypeStruct((LZ - 2,...  4.69 us
    pallas_call x1, Pallas kernels, coefs(): pl.pallas_call(coefs_kernel, out_shape=[jax.ShapeDtypeStruct((4, CROWS, C...  3.95 us
    pallas_call x1, Pallas kernels, edges(): pl.pallas_call(edges_kernel, out_shape=[jax.ShapeDtypeStruct((NEAR, NX),...  2.53 us
    pallas_call x1, Pallas kernels, result(): pl.pallas_call(result_kernel, out_shape=jax.ShapeDtypeStruct((LZ, NY, NX)...  1.87 us
  transfers between devices with their start and end apart: 8, of which 3 were waited for; matrix products, arithmetic and copies ran while one was open for 0% of the time, Pallas kernels for 13%

profile of v8, /device:TPU:5, one launch (start us, length us, event | category | flops | bytes accessed | tf_op | source)
XLA Modules:
  0.0 68.5 jit_solution(17683618981796145499)
XLA Ops:
  0.0 2.5 %edges.1 = (f32[208,1024]{1,0:T(8,128)S(1)}, f32[144,1024]{1,0:T(8,128)S(1)}, f32[64,1024]{1,0:T(8,128)S(1)}) custom-call(f32[8,64,1024]{2,1,0:T(8,128)} %bitcast.3, f32[3,8,64,1024]{3,2,1,0:T(8,128)} %vel.3, f32[8,64,1024]{2,1,0:T(8,128)} %dif.3), custom_call_target="tpu_custom_call" | custom-call | tf_op jit(solution)/shard_map/edges/pallas_call | solution.py:159
  2.5 0.8 %collective-permute-start = (f32[208,1024]{1,0:T(8,128)S(1)}, f32[208,1024]{1,0:T(8,128)S(1)}, u32[]{:S(2)}, u32[]{:S(2)}) collective-permute-start(f32[208,1024]{1,0:T(8,128)S(1)} %get-tuple-element.28.onear), channel_id=1, source_target_pairs={{0,1},{1,0},{2,3},{3,2},{4,5},{5,4},{6,7},{7,6},{8,9},{9,8},{10,11... | collective-permute-start | bytes 2555912 | tf_op jit(solution)/shard_map/ppermute | solution.py:548
  3.3 3.4 %collective-permute-start.1 = (f32[144,1024]{1,0:T(8,128)S(1)}, f32[144,1024]{1,0:T(8,128)S(1)}, u32[]{:S(2)}, u32[]{:S(2)}) collective-permute-start(f32[144,1024]{1,0:T(8,128)S(1)} %get-tuple-element.29.ofar), channel_id=1, source_target_pairs={{1,2},{2,1},{3,4},{4,3},{5,6},{6,5},{7,8},{8,7},{9,10},{10,9},{11,... | collective-permute-start | bytes 1769480 | tf_op jit(solution)/shard_map/ppermute | solution.py:548
  6.7 0.0 copy-start
  6.8 4.6 %collective-permute-start.2 = (f32[64,1024]{1,0:T(8,128)S(1)}, f32[64,1024]{1,0:T(8,128)S(1)}, u32[]{:S(2)}, u32[]{:S(2)}) collective-permute-start(f32[64,1024]{1,0:T(8,128)S(1)} %get-tuple-element.30.ofac), channel_id=1, source_target_pairs={{1,18},{2,17},{3,20},{4,19},{5,22},{6,21},{7,24},{8,23},{9,26},{10... | collective-permute-start | bytes 786440 | tf_op jit(solution)/shard_map/ppermute | solution.py:548
  11.4 4.0 %coefs.1 = (f32[4,544,128]{2,1,0:T(8,128)S(1)}, f32[4,32,128]{2,1,0:T(8,128)S(1)}, f32[4,32,128]{2,1,0:T(8,128)S(1)}, f32[4,32,128]{2,1,0:T(8,128)S(1)}, f32[4,3...) custom-call(f32[3,8,64,1024]{3,2,1,0:T(8,128)} %vel.3, ...), custom_call_target="tpu_custom_call" | custom-call | flops 20000000 | bytes 9000000 | tf_op jit(solution)/shard_map/coefs/pallas_call | solution.py:220
  15.4 1.0 %collective-permute-start.3 = (f32[4,32,128]{2,1,0:T(8,128)S(1)}, f32[4,32,128]{2,1,0:T(8,128)S(1)}, u32[]{:S(2)}, u32[]{:S(2)}) collective-permute-start(f32[4,32,128]{2,1,0:T(8,128)S(1)} %get-tuple-element.32), channel_id=1, source_target_pairs={{0,1},{1,0},{2,3},{3,2},{4,5},{5,4},{6,7},{7,6},{8,9},{9,8},{10,11... | collective-permute-start | bytes 196616 | tf_op jit(solution)/shard_map/ppermute | solution.py:548
  16.4 0.5 collective-permute-start.4
  16.9 0.4 collective-permute-done.3.w1
  17.3 2.0 %collective-permute-start.5 = (f32[4,32,128]{2,1,0:T(8,128)S(1)}, f32[4,32,128]{2,1,0:T(8,128)S(1)}, u32[]{:S(2)}, u32[]{:S(2)}) collective-permute-start(f32[4,32,128]{2,1,0:T(8,128)S(1)} %get-tuple-element.34), channel_id=1, source_target_pairs={{0,19},{1,18},{2,17},{3,16},{4,23},{5,22},{6,21},{7,20},{8,27},{9,... | collective-permute-start | bytes 196616 | tf_op jit(solution)/shard_map/ppermute | solution.py:548
  19.3 0.0 copy-done
  19.3 4.7 %interior.1 = (f32[6,64,1024]{2,1,0:T(8,128)S(1)}, f32[4,64,1024]{2,1,0:T(8,128)S(1)}, f32[512,128]{1,0:T(8,128)S(1)}, f32[512,128]{1,0:T(8,128)S(1)}, f32[8,64,128]{2,1,0:T(8,128)S(1)}) custom-call(f32[8,64,1024]{2,1,0:T(8,128)S(1)} %bitcast.4, f32[8,64,1024]{2,1,0:T(8,128)S(1)} %get-tuple-element.35.vx, f32[8,64,1024]{2,1,0:T(8,128)S(1)} %get-tuple-element.36.vy, ...), custom_call_target="tpu_custom_call" | custom-call | flops 60000000 | bytes 20000000 | tf_op jit(solution)/shard_map/interior/pallas_call | solution.py:295
  24.0 0.0 collective-permute-done.4.w2
  24.0 0.0 collective-permute-done.5.w3
  24.0 0.0 collective-permute-done.2.rfac
  24.1 0.0 collective-permute-done.1.rfar
  24.1 0.0 collective-permute-done.rnear
  24.1 1.2 %finish.1 = (f32[4,64,1024]{2,1,0:T(8,128)S(1)}, f32[32,32,128]{2,1,0:T(8,128)S(1)}, f32[512,128]{1,0:T(8,128)S(1)}, f32[4,4,32,128]{3,2,1,0:T(8,128)S(1)}) custom-call(f32[208,1024]{1,0:T(8,128)S(1)} %collective-permute-done.rnear, f32[144,1024]{1,0:T(8,128)S(1)} %collective-permute-done.1.rfar, f32[64,1024]{1,0:T(8,128)S(1)} %collective-permute-done.2.rfac, ...), custom_call_target="tpu_custom_call" | custom-call | tf_op jit(solution)/shard_map/finish/pallas_call | solution.py:373
  25.2 17.0 %all_to_all.10.got = f32[32,32,128]{2,1,0:T(8,128)S(1)} all-to-all(f32[32,32,128]{2,1,0:T(8,128)S(1)} %get-tuple-element.45), channel_id=1, replica_groups=mesh['tm'=8,'px'=4,'pz'=2,'core'=2] {'tm','pz','core'}, dimensions={0} | all-to-all | bytes 1048576 | tf_op jit(solution)/shard_map/all_to_all | solution.py:582
  42.2 0.1 pick.1
  42.4 0.8 %collective-permute-start.6 = (f32[13,32,128]{2,1,0:T(8,128)S(1)}, f32[13,32,128]{2,1,0:T(8,128)S(1)}, u32[]{:S(2)}, u32[]{:S(2)}) collective-permute-start(f32[13,32,128]{2,1,0:T(8,128)S(1)} %get-tuple-element.47), channel_id=1, source_target_pairs={{0,4},{4,0},{8,12},{12,8},{1,5},{5,1},{9,13},{13,9},{2,6},{6,2},{1... | collective-permute-start | bytes 638984 | tf_op jit(solution)/shard_map/ppermute | solution.py:548
  43.2 1.9 %collective-permute-start.7 = (f32[13,32,128]{2,1,0:T(8,128)S(1)}, f32[13,32,128]{2,1,0:T(8,128)S(1)}, u32[]{:S(2)}, u32[]{:S(2)}) collective-permute-start(f32[13,32,128]{2,1,0:T(8,128)S(1)} %get-tuple-element.48), channel_id=1, source_target_pairs={{4,8},{8,4},{5,9},{9,5},{6,10},{10,6},{7,11},{11,7},{20,24},{24,20... | collective-permute-start | bytes 638984 | tf_op jit(solution)/shard_map/ppermute | solution.py:548
  45.1 4.4 %collective-permute-done.6.even = f32[13,32,128]{2,1,0:T(8,128)S(1)} collective-permute-done((f32[13,32,128]{2,1,0:T(8,128)S(1)}, f32[13,32,128]{2,1,0:T(8,128)S(1)}, u32[]{:S(2)}, u32[]{:S(2)}) %collective-permute-start.6) | collective-permute-done | bytes 213024 | tf_op jit(solution)/shard_map/ppermute | solution.py:548
  49.4 2.4 %collective-permute-done.7.odd = f32[13,32,128]{2,1,0:T(8,128)S(1)} collective-permute-done((f32[13,32,128]{2,1,0:T(8,128)S(1)}, f32[13,32,128]{2,1,0:T(8,128)S(1)}, u32[]{:S(2)}, u32[]{:S(2)}) %collective-permute-start.7) | collective-permute-done | bytes 213024 | tf_op jit(solution)/shard_map/ppermute | solution.py:548
  51.9 1.8 %chain.1 = f32[32,16,128]{2,1,0:T(8,128)S(1)} custom-call(f32[32,32,128]{2,1,0:T(8,128)S(1)} %all_to_all.10.got, f32[4,4,32,128]{3,2,1,0:T(8,128)S(1)} %get-tuple-element.46.quad, f32[13,32,128]{2,1,0:T(8,128)S(1)} %collective-permute-done.6.even, f32[13,32,128]{2,1,0:T(8,128)S(1)} %collective-permute-done.7.odd), custom_call_target="tpu_custom_call" | custom-call | tf_op jit(solution)/shard_map/chain/pallas_call | solution.py:493
  53.7 13.0 %all_to_all.11 = f32[32,16,128]{2,1,0:T(8,128)S(1)} all-to-all(f32[32,16,128]{2,1,0:T(8,128)S(1)} %chain.1), channel_id=1, replica_groups=mesh['tm'=8,'px'=4,'pz'=2,'core'=2] {'tm','pz','core'}, dimensions={0} | all-to-all | bytes 524288 | tf_op jit(solution)/shard_map/all_to_all | solution.py:586
  66.7 1.9 %result.1 = f32[8,64,1024]{2,1,0:T(8,128)} custom-call(f32[512,128]{1,0:T(8,128)S(1)} %bitcast.5, f32[512,128]{1,0:T(8,128)S(1)} %get-tuple-element.49.gc, f32[6,64,1024]{2,1,0:T(8,128)S(1)} %get-tuple-element.40.fin, f32[4,64,1024]{2,1,0:T(8,128)S(1)} %get-tuple-element.50.ub), custom_call_target="tpu_custom_call" | custom-call | tf_op jit(solution)/shard_map/result/pallas_call | solution.py:531
Async XLA Ops:
  2.5 21.5 %collective-permute-start = (f32[208,1024]{1,0:T(8,128)S(1)}, f32[208,1024]{1,0:T(8,128)S(1)}, u32[]{:S(2)}, u32[]{:S(2)}) collective-permute-start(f32[208,1024]{1,0:T(8,128)S(1)} %get-tuple-element.28.onear), channel_id=1, source_target_pairs={{0,1},{1,0},{2,3},{3,2},{4,5},{5,4},{6,7},{7,6},{8,9},{9,8},{10,11... | collective-permute-start | bytes 2555912 | tf_op jit(solution)/shard_map/ppermute | solution.py:548
  3.3 20.8 %collective-permute-start.1 = (f32[144,1024]{1,0:T(8,128)S(1)}, f32[144,1024]{1,0:T(8,128)S(1)}, u32[]{:S(2)}, u32[]{:S(2)}) collective-permute-start(f32[144,1024]{1,0:T(8,128)S(1)} %get-tuple-element.29.ofar), channel_id=1, source_target_pairs={{1,2},{2,1},{3,4},{4,3},{5,6},{6,5},{7,8},{8,7},{9,10},{10,9},{11,... | collective-permute-start | bytes 1769480 | tf_op jit(solution)/shard_map/ppermute | solution.py:548
  6.7 12.6 %copy-start = (f32[1,8,64,1024]{3,2,1,0:T(8,128)S(1)}, f32[1,8,64,1024]{3,2,1,0:T(8,128)}, u32[]{:S(2)}) copy-start(f32[1,8,64,1024]{3,2,1,0:T(8,128)} %param.3) | copy-start | bytes 6291460
  6.8 17.3 %collective-permute-start.2 = (f32[64,1024]{1,0:T(8,128)S(1)}, f32[64,1024]{1,0:T(8,128)S(1)}, u32[]{:S(2)}, u32[]{:S(2)}) collective-permute-start(f32[64,1024]{1,0:T(8,128)S(1)} %get-tuple-element.30.ofac), channel_id=1, source_target_pairs={{1,18},{2,17},{3,20},{4,19},{5,22},{6,21},{7,24},{8,23},{9,26},{10... | collective-permute-start | bytes 786440 | tf_op jit(solution)/shard_map/ppermute | solution.py:548
  15.4 1.9 %collective-permute-start.3 = (f32[4,32,128]{2,1,0:T(8,128)S(1)}, f32[4,32,128]{2,1,0:T(8,128)S(1)}, u32[]{:S(2)}, u32[]{:S(2)}) collective-permute-start(f32[4,32,128]{2,1,0:T(8,128)S(1)} %get-tuple-element.32), channel_id=1, source_target_pairs={{0,1},{1,0},{2,3},{3,2},{4,5},{5,4},{6,7},{7,6},{8,9},{9,8},{10,11... | collective-permute-start | bytes 196616 | tf_op jit(solution)/shard_map/ppermute | solution.py:548
  16.4 7.6 %collective-permute-start.4 = (f32[4,32,128]{2,1,0:T(8,128)S(1)}, f32[4,32,128]{2,1,0:T(8,128)S(1)}, u32[]{:S(2)}, u32[]{:S(2)}) collective-permute-start(f32[4,32,128]{2,1,0:T(8,128)S(1)} %get-tuple-element.33), channel_id=1, source_target_pairs={{0,18},{1,19},{2,16},{3,17},{4,22},{5,23},{6,20},{7,21},{8,26},{9,... | collective-permute-start | bytes 196616 | tf_op jit(solution)/shard_map/ppermute | solution.py:548
  17.3 6.8 %collective-permute-start.5 = (f32[4,32,128]{2,1,0:T(8,128)S(1)}, f32[4,32,128]{2,1,0:T(8,128)S(1)}, u32[]{:S(2)}, u32[]{:S(2)}) collective-permute-start(f32[4,32,128]{2,1,0:T(8,128)S(1)} %get-tuple-element.34), channel_id=1, source_target_pairs={{0,19},{1,18},{2,17},{3,16},{4,23},{5,22},{6,21},{7,20},{8,27},{9,... | collective-permute-start | bytes 196616 | tf_op jit(solution)/shard_map/ppermute | solution.py:548
  42.4 7.1 %collective-permute-start.6 = (f32[13,32,128]{2,1,0:T(8,128)S(1)}, f32[13,32,128]{2,1,0:T(8,128)S(1)}, u32[]{:S(2)}, u32[]{:S(2)}) collective-permute-start(f32[13,32,128]{2,1,0:T(8,128)S(1)} %get-tuple-element.47), channel_id=1, source_target_pairs={{0,4},{4,0},{8,12},{12,8},{1,5},{5,1},{9,13},{13,9},{2,6},{6,2},{1... | collective-permute-start | bytes 638984 | tf_op jit(solution)/shard_map/ppermute | solution.py:548
  43.2 8.7 %collective-permute-start.7 = (f32[13,32,128]{2,1,0:T(8,128)S(1)}, f32[13,32,128]{2,1,0:T(8,128)S(1)}, u32[]{:S(2)}, u32[]{:S(2)}) collective-permute-start(f32[13,32,128]{2,1,0:T(8,128)S(1)} %get-tuple-element.48), channel_id=1, source_target_pairs={{4,8},{8,4},{5,9},{9,5},{6,10},{10,6},{7,11},{11,7},{20,24},{24,20... | collective-permute-start | bytes 638984 | tf_op jit(solution)/shard_map/ppermute | solution.py:548

commit v9 on v8

--- a/solution.py
+++ b/solution.py
@@ -1,3 +1,5 @@
+import functools
+
 import jax
 import jax.numpy as jnp
 from jax import lax
@@ -87,13 +89,13 @@
 def lane_neighbours(c):
     y = lax.rem(lax.broadcasted_iota(jnp.int32, c.shape, 1), 32)
     below, above = pltpu.roll(c, 32, 1), pltpu.roll(c, CL - 32, 1)
-    s = pltpu.roll(jnp.where(y == 31, above, c), 1, 1)
-    n = pltpu.roll(jnp.where(y == 0, below, c), CL - 1, 1)
+    s = jnp.where(y == 0, pltpu.roll(c, CL - 31, 1), pltpu.roll(c, 1, 1))
+    n = jnp.where(y == 31, pltpu.roll(c, 31, 1), pltpu.roll(c, CL - 1, 1))
     return below, above, s, n
 
 
 FAR = 2 * NY + 16
-NEAR = FAR + NY
+TAIL = 16 + NY
 CROWS = CX + 32
 
 
@@ -101,50 +103,36 @@
     return lax.axis_index("core") == kind
 
 
-def edges_kernel(st, vel, dif, near, far, factor, u, v, d, zs, sems):
-    tops = [edge_is_top(kind) for kind in range(2)]
-    copies = []
-    for kind, top in enumerate(tops):
-        z, beside = jnp.where(top, LZ - 1, 0), jnp.where(top, LZ - 2, 1)
-        pairs = (
-            (st.at[z], u.at[kind]),
-            (vel.at[:, z], v.at[kind]),
-            (dif.at[z], d.at[kind]),
-            (st.at[beside], u.at[2 + kind]),
-        )
-        copies.append([pltpu.make_async_copy(a, b, sems.at[kind, i]) for i, (a, b) in enumerate(pairs)])
-    for kind in (1, 0):
-        for copy in copies[kind]:
-            copy.start()
-    for kind in (1, 0):
-        top, out = tops[kind], (near, far)[kind]
-        for copy in copies[kind]:
-            copy.wait()
-        for r, rows, (c, w, e, s, n) in planes(u, kind):
-            inside = u[2 + kind, rows, :]
-            ax, ay, k = v[kind, 0, rows, :], v[kind, 1, rows, :], d[kind, rows, :]
-            up = jnp.where(top, v[kind, 2, rows, :], -v[kind, 2, rows, :])
-            out[r : r + 8, :] = c
-            out[NY + r : NY + r + 8, :] = advanced(c, w, e, s, n, inside, jnp.zeros_like(c), ax, ay, up, k)
-            b = k - jnp.minimum(up, 0.0)
-            if kind == 0:
-                near[FAR + r : FAR + r + 8, :] = b
-            else:
-                factor[rows, :] = b
-            put_columns(zs, slice(kind * NY + r, kind * NY + r + 8), c + inside)
-    lane = lax.broadcasted_iota(jnp.int32, (128, 128), 1)
-    cnear = jnp.zeros((128, 128), F32)
-    cfar = jnp.zeros((128, 128), F32)
+def edge_kernel(kind, st, vel, dif, *rest):
+    if kind == 0:
+        _, out, tail, u, v, d, zs, sems = rest
+        coarse_out, coarse_at, factor, factor_at = tail, 0, tail, 16
+    else:
+        out, factor, u, v, d, zs, sems = rest
+        coarse_out, coarse_at, factor_at = out, 2 * NY, 0
+    top = edge_is_top(kind)
+    z, beside = jnp.where(top, LZ - 1, 0), jnp.where(top, LZ - 2, 1)
+    pairs = ((st.at[z], u.at[0]), (vel.at[:, z], v), (dif.at[z], d), (st.at[beside], u.at[1]))
+    copies = [pltpu.make_async_copy(a, b, sems.at[i]) for i, (a, b) in enumerate(pairs)]
+    for copy in copies:
+        copy.start()
+    for copy in copies:
+        copy.wait()
+    for r, rows, (c, w, e, s, n) in planes(u, 0):
+        inside = u[1, rows, :]
+        ax, ay, k = v[0, rows, :], v[1, rows, :], d[rows, :]
+        up = jnp.where(top, v[2, rows, :], -v[2, rows, :])
+        out[r : r + 8, :] = c
+        out[NY + r : NY + r + 8, :] = advanced(c, w, e, s, n, inside, jnp.zeros_like(c), ax, ay, up, k)
+        factor[factor_at + r : factor_at + r + 8, :] = k - jnp.minimum(up, 0.0)
+        put_columns(zs, rows, c + inside)
+    coarse = jnp.zeros((128, 128), F32)
     for b in range(4):
-        part = jnp.concatenate([paired(zs, 2 * b + i, 0, 64) for i in range(2)], axis=1)
-        t = halved_x(jnp.concatenate([part, jnp.zeros_like(part)], axis=0))
-        tn = jnp.where(lane < 32, t, 0.0)
-        tf = jnp.where((lane >= 32) & (lane < 64), t, 0.0)
-        cnear += pltpu.roll(tn, 32 * b, 1) if b else tn
-        cfar += pltpu.roll(tf, (32 * b - 32) % 128, 1) if b != 1 else tf
+        part = jnp.concatenate([paired(zs, 2 * b + i, 0, 32) for i in range(2)], axis=1)
+        t = halved_x(jnp.concatenate([part, jnp.zeros((96, 256), F32)], axis=0))
+        coarse += pltpu.roll(t, 32 * b, 1) if b else t
     for i in range(8):
-        near[2 * NY : FAR, 128 * i : 128 * i + 128] = cnear[16 * i : 16 * i + 16, :]
-        far[2 * NY : FAR, 128 * i : 128 * i + 128] = cfar[16 * i : 16 * i + 16, :]
+        coarse_out[coarse_at : coarse_at + 16, 128 * i : 128 * i + 128] = coarse[16 * i : 16 * i + 16, :]
 
 
 def whole():
@@ -155,51 +143,37 @@
     return pl.BlockSpec(memory_space=pltpu.HBM)
 
 
-def edges(state, velocity, diffusivity):
-    return pl.pallas_call(
-        edges_kernel,
-        out_shape=[
-            jax.ShapeDtypeStruct((NEAR, NX), F32),
-            jax.ShapeDtypeStruct((FAR, NX), F32),
-            jax.ShapeDtypeStruct((NY, NX), F32),
-        ],
-        in_specs=[remains()] * 3,
-        out_specs=[whole()] * 3,
+def edge_message(kind, state, velocity, diffusivity, *after):
+    shapes = [((2 * NY, NX), (TAIL, NX)), ((FAR, NX), (NY, NX))][kind]
+    return pl.pallas_call(
+        functools.partial(edge_kernel, kind),
+        out_shape=[jax.ShapeDtypeStruct(shape, F32) for shape in shapes],
+        in_specs=[remains()] * 3 + [whole()] * len(after),
+        out_specs=[whole()] * len(shapes),
         scratch_shapes=[
-            pltpu.VMEM((4, NY, NX), F32),
-            pltpu.VMEM((2, 3, NY, NX), F32),
             pltpu.VMEM((2, NY, NX), F32),
-            pltpu.VMEM((8, 2 * NY, 128), F32),
-            pltpu.SemaphoreType.DMA((2, 4)),
-        ],
-        compiler_params=params(52),
-        name="edges",
-    )(state, velocity, diffusivity)
+            pltpu.VMEM((3, NY, NX), F32),
+            pltpu.VMEM((NY, NX), F32),
+            pltpu.VMEM((8, NY, 128), F32),
+            pltpu.SemaphoreType.DMA((4,)),
+        ],
+        compiler_params=params([8, 52][kind]),
+        cost_estimate=pl.CostEstimate(flops=15_000_000, bytes_accessed=[12_000_000, 3_000_000][kind], transcendentals=0),
+        name=["near_message", "far_message"][kind],
+    )(state, velocity, diffusivity, *after)
 
 
 def quad_rank():
     return lax.axis_index("pz") * 2 + lax.axis_index("core")
 
 
-def coefs_kernel(vel, dif, ct, w0, w1, w2, w3, vx, vy, vz, d, zs, sems):
-    fields = (vx, vy, vz, d)
-
-    def part(comp, zc):
-        layers = slice(2 * zc, 2 * zc + 2)
-        source = dif.at[layers] if comp == 3 else vel.at[comp, layers]
-        return pltpu.make_async_copy(source, fields[comp].at[layers], sems.at[comp, zc])
-
+def coefs_kernel(vel, dif, after, ct, w0, w1, w2, w3, zs):
     for comp in range(4):
         for zc in range(4):
-            part(comp, zc).start()
-    for comp, ref in enumerate(fields):
-        for zc in range(4):
-            part(comp, zc).wait()
             for r in range(0, NY, 8):
                 rows = slice(r, r + 8)
-                put_columns(
-                    zs.at[comp], slice(zc * NY + r, zc * NY + r + 8), ref[2 * zc, rows, :] + ref[2 * zc + 1, rows, :]
-                )
+                two = [dif[z, rows, :] if comp == 3 else vel[comp, z, rows, :] for z in (2 * zc, 2 * zc + 1)]
+                put_columns(zs.at[comp], slice(zc * NY + r, zc * NY + r + 8), two[0] + two[1])
         for b in range(4):
             ct[comp, 8 + 128 * b : 136 + 128 * b, :] = halved_x(
                 jnp.concatenate([paired(zs.at[comp], 2 * b + i, 0, 128) for i in range(2)], axis=1)
@@ -207,37 +181,33 @@
         ct[comp, 0:8, :] = ct[comp, CX : CX + 8, :]
         ct[comp, CX + 8 : CX + 32, :] = ct[comp, 8:32, :]
     mine = quad_rank()
+    slice_index = lax.axis_index("tm")
     for i, out in enumerate((w0, w1, w2, w3)):
-        slice_index = lax.axis_index("tm")
         block = (slice_index if i < 2 else slice_index ^ 1) * QUAD + (mine ^ i)
         for comp in range(4):
             out[comp] = ct[comp, pl.ds(pl.multiple_of(block * XB, XB), WIN), :]
 
 
-def coefs(velocity, diffusivity):
+def coefs(velocity, diffusivity, after):
     window = jax.ShapeDtypeStruct((4, WIN, CL), F32)
-    slab = jax.ShapeDtypeStruct((LZ, NY, NX), F32)
     return pl.pallas_call(
         coefs_kernel,
-        out_shape=[jax.ShapeDtypeStruct((4, CROWS, CL), F32)] + [window] * 4 + [slab] * 4,
-        in_specs=[remains()] * 2,
-        out_specs=[whole()] * 9,
-        scratch_shapes=[
-            pltpu.VMEM((4, 8, 4 * NY, 128), F32),
-            pltpu.SemaphoreType.DMA((4, 4)),
-        ],
-        compiler_params=params(44),
+        out_shape=[jax.ShapeDtypeStruct((4, CROWS, CL), F32)] + [window] * 4,
+        in_specs=[whole()] * 3,
+        out_specs=[whole()] * 5,
+        scratch_shapes=[pltpu.VMEM((4, 8, 4 * NY, 128), F32)],
+        compiler_params=params(12),
         cost_estimate=pl.CostEstimate(flops=20_000_000, bytes_accessed=9_000_000, transcendentals=0),
         name="coefs",
-    )(velocity, diffusivity)
-
-
-def interior_kernel(u, vx, vy, vz, d, ct, fin, edge, gcp, cb, ymid, u1, zs, zf, ct0):
+    )(velocity, diffusivity, after)
+
+
+def interior_kernel(u, v, d, ct, after, fin, edge, gcp, cb, ymid, u1, zs, zf, ct0):
     def first(z, _):
         for _, rows, (c, w, e, s, n) in planes(u, z):
             u1[z, rows, :] = advanced(
                 c, w, e, s, n, u[z - 1, rows, :], u[z + 1, rows, :],
-                vx[z, rows, :], vy[z, rows, :], vz[z, rows, :], d[z, rows, :],
+                v[0, z, rows, :], v[1, z, rows, :], v[2, z, rows, :], d[z, rows, :],
             )
         return 0
 
@@ -251,13 +221,13 @@
         for _, rows, (c, w, e, s, n) in planes(u1, z):
             fin[z - 1, rows, :] = advanced(
                 c, w, e, s, n, u1[z - 1, rows, :], u1[z + 1, rows, :],
-                vx[z, rows, :], vy[z, rows, :], vz[z, rows, :], d[z, rows, :],
+                v[0, z, rows, :], v[1, z, rows, :], v[2, z, rows, :], d[z, rows, :],
             )
         return 0
 
     lax.fori_loop(1, LZ - 1, second, 0)
-    edge[2] = d[1] + jnp.maximum(vz[1], 0.0)
-    edge[3] = d[LZ - 2] - jnp.minimum(vz[LZ - 2], 0.0)
+    edge[2] = d[1] + jnp.maximum(v[2, 1], 0.0)
+    edge[3] = d[LZ - 2] - jnp.minimum(v[2, LZ - 2], 0.0)
     for zc in (1, 2):
         for r in range(0, NY, 8):
             rows = slice(r, r + 8)
@@ -290,7 +260,7 @@
         cb[r : r + 64, :] = jnp.where(lane < 32, zl, jnp.where(lane >= 96, zh, 0.0))
 
 
-def interior(state, fields, ct):
+def interior(state, velocity, diffusivity, ct, after):
     small = jax.ShapeDtypeStruct((CX, CL), F32)
     return pl.pallas_call(
         interior_kernel,
@@ -301,7 +271,7 @@
             small,
             jax.ShapeDtypeStruct((8, 64, 128), F32),
         ],
-        in_specs=[whole()] * 6,
+        in_specs=[whole()] * 5,
         out_specs=[whole()] * 5,
         scratch_shapes=[
             pltpu.VMEM((LZ, NY, NX), F32),
@@ -312,18 +282,17 @@
         compiler_params=params(16),
         cost_estimate=pl.CostEstimate(flops=60_000_000, bytes_accessed=20_000_000, transcendentals=0),
         name="interior",
-    )(state, *fields, ct)
+    )(state, velocity, diffusivity, ct, after)
 
 
 def finish_kernel(
-    rnear, rfar, rfac, onear, ofar, ofac, w0, w1, w2, w3, fin, edge, vx, vy, vz, d, gcp, cb, ymid, ub, msg, gc, quad, u1, zs, jp
+    rnear, rtail, rfar, rfac, onear, otail, ofar, ofac, w0, w1, w2, w3, fin, edge, v, d, gcp, cb, ymid,
+    ub, msg, gc, quad, u1, zs, jp,
 ):
     mine = quad_rank()
     for i, window in enumerate((w0, w1, w2, w3)):
         quad[mine ^ i] = window[...]
-    for kind, (rec, own, recb, ownb, at) in enumerate(
-        ((rnear, onear, rnear, onear, FAR), (rfar, ofar, rfac, ofac, 0))
-    ):
+    for kind, (rec, own, recb, ownb, at) in enumerate(((rnear, onear, rtail, otail, 16), (rfar, ofar, rfac, ofac, 0))):
         top = edge_is_top(kind)
         side = jnp.where(top, 1, 0)
         for r in range(0, NY, 8):
@@ -334,14 +303,14 @@
         for r, rows, (c, w, e, s, n) in planes(u1, kind):
             outside = rec[NY + r : NY + r + 8, :] + recb[at + r : at + r + 8, :] * own[r : r + 8, :]
             inside = edge[side, rows, :]
-            ax, ay, az, k = vx[z, rows, :], vy[z, rows, :], vz[z, rows, :], d[z, rows, :]
+            ax, ay, az, k = v[0, z, rows, :], v[1, z, rows, :], v[2, z, rows, :], d[z, rows, :]
             last = advanced(c, w, e, s, n, inside, outside, ax, ay, jnp.where(top, az, -az), k)
             near = fin[5 * side, rows, :] + edge[2 + side, rows, :] * c
             ub[3 * side, rows, :] = last
             ub[1 + side, rows, :] = near
             put_columns(zs.at[side], rows, last + near)
     lane = lax.broadcasted_iota(jnp.int32, (128, 128), 1)
-    hnear = jnp.concatenate([rnear[2 * NY : FAR, 128 * i : 128 * i + 128] for i in range(8)], axis=0)
+    hnear = jnp.concatenate([rtail[0:16, 128 * i : 128 * i + 128] for i in range(8)], axis=0)
     hfar = jnp.concatenate([rfar[2 * NY : FAR, 128 * i : 128 * i + 128] for i in range(8)], axis=0)
     first_core = lax.axis_index("core") == 0
     halo_lo, halo_hi = jnp.where(first_core, hfar, hnear), jnp.where(first_core, hnear, hfar)
@@ -369,7 +338,7 @@
         msg[i] = jp[XB * i : XB * i + WIN, :]
 
 
-def finish(messages, windows, fin, edge, fields, gcp, cb, ymid):
+def finish(messages, windows, fin, edge, velocity, diffusivity, gcp, cb, ymid):
     return pl.pallas_call(
         finish_kernel,
         out_shape=[
@@ -387,7 +356,7 @@
         ],
         compiler_params=params(16),
         name="finish",
-    )(*messages, *windows, fin, edge, *fields, gcp, cb, ymid)
+    )(*messages, *windows, fin, edge, velocity, diffusivity, gcp, cb, ymid)
 
 
 HALO = 13
@@ -565,20 +534,22 @@
 
 def shards(state_old, velocity, diffusivity):
     state = state_old[0]
-    onear, ofar, ofac = edges(state, velocity, diffusivity)
-    rnear = swap(onear, SPACE, lambda i: i ^ 1)
+    ofar, ofac = edge_message(1, state, velocity, diffusivity)
     rfar = swap(ofar, SPACE, off_chip)
     rfac = swap(ofac, ("tm",) + SPACE, off_chip_copy)
-    ct, w0, w1, w2, w3, *fields = coefs(velocity, diffusivity)
+    onear, otail = edge_message(0, state, velocity, diffusivity, ofac)
+    rnear = swap(onear, SPACE, lambda i: i ^ 1)
+    rtail = swap(otail, SPACE, lambda i: i ^ 1)
+    ct, w0, w1, w2, w3 = coefs(velocity, diffusivity, rtail)
     windows = (
         w0,
         swap(w1, SPACE, lambda i: i ^ 1),
         swap(w2, ("tm",) + SPACE, lambda i: i ^ 18),
         swap(w3, ("tm",) + SPACE, lambda i: i ^ 19),
     )
-    fin, edge, gcp, cb, ymid = interior(state, fields, ct)
-    messages = (rnear, rfar, rfac, onear, ofar, ofac)
-    ub, msg, gc, quad = finish(messages, windows, fin, edge, fields, gcp, cb, ymid)
+    fin, edge, gcp, cb, ymid = interior(state, velocity, diffusivity, ct, windows[1])
+    messages = (rnear, rtail, rfar, rfac, onear, otail, ofar, ofac)
+    ub, msg, gc, quad = finish(messages, windows, fin, edge, velocity, diffusivity, gcp, cb, ymid)
     got = lax.all_to_all(msg, GROUP, 0, 0)
     even, odd = pick(got, quad)
     even = swap(even, "px", lambda i: i ^ 1)

time: 68.8 us -> 68.4 us (level)
  Pallas kernels: 16.1 us -> 13.5 us
  blocking collectives: 30 us -> 31.4 us
    pallas_call x1, Pallas kernels: 3.95 us -> 1.19 us  [coefs(): pl.pallas_call(coefs_kernel, out_shape=[jax.ShapeDtypeStruct((4, CROWS, C...]
    all_to_all x1, blocking collectives: 17 us -> 18.4 us  [shards(): got = lax.all_to_all(msg, GROUP, 0, 0)]
    pallas_call x1 -> x2, Pallas kernels: 2.53 us -> 2.96 us  [edge_message(): pl.pallas_call(functools.partial(edge_kernel, kind), out_shape=[jax.Shape...]
    ppermute x8 -> x9, waiting for transfers between devices: 7.21 us -> 7.44 us  [swap(): lax.ppermute(value, axes, [(i, j) for i, j in pairs if j is not None])]
    ppermute x8 -> x9, starting transfers between devices: 15.1 us -> 15.3 us  [swap(): lax.ppermute(value, axes, [(i, j) for i, j in pairs if j is not None])]
  transfers between devices with their start and end apart: 8 -> 9, of which waited for: 3 -> 4; matrix products, arithmetic and copies ran while one was open for 0% -> 0% of each run, Pallas kernels for 13% -> 10%
where the time goes in v9:
time: 68.4 us; the launch traced here: 67.8 us
  blocking collectives  31.4 us (46%)
  starting transfers between devices  15.3 us (22%)
  Pallas kernels  13.5 us (20%)
  waiting for transfers between devices  7.44 us (11%)
    all_to_all x1, blocking collectives, shards(): got = lax.all_to_all(msg, GROUP, 0, 0)  18.4 us
    ppermute x9, starting transfers between devices, swap(): lax.ppermute(value, axes, [(i, j) for i, j in pairs if j is not None])  15.3 us
    all_to_all x1, blocking collectives, shards(): back = lax.all_to_all(chain(got, quad, even, odd), GROUP, 0, 0)  13 us
    ppermute x9, waiting for transfers between devices, swap(): lax.ppermute(value, axes, [(i, j) for i, j in pairs if j is not None])  7.44 us
    pallas_call x1, Pallas kernels, interior(): pl.pallas_call(interior_kernel, out_shape=[jax.ShapeDtypeStruct((LZ - 2,...  4.76 us
    pallas_call x2, Pallas kernels, edge_message(): pl.pallas_call(functools.partial(edge_kernel, kind), out_shape=[jax.Shape...  2.96 us
    pallas_call x1, Pallas kernels, result(): pl.pallas_call(result_kernel, out_shape=jax.ShapeDtypeStruct((LZ, NY, NX)...  1.87 us
    pallas_call x1, Pallas kernels, chain(): pl.pallas_call(chain_kernel, out_shape=jax.ShapeDtypeStruct((BLOCKS, XB,...  1.41 us
  transfers between devices with their start and end apart: 9, of which 4 were waited for; matrix products, arithmetic and copies ran while one was open for 0% of the time, Pallas kernels for 10%

profile of v9, /device:TPU:5, one launch (start us, length us, event | category | flops | bytes accessed | tf_op | source)
XLA Modules:
  0.0 67.8 jit_solution(4280119097787947394)
XLA Ops:
  0.0 0.0 copy-start
  0.0 0.0 copy-start.1
  0.0 0.0 copy-start.2
  0.0 2.1 %far_message.1 = (f32[144,1024]{1,0:T(8,128)S(1)}, f32[64,1024]{1,0:T(8,128)S(1)}) custom-call(f32[8,64,1024]{2,1,0:T(8,128)} %bitcast.3, f32[3,8,64,1024]{3,2,1,0:T(8,128)} %v.3, f32[8,64,1024]{2,1,0:T(8,128)} %d.3), custom_call_target="tpu_custom_call" | custom-call | flops 15000000 | bytes 3000000 | tf_op jit(solution)/shard_map/far_message/pallas_call | solution.py:148
  2.1 4.4 %collective-permute-start.2 = (f32[144,1024]{1,0:T(8,128)S(1)}, f32[144,1024]{1,0:T(8,128)S(1)}, u32[]{:S(2)}, u32[]{:S(2)}) collective-permute-start(f32[144,1024]{1,0:T(8,128)S(1)} %get-tuple-element.28.ofar), channel_id=1, source_target_pairs={{1,2},{2,1},{3,4},{4,3},{5,6},{6,5},{7,8},{8,7},{9,10},{10,9},{11,... | collective-permute-start | bytes 1769480 | tf_op jit(solution)/shard_map/ppermute | solution.py:517
  6.5 0.0 copy-done
  6.5 0.0 copy-done.1
  6.5 0.0 copy-done.2
  6.6 0.8 %near_message.1 = (f32[128,1024]{1,0:T(8,128)S(1)}, f32[80,1024]{1,0:T(8,128)S(1)}) custom-call(f32[8,64,1024]{2,1,0:T(8,128)S(1)} %bitcast.4, f32[3,8,64,1024]{3,2,1,0:T(8,128)S(1)} %copy-done, f32[8,64,1024]{2,1,0:T(8,128)S(1)} %copy-done.1, f32[64,1024]{1,0:T(8,128)S(1)} %get-tuple-element.25.rest_0_.ofac), custom_call_target="tpu_custom_call" | custom-call | flops 15000000 | bytes 12000000 | tf_op jit(solution)/shard_map/near_message/pallas_call | solution.py:148
  7.4 0.1 collective-permute-start
  7.5 0.5 collective-permute-start.1
  8.0 4.7 %collective-permute-start.3 = (f32[64,1024]{1,0:T(8,128)S(1)}, f32[64,1024]{1,0:T(8,128)S(1)}, u32[]{:S(2)}, u32[]{:S(2)}) collective-permute-start(f32[64,1024]{1,0:T(8,128)S(1)} %get-tuple-element.25.rest_0_.ofac), channel_id=1, source_target_pairs={{1,18},{2,17},{3,20},{4,19},{5,22},{6,21},{7,24},{8,23},{9,26},{10... | collective-permute-start | bytes 786440 | tf_op jit(solution)/shard_map/ppermute | solution.py:517
  12.7 0.0 collective-permute-done.1.after.rtail
  12.8 1.2 %coefs.1 = (f32[4,544,128]{2,1,0:T(8,128)S(1)}, f32[4,32,128]{2,1,0:T(8,128)S(1)}, f32[4,32,128]{2,1,0:T(8,128)S(1)}, f32[4,32,128]{2,1,0:T(8,128)S(1)}, f32[4,32,128]{2,1,0:T(8,128)S(1)}) custom-call(f32[3,8,64,1024]{3,2,1,0:T(8,128)S(1)} %copy-done, f32[8,64,1024]{2,1,0:T(8,128)S(1)} %copy-done.1, f32[80,1024]{1,0:T(8,128)S(1)} %collective-permute-done.1.after.rtail), custom_call_target="tpu_custom_call" | custom-call | flops 20000000 | bytes 9000000 | tf_op jit(solution)/shard_map/coefs/pallas_call | solution.py:193
  14.0 0.8 %collective-permute-start.4 = (f32[4,32,128]{2,1,0:T(8,128)S(1)}, f32[4,32,128]{2,1,0:T(8,128)S(1)}, u32[]{:S(2)}, u32[]{:S(2)}) collective-permute-start(f32[4,32,128]{2,1,0:T(8,128)S(1)} %get-tuple-element.30), channel_id=1, source_target_pairs={{0,1},{1,0},{2,3},{3,2},{4,5},{5,4},{6,7},{7,6},{8,9},{9,8},{10,11... | collective-permute-start | bytes 196616 | tf_op jit(solution)/shard_map/ppermute | solution.py:517
  14.7 0.0 collective-permute-start.5
  14.7 0.9 %collective-permute-done.4.after.w1 = f32[4,32,128]{2,1,0:T(8,128)S(1)} collective-permute-done((f32[4,32,128]{2,1,0:T(8,128)S(1)}, f32[4,32,128]{2,1,0:T(8,128)S(1)}, u32[]{:S(2)}, u32[]{:S(2)}) %collective-permute-start.4) | collective-permute-done | bytes 65568 | tf_op jit(solution)/shard_map/ppermute | solution.py:517
  15.6 2.0 %collective-permute-start.6 = (f32[4,32,128]{2,1,0:T(8,128)S(1)}, f32[4,32,128]{2,1,0:T(8,128)S(1)}, u32[]{:S(2)}, u32[]{:S(2)}) collective-permute-start(f32[4,32,128]{2,1,0:T(8,128)S(1)} %get-tuple-element.32), channel_id=1, source_target_pairs={{0,19},{1,18},{2,17},{3,16},{4,23},{5,22},{6,21},{7,20},{8,27},{9,... | collective-permute-start | bytes 196616 | tf_op jit(solution)/shard_map/ppermute | solution.py:517
  17.7 4.8 %interior.1 = (f32[6,64,1024]{2,1,0:T(8,128)S(1)}, f32[4,64,1024]{2,1,0:T(8,128)S(1)}, f32[512,128]{1,0:T(8,128)S(1)}, f32[512,128]{1,0:T(8,128)S(1)}, f32[8,64,128]{2,1,0:T(8,128)S(1)}) custom-call(f32[8,64,1024]{2,1,0:T(8,128)S(1)} %bitcast.5, f32[3,8,64,1024]{3,2,1,0:T(8,128)S(1)} %copy-done, f32[8,64,1024]{2,1,0:T(8,128)S(1)} %copy-done.1, ...), custom_call_target="tpu_custom_call" | custom-call | flops 60000000 | bytes 20000000 | tf_op jit(solution)/shard_map/interior/pallas_call | solution.py:265
  22.4 0.0 collective-permute-done.3.rfac
  22.4 0.0 collective-permute-done.5.w2
  22.4 0.4 collective-permute-done.6.w3
  22.8 0.0 collective-permute-done.rnear
  22.8 0.0 collective-permute-done.2.rfar
  22.8 1.2 %finish.1 = (f32[4,64,1024]{2,1,0:T(8,128)S(1)}, f32[32,32,128]{2,1,0:T(8,128)S(1)}, f32[512,128]{1,0:T(8,128)S(1)}, f32[4,4,32,128]{3,2,1,0:T(8,128)S(1)}) custom-call(f32[128,1024]{1,0:T(8,128)S(1)} %collective-permute-done.rnear, f32[80,1024]{1,0:T(8,128)S(1)} %collective-permute-done.1.after.rtail, f32[144,1024]{1,0:T(8,128)S(1)} %collective-permute-done.2.rfar, ...), custom_call_target="tpu_custom_call" | custom-call | tf_op jit(solution)/shard_map/finish/pallas_call | solution.py:342
  24.0 18.4 %all_to_all.10.got = f32[32,32,128]{2,1,0:T(8,128)S(1)} all-to-all(f32[32,32,128]{2,1,0:T(8,128)S(1)} %get-tuple-element.39), channel_id=1, replica_groups=mesh['tm'=8,'px'=4,'pz'=2,'core'=2] {'tm','pz','core'}, dimensions={0} | all-to-all | bytes 1048576 | tf_op jit(solution)/shard_map/all_to_all | solution.py:553
  42.4 0.1 pick.1
  42.5 0.2 collective-permute-start.7
  42.8 2.6 %collective-permute-start.8 = (f32[13,32,128]{2,1,0:T(8,128)S(1)}, f32[13,32,128]{2,1,0:T(8,128)S(1)}, u32[]{:S(2)}, u32[]{:S(2)}) collective-permute-start(f32[13,32,128]{2,1,0:T(8,128)S(1)} %get-tuple-element.42), channel_id=1, source_target_pairs={{4,8},{8,4},{5,9},{9,5},{6,10},{10,6},{7,11},{11,7},{20,24},{24,20... | collective-permute-start | bytes 638984 | tf_op jit(solution)/shard_map/ppermute | solution.py:517
  45.3 4.3 %collective-permute-done.7.even = f32[13,32,128]{2,1,0:T(8,128)S(1)} collective-permute-done((f32[13,32,128]{2,1,0:T(8,128)S(1)}, f32[13,32,128]{2,1,0:T(8,128)S(1)}, u32[]{:S(2)}, u32[]{:S(2)}) %collective-permute-start.7) | collective-permute-done | bytes 213024 | tf_op jit(solution)/shard_map/ppermute | solution.py:517
  49.6 1.9 %collective-permute-done.8.odd = f32[13,32,128]{2,1,0:T(8,128)S(1)} collective-permute-done((f32[13,32,128]{2,1,0:T(8,128)S(1)}, f32[13,32,128]{2,1,0:T(8,128)S(1)}, u32[]{:S(2)}, u32[]{:S(2)}) %collective-permute-start.8) | collective-permute-done | bytes 213024 | tf_op jit(solution)/shard_map/ppermute | solution.py:517
  51.5 1.4 %chain.1 = f32[32,16,128]{2,1,0:T(8,128)S(1)} custom-call(f32[32,32,128]{2,1,0:T(8,128)S(1)} %all_to_all.10.got, f32[4,4,32,128]{3,2,1,0:T(8,128)S(1)} %get-tuple-element.40.quad, f32[13,32,128]{2,1,0:T(8,128)S(1)} %collective-permute-done.7.even, f32[13,32,128]{2,1,0:T(8,128)S(1)} %collective-permute-done.8.odd), custom_call_target="tpu_custom_call" | custom-call | tf_op jit(solution)/shard_map/chain/pallas_call | solution.py:462
  52.9 13.0 %all_to_all.11 = f32[32,16,128]{2,1,0:T(8,128)S(1)} all-to-all(f32[32,16,128]{2,1,0:T(8,128)S(1)} %chain.1), channel_id=1, replica_groups=mesh['tm'=8,'px'=4,'pz'=2,'core'=2] {'tm','pz','core'}, dimensions={0} | all-to-all | bytes 524288 | tf_op jit(solution)/shard_map/all_to_all | solution.py:557
  65.9 1.9 %result.1 = f32[8,64,1024]{2,1,0:T(8,128)} custom-call(f32[512,128]{1,0:T(8,128)S(1)} %bitcast.6, f32[512,128]{1,0:T(8,128)S(1)} %get-tuple-element.43.gc, f32[6,64,1024]{2,1,0:T(8,128)S(1)} %get-tuple-element.34.fin, f32[4,64,1024]{2,1,0:T(8,128)S(1)} %get-tuple-element.44.ub), custom_call_target="tpu_custom_call" | custom-call | tf_op jit(solution)/shard_map/result/pallas_call | solution.py:500
Async XLA Ops:
  0.0 6.5 %copy-start = (f32[3,8,64,1024]{3,2,1,0:T(8,128)S(1)}, f32[3,8,64,1024]{3,2,1,0:T(8,128)}, u32[]{:S(2)}) copy-start(f32[3,8,64,1024]{3,2,1,0:T(8,128)} %v.3) | copy-start | bytes 18874372
  0.0 6.5 %copy-start.1 = (f32[8,64,1024]{2,1,0:T(8,128)S(1)}, f32[8,64,1024]{2,1,0:T(8,128)}, u32[]{:S(2)}) copy-start(f32[8,64,1024]{2,1,0:T(8,128)} %d.3) | copy-start | bytes 6291460
  0.0 6.5 %copy-start.2 = (f32[1,8,64,1024]{3,2,1,0:T(8,128)S(1)}, f32[1,8,64,1024]{3,2,1,0:T(8,128)}, u32[]{:S(2)}) copy-start(f32[1,8,64,1024]{3,2,1,0:T(8,128)} %param.3) | copy-start | bytes 6291460
  2.1 20.7 %collective-permute-start.2 = (f32[144,1024]{1,0:T(8,128)S(1)}, f32[144,1024]{1,0:T(8,128)S(1)}, u32[]{:S(2)}, u32[]{:S(2)}) collective-permute-start(f32[144,1024]{1,0:T(8,128)S(1)} %get-tuple-element.28.ofar), channel_id=1, source_target_pairs={{1,2},{2,1},{3,4},{4,3},{5,6},{6,5},{7,8},{8,7},{9,10},{10,9},{11,... | collective-permute-start | bytes 1769480 | tf_op jit(solution)/shard_map/ppermute | solution.py:517
  7.4 15.4 %collective-permute-start = (f32[128,1024]{1,0:T(8,128)S(1)}, f32[128,1024]{1,0:T(8,128)S(1)}, u32[]{:S(2)}, u32[]{:S(2)}) collective-permute-start(f32[128,1024]{1,0:T(8,128)S(1)} %get-tuple-element.26.onear), channel_id=1, source_target_pairs={{0,1},{1,0},{2,3},{3,2},{4,5},{5,4},{6,7},{7,6},{8,9},{9,8},{10,11... | collective-permute-start | bytes 1572872 | tf_op jit(solution)/shard_map/ppermute | solution.py:517
  7.5 5.3 %collective-permute-start.1 = (f32[80,1024]{1,0:T(8,128)S(1)}, f32[80,1024]{1,0:T(8,128)S(1)}, u32[]{:S(2)}, u32[]{:S(2)}) collective-permute-start(f32[80,1024]{1,0:T(8,128)S(1)} %get-tuple-element.27.otail), channel_id=1, source_target_pairs={{0,1},{1,0},{2,3},{3,2},{4,5},{5,4},{6,7},{7,6},{8,9},{9,8},{10,11... | collective-permute-start | bytes 983048 | tf_op jit(solution)/shard_map/ppermute | solution.py:517
  8.0 14.4 %collective-permute-start.3 = (f32[64,1024]{1,0:T(8,128)S(1)}, f32[64,1024]{1,0:T(8,128)S(1)}, u32[]{:S(2)}, u32[]{:S(2)}) collective-permute-start(f32[64,1024]{1,0:T(8,128)S(1)} %get-tuple-element.25.rest_0_.ofac), channel_id=1, source_target_pairs={{1,18},{2,17},{3,20},{4,19},{5,22},{6,21},{7,24},{8,23},{9,26},{10... | collective-permute-start | bytes 786440 | tf_op jit(solution)/shard_map/ppermute | solution.py:517
  14.0 1.7 %collective-permute-start.4 = (f32[4,32,128]{2,1,0:T(8,128)S(1)}, f32[4,32,128]{2,1,0:T(8,128)S(1)}, u32[]{:S(2)}, u32[]{:S(2)}) collective-permute-start(f32[4,32,128]{2,1,0:T(8,128)S(1)} %get-tuple-element.30), channel_id=1, source_target_pairs={{0,1},{1,0},{2,3},{3,2},{4,5},{5,4},{6,7},{7,6},{8,9},{9,8},{10,11... | collective-permute-start | bytes 196616 | tf_op jit(solution)/shard_map/ppermute | solution.py:517
  14.7 7.7 %collective-permute-start.5 = (f32[4,32,128]{2,1,0:T(8,128)S(1)}, f32[4,32,128]{2,1,0:T(8,128)S(1)}, u32[]{:S(2)}, u32[]{:S(2)}) collective-permute-start(f32[4,32,128]{2,1,0:T(8,128)S(1)} %get-tuple-element.31), channel_id=1, source_target_pairs={{0,18},{1,19},{2,16},{3,17},{4,22},{5,23},{6,20},{7,21},{8,26},{9,... | collective-permute-start | bytes 196616 | tf_op jit(solution)/shard_map/ppermute | solution.py:517
  15.6 7.2 %collective-permute-start.6 = (f32[4,32,128]{2,1,0:T(8,128)S(1)}, f32[4,32,128]{2,1,0:T(8,128)S(1)}, u32[]{:S(2)}, u32[]{:S(2)}) collective-permute-start(f32[4,32,128]{2,1,0:T(8,128)S(1)} %get-tuple-element.32), channel_id=1, source_target_pairs={{0,19},{1,18},{2,17},{3,16},{4,23},{5,22},{6,21},{7,20},{8,27},{9,... | collective-permute-start | bytes 196616 | tf_op jit(solution)/shard_map/ppermute | solution.py:517
  42.5 7.1 %collective-permute-start.7 = (f32[13,32,128]{2,1,0:T(8,128)S(1)}, f32[13,32,128]{2,1,0:T(8,128)S(1)}, u32[]{:S(2)}, u32[]{:S(2)}) collective-permute-start(f32[13,32,128]{2,1,0:T(8,128)S(1)} %get-tuple-element.41), channel_id=1, source_target_pairs={{0,4},{4,0},{8,12},{12,8},{1,5},{5,1},{9,13},{13,9},{2,6},{6,2},{1... | collective-permute-start | bytes 638984 | tf_op jit(solution)/shard_map/ppermute | solution.py:517
  42.8 8.7 %collective-permute-start.8 = (f32[13,32,128]{2,1,0:T(8,128)S(1)}, f32[13,32,128]{2,1,0:T(8,128)S(1)}, u32[]{:S(2)}, u32[]{:S(2)}) collective-permute-start(f32[13,32,128]{2,1,0:T(8,128)S(1)} %get-tuple-element.42), channel_id=1, source_target_pairs={{4,8},{8,4},{5,9},{9,5},{6,10},{10,6},{7,11},{11,7},{20,24},{24,20... | collective-permute-start | bytes 638984 | tf_op jit(solution)/shard_map/ppermute | solution.py:517

commit v10 on v9

--- a/solution.py
+++ b/solution.py
@@ -285,6 +285,15 @@
     )(state, velocity, diffusivity, ct, after)
 
 
+def at_end():
+    slab = lax.axis_index("px") * QUAD + quad_rank()
+    return (slab == 0) | (slab == 15)
+
+
+def dropped(beyond, value):
+    return value if beyond is False else jnp.where(beyond, 0.0, value)
+
+
 def finish_kernel(
     rnear, rtail, rfar, rfac, onear, otail, ofar, ofac, w0, w1, w2, w3, fin, edge, v, d, gcp, cb, ymid,
     ub, msg, gc, quad, u1, zs, jp,
@@ -295,13 +304,15 @@
     for kind, (rec, own, recb, ownb, at) in enumerate(((rnear, onear, rtail, otail, 16), (rfar, ofar, rfac, ofac, 0))):
         top = edge_is_top(kind)
         side = jnp.where(top, 1, 0)
+        beyond = kind == 1 and at_end()
         for r in range(0, NY, 8):
             u1[kind, r : r + 8, :] = (
-                own[NY + r : NY + r + 8, :] + ownb[at + r : at + r + 8, :] * rec[r : r + 8, :]
+                own[NY + r : NY + r + 8, :] + ownb[at + r : at + r + 8, :] * dropped(beyond, rec[r : r + 8, :])
             )
         z = side * (LZ - 1)
         for r, rows, (c, w, e, s, n) in planes(u1, kind):
             outside = rec[NY + r : NY + r + 8, :] + recb[at + r : at + r + 8, :] * own[r : r + 8, :]
+            outside = dropped(beyond, outside)
             inside = edge[side, rows, :]
             ax, ay, az, k = v[0, z, rows, :], v[1, z, rows, :], v[2, z, rows, :], d[z, rows, :]
             last = advanced(c, w, e, s, n, inside, outside, ax, ay, jnp.where(top, az, -az), k)
@@ -312,6 +323,7 @@
     lane = lax.broadcasted_iota(jnp.int32, (128, 128), 1)
     hnear = jnp.concatenate([rtail[0:16, 128 * i : 128 * i + 128] for i in range(8)], axis=0)
     hfar = jnp.concatenate([rfar[2 * NY : FAR, 128 * i : 128 * i + 128] for i in range(8)], axis=0)
+    hfar = dropped(at_end(), hfar)
     first_core = lax.axis_index("core") == 0
     halo_lo, halo_hi = jnp.where(first_core, hfar, hnear), jnp.where(first_core, hnear, hfar)
     for b in range(4):
@@ -398,13 +410,14 @@
 
 
 def chain_kernel(got, quad, even, odd, out, cf, e):
-    first = lax.rem(lax.axis_index("px"), 2) == 0
+    place = lax.axis_index("px")
+    first = lax.rem(place, 2) == 0
 
     def below(i):
-        return jnp.where(first, odd[i], even[i])
+        return jnp.where(place == 0, 0.0, jnp.where(first, odd[i], even[i]))
 
     def above(i):
-        return jnp.where(first, even[i], odd[i])
+        return jnp.where(place == 3, 0.0, jnp.where(first, even[i], odd[i]))
 
     def source(j, block):
         if 2 <= block < 6:
@@ -513,23 +526,19 @@
 
 
 def swap(value, axes, partner):
-    pairs = [(i, partner(i)) for i in range(lax.axis_size(axes))]
-    return lax.ppermute(value, axes, [(i, j) for i, j in pairs if j is not None])
+    return lax.ppermute(value, axes, [(i, partner(i)) for i in range(lax.axis_size(axes))])
 
 
 def off_chip(i):
-    j = i + 1 if i % 2 else i - 1
-    return j if 0 <= j < 16 else None
+    return (i + 1 if i % 2 else i - 1) % 16
 
 
 def off_chip_copy(i):
-    j = off_chip(i % 16)
-    return None if j is None else (i // 16 ^ 1) * 16 + j
+    return (i // 16 ^ 1) * 16 + off_chip(i % 16)
 
 
 def quad_beside(i):
-    j = i + 1 if i % 2 else i - 1
-    return j if 0 <= j < 4 else None
+    return (i + 1 if i % 2 else i - 1) % 4
 
 
 def shards(state_old, velocity, diffusivity):

time: 68.4 us -> 66.6 us (0.974)
  the two profiles are of different devices: /device:TPU:5 before, /device:TPU:1 now
where the time goes in v10:
time: 66.6 us; the launch traced here: 66.5 us
  blocking collectives  29.7 us (45%)
  starting transfers between devices  15.6 us (23%)
  Pallas kernels  13.5 us (20%)
  waiting for transfers between devices  7.57 us (11%)
    all_to_all x1, blocking collectives, shards(): got = lax.all_to_all(msg, GROUP, 0, 0)  16.8 us
    ppermute x9, starting transfers between devices, swap(): lax.ppermute(value, axes, [(i, partner(i)) for i in range(lax.axis_size(a...  15.6 us
    all_to_all x1, blocking collectives, shards(): back = lax.all_to_all(chain(got, quad, even, odd), GROUP, 0, 0)  13 us
    ppermute x9, waiting for transfers between devices, swap(): lax.ppermute(value, axes, [(i, partner(i)) for i in range(lax.axis_size(a...  7.57 us
    pallas_call x1, Pallas kernels, interior(): pl.pallas_call(interior_kernel, out_shape=[jax.ShapeDtypeStruct((LZ - 2,...  4.76 us
    pallas_call x2, Pallas kernels, edge_message(): pl.pallas_call(functools.partial(edge_kernel, kind), out_shape=[jax.Shape...  2.95 us
    pallas_call x1, Pallas kernels, result(): pl.pallas_call(result_kernel, out_shape=jax.ShapeDtypeStruct((LZ, NY, NX)...  1.87 us
    pallas_call x1, Pallas kernels, chain(): pl.pallas_call(chain_kernel, out_shape=jax.ShapeDtypeStruct((BLOCKS, XB,...  1.41 us
  transfers between devices with their start and end apart: 9, of which 4 were waited for; matrix products, arithmetic and copies ran while one was open for 0% of the time, Pallas kernels for 10%

profile of v10, /device:TPU:1, one launch (start us, length us, event | category | flops | bytes accessed | tf_op | source)
XLA Modules:
  0.0 66.5 jit_solution(10779666391656936508)
XLA Ops:
  0.0 0.0 copy-start
  0.0 0.0 copy-start.1
  0.0 0.0 copy-start.2
  0.0 2.1 %far_message.1 = (f32[144,1024]{1,0:T(8,128)S(1)}, f32[64,1024]{1,0:T(8,128)S(1)}) custom-call(f32[8,64,1024]{2,1,0:T(8,128)} %bitcast.3, f32[3,8,64,1024]{3,2,1,0:T(8,128)} %v.3, f32[8,64,1024]{2,1,0:T(8,128)} %d.3), custom_call_target="tpu_custom_call" | custom-call | flops 15000000 | bytes 3000000 | tf_op jit(solution)/shard_map/far_message/pallas_call | solution.py:148
  2.1 3.1 %collective-permute-start.2 = (f32[144,1024]{1,0:T(8,128)S(1)}, f32[144,1024]{1,0:T(8,128)S(1)}, u32[]{:S(2)}, u32[]{:S(2)}) collective-permute-start(f32[144,1024]{1,0:T(8,128)S(1)} %get-tuple-element.28.ofar), channel_id=1, source_target_pairs={{0,15},{1,2},{2,1},{3,4},{4,3},{5,6},{6,5},{7,8},{8,7},{9,10},{10,... | collective-permute-start | bytes 1769480 | tf_op jit(solution)/shard_map/ppermute | solution.py:529
  5.3 0.0 copy-done
  5.3 0.0 copy-done.1
  5.3 0.0 copy-done.2
  5.3 0.8 %near_message.1 = (f32[128,1024]{1,0:T(8,128)S(1)}, f32[80,1024]{1,0:T(8,128)S(1)}) custom-call(f32[8,64,1024]{2,1,0:T(8,128)S(1)} %bitcast.4, f32[3,8,64,1024]{3,2,1,0:T(8,128)S(1)} %copy-done, f32[8,64,1024]{2,1,0:T(8,128)S(1)} %copy-done.1, f32[64,1024]{1,0:T(8,128)S(1)} %get-tuple-element.25.rest_0_.ofac), custom_call_target="tpu_custom_call" | custom-call | flops 15000000 | bytes 12000000 | tf_op jit(solution)/shard_map/near_message/pallas_call | solution.py:148
  6.1 2.1 %collective-permute-start = (f32[128,1024]{1,0:T(8,128)S(1)}, f32[128,1024]{1,0:T(8,128)S(1)}, u32[]{:S(2)}, u32[]{:S(2)}) collective-permute-start(f32[128,1024]{1,0:T(8,128)S(1)} %get-tuple-element.26.onear), channel_id=1, source_target_pairs={{0,1},{1,0},{2,3},{3,2},{4,5},{5,4},{6,7},{7,6},{8,9},{9,8},{10,11... | collective-permute-start | bytes 1572872 | tf_op jit(solution)/shard_map/ppermute | solution.py:529
  8.2 0.1 collective-permute-start.1
  8.3 2.7 %collective-permute-start.3 = (f32[64,1024]{1,0:T(8,128)S(1)}, f32[64,1024]{1,0:T(8,128)S(1)}, u32[]{:S(2)}, u32[]{:S(2)}) collective-permute-start(f32[64,1024]{1,0:T(8,128)S(1)} %get-tuple-element.25.rest_0_.ofac), channel_id=1, source_target_pairs={{0,31},{1,18},{2,17},{3,20},{4,19},{5,22},{6,21},{7,24},{8,23},{9,... | collective-permute-start | bytes 786440 | tf_op jit(solution)/shard_map/ppermute | solution.py:529
  11.0 0.0 collective-permute-done.1.after.rtail
  11.0 1.2 %coefs.1 = (f32[4,544,128]{2,1,0:T(8,128)S(1)}, f32[4,32,128]{2,1,0:T(8,128)S(1)}, f32[4,32,128]{2,1,0:T(8,128)S(1)}, f32[4,32,128]{2,1,0:T(8,128)S(1)}, f32[4,32,128]{2,1,0:T(8,128)S(1)}) custom-call(f32[3,8,64,1024]{3,2,1,0:T(8,128)S(1)} %copy-done, f32[8,64,1024]{2,1,0:T(8,128)S(1)} %copy-done.1, f32[80,1024]{1,0:T(8,128)S(1)} %collective-permute-done.1.after.rtail), custom_call_target="tpu_custom_call" | custom-call | flops 20000000 | bytes 9000000 | tf_op jit(solution)/shard_map/coefs/pallas_call | solution.py:193
  12.2 2.4 %collective-permute-start.4 = (f32[4,32,128]{2,1,0:T(8,128)S(1)}, f32[4,32,128]{2,1,0:T(8,128)S(1)}, u32[]{:S(2)}, u32[]{:S(2)}) collective-permute-start(f32[4,32,128]{2,1,0:T(8,128)S(1)} %get-tuple-element.30), channel_id=1, source_target_pairs={{0,1},{1,0},{2,3},{3,2},{4,5},{5,4},{6,7},{7,6},{8,9},{9,8},{10,11... | collective-permute-start | bytes 196616 | tf_op jit(solution)/shard_map/ppermute | solution.py:529
  14.6 0.0 collective-permute-start.5
  14.6 0.9 %collective-permute-done.4.after.w1 = f32[4,32,128]{2,1,0:T(8,128)S(1)} collective-permute-done((f32[4,32,128]{2,1,0:T(8,128)S(1)}, f32[4,32,128]{2,1,0:T(8,128)S(1)}, u32[]{:S(2)}, u32[]{:S(2)}) %collective-permute-start.4) | collective-permute-done | bytes 65568 | tf_op jit(solution)/shard_map/ppermute | solution.py:529
  15.5 2.0 %collective-permute-start.6 = (f32[4,32,128]{2,1,0:T(8,128)S(1)}, f32[4,32,128]{2,1,0:T(8,128)S(1)}, u32[]{:S(2)}, u32[]{:S(2)}) collective-permute-start(f32[4,32,128]{2,1,0:T(8,128)S(1)} %get-tuple-element.32), channel_id=1, source_target_pairs={{0,19},{1,18},{2,17},{3,16},{4,23},{5,22},{6,21},{7,20},{8,27},{9,... | collective-permute-start | bytes 196616 | tf_op jit(solution)/shard_map/ppermute | solution.py:529
  17.5 4.8 %interior.1 = (f32[6,64,1024]{2,1,0:T(8,128)S(1)}, f32[4,64,1024]{2,1,0:T(8,128)S(1)}, f32[512,128]{1,0:T(8,128)S(1)}, f32[512,128]{1,0:T(8,128)S(1)}, f32[8,64,128]{2,1,0:T(8,128)S(1)}) custom-call(f32[8,64,1024]{2,1,0:T(8,128)S(1)} %bitcast.5, f32[3,8,64,1024]{3,2,1,0:T(8,128)S(1)} %copy-done, f32[8,64,1024]{2,1,0:T(8,128)S(1)} %copy-done.1, ...), custom_call_target="tpu_custom_call" | custom-call | flops 60000000 | bytes 20000000 | tf_op jit(solution)/shard_map/interior/pallas_call | solution.py:265
  22.3 0.0 collective-permute-done.3.rfac
  22.3 0.0 collective-permute-done.5.w2
  22.3 0.4 collective-permute-done.6.w3
  22.8 0.0 collective-permute-done.rnear
  22.8 0.0 collective-permute-done.2.rfar
  22.8 1.2 %finish.1 = (f32[4,64,1024]{2,1,0:T(8,128)S(1)}, f32[32,32,128]{2,1,0:T(8,128)S(1)}, f32[512,128]{1,0:T(8,128)S(1)}, f32[4,4,32,128]{3,2,1,0:T(8,128)S(1)}) custom-call(f32[128,1024]{1,0:T(8,128)S(1)} %collective-permute-done.rnear, f32[80,1024]{1,0:T(8,128)S(1)} %collective-permute-done.1.after.rtail, f32[144,1024]{1,0:T(8,128)S(1)} %collective-permute-done.2.rfar, ...), custom_call_target="tpu_custom_call" | custom-call | tf_op jit(solution)/shard_map/finish/pallas_call | solution.py:354
  24.0 16.8 %all_to_all.10.got = f32[32,32,128]{2,1,0:T(8,128)S(1)} all-to-all(f32[32,32,128]{2,1,0:T(8,128)S(1)} %get-tuple-element.39), channel_id=1, replica_groups=mesh['tm'=8,'px'=4,'pz'=2,'core'=2] {'tm','pz','core'}, dimensions={0} | all-to-all | bytes 1048576 | tf_op jit(solution)/shard_map/all_to_all | solution.py:562
  40.7 0.1 pick.1
  40.8 1.3 %collective-permute-start.7 = (f32[13,32,128]{2,1,0:T(8,128)S(1)}, f32[13,32,128]{2,1,0:T(8,128)S(1)}, u32[]{:S(2)}, u32[]{:S(2)}) collective-permute-start(f32[13,32,128]{2,1,0:T(8,128)S(1)} %get-tuple-element.41), channel_id=1, source_target_pairs={{0,4},{4,0},{8,12},{12,8},{1,5},{5,1},{9,13},{13,9},{2,6},{6,2},{1... | collective-permute-start | bytes 638984 | tf_op jit(solution)/shard_map/ppermute | solution.py:529
  42.1 1.8 %collective-permute-start.8 = (f32[13,32,128]{2,1,0:T(8,128)S(1)}, f32[13,32,128]{2,1,0:T(8,128)S(1)}, u32[]{:S(2)}, u32[]{:S(2)}) collective-permute-start(f32[13,32,128]{2,1,0:T(8,128)S(1)} %get-tuple-element.42), channel_id=1, source_target_pairs={{0,12},{4,8},{8,4},{12,0},{1,13},{5,9},{9,5},{13,1},{2,14},{6,10},... | collective-permute-start | bytes 638984 | tf_op jit(solution)/shard_map/ppermute | solution.py:529
  44.0 4.0 %collective-permute-done.7.even = f32[13,32,128]{2,1,0:T(8,128)S(1)} collective-permute-done((f32[13,32,128]{2,1,0:T(8,128)S(1)}, f32[13,32,128]{2,1,0:T(8,128)S(1)}, u32[]{:S(2)}, u32[]{:S(2)}) %collective-permute-start.7) | collective-permute-done | bytes 213024 | tf_op jit(solution)/shard_map/ppermute | solution.py:529
  47.9 2.2 %collective-permute-done.8.odd = f32[13,32,128]{2,1,0:T(8,128)S(1)} collective-permute-done((f32[13,32,128]{2,1,0:T(8,128)S(1)}, f32[13,32,128]{2,1,0:T(8,128)S(1)}, u32[]{:S(2)}, u32[]{:S(2)}) %collective-permute-start.8) | collective-permute-done | bytes 213024 | tf_op jit(solution)/shard_map/ppermute | solution.py:529
  50.2 1.4 %chain.1 = f32[32,16,128]{2,1,0:T(8,128)S(1)} custom-call(f32[32,32,128]{2,1,0:T(8,128)S(1)} %all_to_all.10.got, f32[4,4,32,128]{3,2,1,0:T(8,128)S(1)} %get-tuple-element.40.quad, f32[13,32,128]{2,1,0:T(8,128)S(1)} %collective-permute-done.7.even, f32[13,32,128]{2,1,0:T(8,128)S(1)} %collective-permute-done.8.odd), custom_call_target="tpu_custom_call" | custom-call | tf_op jit(solution)/shard_map/chain/pallas_call | solution.py:475
  51.6 13.0 %all_to_all.11 = f32[32,16,128]{2,1,0:T(8,128)S(1)} all-to-all(f32[32,16,128]{2,1,0:T(8,128)S(1)} %chain.1), channel_id=1, replica_groups=mesh['tm'=8,'px'=4,'pz'=2,'core'=2] {'tm','pz','core'}, dimensions={0} | all-to-all | bytes 524288 | tf_op jit(solution)/shard_map/all_to_all | solution.py:566
  64.6 1.9 %result.1 = f32[8,64,1024]{2,1,0:T(8,128)} custom-call(f32[512,128]{1,0:T(8,128)S(1)} %bitcast.6, f32[512,128]{1,0:T(8,128)S(1)} %get-tuple-element.43.gc, f32[6,64,1024]{2,1,0:T(8,128)S(1)} %get-tuple-element.34.fin, f32[4,64,1024]{2,1,0:T(8,128)S(1)} %get-tuple-element.44.ub), custom_call_target="tpu_custom_call" | custom-call | tf_op jit(solution)/shard_map/result/pallas_call | solution.py:513
Async XLA Ops:
  0.0 5.3 %copy-start = (f32[3,8,64,1024]{3,2,1,0:T(8,128)S(1)}, f32[3,8,64,1024]{3,2,1,0:T(8,128)}, u32[]{:S(2)}) copy-start(f32[3,8,64,1024]{3,2,1,0:T(8,128)} %v.3) | copy-start | bytes 18874372
  0.0 5.3 %copy-start.1 = (f32[8,64,1024]{2,1,0:T(8,128)S(1)}, f32[8,64,1024]{2,1,0:T(8,128)}, u32[]{:S(2)}) copy-start(f32[8,64,1024]{2,1,0:T(8,128)} %d.3) | copy-start | bytes 6291460
  0.0 5.3 %copy-start.2 = (f32[1,8,64,1024]{3,2,1,0:T(8,128)S(1)}, f32[1,8,64,1024]{3,2,1,0:T(8,128)}, u32[]{:S(2)}) copy-start(f32[1,8,64,1024]{3,2,1,0:T(8,128)} %param.3) | copy-start | bytes 6291460
  2.1 20.6 %collective-permute-start.2 = (f32[144,1024]{1,0:T(8,128)S(1)}, f32[144,1024]{1,0:T(8,128)S(1)}, u32[]{:S(2)}, u32[]{:S(2)}) collective-permute-start(f32[144,1024]{1,0:T(8,128)S(1)} %get-tuple-element.28.ofar), channel_id=1, source_target_pairs={{0,15},{1,2},{2,1},{3,4},{4,3},{5,6},{6,5},{7,8},{8,7},{9,10},{10,... | collective-permute-start | bytes 1769480 | tf_op jit(solution)/shard_map/ppermute | solution.py:529
  6.1 16.7 %collective-permute-start = (f32[128,1024]{1,0:T(8,128)S(1)}, f32[128,1024]{1,0:T(8,128)S(1)}, u32[]{:S(2)}, u32[]{:S(2)}) collective-permute-start(f32[128,1024]{1,0:T(8,128)S(1)} %get-tuple-element.26.onear), channel_id=1, source_target_pairs={{0,1},{1,0},{2,3},{3,2},{4,5},{5,4},{6,7},{7,6},{8,9},{9,8},{10,11... | collective-permute-start | bytes 1572872 | tf_op jit(solution)/shard_map/ppermute | solution.py:529
  8.2 2.8 %collective-permute-start.1 = (f32[80,1024]{1,0:T(8,128)S(1)}, f32[80,1024]{1,0:T(8,128)S(1)}, u32[]{:S(2)}, u32[]{:S(2)}) collective-permute-start(f32[80,1024]{1,0:T(8,128)S(1)} %get-tuple-element.27.otail), channel_id=1, source_target_pairs={{0,1},{1,0},{2,3},{3,2},{4,5},{5,4},{6,7},{7,6},{8,9},{9,8},{10,11... | collective-permute-start | bytes 983048 | tf_op jit(solution)/shard_map/ppermute | solution.py:529
  8.3 14.0 %collective-permute-start.3 = (f32[64,1024]{1,0:T(8,128)S(1)}, f32[64,1024]{1,0:T(8,128)S(1)}, u32[]{:S(2)}, u32[]{:S(2)}) collective-permute-start(f32[64,1024]{1,0:T(8,128)S(1)} %get-tuple-element.25.rest_0_.ofac), channel_id=1, source_target_pairs={{0,31},{1,18},{2,17},{3,20},{4,19},{5,22},{6,21},{7,24},{8,23},{9,... | collective-permute-start | bytes 786440 | tf_op jit(solution)/shard_map/ppermute | solution.py:529
  12.2 3.3 %collective-permute-start.4 = (f32[4,32,128]{2,1,0:T(8,128)S(1)}, f32[4,32,128]{2,1,0:T(8,128)S(1)}, u32[]{:S(2)}, u32[]{:S(2)}) collective-permute-start(f32[4,32,128]{2,1,0:T(8,128)S(1)} %get-tuple-element.30), channel_id=1, source_target_pairs={{0,1},{1,0},{2,3},{3,2},{4,5},{5,4},{6,7},{7,6},{8,9},{9,8},{10,11... | collective-permute-start | bytes 196616 | tf_op jit(solution)/shard_map/ppermute | solution.py:529
  14.6 7.7 %collective-permute-start.5 = (f32[4,32,128]{2,1,0:T(8,128)S(1)}, f32[4,32,128]{2,1,0:T(8,128)S(1)}, u32[]{:S(2)}, u32[]{:S(2)}) collective-permute-start(f32[4,32,128]{2,1,0:T(8,128)S(1)} %get-tuple-element.31), channel_id=1, source_target_pairs={{0,18},{1,19},{2,16},{3,17},{4,22},{5,23},{6,20},{7,21},{8,26},{9,... | collective-permute-start | bytes 196616 | tf_op jit(solution)/shard_map/ppermute | solution.py:529
  15.5 7.3 %collective-permute-start.6 = (f32[4,32,128]{2,1,0:T(8,128)S(1)}, f32[4,32,128]{2,1,0:T(8,128)S(1)}, u32[]{:S(2)}, u32[]{:S(2)}) collective-permute-start(f32[4,32,128]{2,1,0:T(8,128)S(1)} %get-tuple-element.32), channel_id=1, source_target_pairs={{0,19},{1,18},{2,17},{3,16},{4,23},{5,22},{6,21},{7,20},{8,27},{9,... | collective-permute-start | bytes 196616 | tf_op jit(solution)/shard_map/ppermute | solution.py:529
  40.8 7.1 %collective-permute-start.7 = (f32[13,32,128]{2,1,0:T(8,128)S(1)}, f32[13,32,128]{2,1,0:T(8,128)S(1)}, u32[]{:S(2)}, u32[]{:S(2)}) collective-permute-start(f32[13,32,128]{2,1,0:T(8,128)S(1)} %get-tuple-element.41), channel_id=1, source_target_pairs={{0,4},{4,0},{8,12},{12,8},{1,5},{5,1},{9,13},{13,9},{2,6},{6,2},{1... | collective-permute-start | bytes 638984 | tf_op jit(solution)/shard_map/ppermute | solution.py:529
  42.1 8.0 %collective-permute-start.8 = (f32[13,32,128]{2,1,0:T(8,128)S(1)}, f32[13,32,128]{2,1,0:T(8,128)S(1)}, u32[]{:S(2)}, u32[]{:S(2)}) collective-permute-start(f32[13,32,128]{2,1,0:T(8,128)S(1)} %get-tuple-element.42), channel_id=1, source_target_pairs={{0,12},{4,8},{8,4},{12,0},{1,13},{5,9},{9,5},{13,1},{2,14},{6,10},... | collective-permute-start | bytes 638984 | tf_op jit(solution)/shard_map/ppermute | solution.py:529

commit v11 on v10

--- a/solution.py
+++ b/solution.py
@@ -295,12 +295,9 @@
 
 
 def finish_kernel(
-    rnear, rtail, rfar, rfac, onear, otail, ofar, ofac, w0, w1, w2, w3, fin, edge, v, d, gcp, cb, ymid,
-    ub, msg, gc, quad, u1, zs, jp,
+    rnear, rtail, rfar, rfac, onear, otail, ofar, ofac, fin, edge, v, d, gcp, cb, ymid,
+    ub, jp, gc, u1, zs,
 ):
-    mine = quad_rank()
-    for i, window in enumerate((w0, w1, w2, w3)):
-        quad[mine ^ i] = window[...]
     for kind, (rec, own, recb, ownb, at) in enumerate(((rnear, onear, rtail, otail, 16), (rfar, ofar, rfac, ofac, 0))):
         top = edge_is_top(kind)
         side = jnp.where(top, 1, 0)
@@ -346,40 +343,63 @@
         jp[8 + 128 * b : 136 + 128 * b, :] = t - g
     jp[0:8, :] = jp[CX : CX + 8, :]
     jp[CX + 8 : CX + 24, :] = jp[8:24, :]
-    for i in range(BLOCKS):
-        msg[i] = jp[XB * i : XB * i + WIN, :]
-
-
-def finish(messages, windows, fin, edge, velocity, diffusivity, gcp, cb, ymid):
+
+
+def finish(messages, fin, edge, velocity, diffusivity, gcp, cb, ymid):
     return pl.pallas_call(
         finish_kernel,
         out_shape=[
             jax.ShapeDtypeStruct((4, NY, NX), F32),
-            jax.ShapeDtypeStruct((BLOCKS, WIN, CL), F32),
+            jax.ShapeDtypeStruct((CX + 24, CL), F32),
             jax.ShapeDtypeStruct((CX, CL), F32),
-            jax.ShapeDtypeStruct((QUAD, 4, WIN, CL), F32),
-        ],
-        in_specs=[whole()] * 19,
-        out_specs=[whole()] * 4,
+        ],
+        in_specs=[whole()] * 15,
+        out_specs=[whole()] * 3,
         scratch_shapes=[
             pltpu.VMEM((2, NY, NX), F32),
             pltpu.VMEM((2, 8, NY, 128), F32),
-            pltpu.VMEM((CX + 24, CL), F32),
         ],
         compiler_params=params(16),
         name="finish",
-    )(*messages, *windows, fin, edge, velocity, diffusivity, gcp, cb, ymid)
-
-
-HALO = 13
+    )(*messages, fin, edge, velocity, diffusivity, gcp, cb, ymid)
+
+
+def spread_kernel(jp, w0, w1, w2, w3, msg, quad):
+    for i in range(BLOCKS):
+        msg[i] = jp[XB * i : XB * i + WIN, :]
+    mine = quad_rank()
+    for i, window in enumerate((w0, w1, w2, w3)):
+        quad[mine ^ i] = window[...]
+
+
+def spread(sources, windows):
+    return pl.pallas_call(
+        spread_kernel,
+        out_shape=[
+            jax.ShapeDtypeStruct((BLOCKS, WIN, CL), F32),
+            jax.ShapeDtypeStruct((QUAD, 4, WIN, CL), F32),
+        ],
+        in_specs=[whole()] * 5,
+        out_specs=[whole()] * 2,
+        compiler_params=params(16),
+        name="spread",
+    )(sources, *windows)
+
+
+HALO_ROWS = (32, 32, 24, 24, 24, 24, 24, 32, 32, 32, 32, 24, 24)
+HALO_AT = tuple(sum(HALO_ROWS[:i]) for i in range(len(HALO_ROWS) + 1))
 SHARED = ((0, 6, 96), (1, 5, 64), (2, 4, 32))
 
 
 def pick_kernel(got, quad, even, odd):
-    lane = lax.broadcasted_iota(jnp.int32, (WIN, CL), 1)
+    lane = lax.broadcasted_iota(jnp.int32, (24, CL), 1)
+    inner = slice(4, 28)
     for parity, out in enumerate((even, odd)):
         up = lax.rem(lax.axis_index("px"), 2) == parity
         near, far = jnp.where(up, 3, 0), jnp.where(up, 2, 1)
+
+        def put(i, value):
+            out[HALO_AT[i] : HALO_AT[i + 1], :] = value
 
         def shared(main, other, width):
             return jnp.where(
@@ -389,16 +409,16 @@
             )
 
         for j in range(4):
-            out[j] = got[QUAD * j + near]
-            out[7 + j] = quad[near, j]
+            put(j, got[QUAD * j + near] if HALO_ROWS[j] == WIN else got[QUAD * j + near, inner, :])
+            put(7 + j, quad[near, j])
         for j, other, width in SHARED:
-            out[4 + j] = shared(got[QUAD * j + far], got[QUAD * other + near], width)
+            put(4 + j, shared(got[QUAD * j + far, inner, :], got[QUAD * other + near, inner, :], width))
         for j in range(2):
-            out[11 + j] = shared(quad[far, 2 * j], quad[far, 2 * j + 1], 64)
+            put(11 + j, shared(quad[far, 2 * j, inner, :], quad[far, 2 * j + 1, inner, :], 64))
 
 
 def pick(got, quad):
-    halo = jax.ShapeDtypeStruct((HALO, WIN, CL), F32)
+    halo = jax.ShapeDtypeStruct((HALO_AT[-1], CL), F32)
     return pl.pallas_call(
         pick_kernel,
         out_shape=[halo, halo],
@@ -413,11 +433,18 @@
     place = lax.axis_index("px")
     first = lax.rem(place, 2) == 0
 
+    def block_of(ref, i):
+        value = ref[HALO_AT[i] : HALO_AT[i + 1], :]
+        if HALO_ROWS[i] == WIN:
+            return value
+        rest = jnp.zeros((4, CL), F32)
+        return jnp.concatenate([rest, value, rest], axis=0)
+
     def below(i):
-        return jnp.where(place == 0, 0.0, jnp.where(first, odd[i], even[i]))
+        return jnp.where(place == 0, 0.0, jnp.where(first, block_of(odd, i), block_of(even, i)))
 
     def above(i):
-        return jnp.where(place == 3, 0.0, jnp.where(first, even[i], odd[i]))
+        return jnp.where(place == 3, 0.0, jnp.where(first, block_of(even, i), block_of(odd, i)))
 
     def source(j, block):
         if 2 <= block < 6:
@@ -558,7 +585,8 @@
     )
     fin, edge, gcp, cb, ymid = interior(state, velocity, diffusivity, ct, windows[1])
     messages = (rnear, rtail, rfar, rfac, onear, otail, ofar, ofac)
-    ub, msg, gc, quad = finish(messages, windows, fin, edge, velocity, diffusivity, gcp, cb, ymid)
+    ub, sources, gc = finish(messages, fin, edge, velocity, diffusivity, gcp, cb, ymid)
+    msg, quad = spread(sources, windows)
     got = lax.all_to_all(msg, GROUP, 0, 0)
     even, odd = pick(got, quad)
     even = swap(even, "px", lambda i: i ^ 1)

time: 66.6 us -> 65.5 us (0.983)
  waiting for transfers between devices: 7.57 us -> 6.51 us
    ppermute x9, waiting for transfers between devices: 7.57 us -> 6.51 us  [swap(): lax.ppermute(value, axes, [(i, partner(i)) for i in range(lax.axis_size(a...]
  transfers between devices with their start and end apart: 9 -> 9, of which waited for: 4 -> 3; matrix products, arithmetic and copies ran while one was open for 0% -> 0% of each run, Pallas kernels for 10% -> 12%
where the time goes in v11:
time: 65.5 us; the launch traced here: 65.3 us
  blocking collectives  29.8 us (45%)
  starting transfers between devices  15.3 us (23%)
  Pallas kernels  13.6 us (21%)
  waiting for transfers between devices  6.51 us (10%)
    all_to_all x1, blocking collectives, shards(): got = lax.all_to_all(msg, GROUP, 0, 0)  16.8 us
    ppermute x9, starting transfers between devices, swap(): lax.ppermute(value, axes, [(i, partner(i)) for i in range(lax.axis_size(a...  15.3 us
    all_to_all x1, blocking collectives, shards(): back = lax.all_to_all(chain(got, quad, even, odd), GROUP, 0, 0)  13 us
    ppermute x9, waiting for transfers between devices, swap(): lax.ppermute(value, axes, [(i, partner(i)) for i in range(lax.axis_size(a...  6.51 us
    pallas_call x1, Pallas kernels, interior(): pl.pallas_call(interior_kernel, out_shape=[jax.ShapeDtypeStruct((LZ - 2,...  4.76 us
    pallas_call x2, Pallas kernels, edge_message(): pl.pallas_call(functools.partial(edge_kernel, kind), out_shape=[jax.Shape...  2.95 us
    pallas_call x1, Pallas kernels, result(): pl.pallas_call(result_kernel, out_shape=jax.ShapeDtypeStruct((LZ, NY, NX)...  1.87 us
    pallas_call x1, Pallas kernels, chain(): pl.pallas_call(chain_kernel, out_shape=jax.ShapeDtypeStruct((BLOCKS, XB,...  1.44 us
  transfers between devices with their start and end apart: 9, of which 3 were waited for; matrix products, arithmetic and copies ran while one was open for 0% of the time, Pallas kernels for 12%

profile of v11, /device:TPU:1, one launch (start us, length us, event | category | flops | bytes accessed | tf_op | source)
XLA Modules:
  0.0 65.3 jit_solution(18425366826711720251)
XLA Ops:
  0.0 0.0 copy-start
  0.0 0.0 copy-start.1
  0.0 0.0 copy-start.2
  0.0 2.1 %far_message.1 = (f32[144,1024]{1,0:T(8,128)S(1)}, f32[64,1024]{1,0:T(8,128)S(1)}) custom-call(f32[8,64,1024]{2,1,0:T(8,128)} %bitcast.3, f32[3,8,64,1024]{3,2,1,0:T(8,128)} %v.3, f32[8,64,1024]{2,1,0:T(8,128)} %d.3), custom_call_target="tpu_custom_call" | custom-call | flops 15000000 | bytes 3000000 | tf_op jit(solution)/shard_map/far_message/pallas_call | solution.py:148
  2.1 3.1 %collective-permute-start.2 = (f32[144,1024]{1,0:T(8,128)S(1)}, f32[144,1024]{1,0:T(8,128)S(1)}, u32[]{:S(2)}, u32[]{:S(2)}) collective-permute-start(f32[144,1024]{1,0:T(8,128)S(1)} %get-tuple-element.29.ofar), channel_id=1, source_target_pairs={{0,15},{1,2},{2,1},{3,4},{4,3},{5,6},{6,5},{7,8},{8,7},{9,10},{10,... | collective-permute-start | bytes 1769480 | tf_op jit(solution)/shard_map/ppermute | solution.py:556
  5.3 0.0 copy-done
  5.3 0.0 copy-done.1
  5.3 0.0 copy-done.2
  5.3 0.8 %near_message.1 = (f32[128,1024]{1,0:T(8,128)S(1)}, f32[80,1024]{1,0:T(8,128)S(1)}) custom-call(f32[8,64,1024]{2,1,0:T(8,128)S(1)} %bitcast.4, f32[3,8,64,1024]{3,2,1,0:T(8,128)S(1)} %copy-done, f32[8,64,1024]{2,1,0:T(8,128)S(1)} %copy-done.1, f32[64,1024]{1,0:T(8,128)S(1)} %get-tuple-element.26.rest_0_.ofac), custom_call_target="tpu_custom_call" | custom-call | flops 15000000 | bytes 12000000 | tf_op jit(solution)/shard_map/near_message/pallas_call | solution.py:148
  6.1 2.1 %collective-permute-start = (f32[128,1024]{1,0:T(8,128)S(1)}, f32[128,1024]{1,0:T(8,128)S(1)}, u32[]{:S(2)}, u32[]{:S(2)}) collective-permute-start(f32[128,1024]{1,0:T(8,128)S(1)} %get-tuple-element.27.onear), channel_id=1, source_target_pairs={{0,1},{1,0},{2,3},{3,2},{4,5},{5,4},{6,7},{7,6},{8,9},{9,8},{10,11... | collective-permute-start | bytes 1572872 | tf_op jit(solution)/shard_map/ppermute | solution.py:556
  8.2 0.1 collective-permute-start.1
  8.3 2.7 %collective-permute-start.3 = (f32[64,1024]{1,0:T(8,128)S(1)}, f32[64,1024]{1,0:T(8,128)S(1)}, u32[]{:S(2)}, u32[]{:S(2)}) collective-permute-start(f32[64,1024]{1,0:T(8,128)S(1)} %get-tuple-element.26.rest_0_.ofac), channel_id=1, source_target_pairs={{0,31},{1,18},{2,17},{3,20},{4,19},{5,22},{6,21},{7,24},{8,23},{9,... | collective-permute-start | bytes 786440 | tf_op jit(solution)/shard_map/ppermute | solution.py:556
  11.0 0.0 collective-permute-done.1.after.rtail
  11.0 1.2 %coefs.1 = (f32[4,544,128]{2,1,0:T(8,128)S(1)}, f32[4,32,128]{2,1,0:T(8,128)S(1)}, f32[4,32,128]{2,1,0:T(8,128)S(1)}, f32[4,32,128]{2,1,0:T(8,128)S(1)}, f32[4,32,128]{2,1,0:T(8,128)S(1)}) custom-call(f32[3,8,64,1024]{3,2,1,0:T(8,128)S(1)} %copy-done, f32[8,64,1024]{2,1,0:T(8,128)S(1)} %copy-done.1, f32[80,1024]{1,0:T(8,128)S(1)} %collective-permute-done.1.after.rtail), custom_call_target="tpu_custom_call" | custom-call | flops 20000000 | bytes 9000000 | tf_op jit(solution)/shard_map/coefs/pallas_call | solution.py:193
  12.2 2.4 %collective-permute-start.4 = (f32[4,32,128]{2,1,0:T(8,128)S(1)}, f32[4,32,128]{2,1,0:T(8,128)S(1)}, u32[]{:S(2)}, u32[]{:S(2)}) collective-permute-start(f32[4,32,128]{2,1,0:T(8,128)S(1)} %get-tuple-element.31), channel_id=1, source_target_pairs={{0,1},{1,0},{2,3},{3,2},{4,5},{5,4},{6,7},{7,6},{8,9},{9,8},{10,11... | collective-permute-start | bytes 196616 | tf_op jit(solution)/shard_map/ppermute | solution.py:556
  14.6 0.0 collective-permute-start.5
  14.6 0.9 %collective-permute-done.4.after.w1 = f32[4,32,128]{2,1,0:T(8,128)S(1)} collective-permute-done((f32[4,32,128]{2,1,0:T(8,128)S(1)}, f32[4,32,128]{2,1,0:T(8,128)S(1)}, u32[]{:S(2)}, u32[]{:S(2)}) %collective-permute-start.4) | collective-permute-done | bytes 65568 | tf_op jit(solution)/shard_map/ppermute | solution.py:556
  15.5 2.0 %collective-permute-start.6 = (f32[4,32,128]{2,1,0:T(8,128)S(1)}, f32[4,32,128]{2,1,0:T(8,128)S(1)}, u32[]{:S(2)}, u32[]{:S(2)}) collective-permute-start(f32[4,32,128]{2,1,0:T(8,128)S(1)} %get-tuple-element.40), channel_id=1, source_target_pairs={{0,19},{1,18},{2,17},{3,16},{4,23},{5,22},{6,21},{7,20},{8,27},{9,... | collective-permute-start | bytes 196616 | tf_op jit(solution)/shard_map/ppermute | solution.py:556
  17.5 4.8 %interior.1 = (f32[6,64,1024]{2,1,0:T(8,128)S(1)}, f32[4,64,1024]{2,1,0:T(8,128)S(1)}, f32[512,128]{1,0:T(8,128)S(1)}, f32[512,128]{1,0:T(8,128)S(1)}, f32[8,64,128]{2,1,0:T(8,128)S(1)}) custom-call(f32[8,64,1024]{2,1,0:T(8,128)S(1)} %bitcast.5, f32[3,8,64,1024]{3,2,1,0:T(8,128)S(1)} %copy-done, f32[8,64,1024]{2,1,0:T(8,128)S(1)} %copy-done.1, ...), custom_call_target="tpu_custom_call" | custom-call | flops 60000000 | bytes 20000000 | tf_op jit(solution)/shard_map/interior/pallas_call | solution.py:265
  22.3 0.0 collective-permute-done.3.rfac
  22.3 0.0 collective-permute-done.rnear
  22.3 0.0 collective-permute-done.2.rfar
  22.4 1.2 %finish.1 = (f32[4,64,1024]{2,1,0:T(8,128)S(1)}, f32[536,128]{1,0:T(8,128)S(1)}, f32[512,128]{1,0:T(8,128)S(1)}) custom-call(f32[128,1024]{1,0:T(8,128)S(1)} %collective-permute-done.rnear, f32[80,1024]{1,0:T(8,128)S(1)} %collective-permute-done.1.after.rtail, f32[144,1024]{1,0:T(8,128)S(1)} %collective-permute-done.2.rfar, ...), custom_call_target="tpu_custom_call" | custom-call | tf_op jit(solution)/shard_map/finish/pallas_call | solution.py:349
  23.5 0.0 collective-permute-done.5.w2
  23.5 0.0 collective-permute-done.6.w3
  23.6 0.1 spread.1
  23.6 16.8 %all_to_all.10.got = f32[32,32,128]{2,1,0:T(8,128)S(1)} all-to-all(f32[32,32,128]{2,1,0:T(8,128)S(1)} %get-tuple-element.41), channel_id=1, replica_groups=mesh['tm'=8,'px'=4,'pz'=2,'core'=2] {'tm','pz','core'}, dimensions={0} | all-to-all | bytes 1048576 | tf_op jit(solution)/shard_map/all_to_all | solution.py:590
  40.4 0.1 pick.1
  40.5 1.0 %collective-permute-start.7 = (f32[360,128]{1,0:T(8,128)S(1)}, f32[360,128]{1,0:T(8,128)S(1)}, u32[]{:S(2)}, u32[]{:S(2)}) collective-permute-start(f32[360,128]{1,0:T(8,128)S(1)} %get-tuple-element.43), channel_id=1, source_target_pairs={{0,4},{4,0},{8,12},{12,8},{1,5},{5,1},{9,13},{13,9},{2,6},{6,2},{1... | collective-permute-start | bytes 552968 | tf_op jit(solution)/shard_map/ppermute | solution.py:556
  41.6 1.8 %collective-permute-start.8 = (f32[360,128]{1,0:T(8,128)S(1)}, f32[360,128]{1,0:T(8,128)S(1)}, u32[]{:S(2)}, u32[]{:S(2)}) collective-permute-start(f32[360,128]{1,0:T(8,128)S(1)} %get-tuple-element.44), channel_id=1, source_target_pairs={{0,12},{4,8},{8,4},{12,0},{1,13},{5,9},{9,5},{13,1},{2,14},{6,10},... | collective-permute-start | bytes 552968 | tf_op jit(solution)/shard_map/ppermute | solution.py:556
  43.4 3.6 %collective-permute-done.7.even = f32[360,128]{1,0:T(8,128)S(1)} collective-permute-done((f32[360,128]{1,0:T(8,128)S(1)}, f32[360,128]{1,0:T(8,128)S(1)}, u32[]{:S(2)}, u32[]{:S(2)}) %collective-permute-start.7) | collective-permute-done | bytes 184352 | tf_op jit(solution)/shard_map/ppermute | solution.py:556
  47.0 2.0 %collective-permute-done.8.odd = f32[360,128]{1,0:T(8,128)S(1)} collective-permute-done((f32[360,128]{1,0:T(8,128)S(1)}, f32[360,128]{1,0:T(8,128)S(1)}, u32[]{:S(2)}, u32[]{:S(2)}) %collective-permute-start.8) | collective-permute-done | bytes 184352 | tf_op jit(solution)/shard_map/ppermute | solution.py:556
  49.0 1.4 %chain.1 = f32[32,16,128]{2,1,0:T(8,128)S(1)} custom-call(f32[32,32,128]{2,1,0:T(8,128)S(1)} %all_to_all.10.got, f32[4,4,32,128]{3,2,1,0:T(8,128)S(1)} %get-tuple-element.42.quad, f32[360,128]{1,0:T(8,128)S(1)} %collective-permute-done.7.even, f32[360,128]{1,0:T(8,128)S(1)} %collective-permute-done.8.odd), custom_call_target="tpu_custom_call" | custom-call | tf_op jit(solution)/shard_map/chain/pallas_call | solution.py:502
  50.4 13.0 %all_to_all.11 = f32[32,16,128]{2,1,0:T(8,128)S(1)} all-to-all(f32[32,16,128]{2,1,0:T(8,128)S(1)} %chain.1), channel_id=1, replica_groups=mesh['tm'=8,'px'=4,'pz'=2,'core'=2] {'tm','pz','core'}, dimensions={0} | all-to-all | bytes 524288 | tf_op jit(solution)/shard_map/all_to_all | solution.py:594
  63.4 1.9 %result.1 = f32[8,64,1024]{2,1,0:T(8,128)} custom-call(f32[512,128]{1,0:T(8,128)S(1)} %bitcast.6, f32[512,128]{1,0:T(8,128)S(1)} %get-tuple-element.45.gc, f32[6,64,1024]{2,1,0:T(8,128)S(1)} %get-tuple-element.32.fin, f32[4,64,1024]{2,1,0:T(8,128)S(1)} %get-tuple-element.46.ub), custom_call_target="tpu_custom_call" | custom-call | tf_op jit(solution)/shard_map/result/pallas_call | solution.py:540
Async XLA Ops:
  0.0 5.3 %copy-start = (f32[3,8,64,1024]{3,2,1,0:T(8,128)S(1)}, f32[3,8,64,1024]{3,2,1,0:T(8,128)}, u32[]{:S(2)}) copy-start(f32[3,8,64,1024]{3,2,1,0:T(8,128)} %v.3) | copy-start | bytes 18874372
  0.0 5.3 %copy-start.1 = (f32[8,64,1024]{2,1,0:T(8,128)S(1)}, f32[8,64,1024]{2,1,0:T(8,128)}, u32[]{:S(2)}) copy-start(f32[8,64,1024]{2,1,0:T(8,128)} %d.3) | copy-start | bytes 6291460
  0.0 5.3 %copy-start.2 = (f32[1,8,64,1024]{3,2,1,0:T(8,128)S(1)}, f32[1,8,64,1024]{3,2,1,0:T(8,128)}, u32[]{:S(2)}) copy-start(f32[1,8,64,1024]{3,2,1,0:T(8,128)} %param.3) | copy-start | bytes 6291460
  2.1 20.2 %collective-permute-start.2 = (f32[144,1024]{1,0:T(8,128)S(1)}, f32[144,1024]{1,0:T(8,128)S(1)}, u32[]{:S(2)}, u32[]{:S(2)}) collective-permute-start(f32[144,1024]{1,0:T(8,128)S(1)} %get-tuple-element.29.ofar), channel_id=1, source_target_pairs={{0,15},{1,2},{2,1},{3,4},{4,3},{5,6},{6,5},{7,8},{8,7},{9,10},{10,... | collective-permute-start | bytes 1769480 | tf_op jit(solution)/shard_map/ppermute | solution.py:556
  6.1 16.2 %collective-permute-start = (f32[128,1024]{1,0:T(8,128)S(1)}, f32[128,1024]{1,0:T(8,128)S(1)}, u32[]{:S(2)}, u32[]{:S(2)}) collective-permute-start(f32[128,1024]{1,0:T(8,128)S(1)} %get-tuple-element.27.onear), channel_id=1, source_target_pairs={{0,1},{1,0},{2,3},{3,2},{4,5},{5,4},{6,7},{7,6},{8,9},{9,8},{10,11... | collective-permute-start | bytes 1572872 | tf_op jit(solution)/shard_map/ppermute | solution.py:556
  8.2 2.8 %collective-permute-start.1 = (f32[80,1024]{1,0:T(8,128)S(1)}, f32[80,1024]{1,0:T(8,128)S(1)}, u32[]{:S(2)}, u32[]{:S(2)}) collective-permute-start(f32[80,1024]{1,0:T(8,128)S(1)} %get-tuple-element.28.otail), channel_id=1, source_target_pairs={{0,1},{1,0},{2,3},{3,2},{4,5},{5,4},{6,7},{7,6},{8,9},{9,8},{10,11... | collective-permute-start | bytes 983048 | tf_op jit(solution)/shard_map/ppermute | solution.py:556
  8.3 14.0 %collective-permute-start.3 = (f32[64,1024]{1,0:T(8,128)S(1)}, f32[64,1024]{1,0:T(8,128)S(1)}, u32[]{:S(2)}, u32[]{:S(2)}) collective-permute-start(f32[64,1024]{1,0:T(8,128)S(1)} %get-tuple-element.26.rest_0_.ofac), channel_id=1, source_target_pairs={{0,31},{1,18},{2,17},{3,20},{4,19},{5,22},{6,21},{7,24},{8,23},{9,... | collective-permute-start | bytes 786440 | tf_op jit(solution)/shard_map/ppermute | solution.py:556
  12.2 3.3 %collective-permute-start.4 = (f32[4,32,128]{2,1,0:T(8,128)S(1)}, f32[4,32,128]{2,1,0:T(8,128)S(1)}, u32[]{:S(2)}, u32[]{:S(2)}) collective-permute-start(f32[4,32,128]{2,1,0:T(8,128)S(1)} %get-tuple-element.31), channel_id=1, source_target_pairs={{0,1},{1,0},{2,3},{3,2},{4,5},{5,4},{6,7},{7,6},{8,9},{9,8},{10,11... | collective-permute-start | bytes 196616 | tf_op jit(solution)/shard_map/ppermute | solution.py:556
  14.6 8.9 %collective-permute-start.5 = (f32[4,32,128]{2,1,0:T(8,128)S(1)}, f32[4,32,128]{2,1,0:T(8,128)S(1)}, u32[]{:S(2)}, u32[]{:S(2)}) collective-permute-start(f32[4,32,128]{2,1,0:T(8,128)S(1)} %get-tuple-element.39), channel_id=1, source_target_pairs={{0,18},{1,19},{2,16},{3,17},{4,22},{5,23},{6,20},{7,21},{8,26},{9,... | collective-permute-start | bytes 196616 | tf_op jit(solution)/shard_map/ppermute | solution.py:556
  15.5 8.0 %collective-permute-start.6 = (f32[4,32,128]{2,1,0:T(8,128)S(1)}, f32[4,32,128]{2,1,0:T(8,128)S(1)}, u32[]{:S(2)}, u32[]{:S(2)}) collective-permute-start(f32[4,32,128]{2,1,0:T(8,128)S(1)} %get-tuple-element.40), channel_id=1, source_target_pairs={{0,19},{1,18},{2,17},{3,16},{4,23},{5,22},{6,21},{7,20},{8,27},{9,... | collective-permute-start | bytes 196616 | tf_op jit(solution)/shard_map/ppermute | solution.py:556
  40.5 6.5 %collective-permute-start.7 = (f32[360,128]{1,0:T(8,128)S(1)}, f32[360,128]{1,0:T(8,128)S(1)}, u32[]{:S(2)}, u32[]{:S(2)}) collective-permute-start(f32[360,128]{1,0:T(8,128)S(1)} %get-tuple-element.43), channel_id=1, source_target_pairs={{0,4},{4,0},{8,12},{12,8},{1,5},{5,1},{9,13},{13,9},{2,6},{6,2},{1... | collective-permute-start | bytes 552968 | tf_op jit(solution)/shard_map/ppermute | solution.py:556
  41.6 7.4 %collective-permute-start.8 = (f32[360,128]{1,0:T(8,128)S(1)}, f32[360,128]{1,0:T(8,128)S(1)}, u32[]{:S(2)}, u32[]{:S(2)}) collective-permute-start(f32[360,128]{1,0:T(8,128)S(1)} %get-tuple-element.44), channel_id=1, source_target_pairs={{0,12},{4,8},{8,4},{12,0},{1,13},{5,9},{9,5},{13,1},{2,14},{6,10},... | collective-permute-start | bytes 552968 | tf_op jit(solution)/shard_map/ppermute | solution.py:556

commit v12 on v11

--- a/solution.py
+++ b/solution.py
@@ -294,41 +294,62 @@
     return value if beyond is False else jnp.where(beyond, 0.0, value)
 
 
-def finish_kernel(
-    rnear, rtail, rfar, rfac, onear, otail, ofar, ofac, fin, edge, v, d, gcp, cb, ymid,
-    ub, jp, gc, u1, zs,
-):
-    for kind, (rec, own, recb, ownb, at) in enumerate(((rnear, onear, rtail, otail, 16), (rfar, ofar, rfac, ofac, 0))):
-        top = edge_is_top(kind)
-        side = jnp.where(top, 1, 0)
-        beyond = kind == 1 and at_end()
-        for r in range(0, NY, 8):
-            u1[kind, r : r + 8, :] = (
-                own[NY + r : NY + r + 8, :] + ownb[at + r : at + r + 8, :] * dropped(beyond, rec[r : r + 8, :])
-            )
-        z = side * (LZ - 1)
-        for r, rows, (c, w, e, s, n) in planes(u1, kind):
-            outside = rec[NY + r : NY + r + 8, :] + recb[at + r : at + r + 8, :] * own[r : r + 8, :]
-            outside = dropped(beyond, outside)
-            inside = edge[side, rows, :]
-            ax, ay, az, k = v[0, z, rows, :], v[1, z, rows, :], v[2, z, rows, :], d[z, rows, :]
-            last = advanced(c, w, e, s, n, inside, outside, ax, ay, jnp.where(top, az, -az), k)
-            near = fin[5 * side, rows, :] + edge[2 + side, rows, :] * c
-            ub[3 * side, rows, :] = last
-            ub[1 + side, rows, :] = near
-            put_columns(zs.at[side], rows, last + near)
+def edge_layers(kind, rec, own, recb, ownb, at, fin, edge, v, d, ub, zs, u1):
+    top = edge_is_top(kind)
+    side = jnp.where(top, 1, 0)
+    beyond = kind == 1 and at_end()
+    for r in range(0, NY, 8):
+        u1[0, r : r + 8, :] = (
+            own[NY + r : NY + r + 8, :] + ownb[at + r : at + r + 8, :] * dropped(beyond, rec[r : r + 8, :])
+        )
+    z = side * (LZ - 1)
+    for r, rows, (c, w, e, s, n) in planes(u1, 0):
+        outside = rec[NY + r : NY + r + 8, :] + recb[at + r : at + r + 8, :] * own[r : r + 8, :]
+        outside = dropped(beyond, outside)
+        inside = edge[side, rows, :]
+        ax, ay, az, k = v[0, z, rows, :], v[1, z, rows, :], v[2, z, rows, :], d[z, rows, :]
+        last = advanced(c, w, e, s, n, inside, outside, ax, ay, jnp.where(top, az, -az), k)
+        near = fin[5 * side, rows, :] + edge[2 + side, rows, :] * c
+        ub[0, rows, :] = last
+        ub[1, rows, :] = near
+        put_columns(zs, rows, last + near)
+
+
+def finish_near_kernel(rnear, rtail, onear, otail, fin, edge, v, d, ub, zs, u1):
+    edge_layers(0, rnear, onear, rtail, otail, 16, fin, edge, v, d, ub, zs, u1)
+
+
+def finish_near(messages, fin, edge, velocity, diffusivity):
+    return pl.pallas_call(
+        finish_near_kernel,
+        out_shape=[jax.ShapeDtypeStruct((2, NY, NX), F32), jax.ShapeDtypeStruct((8, NY, 128), F32)],
+        in_specs=[whole()] * 8,
+        out_specs=[whole()] * 2,
+        scratch_shapes=[pltpu.VMEM((1, NY, NX), F32)],
+        compiler_params=params(16),
+        name="finish_near",
+    )(*messages, fin, edge, velocity, diffusivity)
+
+
+def finish_kernel(rtail, rfar, rfac, ofar, ofac, fin, edge, v, d, gcp, cb, ymid, zs_near, ub, jp, gc, u1, zs):
+    edge_layers(1, rfar, ofar, rfac, ofac, 0, fin, edge, v, d, ub, zs, u1)
     lane = lax.broadcasted_iota(jnp.int32, (128, 128), 1)
     hnear = jnp.concatenate([rtail[0:16, 128 * i : 128 * i + 128] for i in range(8)], axis=0)
     hfar = jnp.concatenate([rfar[2 * NY : FAR, 128 * i : 128 * i + 128] for i in range(8)], axis=0)
     hfar = dropped(at_end(), hfar)
     first_core = lax.axis_index("core") == 0
     halo_lo, halo_hi = jnp.where(first_core, hfar, hnear), jnp.where(first_core, hnear, hfar)
+
+    def sides(i):
+        a, b = paired(zs, i, 0, 32), paired(zs_near, i, 0, 32)
+        return [jnp.where(first_core, a, b), ymid[i], jnp.where(first_core, b, a)]
+
     for b in range(4):
         rows = slice(128 * b, 128 * b + 128)
         t = halved_x(
             jnp.concatenate(
                 [
-                    jnp.concatenate([paired(zs.at[0], i, 0, 32), ymid[i], paired(zs.at[1], i, 0, 32)], axis=0)
+                    jnp.concatenate(sides(i), axis=0)
                     for i in (2 * b, 2 * b + 1)
                 ],
                 axis=1,
@@ -345,23 +366,20 @@
     jp[CX + 8 : CX + 24, :] = jp[8:24, :]
 
 
-def finish(messages, fin, edge, velocity, diffusivity, gcp, cb, ymid):
+def finish(messages, fin, edge, velocity, diffusivity, gcp, cb, ymid, zs_near):
     return pl.pallas_call(
         finish_kernel,
         out_shape=[
-            jax.ShapeDtypeStruct((4, NY, NX), F32),
+            jax.ShapeDtypeStruct((2, NY, NX), F32),
             jax.ShapeDtypeStruct((CX + 24, CL), F32),
             jax.ShapeDtypeStruct((CX, CL), F32),
         ],
-        in_specs=[whole()] * 15,
+        in_specs=[whole()] * 13,
         out_specs=[whole()] * 3,
-        scratch_shapes=[
-            pltpu.VMEM((2, NY, NX), F32),
-            pltpu.VMEM((2, 8, NY, 128), F32),
-        ],
+        scratch_shapes=[pltpu.VMEM((1, NY, NX), F32), pltpu.VMEM((8, NY, 128), F32)],
         compiler_params=params(16),
         name="finish",
-    )(*messages, fin, edge, velocity, diffusivity, gcp, cb, ymid)
+    )(*messages, fin, edge, velocity, diffusivity, gcp, cb, ymid, zs_near)
 
 
 def spread_kernel(jp, w0, w1, w2, w3, msg, quad):
@@ -513,7 +531,8 @@
     )(got, quad, even, odd)
 
 
-def result_kernel(y, gc, fin, ub, out, copied, buf, sems):
+def result_kernel(y, gc, fin, near, far, out, copied, buf, sems):
+    first_core = lax.axis_index("core") == 0
     copy_y = table((256, CL), lambda r, c: r // 2 == c)
     copy_x = table((128, 256), lambda r, c: r == c // 2)
     for b in range(4):
@@ -527,7 +546,12 @@
             cols = slice(256 * b, 256 * b + 256)
             fine = sum(dot(copied[i, rows, 128 * b : 128 * b + 128], copy_x, 1, 0) for i in range(3))
             for z in (2 * zc, 2 * zc + 1):
-                base = fin[z - 1, :, cols] if 2 <= z < 6 else ub[z if z < 2 else z - 4, :, cols]
+                if 2 <= z < 6:
+                    base = fin[z - 1, :, cols]
+                else:
+                    here, there = (far, near) if z < 2 else (near, far)
+                    i = min(z, LZ - 1 - z)
+                    base = jnp.where(first_core, here[i, :, cols], there[i, :, cols])
                 buf[z, :, cols] = base + fine
         layers = slice(2 * zc, 2 * zc + 2)
         copies.append(pltpu.make_async_copy(buf.at[layers], out.at[layers], sems.at[zc]))
@@ -536,11 +560,11 @@
         copy.wait()
 
 
-def result(y, gc, fin, ub):
+def result(y, gc, fin, near, far):
     return pl.pallas_call(
         result_kernel,
         out_shape=jax.ShapeDtypeStruct((LZ, NY, NX), F32),
-        in_specs=[whole()] * 4,
+        in_specs=[whole()] * 5,
         out_specs=remains(),
         scratch_shapes=[
             pltpu.VMEM((3, 4 * NY, CX), BF16),
@@ -549,7 +573,7 @@
         ],
         compiler_params=params(16),
         name="result",
-    )(y, gc, fin, ub)
+    )(y, gc, fin, near, far)
 
 
 def swap(value, axes, partner):
@@ -584,15 +608,16 @@
         swap(w3, ("tm",) + SPACE, lambda i: i ^ 19),
     )
     fin, edge, gcp, cb, ymid = interior(state, velocity, diffusivity, ct, windows[1])
-    messages = (rnear, rtail, rfar, rfac, onear, otail, ofar, ofac)
-    ub, sources, gc = finish(messages, fin, edge, velocity, diffusivity, gcp, cb, ymid)
+    near, zs_near = finish_near((rnear, rtail, onear, otail), fin, edge, velocity, diffusivity)
+    messages = (rtail, rfar, rfac, ofar, ofac)
+    far, sources, gc = finish(messages, fin, edge, velocity, diffusivity, gcp, cb, ymid, zs_near)
     msg, quad = spread(sources, windows)
     got = lax.all_to_all(msg, GROUP, 0, 0)
     even, odd = pick(got, quad)
     even = swap(even, "px", lambda i: i ^ 1)
     odd = swap(odd, "px", quad_beside)
     back = lax.all_to_all(chain(got, quad, even, odd), GROUP, 0, 0)
-    return result(back.reshape(CX, CL), gc, fin, ub)[None]
+    return result(back.reshape(CX, CL), gc, fin, near, far)[None]
 
 
 def solution(mesh):

time: 65.5 us -> 65.1 us (level)
  no operation moved by 1% of the time
where the time goes in v12:
time: 65.1 us; the launch traced here: 65 us
  blocking collectives  29.8 us (46%)
  starting transfers between devices  14.9 us (23%)
  Pallas kernels  13.6 us (21%)
  waiting for transfers between devices  6.51 us (10%)
    all_to_all x1, blocking collectives, shards(): got = lax.all_to_all(msg, GROUP, 0, 0)  16.8 us
    ppermute x9, starting transfers between devices, swap(): lax.ppermute(value, axes, [(i, partner(i)) for i in range(lax.axis_size(a...  14.9 us
    all_to_all x1, blocking collectives, shards(): back = lax.all_to_all(chain(got, quad, even, odd), GROUP, 0, 0)  13 us
    ppermute x9, waiting for transfers between devices, swap(): lax.ppermute(value, axes, [(i, partner(i)) for i in range(lax.axis_size(a...  6.51 us
    pallas_call x1, Pallas kernels, interior(): pl.pallas_call(interior_kernel, out_shape=[jax.ShapeDtypeStruct((LZ - 2,...  4.76 us
    pallas_call x2, Pallas kernels, edge_message(): pl.pallas_call(functools.partial(edge_kernel, kind), out_shape=[jax.Shape...  2.95 us
    pallas_call x1, Pallas kernels, result(): pl.pallas_call(result_kernel, out_shape=jax.ShapeDtypeStruct((LZ, NY, NX)...  1.88 us
    pallas_call x1, Pallas kernels, chain(): pl.pallas_call(chain_kernel, out_shape=jax.ShapeDtypeStruct((BLOCKS, XB,...  1.44 us
  transfers between devices with their start and end apart: 9, of which 3 were waited for; matrix products, arithmetic and copies ran while one was open for 0% of the time, Pallas kernels for 12%

profile of v12, /device:TPU:1, one launch (start us, length us, event | category | flops | bytes accessed | tf_op | source)
XLA Modules:
  0.0 65.0 jit_solution(17131570998336630712)
XLA Ops:
  0.0 0.0 copy-start
  0.0 0.0 copy-start.1
  0.0 0.0 copy-start.2
  0.0 2.1 %far_message.1 = (f32[144,1024]{1,0:T(8,128)S(1)}, f32[64,1024]{1,0:T(8,128)S(1)}) custom-call(f32[8,64,1024]{2,1,0:T(8,128)} %bitcast.3, f32[3,8,64,1024]{3,2,1,0:T(8,128)} %v.5, f32[8,64,1024]{2,1,0:T(8,128)} %d.5), custom_call_target="tpu_custom_call" | custom-call | flops 15000000 | bytes 3000000 | tf_op jit(solution)/shard_map/far_message/pallas_call | solution.py:148
  2.1 3.1 %collective-permute-start.1 = (f32[144,1024]{1,0:T(8,128)S(1)}, f32[144,1024]{1,0:T(8,128)S(1)}, u32[]{:S(2)}, u32[]{:S(2)}) collective-permute-start(f32[144,1024]{1,0:T(8,128)S(1)} %get-tuple-element.30.ofar), channel_id=1, source_target_pairs={{0,15},{1,2},{2,1},{3,4},{4,3},{5,6},{6,5},{7,8},{8,7},{9,10},{10,... | collective-permute-start | bytes 1769480 | tf_op jit(solution)/shard_map/ppermute | solution.py:580
  5.3 0.0 copy-done
  5.3 0.0 copy-done.1
  5.3 0.0 copy-done.2
  5.3 0.8 %near_message.1 = (f32[128,1024]{1,0:T(8,128)S(1)}, f32[80,1024]{1,0:T(8,128)S(1)}) custom-call(f32[8,64,1024]{2,1,0:T(8,128)S(1)} %bitcast.4, f32[3,8,64,1024]{3,2,1,0:T(8,128)S(1)} %copy-done, f32[8,64,1024]{2,1,0:T(8,128)S(1)} %copy-done.1, f32[64,1024]{1,0:T(8,128)S(1)} %get-tuple-element.28.rest_0_.ofac), custom_call_target="tpu_custom_call" | custom-call | flops 15000000 | bytes 12000000 | tf_op jit(solution)/shard_map/near_message/pallas_call | solution.py:148
  6.1 2.1 %collective-permute-start.4 = (f32[128,1024]{1,0:T(8,128)S(1)}, f32[128,1024]{1,0:T(8,128)S(1)}, u32[]{:S(2)}, u32[]{:S(2)}) collective-permute-start(f32[128,1024]{1,0:T(8,128)S(1)} %get-tuple-element.38.onear), channel_id=1, source_target_pairs={{0,1},{1,0},{2,3},{3,2},{4,5},{5,4},{6,7},{7,6},{8,9},{9,8},{10,11... | collective-permute-start | bytes 1572872 | tf_op jit(solution)/shard_map/ppermute | solution.py:580
  8.2 0.1 collective-permute-start
  8.3 2.7 %collective-permute-start.2 = (f32[64,1024]{1,0:T(8,128)S(1)}, f32[64,1024]{1,0:T(8,128)S(1)}, u32[]{:S(2)}, u32[]{:S(2)}) collective-permute-start(f32[64,1024]{1,0:T(8,128)S(1)} %get-tuple-element.28.rest_0_.ofac), channel_id=1, source_target_pairs={{0,31},{1,18},{2,17},{3,20},{4,19},{5,22},{6,21},{7,24},{8,23},{9,... | collective-permute-start | bytes 786440 | tf_op jit(solution)/shard_map/ppermute | solution.py:580
  11.0 0.0 collective-permute-done.after.rtail
  11.0 1.2 %coefs.1 = (f32[4,544,128]{2,1,0:T(8,128)S(1)}, f32[4,32,128]{2,1,0:T(8,128)S(1)}, f32[4,32,128]{2,1,0:T(8,128)S(1)}, f32[4,32,128]{2,1,0:T(8,128)S(1)}, f32[4,32,128]{2,1,0:T(8,128)S(1)}) custom-call(f32[3,8,64,1024]{3,2,1,0:T(8,128)S(1)} %copy-done, f32[8,64,1024]{2,1,0:T(8,128)S(1)} %copy-done.1, f32[80,1024]{1,0:T(8,128)S(1)} %collective-permute-done.after.rtail), custom_call_target="tpu_custom_call" | custom-call | flops 20000000 | bytes 9000000 | tf_op jit(solution)/shard_map/coefs/pallas_call | solution.py:193
  12.2 2.4 %collective-permute-start.3 = (f32[4,32,128]{2,1,0:T(8,128)S(1)}, f32[4,32,128]{2,1,0:T(8,128)S(1)}, u32[]{:S(2)}, u32[]{:S(2)}) collective-permute-start(f32[4,32,128]{2,1,0:T(8,128)S(1)} %get-tuple-element.32), channel_id=1, source_target_pairs={{0,1},{1,0},{2,3},{3,2},{4,5},{5,4},{6,7},{7,6},{8,9},{9,8},{10,11... | collective-permute-start | bytes 196616 | tf_op jit(solution)/shard_map/ppermute | solution.py:580
  14.6 0.0 collective-permute-start.5
  14.6 0.9 %collective-permute-done.3.after.w1 = f32[4,32,128]{2,1,0:T(8,128)S(1)} collective-permute-done((f32[4,32,128]{2,1,0:T(8,128)S(1)}, f32[4,32,128]{2,1,0:T(8,128)S(1)}, u32[]{:S(2)}, u32[]{:S(2)}) %collective-permute-start.3) | collective-permute-done | bytes 65568 | tf_op jit(solution)/shard_map/ppermute | solution.py:580
  15.5 2.0 %collective-permute-start.6 = (f32[4,32,128]{2,1,0:T(8,128)S(1)}, f32[4,32,128]{2,1,0:T(8,128)S(1)}, u32[]{:S(2)}, u32[]{:S(2)}) collective-permute-start(f32[4,32,128]{2,1,0:T(8,128)S(1)} %get-tuple-element.43), channel_id=1, source_target_pairs={{0,19},{1,18},{2,17},{3,16},{4,23},{5,22},{6,21},{7,20},{8,27},{9,... | collective-permute-start | bytes 196616 | tf_op jit(solution)/shard_map/ppermute | solution.py:580
  17.5 4.8 %interior.1 = (f32[6,64,1024]{2,1,0:T(8,128)S(1)}, f32[4,64,1024]{2,1,0:T(8,128)S(1)}, f32[512,128]{1,0:T(8,128)S(1)}, f32[512,128]{1,0:T(8,128)S(1)}, f32[8,64,128]{2,1,0:T(8,128)S(1)}) custom-call(f32[8,64,1024]{2,1,0:T(8,128)S(1)} %bitcast.5, f32[3,8,64,1024]{3,2,1,0:T(8,128)S(1)} %copy-done, f32[8,64,1024]{2,1,0:T(8,128)S(1)} %copy-done.1, ...), custom_call_target="tpu_custom_call" | custom-call | flops 60000000 | bytes 20000000 | tf_op jit(solution)/shard_map/interior/pallas_call | solution.py:265
  22.3 0.0 collective-permute-done.4.rnear
  22.3 0.4 finish_near.1
  22.8 0.0 collective-permute-done.2.rfac
  22.8 0.0 collective-permute-done.1.rfar
  22.8 0.8 %finish.1 = (f32[2,64,1024]{2,1,0:T(8,128)S(1)}, f32[536,128]{1,0:T(8,128)S(1)}, f32[512,128]{1,0:T(8,128)S(1)}) custom-call(f32[80,1024]{1,0:T(8,128)S(1)} %collective-permute-done.after.rtail, f32[144,1024]{1,0:T(8,128)S(1)} %collective-permute-done.1.rfar, f32[64,1024]{1,0:T(8,128)S(1)} %collective-permute-done.2.rfac, ...), custom_call_target="tpu_custom_call" | custom-call | tf_op jit(solution)/shard_map/finish/pallas_call | solution.py:370
  23.6 0.0 collective-permute-done.5.w2
  23.6 0.0 collective-permute-done.6.w3
  23.6 0.1 spread.1
  23.7 16.8 %all_to_all.10.got = f32[32,32,128]{2,1,0:T(8,128)S(1)} all-to-all(f32[32,32,128]{2,1,0:T(8,128)S(1)} %get-tuple-element.44), channel_id=1, replica_groups=mesh['tm'=8,'px'=4,'pz'=2,'core'=2] {'tm','pz','core'}, dimensions={0} | all-to-all | bytes 1048576 | tf_op jit(solution)/shard_map/all_to_all | solution.py:615
  40.5 0.1 pick.1
  40.6 0.6 collective-permute-start.7
  41.2 1.8 %collective-permute-start.8 = (f32[360,128]{1,0:T(8,128)S(1)}, f32[360,128]{1,0:T(8,128)S(1)}, u32[]{:S(2)}, u32[]{:S(2)}) collective-permute-start(f32[360,128]{1,0:T(8,128)S(1)} %get-tuple-element.47), channel_id=1, source_target_pairs={{0,12},{4,8},{8,4},{12,0},{1,13},{5,9},{9,5},{13,1},{2,14},{6,10},... | collective-permute-start | bytes 552968 | tf_op jit(solution)/shard_map/ppermute | solution.py:580
  43.0 4.0 %collective-permute-done.7.even = f32[360,128]{1,0:T(8,128)S(1)} collective-permute-done((f32[360,128]{1,0:T(8,128)S(1)}, f32[360,128]{1,0:T(8,128)S(1)}, u32[]{:S(2)}, u32[]{:S(2)}) %collective-permute-start.7) | collective-permute-done | bytes 184352 | tf_op jit(solution)/shard_map/ppermute | solution.py:580
  47.1 1.5 %collective-permute-done.8.odd = f32[360,128]{1,0:T(8,128)S(1)} collective-permute-done((f32[360,128]{1,0:T(8,128)S(1)}, f32[360,128]{1,0:T(8,128)S(1)}, u32[]{:S(2)}, u32[]{:S(2)}) %collective-permute-start.8) | collective-permute-done | bytes 184352 | tf_op jit(solution)/shard_map/ppermute | solution.py:580
  48.6 1.4 %chain.1 = f32[32,16,128]{2,1,0:T(8,128)S(1)} custom-call(f32[32,32,128]{2,1,0:T(8,128)S(1)} %all_to_all.10.got, f32[4,4,32,128]{3,2,1,0:T(8,128)S(1)} %get-tuple-element.45.quad, f32[360,128]{1,0:T(8,128)S(1)} %collective-permute-done.7.even, f32[360,128]{1,0:T(8,128)S(1)} %collective-permute-done.8.odd), custom_call_target="tpu_custom_call" | custom-call | tf_op jit(solution)/shard_map/chain/pallas_call | solution.py:520
  50.1 13.0 %all_to_all.11 = f32[32,16,128]{2,1,0:T(8,128)S(1)} all-to-all(f32[32,16,128]{2,1,0:T(8,128)S(1)} %chain.1), channel_id=1, replica_groups=mesh['tm'=8,'px'=4,'pz'=2,'core'=2] {'tm','pz','core'}, dimensions={0} | all-to-all | bytes 524288 | tf_op jit(solution)/shard_map/all_to_all | solution.py:619
  63.1 1.9 %result.1 = f32[8,64,1024]{2,1,0:T(8,128)} custom-call(f32[512,128]{1,0:T(8,128)S(1)} %bitcast.6, f32[512,128]{1,0:T(8,128)S(1)} %get-tuple-element.48.gc, f32[6,64,1024]{2,1,0:T(8,128)S(1)} %get-tuple-element.33.fin, f32[2,64,1024]{2,1,0:T(8,128)S(1)} %get-tuple-element.49.near, f32[2,64,1024]{2,1,0:T(8,128)S(1)} %get-tuple-element.50.far), custom_call_target="tpu_custom_call" | custom-call | tf_op jit(solution)/shard_map/result/pallas_call | solution.py:564
Async XLA Ops:
  0.0 5.3 %copy-start = (f32[3,8,64,1024]{3,2,1,0:T(8,128)S(1)}, f32[3,8,64,1024]{3,2,1,0:T(8,128)}, u32[]{:S(2)}) copy-start(f32[3,8,64,1024]{3,2,1,0:T(8,128)} %v.5) | copy-start | bytes 18874372
  0.0 5.3 %copy-start.1 = (f32[8,64,1024]{2,1,0:T(8,128)S(1)}, f32[8,64,1024]{2,1,0:T(8,128)}, u32[]{:S(2)}) copy-start(f32[8,64,1024]{2,1,0:T(8,128)} %d.5) | copy-start | bytes 6291460
  0.0 5.3 %copy-start.2 = (f32[1,8,64,1024]{3,2,1,0:T(8,128)S(1)}, f32[1,8,64,1024]{3,2,1,0:T(8,128)}, u32[]{:S(2)}) copy-start(f32[1,8,64,1024]{3,2,1,0:T(8,128)} %param.3) | copy-start | bytes 6291460
  2.1 20.6 %collective-permute-start.1 = (f32[144,1024]{1,0:T(8,128)S(1)}, f32[144,1024]{1,0:T(8,128)S(1)}, u32[]{:S(2)}, u32[]{:S(2)}) collective-permute-start(f32[144,1024]{1,0:T(8,128)S(1)} %get-tuple-element.30.ofar), channel_id=1, source_target_pairs={{0,15},{1,2},{2,1},{3,4},{4,3},{5,6},{6,5},{7,8},{8,7},{9,10},{10,... | collective-permute-start | bytes 1769480 | tf_op jit(solution)/shard_map/ppermute | solution.py:580
  6.1 16.2 %collective-permute-start.4 = (f32[128,1024]{1,0:T(8,128)S(1)}, f32[128,1024]{1,0:T(8,128)S(1)}, u32[]{:S(2)}, u32[]{:S(2)}) collective-permute-start(f32[128,1024]{1,0:T(8,128)S(1)} %get-tuple-element.38.onear), channel_id=1, source_target_pairs={{0,1},{1,0},{2,3},{3,2},{4,5},{5,4},{6,7},{7,6},{8,9},{9,8},{10,11... | collective-permute-start | bytes 1572872 | tf_op jit(solution)/shard_map/ppermute | solution.py:580
  8.2 2.8 %collective-permute-start = (f32[80,1024]{1,0:T(8,128)S(1)}, f32[80,1024]{1,0:T(8,128)S(1)}, u32[]{:S(2)}, u32[]{:S(2)}) collective-permute-start(f32[80,1024]{1,0:T(8,128)S(1)} %get-tuple-element.29.otail), channel_id=1, source_target_pairs={{0,1},{1,0},{2,3},{3,2},{4,5},{5,4},{6,7},{7,6},{8,9},{9,8},{10,11... | collective-permute-start | bytes 983048 | tf_op jit(solution)/shard_map/ppermute | solution.py:580
  8.3 14.5 %collective-permute-start.2 = (f32[64,1024]{1,0:T(8,128)S(1)}, f32[64,1024]{1,0:T(8,128)S(1)}, u32[]{:S(2)}, u32[]{:S(2)}) collective-permute-start(f32[64,1024]{1,0:T(8,128)S(1)} %get-tuple-element.28.rest_0_.ofac), channel_id=1, source_target_pairs={{0,31},{1,18},{2,17},{3,20},{4,19},{5,22},{6,21},{7,24},{8,23},{9,... | collective-permute-start | bytes 786440 | tf_op jit(solution)/shard_map/ppermute | solution.py:580
  12.2 3.3 %collective-permute-start.3 = (f32[4,32,128]{2,1,0:T(8,128)S(1)}, f32[4,32,128]{2,1,0:T(8,128)S(1)}, u32[]{:S(2)}, u32[]{:S(2)}) collective-permute-start(f32[4,32,128]{2,1,0:T(8,128)S(1)} %get-tuple-element.32), channel_id=1, source_target_pairs={{0,1},{1,0},{2,3},{3,2},{4,5},{5,4},{6,7},{7,6},{8,9},{9,8},{10,11... | collective-permute-start | bytes 196616 | tf_op jit(solution)/shard_map/ppermute | solution.py:580
  14.6 9.0 %collective-permute-start.5 = (f32[4,32,128]{2,1,0:T(8,128)S(1)}, f32[4,32,128]{2,1,0:T(8,128)S(1)}, u32[]{:S(2)}, u32[]{:S(2)}) collective-permute-start(f32[4,32,128]{2,1,0:T(8,128)S(1)} %get-tuple-element.42), channel_id=1, source_target_pairs={{0,18},{1,19},{2,16},{3,17},{4,22},{5,23},{6,20},{7,21},{8,26},{9,... | collective-permute-start | bytes 196616 | tf_op jit(solution)/shard_map/ppermute | solution.py:580
  15.5 8.1 %collective-permute-start.6 = (f32[4,32,128]{2,1,0:T(8,128)S(1)}, f32[4,32,128]{2,1,0:T(8,128)S(1)}, u32[]{:S(2)}, u32[]{:S(2)}) collective-permute-start(f32[4,32,128]{2,1,0:T(8,128)S(1)} %get-tuple-element.43), channel_id=1, source_target_pairs={{0,19},{1,18},{2,17},{3,16},{4,23},{5,22},{6,21},{7,20},{8,27},{9,... | collective-permute-start | bytes 196616 | tf_op jit(solution)/shard_map/ppermute | solution.py:580
  40.6 6.5 %collective-permute-start.7 = (f32[360,128]{1,0:T(8,128)S(1)}, f32[360,128]{1,0:T(8,128)S(1)}, u32[]{:S(2)}, u32[]{:S(2)}) collective-permute-start(f32[360,128]{1,0:T(8,128)S(1)} %get-tuple-element.46), channel_id=1, source_target_pairs={{0,4},{4,0},{8,12},{12,8},{1,5},{5,1},{9,13},{13,9},{2,6},{6,2},{1... | collective-permute-start | bytes 552968 | tf_op jit(solution)/shard_map/ppermute | solution.py:580
  41.2 7.4 %collective-permute-start.8 = (f32[360,128]{1,0:T(8,128)S(1)}, f32[360,128]{1,0:T(8,128)S(1)}, u32[]{:S(2)}, u32[]{:S(2)}) collective-permute-start(f32[360,128]{1,0:T(8,128)S(1)} %get-tuple-element.47), channel_id=1, source_target_pairs={{0,12},{4,8},{8,4},{12,0},{1,13},{5,9},{9,5},{13,1},{2,14},{6,10},... | collective-permute-start | bytes 552968 | tf_op jit(solution)/shard_map/ppermute | solution.py:580

commit v13 on v12

--- a/solution.py
+++ b/solution.py
@@ -167,7 +167,7 @@
     return lax.axis_index("pz") * 2 + lax.axis_index("core")
 
 
-def coefs_kernel(vel, dif, after, ct, w0, w1, w2, w3, zs):
+def coefs_kernel(vel, dif, ct, zs):
     for comp in range(4):
         for zc in range(4):
             for r in range(0, NY, 8):
@@ -180,6 +180,22 @@
             )
         ct[comp, 0:8, :] = ct[comp, CX : CX + 8, :]
         ct[comp, CX + 8 : CX + 32, :] = ct[comp, 8:32, :]
+
+
+def coefs(velocity, diffusivity):
+    return pl.pallas_call(
+        coefs_kernel,
+        out_shape=jax.ShapeDtypeStruct((4, CROWS, CL), F32),
+        in_specs=[whole()] * 2,
+        out_specs=whole(),
+        scratch_shapes=[pltpu.VMEM((4, 8, 4 * NY, 128), F32)],
+        compiler_params=params(12),
+        cost_estimate=pl.CostEstimate(flops=20_000_000, bytes_accessed=9_000_000, transcendentals=0),
+        name="coefs",
+    )(velocity, diffusivity)
+
+
+def cut_kernel(ct, after, w0, w1, w2, w3):
     mine = quad_rank()
     slice_index = lax.axis_index("tm")
     for i, out in enumerate((w0, w1, w2, w3)):
@@ -188,18 +204,16 @@
             out[comp] = ct[comp, pl.ds(pl.multiple_of(block * XB, XB), WIN), :]
 
 
-def coefs(velocity, diffusivity, after):
+def cut(ct, after):
     window = jax.ShapeDtypeStruct((4, WIN, CL), F32)
     return pl.pallas_call(
-        coefs_kernel,
-        out_shape=[jax.ShapeDtypeStruct((4, CROWS, CL), F32)] + [window] * 4,
-        in_specs=[whole()] * 3,
-        out_specs=[whole()] * 5,
-        scratch_shapes=[pltpu.VMEM((4, 8, 4 * NY, 128), F32)],
+        cut_kernel,
+        out_shape=[window] * 4,
+        in_specs=[whole()] * 2,
+        out_specs=[whole()] * 4,
         compiler_params=params(12),
-        cost_estimate=pl.CostEstimate(flops=20_000_000, bytes_accessed=9_000_000, transcendentals=0),
-        name="coefs",
-    )(velocity, diffusivity, after)
+        name="cut",
+    )(ct, after)
 
 
 def interior_kernel(u, v, d, ct, after, fin, edge, gcp, cb, ymid, u1, zs, zf, ct0):
@@ -447,7 +461,24 @@
     )(got, quad)
 
 
-def chain_kernel(got, quad, even, odd, out, cf, e):
+def prepare_kernel(quad, after, own):
+    for q in range(QUAD):
+        for i, value in enumerate(coarse_coefs(*(quad[q, j] for j in range(4)))):
+            own[i, q] = value
+
+
+def prepare(quad, after):
+    return pl.pallas_call(
+        prepare_kernel,
+        out_shape=jax.ShapeDtypeStruct((6, QUAD, WIN, CL), F32),
+        in_specs=[whole()] * 2,
+        out_specs=whole(),
+        compiler_params=params(16),
+        name="prepare",
+    )(quad, after)
+
+
+def chain_kernel(got, own, even, odd, out, halo_cf, e):
     place = lax.axis_index("px")
     first = lax.rem(place, 2) == 0
 
@@ -477,16 +508,15 @@
 
     for block in range(8):
         halo = below if block < 2 else above
-        if 2 <= block < 6:
-            values = [quad[block - 2, i] for i in range(4)]
-        elif block in (1, 6):
+        values = []
+        if block in (1, 6):
             values = [halo(7 + i) for i in range(4)]
-        else:
-            values = []
+        elif block in (0, 7):
             for i in (11, 12):
                 values += [halo(i), pltpu.roll(halo(i), 64, 1)]
-        for i, value in enumerate(coarse_coefs(*values)):
-            cf[i, block] = value
+        if values:
+            for i, value in enumerate(coarse_coefs(*values)):
+                halo_cf[i, block % 4] = value
         e[0, block] = source(0, block)
     for q in range(QUAD):
         out[q] = jnp.zeros((XB, CL), F32)
@@ -498,6 +528,7 @@
         near = {b: lane_neighbours(e[now, b]) for b in reach}
         for block in range(low, 8 - low):
             c = e[now, block]
+            cf, at = (own, block - 2) if 2 <= block < 6 else (halo_cf, block % 4)
             b, t, s, n = near[block]
             if block > 0:
                 b = jnp.where(lane < 32, near[block - 1][0], b)
@@ -505,9 +536,9 @@
                 t = jnp.where(lane >= 96, near[block + 1][1], t)
             w, x = pltpu.roll(c, 1, 0), pltpu.roll(c, WIN - 1, 0)
             y = c + (
-                (cf[0, block] * (w - c) + cf[1, block] * (x - c))
-                + (cf[2, block] * (s - c) + cf[3, block] * (n - c))
-                + (cf[4, block] * (b - c) + cf[5, block] * (t - c))
+                (cf[0, at] * (w - c) + cf[1, at] * (x - c))
+                + (cf[2, at] * (s - c) + cf[3, at] * (n - c))
+                + (cf[4, at] * (b - c) + cf[5, at] * (t - c))
             )
             if 2 <= block < 6:
                 out[QUAD * k + block - 2] = y[8 : 8 + XB, :]
@@ -516,19 +547,19 @@
                 e[later, block] = y if more is None else y + more
 
 
-def chain(got, quad, even, odd):
+def chain(got, own, even, odd):
     return pl.pallas_call(
         chain_kernel,
         out_shape=jax.ShapeDtypeStruct((BLOCKS, XB, CL), F32),
         in_specs=[whole()] * 4,
         out_specs=whole(),
         scratch_shapes=[
-            pltpu.VMEM((6, 8, WIN, CL), F32),
+            pltpu.VMEM((6, 4, WIN, CL), F32),
             pltpu.VMEM((2, 8, WIN, CL), F32),
         ],
         compiler_params=params(24),
         name="chain",
-    )(got, quad, even, odd)
+    )(got, own, even, odd)
 
 
 def result_kernel(y, gc, fin, near, far, out, copied, buf, sems):
@@ -600,7 +631,8 @@
     onear, otail = edge_message(0, state, velocity, diffusivity, ofac)
     rnear = swap(onear, SPACE, lambda i: i ^ 1)
     rtail = swap(otail, SPACE, lambda i: i ^ 1)
-    ct, w0, w1, w2, w3 = coefs(velocity, diffusivity, rtail)
+    ct = coefs(velocity, diffusivity)
+    w0, w1, w2, w3 = cut(ct, rtail)
     windows = (
         w0,
         swap(w1, SPACE, lambda i: i ^ 1),
@@ -614,9 +646,10 @@
     msg, quad = spread(sources, windows)
     got = lax.all_to_all(msg, GROUP, 0, 0)
     even, odd = pick(got, quad)
+    own = prepare(quad, even)
     even = swap(even, "px", lambda i: i ^ 1)
     odd = swap(odd, "px", quad_beside)
-    back = lax.all_to_all(chain(got, quad, even, odd), GROUP, 0, 0)
+    back = lax.all_to_all(chain(got, own, even, odd), GROUP, 0, 0)
     return result(back.reshape(CX, CL), gc, fin, near, far)[None]
 
 

time: 65.1 us -> 65.1 us (level)
  no operation moved by 1% of the time
where the time goes in v13:
time: 65.1 us; the launch traced here: 64.9 us
  blocking collectives  29.8 us (46%)
  starting transfers between devices  14.9 us (23%)
  Pallas kernels  13.6 us (21%)
  waiting for transfers between devices  6.48 us (10%)
    all_to_all x1, blocking collectives, shards(): got = lax.all_to_all(msg, GROUP, 0, 0)  16.8 us
    ppermute x9, starting transfers between devices, swap(): lax.ppermute(value, axes, [(i, partner(i)) for i in range(lax.axis_size(a...  14.9 us
    all_to_all x1, blocking collectives, shards(): back = lax.all_to_all(chain(got, own, even, odd), GROUP, 0, 0)  13 us
    ppermute x9, waiting for transfers between devices, swap(): lax.ppermute(value, axes, [(i, partner(i)) for i in range(lax.axis_size(a...  6.48 us
    pallas_call x1, Pallas kernels, interior(): pl.pallas_call(interior_kernel, out_shape=[jax.ShapeDtypeStruct((LZ - 2,...  4.76 us
    pallas_call x2, Pallas kernels, edge_message(): pl.pallas_call(functools.partial(edge_kernel, kind), out_shape=[jax.Shape...  2.95 us
    pallas_call x1, Pallas kernels, result(): pl.pallas_call(result_kernel, out_shape=jax.ShapeDtypeStruct((LZ, NY, NX)...  1.88 us
    pallas_call x1, Pallas kernels, chain(): pl.pallas_call(chain_kernel, out_shape=jax.ShapeDtypeStruct((BLOCKS, XB,...  1.41 us
  transfers between devices with their start and end apart: 9, of which 3 were waited for; matrix products, arithmetic and copies ran while one was open for 0% of the time, Pallas kernels for 12%

profile of v13, /device:TPU:1, one launch (start us, length us, event | category | flops | bytes accessed | tf_op | source)
XLA Modules:
  0.0 64.9 jit_solution(6579925021480645857)
XLA Ops:
  0.0 0.0 copy-start
  0.0 0.0 copy-start.1
  0.0 0.0 copy-start.2
  0.0 2.1 %far_message.1 = (f32[144,1024]{1,0:T(8,128)S(1)}, f32[64,1024]{1,0:T(8,128)S(1)}) custom-call(f32[8,64,1024]{2,1,0:T(8,128)} %bitcast.3, f32[3,8,64,1024]{3,2,1,0:T(8,128)} %v.5, f32[8,64,1024]{2,1,0:T(8,128)} %d.5), custom_call_target="tpu_custom_call" | custom-call | flops 15000000 | bytes 3000000 | tf_op jit(solution)/shard_map/far_message/pallas_call | solution.py:148
  2.1 3.1 %collective-permute-start.1 = (f32[144,1024]{1,0:T(8,128)S(1)}, f32[144,1024]{1,0:T(8,128)S(1)}, u32[]{:S(2)}, u32[]{:S(2)}) collective-permute-start(f32[144,1024]{1,0:T(8,128)S(1)} %get-tuple-element.29.ofar), channel_id=1, source_target_pairs={{0,15},{1,2},{2,1},{3,4},{4,3},{5,6},{6,5},{7,8},{8,7},{9,10},{10,... | collective-permute-start | bytes 1769480 | tf_op jit(solution)/shard_map/ppermute | solution.py:611
  5.3 0.0 copy-done
  5.3 0.0 copy-done.1
  5.3 0.0 copy-done.2
  5.3 0.8 %near_message.1 = (f32[128,1024]{1,0:T(8,128)S(1)}, f32[80,1024]{1,0:T(8,128)S(1)}) custom-call(f32[8,64,1024]{2,1,0:T(8,128)S(1)} %bitcast.4, f32[3,8,64,1024]{3,2,1,0:T(8,128)S(1)} %copy-done, f32[8,64,1024]{2,1,0:T(8,128)S(1)} %copy-done.1, f32[64,1024]{1,0:T(8,128)S(1)} %get-tuple-element.27.rest_0_.ofac), custom_call_target="tpu_custom_call" | custom-call | flops 15000000 | bytes 12000000 | tf_op jit(solution)/shard_map/near_message/pallas_call | solution.py:148
  6.1 2.1 %collective-permute-start.4 = (f32[128,1024]{1,0:T(8,128)S(1)}, f32[128,1024]{1,0:T(8,128)S(1)}, u32[]{:S(2)}, u32[]{:S(2)}) collective-permute-start(f32[128,1024]{1,0:T(8,128)S(1)} %get-tuple-element.36.onear), channel_id=1, source_target_pairs={{0,1},{1,0},{2,3},{3,2},{4,5},{5,4},{6,7},{7,6},{8,9},{9,8},{10,11... | collective-permute-start | bytes 1572872 | tf_op jit(solution)/shard_map/ppermute | solution.py:611
  8.2 0.1 collective-permute-start
  8.3 2.7 %collective-permute-start.2 = (f32[64,1024]{1,0:T(8,128)S(1)}, f32[64,1024]{1,0:T(8,128)S(1)}, u32[]{:S(2)}, u32[]{:S(2)}) collective-permute-start(f32[64,1024]{1,0:T(8,128)S(1)} %get-tuple-element.27.rest_0_.ofac), channel_id=1, source_target_pairs={{0,31},{1,18},{2,17},{3,20},{4,19},{5,22},{6,21},{7,24},{8,23},{9,... | collective-permute-start | bytes 786440 | tf_op jit(solution)/shard_map/ppermute | solution.py:611
  11.0 1.2 %coefs.1.ct = f32[4,544,128]{2,1,0:T(8,128)S(1)} custom-call(f32[3,8,64,1024]{3,2,1,0:T(8,128)S(1)} %copy-done, f32[8,64,1024]{2,1,0:T(8,128)S(1)} %copy-done.1), custom_call_target="tpu_custom_call" | custom-call | flops 20000000 | bytes 9000000 | tf_op jit(solution)/shard_map/coefs/pallas_call | solution.py:186
  12.2 0.0 collective-permute-done.after.rtail
  12.3 2.4 %collective-permute-start.3 = (f32[4,32,128]{2,1,0:T(8,128)S(1)}, f32[4,32,128]{2,1,0:T(8,128)S(1)}, u32[]{:S(2)}, u32[]{:S(2)}) collective-permute-start(f32[4,32,128]{2,1,0:T(8,128)S(1)} %get-tuple-element.30), channel_id=1, source_target_pairs={{0,1},{1,0},{2,3},{3,2},{4,5},{5,4},{6,7},{7,6},{8,9},{9,8},{10,11... | collective-permute-start | bytes 196616 | tf_op jit(solution)/shard_map/ppermute | solution.py:611
  14.6 0.0 collective-permute-start.5
  14.6 0.9 %collective-permute-done.3.after.w1 = f32[4,32,128]{2,1,0:T(8,128)S(1)} collective-permute-done((f32[4,32,128]{2,1,0:T(8,128)S(1)}, f32[4,32,128]{2,1,0:T(8,128)S(1)}, u32[]{:S(2)}, u32[]{:S(2)}) %collective-permute-start.3) | collective-permute-done | bytes 65568 | tf_op jit(solution)/shard_map/ppermute | solution.py:611
  15.5 2.0 %collective-permute-start.6 = (f32[4,32,128]{2,1,0:T(8,128)S(1)}, f32[4,32,128]{2,1,0:T(8,128)S(1)}, u32[]{:S(2)}, u32[]{:S(2)}) collective-permute-start(f32[4,32,128]{2,1,0:T(8,128)S(1)} %get-tuple-element.41), channel_id=1, source_target_pairs={{0,19},{1,18},{2,17},{3,16},{4,23},{5,22},{6,21},{7,20},{8,27},{9,... | collective-permute-start | bytes 196616 | tf_op jit(solution)/shard_map/ppermute | solution.py:611
  17.6 4.8 %interior.1 = (f32[6,64,1024]{2,1,0:T(8,128)S(1)}, f32[4,64,1024]{2,1,0:T(8,128)S(1)}, f32[512,128]{1,0:T(8,128)S(1)}, f32[512,128]{1,0:T(8,128)S(1)}, f32[8,64,128]{2,1,0:T(8,128)S(1)}) custom-call(f32[8,64,1024]{2,1,0:T(8,128)S(1)} %bitcast.5, f32[3,8,64,1024]{3,2,1,0:T(8,128)S(1)} %copy-done, f32[8,64,1024]{2,1,0:T(8,128)S(1)} %copy-done.1, ...), custom_call_target="tpu_custom_call" | custom-call | flops 60000000 | bytes 20000000 | tf_op jit(solution)/shard_map/interior/pallas_call | solution.py:279
  22.3 0.0 collective-permute-done.4.rnear
  22.4 0.4 finish_near.1
  22.8 0.0 collective-permute-done.2.rfac
  22.8 0.0 collective-permute-done.1.rfar
  22.8 0.8 %finish.1 = (f32[2,64,1024]{2,1,0:T(8,128)S(1)}, f32[536,128]{1,0:T(8,128)S(1)}, f32[512,128]{1,0:T(8,128)S(1)}) custom-call(f32[80,1024]{1,0:T(8,128)S(1)} %collective-permute-done.after.rtail, f32[144,1024]{1,0:T(8,128)S(1)} %collective-permute-done.1.rfar, f32[64,1024]{1,0:T(8,128)S(1)} %collective-permute-done.2.rfac, ...), custom_call_target="tpu_custom_call" | custom-call | tf_op jit(solution)/shard_map/finish/pallas_call | solution.py:384
  23.6 0.0 collective-permute-done.5.w2
  23.6 0.0 collective-permute-done.6.w3
  23.6 0.1 spread.1
  23.7 16.8 %all_to_all.10.got = f32[32,32,128]{2,1,0:T(8,128)S(1)} all-to-all(f32[32,32,128]{2,1,0:T(8,128)S(1)} %get-tuple-element.42), channel_id=1, replica_groups=mesh['tm'=8,'px'=4,'pz'=2,'core'=2] {'tm','pz','core'}, dimensions={0} | all-to-all | bytes 1048576 | tf_op jit(solution)/shard_map/all_to_all | solution.py:647
  40.5 0.1 pick.1
  40.6 0.6 collective-permute-start.7
  41.2 1.8 %collective-permute-start.8 = (f32[360,128]{1,0:T(8,128)S(1)}, f32[360,128]{1,0:T(8,128)S(1)}, u32[]{:S(2)}, u32[]{:S(2)}) collective-permute-start(f32[360,128]{1,0:T(8,128)S(1)} %get-tuple-element.45), channel_id=1, source_target_pairs={{0,12},{4,8},{8,4},{12,0},{1,13},{5,9},{9,5},{13,1},{2,14},{6,10},... | collective-permute-start | bytes 552968 | tf_op jit(solution)/shard_map/ppermute | solution.py:611
  43.1 4.0 %collective-permute-done.7.even = f32[360,128]{1,0:T(8,128)S(1)} collective-permute-done((f32[360,128]{1,0:T(8,128)S(1)}, f32[360,128]{1,0:T(8,128)S(1)}, u32[]{:S(2)}, u32[]{:S(2)}) %collective-permute-start.7) | collective-permute-done | bytes 184352 | tf_op jit(solution)/shard_map/ppermute | solution.py:611
  47.1 1.5 %collective-permute-done.8.odd = f32[360,128]{1,0:T(8,128)S(1)} collective-permute-done((f32[360,128]{1,0:T(8,128)S(1)}, f32[360,128]{1,0:T(8,128)S(1)}, u32[]{:S(2)}, u32[]{:S(2)}) %collective-permute-start.8) | collective-permute-done | bytes 184352 | tf_op jit(solution)/shard_map/ppermute | solution.py:611
  48.6 1.4 %chain.1 = f32[32,16,128]{2,1,0:T(8,128)S(1)} custom-call(f32[32,32,128]{2,1,0:T(8,128)S(1)} %all_to_all.10.got, f32[6,4,32,128]{3,2,1,0:T(8,128)S(1)} %prepare.1.own, f32[360,128]{1,0:T(8,128)S(1)} %collective-permute-done.7.even, f32[360,128]{1,0:T(8,128)S(1)} %collective-permute-done.8.odd), custom_call_target="tpu_custom_call" | custom-call | tf_op jit(solution)/shard_map/chain/pallas_call | solution.py:551
  50.0 13.0 %all_to_all.11 = f32[32,16,128]{2,1,0:T(8,128)S(1)} all-to-all(f32[32,16,128]{2,1,0:T(8,128)S(1)} %chain.1), channel_id=1, replica_groups=mesh['tm'=8,'px'=4,'pz'=2,'core'=2] {'tm','pz','core'}, dimensions={0} | all-to-all | bytes 524288 | tf_op jit(solution)/shard_map/all_to_all | solution.py:652
  63.0 1.9 %result.1 = f32[8,64,1024]{2,1,0:T(8,128)} custom-call(f32[512,128]{1,0:T(8,128)S(1)} %bitcast.6, f32[512,128]{1,0:T(8,128)S(1)} %get-tuple-element.46.gc, f32[6,64,1024]{2,1,0:T(8,128)S(1)} %get-tuple-element.31.fin, f32[2,64,1024]{2,1,0:T(8,128)S(1)} %get-tuple-element.47.near, f32[2,64,1024]{2,1,0:T(8,128)S(1)} %get-tuple-element.48.far), custom_call_target="tpu_custom_call" | custom-call | tf_op jit(solution)/shard_map/result/pallas_call | solution.py:595
  (2 shorter events, 0.1 us)
Async XLA Ops:
  0.0 5.3 %copy-start = (f32[3,8,64,1024]{3,2,1,0:T(8,128)S(1)}, f32[3,8,64,1024]{3,2,1,0:T(8,128)}, u32[]{:S(2)}) copy-start(f32[3,8,64,1024]{3,2,1,0:T(8,128)} %v.5) | copy-start | bytes 18874372
  0.0 5.3 %copy-start.1 = (f32[8,64,1024]{2,1,0:T(8,128)S(1)}, f32[8,64,1024]{2,1,0:T(8,128)}, u32[]{:S(2)}) copy-start(f32[8,64,1024]{2,1,0:T(8,128)} %d.5) | copy-start | bytes 6291460
  0.0 5.3 %copy-start.2 = (f32[1,8,64,1024]{3,2,1,0:T(8,128)S(1)}, f32[1,8,64,1024]{3,2,1,0:T(8,128)}, u32[]{:S(2)}) copy-start(f32[1,8,64,1024]{3,2,1,0:T(8,128)} %param.3) | copy-start | bytes 6291460
  2.1 20.6 %collective-permute-start.1 = (f32[144,1024]{1,0:T(8,128)S(1)}, f32[144,1024]{1,0:T(8,128)S(1)}, u32[]{:S(2)}, u32[]{:S(2)}) collective-permute-start(f32[144,1024]{1,0:T(8,128)S(1)} %get-tuple-element.29.ofar), channel_id=1, source_target_pairs={{0,15},{1,2},{2,1},{3,4},{4,3},{5,6},{6,5},{7,8},{8,7},{9,10},{10,... | collective-permute-start | bytes 1769480 | tf_op jit(solution)/shard_map/ppermute | solution.py:611
  6.1 16.3 %collective-permute-start.4 = (f32[128,1024]{1,0:T(8,128)S(1)}, f32[128,1024]{1,0:T(8,128)S(1)}, u32[]{:S(2)}, u32[]{:S(2)}) collective-permute-start(f32[128,1024]{1,0:T(8,128)S(1)} %get-tuple-element.36.onear), channel_id=1, source_target_pairs={{0,1},{1,0},{2,3},{3,2},{4,5},{5,4},{6,7},{7,6},{8,9},{9,8},{10,11... | collective-permute-start | bytes 1572872 | tf_op jit(solution)/shard_map/ppermute | solution.py:611
  8.2 4.0 %collective-permute-start = (f32[80,1024]{1,0:T(8,128)S(1)}, f32[80,1024]{1,0:T(8,128)S(1)}, u32[]{:S(2)}, u32[]{:S(2)}) collective-permute-start(f32[80,1024]{1,0:T(8,128)S(1)} %get-tuple-element.28.otail), channel_id=1, source_target_pairs={{0,1},{1,0},{2,3},{3,2},{4,5},{5,4},{6,7},{7,6},{8,9},{9,8},{10,11... | collective-permute-start | bytes 983048 | tf_op jit(solution)/shard_map/ppermute | solution.py:611
  8.3 14.5 %collective-permute-start.2 = (f32[64,1024]{1,0:T(8,128)S(1)}, f32[64,1024]{1,0:T(8,128)S(1)}, u32[]{:S(2)}, u32[]{:S(2)}) collective-permute-start(f32[64,1024]{1,0:T(8,128)S(1)} %get-tuple-element.27.rest_0_.ofac), channel_id=1, source_target_pairs={{0,31},{1,18},{2,17},{3,20},{4,19},{5,22},{6,21},{7,24},{8,23},{9,... | collective-permute-start | bytes 786440 | tf_op jit(solution)/shard_map/ppermute | solution.py:611
  12.3 3.3 %collective-permute-start.3 = (f32[4,32,128]{2,1,0:T(8,128)S(1)}, f32[4,32,128]{2,1,0:T(8,128)S(1)}, u32[]{:S(2)}, u32[]{:S(2)}) collective-permute-start(f32[4,32,128]{2,1,0:T(8,128)S(1)} %get-tuple-element.30), channel_id=1, source_target_pairs={{0,1},{1,0},{2,3},{3,2},{4,5},{5,4},{6,7},{7,6},{8,9},{9,8},{10,11... | collective-permute-start | bytes 196616 | tf_op jit(solution)/shard_map/ppermute | solution.py:611
  14.6 9.0 %collective-permute-start.5 = (f32[4,32,128]{2,1,0:T(8,128)S(1)}, f32[4,32,128]{2,1,0:T(8,128)S(1)}, u32[]{:S(2)}, u32[]{:S(2)}) collective-permute-start(f32[4,32,128]{2,1,0:T(8,128)S(1)} %get-tuple-element.40), channel_id=1, source_target_pairs={{0,18},{1,19},{2,16},{3,17},{4,22},{5,23},{6,20},{7,21},{8,26},{9,... | collective-permute-start | bytes 196616 | tf_op jit(solution)/shard_map/ppermute | solution.py:611
  15.5 8.1 %collective-permute-start.6 = (f32[4,32,128]{2,1,0:T(8,128)S(1)}, f32[4,32,128]{2,1,0:T(8,128)S(1)}, u32[]{:S(2)}, u32[]{:S(2)}) collective-permute-start(f32[4,32,128]{2,1,0:T(8,128)S(1)} %get-tuple-element.41), channel_id=1, source_target_pairs={{0,19},{1,18},{2,17},{3,16},{4,23},{5,22},{6,21},{7,20},{8,27},{9,... | collective-permute-start | bytes 196616 | tf_op jit(solution)/shard_map/ppermute | solution.py:611
  40.6 6.5 %collective-permute-start.7 = (f32[360,128]{1,0:T(8,128)S(1)}, f32[360,128]{1,0:T(8,128)S(1)}, u32[]{:S(2)}, u32[]{:S(2)}) collective-permute-start(f32[360,128]{1,0:T(8,128)S(1)} %get-tuple-element.44.after), channel_id=1, source_target_pairs={{0,4},{4,0},{8,12},{12,8},{1,5},{5,1},{9,13},{13,9},{2,6},{6,2},{1... | collective-permute-start | bytes 552968 | tf_op jit(solution)/shard_map/ppermute | solution.py:611
  41.2 7.4 %collective-permute-start.8 = (f32[360,128]{1,0:T(8,128)S(1)}, f32[360,128]{1,0:T(8,128)S(1)}, u32[]{:S(2)}, u32[]{:S(2)}) collective-permute-start(f32[360,128]{1,0:T(8,128)S(1)} %get-tuple-element.45), channel_id=1, source_target_pairs={{0,12},{4,8},{8,4},{12,0},{1,13},{5,9},{9,5},{13,1},{2,14},{6,10},... | collective-permute-start | bytes 552968 | tf_op jit(solution)/shard_map/ppermute | solution.py:611
